TPU v7x, 512 devices: a whole 4x8x8 slice. The times are simulated.
512 devices in a mesh: rows: 128 (over y, z, core), tilt: 4 (over x).
Axes of the slice: x: 4, y: 8, z: 8, core: 2. Of those that a mesh axis runs over, the one named last changes fastest.
Arguments:
- start: float32 [32, 2621440], P('tilt', 'rows'), may hold values from -6 to 6
- reward: float32 [2621440], P('rows'), may hold values from -1 to 1
- theta: float32 [32], P('tilt'), may hold values from -1 to 1
- kernels: bfloat16 [4, 512, 512], replicated, may hold values from -0.25 to 0.25
- rates: bfloat16 [5120, 12, 512], P('rows'), may hold values from 0.1 to 12, as said below
- pattern: int32 [5120, 12], P('rows'), may hold values from 0 to 5119, as said below
Outputs:
- iterate: float32 [32, 2621440], P('tilt', 'rows')
- growth: float32 [2, 32], P(None, 'tilt')
Inputs may be any that keep to these rules, and one draw needn't show every extreme that they name: `pattern`: entries 0 to 7 of block row i lie within 20 blocks of i, counted cyclically modulo 5120. Among the far entries (8 onward) of the 40 block rows of one index of rows, the blocks of any one index of rows are named exactly 2 times or not at all. Positive rates.
All inputs are finite; a program needn't handle non-finite values.
Results may differ from a plain program's by a relative error of at most 0.0033.
Values may be sent and summed in bfloat16 or wider, within the bound.
No kernel may reach another device: no remote copies, remote signals or barrier semaphores. Data moves between devices by JAX's collectives and lax.ppermute only.
A program may use at most 64 MiB of HBM per device.

v0:
```python
import jax
import jax.numpy as jnp
from jax import lax
from jax.sharding import PartitionSpec as P

NEAR = 8
ITERS = 2


def extended_2(array, sides, width):
    for axis, dim in sides:
        peers, length = (lax.axis_size(axis), array.shape[dim])
        up = [(i, (i + 1) % peers) for i in range(peers)]
        down = [(j, i) for i, j in up]
        last = lax.slice_in_dim(array, length - width, length, axis=dim)
        initial = lax.slice_in_dim(array, 0, width, axis=dim)
        before = lax.ppermute(last, axis, up)
        after = lax.ppermute(initial, axis, down)
        array = jnp.concatenate([before, array, after], axis=dim)
    return array


def on_device(start, reward, theta, kernels, rates, pattern):
    tilt_count = start.shape[0]
    blocks_here = pattern.shape[0]
    slot_count = pattern.shape[1]
    kind_count = kernels.shape[0]
    block_size = kernels.shape[1]
    peer_count = lax.axis_size("rows")
    position = lax.axis_index("rows")
    total_blocks = blocks_here * peer_count
    near_count = NEAR
    far_count = slot_count - near_count
    half_span = blocks_here // 2
    capacity = max(2, blocks_here * far_count // peer_count)
    local_rows = jnp.arange(blocks_here, dtype=jnp.int32)
    global_rows = position * blocks_here + local_rows
    near_cols = pattern[:, :near_count]
    shifts = (near_cols - global_rows[:, None] + half_span) % total_blocks - half_span
    near_index = local_rows[:, None] + shifts + half_span
    far_cols = pattern[:, near_count:]
    owners = (far_cols // blocks_here).reshape(-1)
    request_count = owners.shape[0]
    order_ids = jnp.arange(request_count, dtype=jnp.int32)
    earlier = order_ids[None, :] < order_ids[:, None]
    slot_rank = jnp.sum((owners[:, None] == owners[None, :]) & earlier, axis=1)
    every_far = lax.all_gather(far_cols, "rows", axis=0, tiled=True).reshape(
        peer_count, request_count
    )
    every_owner = every_far // blocks_here
    every_within = every_far % blocks_here
    every_rank = jnp.sum(
        (every_owner[:, :, None] == every_owner[:, None, :]) & earlier[None], axis=2
    )
    slot_ids = jnp.arange(capacity, dtype=jnp.int32)
    wanted = (every_owner == position)[:, :, None] & (
        every_rank[:, :, None] == slot_ids[None, None, :]
    )
    asked_blocks = jnp.sum(jnp.where(wanted, every_within[:, :, None], 0), axis=1)
    rates_full = rates.astype(jnp.float32)
    factor = jnp.exp(theta[:, None] * reward[None, :])
    iterate = start
    growth = []
    for iteration in range(ITERS):
        tilted = (factor * iterate).astype(jnp.bfloat16)
        extended = extended_2(tilted, (("rows", 1),), half_span * block_size)
        extended = extended.reshape(tilt_count, blocks_here + 2 * half_span, block_size)
        near_part = extended[:, near_index]
        local_blocks = tilted.reshape(tilt_count, blocks_here, block_size)
        outgoing = local_blocks[:, asked_blocks]
        arrived = lax.all_to_all(outgoing, "rows", split_axis=1, concat_axis=1, tiled=True)
        far_part = arrived[:, owners, slot_rank].reshape(
            tilt_count, blocks_here, far_count, block_size
        )
        columns = jnp.concatenate([near_part, far_part], axis=2)
        group_count = columns.shape[2] // kind_count
        columns_split = columns.reshape(
            tilt_count, blocks_here, group_count, kind_count, block_size
        )
        rate_split = rates_full.reshape(blocks_here, group_count, kind_count, block_size)
        summed = jnp.zeros((tilt_count, blocks_here, block_size), jnp.float32)
        for kind_index in range(kind_count):
            kernel_out = jnp.einsum(
                "tlmb,ba->tlma",
                columns_split[:, :, :, kind_index],
                kernels[kind_index],
                preferred_element_type=jnp.float32,
            )
            summed = summed + jnp.sum(kernel_out * rate_split[None, :, :, kind_index], axis=2)
        partial_value = jnp.sum(summed * summed, axis=(1, 2))
        total_squares = lax.psum(partial_value, "rows")
        norm_scale = jnp.sqrt(total_squares / (total_blocks * block_size) + 1e-06)
        iterate = summed.reshape(tilt_count, -1) / norm_scale[:, None]
        growth.append(jnp.log(norm_scale))
    return (iterate, jnp.stack(growth))


def solution(mesh):
    placed = (P("tilt", "rows"), P("rows"), P("tilt"), P(), P("rows", None, None), P("rows", None))
    return jax.shard_map(
        on_device,
        mesh=mesh,
        in_specs=placed,
        out_specs=(P("tilt", "rows"), P(None, "tilt")),
        check_vma=False,
    )
```

profile of v0, /device:TPU:1, one launch (start us, length us, event | category | flops | bytes accessed | tf_op | source)
XLA Modules:
  0.0 726.6 jit_solution(16111179661127006807)
XLA Ops:
  0.7 0.8 add_select_fusion.3
  1.4 58.6 %all-gather = s32[128,40,4]{1,2,0:T(4,128)S(1)} all-gather(s32[1,40,4]{1,2,0:T(4,128)S(1)} %get-tuple-element.27), channel_id=1, replica_groups=mesh['rows'=128,'tilt'=4] {'rows'}, dimensions={0}, use_global_device_ids=true | all-gather | bytes 82560 | tf_op jit(solution)/shard_map/all_gather | solution.py:47
  60.4 8.0 %convert_reduce_fusion = s32[128,160]{0,1:T(8,128)S(1)} fusion(s32[128,160]{0,1:T(8,128)S(1)} %get-tuple-element.7, pred[160,160]{1,0:T(8,128)(4,1)S(1)} %iota_compare_fusion.1), kind=kLoop, calls=%fused_computation.6 | loop fusion | flops 13086720 | bytes 189440 | tf_op jit(solution)/shard_map/reduce_sum | solution.py:52
  68.6 0.1 reshape.226
  68.8 0.2 multiply_convert_fusion.2
  68.9 2.1 gather_fusion.1
  71.1 8.5 %all-to-all-start = ((bf16[8,128,2,512]{3,0,2,1:T(8,128)(2,1)}), bf16[8,128,2,512]{3,0,2,1:T(8,128)(2,1)}, u32[]{:S(2)}, u32[]{:S(2)}) async-start(bf16[8,128,2,512]{3,0,2,1:T(8,128)(2,1)} %bitcast.10), calls=%async_computation | async-start | bytes 4194304 | tf_op jit(solution)/shard_map/all_to_all | solution.py:71
  79.6 3.5 collective-permute-start
  83.2 2.1 collective-permute-start.1
  85.6 0.2 convert_reduce_fusion.1
  86.0 0.8 slice_bitcast_fusion.3
  86.9 16.6 %collective-permute-done = bf16[8,10240]{1,0:T(8,128)(2,1)S(1)} collective-permute-done((bf16[8,10240]{1,0:T(8,128)(2,1)S(1)}, bf16[8,10240]{1,0:T(8,128)(2,1)S(1)}, u32[]{:S(2)}, u32[]{:S(2)}) %collective-permute-start) | collective-permute-done | bytes 163872 | tf_op jit(solution)/shard_map/ppermute | solution.py:17
  103.5 7.8 %collective-permute-done.1 = bf16[8,10240]{1,0:T(8,128)(2,1)S(1)} collective-permute-done((bf16[8,10240]{1,0:T(8,128)(2,1)S(1)}, bf16[8,10240]{1,0:T(8,128)(2,1)S(1)}, u32[]{:S(2)}, u32[]{:S(2)}) %collective-permute-start.1) | collective-permute-done | bytes 163872 | tf_op jit(solution)/shard_map/ppermute | solution.py:18
  111.4 3.0 gather_fusion
  114.4 17.2 %all-to-all-done = bf16[8,128,2,512]{3,0,2,1:T(8,128)(2,1)} async-done(((bf16[8,128,2,512]{3,0,2,1:T(8,128)(2,1)}), bf16[8,128,2,512]{3,0,2,1:T(8,128)(2,1)}, u32[]{:S(2)}, u32[]{:S(2)}) %all-to-all-start) | async-done | bytes 2097184 | tf_op jit(solution)/shard_map/all_to_all | solution.py:71
  131.6 4.5 gather_fusion.2
  136.1 1.7 pad_maximum_fusion
  137.8 0.3 fusion.28
  138.0 1.3 copy-done.9
  139.4 0.7 multiply_reduce_fusion.4
  140.1 0.7 multiply_reduce_fusion.5
  140.9 0.2 copy-done.5
  141.1 0.8 multiply_reduce_fusion.6
  141.8 0.8 multiply_reduce_fusion.7
  142.6 1.5 multiply_reduce_fusion.9
  144.1 250.5 %psum.14 = f32[8]{0:T(128)S(1)} all-reduce(f32[8]{0:T(128)S(1)} %get-tuple-element.4), channel_id=1, replica_groups=mesh['rows'=128,'tilt'=4] {'rows'}, use_global_device_ids=true, to_apply=%region_8.9 | all-reduce | flops 8 | bytes 64 | tf_op jit(solution)/shard_map/psum | solution.py:91
  394.6 0.2 multiply_convert_fusion.1
  394.8 1.9 collective-permute-start.2
  396.8 2.6 collective-permute-start.3
  399.3 0.2 multiply_convert_fusion
  399.5 2.1 gather_fusion.4
  401.7 13.2 %all-to-all-start.1 = ((bf16[8,128,2,512]{3,0,2,1:T(8,128)(2,1)}), bf16[8,128,2,512]{3,0,2,1:T(8,128)(2,1)}, u32[]{:S(2)}, u32[]{:S(2)}) async-start(bf16[8,128,2,512]{3,0,2,1:T(8,128)(2,1)} %bitcast.47), calls=%async_computation.1 | async-start | bytes 4194304 | tf_op jit(solution)/shard_map/all_to_all | solution.py:71
  414.9 3.0 gather_fusion.3
  417.9 48.7 %all-to-all-done.1 = bf16[8,128,2,512]{3,0,2,1:T(8,128)(2,1)} async-done(((bf16[8,128,2,512]{3,0,2,1:T(8,128)(2,1)}), bf16[8,128,2,512]{3,0,2,1:T(8,128)(2,1)}, u32[]{:S(2)}, u32[]{:S(2)}) %all-to-all-start.1) | async-done | bytes 2097184 | tf_op jit(solution)/shard_map/all_to_all | solution.py:71
  466.6 4.5 gather_fusion.5
  471.1 1.7 pad_maximum_fusion.1
  472.8 0.4 fusion.27
  473.2 0.5 copy-done.6
  473.7 0.8 copy-done.10
  474.5 0.7 multiply_reduce_fusion.2
  475.2 0.7 multiply_reduce_fusion.3
  476.0 0.7 multiply_reduce_fusion.1
  476.7 0.7 multiply_reduce_fusion
  477.5 0.3 multiply_reduce_fusion.8
  477.8 246.8 %psum.15 = f32[8]{0:T(128)S(1)} all-reduce(f32[8]{0:T(128)S(1)} %get-tuple-element.2), channel_id=1, replica_groups=mesh['rows'=128,'tilt'=4] {'rows'}, use_global_device_ids=true, to_apply=%region_14.15 | all-reduce | flops 8 | bytes 64 | tf_op jit(solution)/shard_map/psum | solution.py:91
  724.7 0.4 copy.187
  725.0 0.6 pad_maximum_fusion.4
  725.6 1.0 broadcast_divide_fusion
  (50 shorter events, 1.3 us)
Async XLA Ops:
  0.6 68.1 %copy-start.3 = (f32[8,20480]{1,0:T(8,128)S(1)}, f32[8,20480]{1,0:T(8,128)}, u32[]{:S(2)}) copy-start(f32[8,20480]{1,0:T(8,128)} %param.6) | copy-start | bytes 1966084
  0.6 68.1 %copy-start.2 = (f32[20480]{0:T(1024)S(1)}, f32[20480]{0:T(1024)}, u32[]{:S(2)}) copy-start(f32[20480]{0:T(1024)} %param.7) | copy-start | bytes 245764
  0.6 68.1 %copy-start.7 = (f32[8]{0:T(128)S(1)}, f32[8]{0:T(128)}, u32[]{:S(2)}) copy-start(f32[8]{0:T(128)} %param.8) | copy-start | bytes 100
  71.1 14.7 %copy-start.8 = (s32[40,12]{0,1:T(8,128)S(1)}, s32[40,12]{0,1:T(8,128)}, u32[]{:S(2)}) copy-start(s32[40,12]{0,1:T(8,128)} %param.11) | copy-start | bytes 5764
  71.1 14.8 %copy-start.4 = (bf16[40,12,512]{2,0,1:T(8,128)(2,1)S(1)}, bf16[40,12,512]{2,0,1:T(8,128)(2,1)}, u32[]{:S(2)}) copy-start(bf16[40,12,512]{2,0,1:T(8,128)(2,1)} %param.10) | copy-start | bytes 1474564
  71.1 60.5 %all-to-all-start = ((bf16[8,128,2,512]{3,0,2,1:T(8,128)(2,1)}), bf16[8,128,2,512]{3,0,2,1:T(8,128)(2,1)}, u32[]{:S(2)}, u32[]{:S(2)}) async-start(bf16[8,128,2,512]{3,0,2,1:T(8,128)(2,1)} %bitcast.10), calls=%async_computation | async-start | bytes 4194304 | tf_op jit(solution)/shard_map/all_to_all | solution.py:71
  79.6 23.9 %collective-permute-start = (bf16[8,10240]{1,0:T(8,128)(2,1)S(1)}, bf16[8,10240]{1,0:T(8,128)(2,1)S(1)}, u32[]{:S(2)}, u32[]{:S(2)}) collective-permute-start(bf16[8,10240]{1,0:T(8,128)(2,1)S(1)} %get-tuple-element.22), channel_id=1, source_target_pairs={{0,4},{4,8},{8,12},{12,16},{16,20},{20,24},{24,28},{28,32},{32,36}... | collective-permute-start | bytes 491528 | tf_op jit(solution)/shard_map/ppermute | solution.py:17
  83.2 28.2 %collective-permute-start.1 = (bf16[8,10240]{1,0:T(8,128)(2,1)S(1)}, bf16[8,10240]{1,0:T(8,128)(2,1)S(1)}, u32[]{:S(2)}, u32[]{:S(2)}) collective-permute-start(bf16[8,10240]{1,0:T(8,128)(2,1)S(1)} %get-tuple-element.23), channel_id=1, source_target_pairs={{4,0},{8,4},{12,8},{16,12},{20,16},{24,20},{28,24},{32,28},{36,32}... | collective-permute-start | bytes 491528 | tf_op jit(solution)/shard_map/ppermute | solution.py:18
  114.4 21.7 %copy-start.1 = (bf16[320,8,512]{2,1,0:T(8,128)(2,1)S(1)}, bf16[320,8,512]{2,1,0:T(8,128)(2,1)}, u32[]{:S(2)}) copy-start(bf16[320,8,512]{2,1,0:T(8,128)(2,1)} %gather_fusion) | copy-start | bytes 7864324
  137.8 1.6 copy-start.9
  140.1 0.9 copy-start.5
  394.8 20.0 %collective-permute-start.2 = (bf16[8,10240]{1,0:T(8,128)(2,1)S(1)}, bf16[8,10240]{1,0:T(8,128)(2,1)S(1)}, u32[]{:S(2)}, u32[]{:S(2)}) collective-permute-start(bf16[8,10240]{1,0:T(8,128)(2,1)S(1)} %get-tuple-element.20), channel_id=1, source_target_pairs={{0,4},{4,8},{8,12},{12,16},{16,20},{20,24},{24,28},{28,32},{32,36}... | collective-permute-start | bytes 491528 | tf_op jit(solution)/shard_map/ppermute | solution.py:17
  396.8 18.1 %collective-permute-start.3 = (bf16[8,10240]{1,0:T(8,128)(2,1)S(1)}, bf16[8,10240]{1,0:T(8,128)(2,1)S(1)}, u32[]{:S(2)}, u32[]{:S(2)}) collective-permute-start(bf16[8,10240]{1,0:T(8,128)(2,1)S(1)} %get-tuple-element.21), channel_id=1, source_target_pairs={{4,0},{8,4},{12,8},{16,12},{20,16},{24,20},{28,24},{32,28},{36,32}... | collective-permute-start | bytes 491528 | tf_op jit(solution)/shard_map/ppermute | solution.py:18
  401.7 65.0 %all-to-all-start.1 = ((bf16[8,128,2,512]{3,0,2,1:T(8,128)(2,1)}), bf16[8,128,2,512]{3,0,2,1:T(8,128)(2,1)}, u32[]{:S(2)}, u32[]{:S(2)}) async-start(bf16[8,128,2,512]{3,0,2,1:T(8,128)(2,1)} %bitcast.47), calls=%async_computation.1 | async-start | bytes 4194304 | tf_op jit(solution)/shard_map/all_to_all | solution.py:71
  417.9 53.1 %copy-start = (bf16[320,8,512]{2,1,0:T(8,128)(2,1)S(1)}, bf16[320,8,512]{2,1,0:T(8,128)(2,1)}, u32[]{:S(2)}) copy-start(bf16[320,8,512]{2,1,0:T(8,128)(2,1)} %gather_fusion.3) | copy-start | bytes 7864324
  472.8 0.9 copy-start.6
  472.8 1.7 copy-start.10
where the time goes:
time: 727 us
  blocking collectives  556 us (76%)
  waiting for transfers between devices  90.3 us (12%)
  starting transfers between devices  31.8 us (4%)
  local copies, waits for them, and re-layouts  24.8 us (3%)
  other arithmetic  16.8 us (2%)
    psum x2, blocking collectives, on_device(): total_squares = lax.psum(partial_value, 'rows')  497 us
    all_to_all x2, waiting for transfers between devices, on_device(): lax.all_to_all(outgoing, 'rows', split_axis=1, concat_axis=1, tiled=True)  65.9 us
    all_gather x1, blocking collectives, on_device(): lax.all_gather(far_cols, 'rows', axis=0, tiled=True)  58.6 us
    all_to_all x2, starting transfers between devices, on_device(): lax.all_to_all(outgoing, 'rows', split_axis=1, concat_axis=1, tiled=True)  21.7 us
    ppermute x2, waiting for transfers between devices, extended_2(): before = lax.ppermute(last, axis, up)  16.6 us
  transfers between devices with their start and end apart: 6, of which 4 were waited for; matrix products, arithmetic and copies ran while one was open for 1% of the time, Pallas kernels for 0%

commit v1 on v0

v1 whole, which is shorter than its diff:
```python
import jax
import jax.numpy as jnp
from jax import lax
from jax.sharding import PartitionSpec as P

NEAR = 8
ITERS = 2


def on_device(start, reward, theta, kernels, rates, pattern):
    tilt_count = start.shape[0]
    blocks_here, slot_count = pattern.shape
    kind_count, block_size = kernels.shape[0], kernels.shape[1]
    peer_count = lax.axis_size("rows")
    position = lax.axis_index("rows")
    total_blocks = blocks_here * peer_count
    far_count = slot_count - NEAR
    half_span = blocks_here // 2
    capacity = max(2, blocks_here * far_count // peer_count)
    local_rows = jnp.arange(blocks_here, dtype=jnp.int32)
    global_rows = position * blocks_here + local_rows
    shifts = (pattern[:, :NEAR] - global_rows[:, None] + half_span) % total_blocks - half_span
    near_index = local_rows[:, None] + shifts + half_span

    far_cols = pattern[:, NEAR:].reshape(-1)
    owners = far_cols // blocks_here
    within = far_cols % blocks_here
    order_ids = jnp.arange(far_cols.shape[0], dtype=jnp.int32)
    earlier = order_ids[None, :] < order_ids[:, None]
    slot_rank = jnp.sum((owners[:, None] == owners[None, :]) & earlier, axis=1)
    peers = jnp.arange(peer_count, dtype=jnp.int32)
    places = jnp.arange(capacity, dtype=jnp.int32)
    asks = (owners[:, None, None] == peers[None, :, None]) & (
        slot_rank[:, None, None] == places[None, None, :]
    )
    requests = jnp.sum(jnp.where(asks, within[:, None, None], 0), axis=0)
    asked_blocks = lax.all_to_all(requests, "rows", split_axis=0, concat_axis=0, tiled=True)
    far_index = (owners * capacity + slot_rank).reshape(blocks_here, far_count)

    up = [(i, (i + 1) % peer_count) for i in range(peer_count)]
    down = [(j, i) for i, j in up]
    rate_split = rates.astype(jnp.float32)
    factor = jnp.exp(theta[None, :, None] * reward.reshape(blocks_here, 1, block_size))

    def apply(columns, rate_part):
        groups = columns.shape[1] // kind_count
        columns = columns.reshape(blocks_here, groups, kind_count, tilt_count, block_size)
        rate_part = rate_part.reshape(blocks_here, groups, kind_count, 1, block_size)
        summed = 0.0
        for kind in range(kind_count):
            out = jnp.einsum(
                "lmtb,ba->lmta",
                columns[:, :, kind],
                kernels[kind],
                preferred_element_type=jnp.float32,
            )
            summed = summed + jnp.sum(out * rate_part[:, :, kind], axis=1)
        return summed

    mapped = start.reshape(tilt_count, blocks_here, block_size).transpose(1, 0, 2)
    squares = []
    for _ in range(ITERS):
        tilted = (factor * mapped).astype(jnp.bfloat16)
        before = lax.ppermute(tilted[blocks_here - half_span :], "rows", up)
        after = lax.ppermute(tilted[:half_span], "rows", down)
        outgoing = tilted[asked_blocks.reshape(-1)]
        arrived = lax.all_to_all(outgoing, "rows", split_axis=0, concat_axis=0, tiled=True)
        extended = jnp.concatenate([before, tilted, after], axis=0)
        near_sum = apply(extended[near_index], rate_split[:, :NEAR])
        far_sum = apply(arrived[far_index], rate_split[:, NEAR:])
        mapped = near_sum + far_sum
        squares.append(jnp.sum(mapped * mapped, axis=(0, 2)))

    partial = jnp.concatenate(squares)
    spread = jnp.broadcast_to(partial, (peer_count, partial.shape[0]))
    gathered = lax.all_to_all(spread, "rows", split_axis=0, concat_axis=0, tiled=True)
    totals = jnp.sum(gathered, axis=0).reshape(ITERS, tilt_count)
    states = total_blocks * block_size
    product = jnp.ones((tilt_count,), jnp.float32)
    growth = []
    for j in range(ITERS):
        scale = jnp.sqrt(totals[j] / product / product / states + 1e-06)
        product = product * scale
        growth.append(jnp.log(scale))
    iterate = mapped / product[None, :, None]
    return (iterate.transpose(1, 0, 2).reshape(tilt_count, -1), jnp.stack(growth))


def solution(mesh):
    placed = (P("tilt", "rows"), P("rows"), P("tilt"), P(), P("rows", None, None), P("rows", None))
    return jax.shard_map(
        on_device,
        mesh=mesh,
        in_specs=placed,
        out_specs=(P("tilt", "rows"), P(None, "tilt")),
        check_vma=False,
    )
```

time: 727 us -> 218 us (0.30)
  blocking collectives: 556 us -> 29.7 us
  starting transfers between devices: 31.8 us -> 56.7 us
  matrix products: 5.96 us -> 22.7 us
  waiting for transfers between devices: 90.3 us -> 78.2 us
  other arithmetic: 16.8 us -> 6.87 us
    psum x2 -> x0, blocking collectives: 497 us -> none  [on_device(): total_squares = lax.psum(partial_value, 'rows')]
    all_gather x1 -> x0, blocking collectives: 58.6 us -> none  [on_device(): lax.all_gather(far_cols, 'rows', axis=0, tiled=True)]
    all_to_all x2 -> x3, waiting for transfers between devices: 65.9 us -> 31.2 us  [the longest x2 22 us: on_device(): lax.all_to_all(outgoing, 'rows', split_axis=0, concat_axis=0, tiled=True)]
    all_to_all x0 -> x1, blocking collectives: none -> 29.7 us  [on_device(): lax.all_to_all(spread, 'rows', split_axis=0, concat_axis=0, tiled=True)]
    all_to_all x2 -> x3, starting transfers between devices: 21.7 us -> 45.8 us  [the longest x2 27.4 us: on_device(): lax.all_to_all(outgoing, 'rows', split_axis=0, concat_axis=0, tiled=True)]
    ppermute x4, waiting for transfers between devices: 24.4 us -> 47 us  [the longest x2 34.9 us: on_device(): before = lax.ppermute(tilted[blocks_here - half_span:], 'rows', up)]
    dot_general x8 -> x16, matrix products: 5.96 us -> 22.7 us  [apply(): jnp.einsum('lmtb,ba->lmta', columns[:, :, kind], kernels[kind], preferred...]
    reduce_sum x4 -> x2, other arithmetic: 9.91 us -> 0.3 us  [the longest x1 0.15 us: on_device(): totals = jnp.sum(gathered, axis=0).reshape(ITERS, tilt_count)]
  transfers between devices with their start and end apart: 6 -> 7, of which waited for: 4 -> 7; matrix products, arithmetic and copies ran while one was open for 1% -> 12% of each run, Pallas kernels for 0% -> 0%
where the time goes in v1:
time: 218 us; the launch traced here: 217 us
  waiting for transfers between devices  78.2 us (36%)
  starting transfers between devices  56.7 us (26%)
  blocking collectives  29.7 us (14%)
  matrix products  22.7 us (10%)
  local copies, waits for them, and re-layouts  21.9 us (10%)
  other arithmetic  6.87 us (3%)
    ppermute x2, waiting for transfers between devices, on_device(): before = lax.ppermute(tilted[blocks_here - half_span:], 'rows', up)  34.9 us
    all_to_all x1, blocking collectives, on_device(): lax.all_to_all(spread, 'rows', split_axis=0, concat_axis=0, tiled=True)  29.7 us
    all_to_all x2, starting transfers between devices, on_device(): lax.all_to_all(outgoing, 'rows', split_axis=0, concat_axis=0, tiled=True)  27.4 us
    dot_general x16, matrix products, apply(): jnp.einsum('lmtb,ba->lmta', columns[:, :, kind], kernels[kind], preferred...  22.7 us
    all_to_all x2, waiting for transfers between devices, on_device(): lax.all_to_all(outgoing, 'rows', split_axis=0, concat_axis=0, tiled=True)  22 us
    all_to_all x1, starting transfers between devices, on_device(): lax.all_to_all(requests, 'rows', split_axis=0, concat_axis=0, tiled=True)  18.4 us
    ppermute x2, waiting for transfers between devices, on_device(): after = lax.ppermute(tilted[:half_span], 'rows', down)  12.2 us
    all_to_all x1, waiting for transfers between devices, on_device(): lax.all_to_all(requests, 'rows', split_axis=0, concat_axis=0, tiled=True)  9.24 us
  transfers between devices with their start and end apart: 7, of which 7 were waited for; matrix products, arithmetic and copies ran while one was open for 12% of the time, Pallas kernels for 0%

profile of v1, /device:TPU:1, one launch (start us, length us, event | category | flops | bytes accessed | tf_op | source)
XLA Modules:
  0.0 217.4 jit_solution(8233949160602534900)
XLA Ops:
  0.6 0.7 slice.154
  2.2 0.7 copy.97
  3.0 18.4 %all-to-all-start = ((s32[128,1,2]{2,1,0:T(1,128)}), s32[128,1,2]{2,1,0:T(1,128)S(1)}, u32[]{:S(2)}, u32[]{:S(2)}) async-start(s32[128,1,2]{2,1,0:T(1,128)} %copy.97), calls=%async_computation | async-start | bytes 131072 | tf_op jit(solution)/shard_map/all_to_all | solution.py:37
  21.4 0.9 mul.187
  22.3 1.3 multiply_convert_fusion.1
  23.6 9.2 %all-to-all-done = s32[128,1,2]{2,1,0:T(1,128)S(1)} async-done(((s32[128,1,2]{2,1,0:T(1,128)}), s32[128,1,2]{2,1,0:T(1,128)S(1)}, u32[]{:S(2)}, u32[]{:S(2)}) %all-to-all-start) | async-done | bytes 1056 | tf_op jit(solution)/shard_map/all_to_all | solution.py:37
  32.9 0.5 broadcast.267
  33.4 0.8 reduce.4
  34.4 2.1 gather_fusion.1
  36.5 6.9 %all-to-all-start.1 = ((bf16[256,8,512]{2,1,0:T(8,128)(2,1)}), bf16[256,8,512]{2,1,0:T(8,128)(2,1)}, u32[]{:S(2)}, u32[]{:S(2)}) async-start(bf16[256,8,512]{2,1,0:T(8,128)(2,1)} %gather_fusion.1), calls=%async_computation.1 | async-start | bytes 4194304 | tf_op jit(solution)/shard_map/all_to_all | solution.py:67
  43.5 0.7 fusion.55
  44.2 3.5 %collective-permute-start = (bf16[20,8,512]{2,1,0:T(8,128)(2,1)}, bf16[20,8,512]{2,1,0:T(8,128)(2,1)S(1)}, u32[]{:S(2)}, u32[]{:S(2)}) collective-permute-start(bf16[20,8,512]{2,1,0:T(8,128)(2,1)} %get-tuple-element.16), channel_id=1, source_target_pairs={{0,4},{4,8},{8,12},{12,16},{16,20},{20,24},{24,28},{28,32},{32,36}... | collective-permute-start | bytes 491528 | tf_op jit(solution)/shard_map/ppermute | solution.py:64
  47.7 1.9 collective-permute-start.1
  50.3 0.8 slice_bitcast_fusion.36
  51.8 16.4 %collective-permute-done = bf16[20,8,512]{2,1,0:T(8,128)(2,1)S(1)} collective-permute-done((bf16[20,8,512]{2,1,0:T(8,128)(2,1)}, bf16[20,8,512]{2,1,0:T(8,128)(2,1)S(1)}, u32[]{:S(2)}, u32[]{:S(2)}) %collective-permute-start) | collective-permute-done | bytes 163872 | tf_op jit(solution)/shard_map/ppermute | solution.py:64
  68.2 0.7 copy-done.25
  68.9 4.4 %collective-permute-done.1 = bf16[20,8,512]{2,1,0:T(8,128)(2,1)} collective-permute-done((bf16[20,8,512]{2,1,0:T(8,128)(2,1)}, bf16[20,8,512]{2,1,0:T(8,128)(2,1)}, u32[]{:S(2)}, u32[]{:S(2)}) %collective-permute-start.1) | collective-permute-done | bytes 163872 | tf_op jit(solution)/shard_map/ppermute | solution.py:65
  73.2 1.1 pad_maximum_fusion
  74.3 3.0 %gather_fusion = bf16[320,8,512]{2,1,0:T(8,128)(2,1)} fusion(bf16[80,8,512]{2,1,0:T(8,128)(2,1)S(1)} %pad_maximum_fusion, s32[1024]{0:T(1024)S(1)} %pad_clamp_fusion.2), kind=kCustom, calls=%fused_computation | custom fusion | bytes 5244160 | tf_op jit(solution)/shard_map/gather | solution.py:69
  77.4 2.6 %fusion.2 = f32[40,8,512]{2,1,0:T(8,128)} fusion(bf16[40,2,4,8,512]{4,3,2,1,0:T(8,128)(2,1)} %bitcast.192, f32[40,2,512]{2,1,0:T(2,128)S(1)} %get-tuple-element.27, bf16[4,512,512]{2,1,0:T(8,128)(2,1)S(1)} %copy-done), kind=kOutput, calls=%fused_computation.16 | convolution fusion | flops 336035840 | bytes 1998848 | tf_op jit(solution)/shard_map/lmtb,ba->lmta/dot_general | solution.py:51
  80.0 1.4 fusion.1
  81.4 1.4 fusion
  82.7 1.4 fusion.3
  84.1 11.5 %all-to-all-done.1 = bf16[256,8,512]{2,1,0:T(8,128)(2,1)} async-done(((bf16[256,8,512]{2,1,0:T(8,128)(2,1)}), bf16[256,8,512]{2,1,0:T(8,128)(2,1)}, u32[]{:S(2)}, u32[]{:S(2)}) %all-to-all-start.1) | async-done | bytes 2097184 | tf_op jit(solution)/shard_map/all_to_all | solution.py:67
  95.6 2.4 %gather_fusion.2 = bf16[160,8,512]{2,1,0:T(8,128)(2,1)S(1)} fusion(bf16[256,8,512]{2,1,0:T(8,128)(2,1)} %all-to-all-done.1, s32[1024]{0:T(1024)S(1)} %pad_clamp_fusion), kind=kCustom, calls=%fused_computation.2 | custom fusion | bytes 2622080 | tf_op jit(solution)/shard_map/gather | solution.py:70
  98.1 1.7 convolution_multiply_fusion.13
  99.8 1.2 convolution_multiply_fusion.14
  101.1 0.3 convolution_multiply_fusion.12
  101.5 1.7 multiply_reduce_fusion.1
  103.2 2.1 gather_fusion.4
  105.3 20.4 %all-to-all-start.2 = ((bf16[256,8,512]{2,1,0:T(8,128)(2,1)}), bf16[256,8,512]{2,1,0:T(8,128)(2,1)}, u32[]{:S(2)}, u32[]{:S(2)}) async-start(bf16[256,8,512]{2,1,0:T(8,128)(2,1)} %gather_fusion.4), calls=%async_computation.2 | async-start | bytes 4194304 | tf_op jit(solution)/shard_map/all_to_all | solution.py:67
  125.8 3.5 %collective-permute-start.2 = (bf16[20,8,512]{2,1,0:T(8,128)(2,1)S(1)}, bf16[20,8,512]{2,1,0:T(8,128)(2,1)S(1)}, u32[]{:S(2)}, u32[]{:S(2)}) collective-permute-start(bf16[20,8,512]{2,1,0:T(8,128)(2,1)S(1)} %get-tuple-element.10), channel_id=1, source_target_pairs={{0,4},{4,8},{8,12},{12,16},{16,20},{20,24},{24,28},{28,32},{32,36}... | collective-permute-start | bytes 491528 | tf_op jit(solution)/shard_map/ppermute | solution.py:64
  129.3 1.9 collective-permute-start.3
  131.3 18.4 %collective-permute-done.2 = bf16[20,8,512]{2,1,0:T(8,128)(2,1)S(1)} collective-permute-done((bf16[20,8,512]{2,1,0:T(8,128)(2,1)S(1)}, bf16[20,8,512]{2,1,0:T(8,128)(2,1)S(1)}, u32[]{:S(2)}, u32[]{:S(2)}) %collective-permute-start.2) | collective-permute-done | bytes 163872 | tf_op jit(solution)/shard_map/ppermute | solution.py:64
  149.7 7.8 %collective-permute-done.3 = bf16[20,8,512]{2,1,0:T(8,128)(2,1)S(1)} collective-permute-done((bf16[20,8,512]{2,1,0:T(8,128)(2,1)S(1)}, bf16[20,8,512]{2,1,0:T(8,128)(2,1)S(1)}, u32[]{:S(2)}, u32[]{:S(2)}) %collective-permute-start.3) | collective-permute-done | bytes 163872 | tf_op jit(solution)/shard_map/ppermute | solution.py:65
  157.6 3.0 %gather_fusion.3 = bf16[320,8,512]{2,1,0:T(8,128)(2,1)} fusion(bf16[80,8,512]{2,1,0:T(8,128)(2,1)S(1)} %pad_maximum_fusion.1, s32[1024]{0:T(1024)S(1)} %pad_clamp_fusion.2), kind=kCustom, calls=%fused_computation.3 | custom fusion | bytes 5244160 | tf_op jit(solution)/shard_map/gather | solution.py:69
  160.6 2.6 %fusion.6 = f32[40,8,512]{2,1,0:T(8,128)} fusion(bf16[40,2,4,8,512]{4,3,2,1,0:T(8,128)(2,1)} %bitcast.188, f32[40,2,512]{2,1,0:T(2,128)S(1)} %copy-done.24, bf16[4,512,512]{2,1,0:T(8,128)(2,1)S(1)} %copy-done), kind=kOutput, calls=%fused_computation.20 | convolution fusion | flops 336035840 | bytes 1998848 | tf_op jit(solution)/shard_map/lmtb,ba->lmta/dot_general | solution.py:51
  163.3 1.4 fusion.5
  164.6 1.4 fusion.4
  166.0 1.3 fusion.7
  167.3 10.5 %all-to-all-done.2 = bf16[256,8,512]{2,1,0:T(8,128)(2,1)} async-done(((bf16[256,8,512]{2,1,0:T(8,128)(2,1)}), bf16[256,8,512]{2,1,0:T(8,128)(2,1)}, u32[]{:S(2)}, u32[]{:S(2)}) %all-to-all-start.2) | async-done | bytes 2097184 | tf_op jit(solution)/shard_map/all_to_all | solution.py:67
  177.8 2.4 %gather_fusion.5 = bf16[160,8,512]{2,1,0:T(8,128)(2,1)S(1)} fusion(bf16[256,8,512]{2,1,0:T(8,128)(2,1)} %all-to-all-done.2, s32[1024]{0:T(1024)S(1)} %pad_clamp_fusion), kind=kCustom, calls=%fused_computation.5 | custom fusion | bytes 2622080 | tf_op jit(solution)/shard_map/gather | solution.py:70
  180.3 1.4 convolution_multiply_fusion.9
  181.7 1.2 convolution_multiply_fusion.10
  183.3 1.4 multiply_reduce_fusion
  184.8 29.7 %all_to_all.25 = f32[128,1,16]{2,1,0:T(1,128)S(1)} all-to-all(f32[128,1,16]{2,1,0:T(1,128)S(1)} %broadcast_in_dim.22), channel_id=1, replica_groups=mesh['rows'=128,'tilt'=4] {'rows'}, dimensions={0} | all-to-all | bytes 16384 | tf_op jit(solution)/shard_map/all_to_all | solution.py:76
  214.8 0.6 pad_maximum_fusion.2
  215.3 2.1 broadcast_divide_fusion
  (92 shorter events, 3.1 us)
Async XLA Ops:
  3.0 29.9 %all-to-all-start = ((s32[128,1,2]{2,1,0:T(1,128)}), s32[128,1,2]{2,1,0:T(1,128)S(1)}, u32[]{:S(2)}, u32[]{:S(2)}) async-start(s32[128,1,2]{2,1,0:T(1,128)} %copy.97), calls=%async_computation | async-start | bytes 131072 | tf_op jit(solution)/shard_map/all_to_all | solution.py:37
  22.3 14.2 %copy-start.5 = (f32[40,512]{1,0:T(8,128)}, f32[40,512]{1,0:T(8,128)S(1)}, u32[]{:S(2)}) copy-start(f32[40,512]{1,0:T(8,128)S(1)} %mul.187) | copy-start | bytes 245764
  36.5 13.3 %copy-start.2 = (bf16[40,12,512]{2,0,1:T(8,128)(2,1)S(1)}, bf16[40,12,512]{2,0,1:T(8,128)(2,1)}, u32[]{:S(2)}) copy-start(bf16[40,12,512]{2,0,1:T(8,128)(2,1)} %param.10) | copy-start | bytes 1474564
  36.5 59.1 %all-to-all-start.1 = ((bf16[256,8,512]{2,1,0:T(8,128)(2,1)}), bf16[256,8,512]{2,1,0:T(8,128)(2,1)}, u32[]{:S(2)}, u32[]{:S(2)}) async-start(bf16[256,8,512]{2,1,0:T(8,128)(2,1)} %gather_fusion.1), calls=%async_computation.1 | async-start | bytes 4194304 | tf_op jit(solution)/shard_map/all_to_all | solution.py:67
  43.5 6.5 %copy-start.26 = (s32[40,12]{0,1:T(8,128)S(1)}, s32[40,12]{0,1:T(8,128)}, u32[]{:S(2)}) copy-start(s32[40,12]{0,1:T(8,128)} %param.11) | copy-start | bytes 5764
  44.2 24.0 %collective-permute-start = (bf16[20,8,512]{2,1,0:T(8,128)(2,1)}, bf16[20,8,512]{2,1,0:T(8,128)(2,1)S(1)}, u32[]{:S(2)}, u32[]{:S(2)}) collective-permute-start(bf16[20,8,512]{2,1,0:T(8,128)(2,1)} %get-tuple-element.16), channel_id=1, source_target_pairs={{0,4},{4,8},{8,12},{12,16},{16,20},{20,24},{24,28},{28,32},{32,36}... | collective-permute-start | bytes 491528 | tf_op jit(solution)/shard_map/ppermute | solution.py:64
  47.7 25.5 %collective-permute-start.1 = (bf16[20,8,512]{2,1,0:T(8,128)(2,1)}, bf16[20,8,512]{2,1,0:T(8,128)(2,1)}, u32[]{:S(2)}, u32[]{:S(2)}) collective-permute-start(bf16[20,8,512]{2,1,0:T(8,128)(2,1)} %get-tuple-element.17), channel_id=1, source_target_pairs={{4,0},{8,4},{12,8},{16,12},{20,16},{24,20},{28,24},{32,28},{36,32}... | collective-permute-start | bytes 491528 | tf_op jit(solution)/shard_map/ppermute | solution.py:65
  51.3 28.7 %copy-start.19 = (f32[40,2,512]{2,1,0:T(2,128)}, f32[40,2,512]{2,1,0:T(2,128)S(1)}, u32[]{:S(2)}) copy-start(f32[40,2,512]{2,1,0:T(2,128)S(1)} %get-tuple-element.28) | copy-start | bytes 491524
  51.3 30.0 %copy-start.17 = (f32[40,2,512]{2,1,0:T(2,128)}, f32[40,2,512]{2,1,0:T(2,128)S(1)}, u32[]{:S(2)}) copy-start(f32[40,2,512]{2,1,0:T(2,128)S(1)} %get-tuple-element.29) | copy-start | bytes 491524
  51.6 25.7 %copy-start.23 = (f32[40,2,512]{2,1,0:T(2,128)}, f32[40,2,512]{2,1,0:T(2,128)S(1)}, u32[]{:S(2)}) copy-start(f32[40,2,512]{2,1,0:T(2,128)S(1)} %get-tuple-element.27) | copy-start | bytes 491524
  51.6 31.1 %copy-start.21 = (f32[40,2,512]{2,1,0:T(2,128)}, f32[40,2,512]{2,1,0:T(2,128)S(1)}, u32[]{:S(2)}) copy-start(f32[40,2,512]{2,1,0:T(2,128)S(1)} %get-tuple-element.26) | copy-start | bytes 491524
  68.2 0.7 copy-start.25
  74.3 3.0 %copy-start = (bf16[4,512,512]{2,1,0:T(8,128)(2,1)S(1)}, bf16[4,512,512]{2,1,0:T(8,128)(2,1)}, u32[]{:S(2)}) copy-start(bf16[4,512,512]{2,1,0:T(8,128)(2,1)} %param.9) | copy-start | bytes 6291460
  77.3 2.6 %copy-start.4 = (bf16[320,8,512]{2,1,0:T(8,128)(2,1)S(1)}, bf16[320,8,512]{2,1,0:T(8,128)(2,1)}, u32[]{:S(2)}) copy-start(bf16[320,8,512]{2,1,0:T(8,128)(2,1)} %gather_fusion) | copy-start | bytes 7864324
  98.0 3.4 %copy-start.1 = (bf16[160,8,512]{2,1,0:T(8,128)(2,1)}, bf16[160,8,512]{2,1,0:T(8,128)(2,1)S(1)}, u32[]{:S(2)}) copy-start(bf16[160,8,512]{2,1,0:T(8,128)(2,1)S(1)} %gather_fusion.2) | copy-start | bytes 3932164
  98.0 3.4 %copy-start.6 = (f32[40,512]{1,0:T(8,128)S(1)}, f32[40,512]{1,0:T(8,128)}, u32[]{:S(2)}) copy-start(f32[40,512]{1,0:T(8,128)} %copy-done.5) | copy-start | bytes 245764
  98.0 3.4 %copy-start.7 = (f32[40,512]{1,0:T(8,128)S(1)}, f32[40,512]{1,0:T(8,128)}, u32[]{:S(2)}) copy-start(f32[40,512]{1,0:T(8,128)} %get-tuple-element.12) | copy-start | bytes 245764
  98.1 3.4 %copy-start.13 = (f32[40,8,512]{2,1,0:T(8,128)S(1)}, f32[40,8,512]{2,1,0:T(8,128)}, u32[]{:S(2)}) copy-start(f32[40,8,512]{2,1,0:T(8,128)} %fusion.2) | copy-start | bytes 1966084
  98.1 3.4 %copy-start.14 = (f32[40,8,512]{2,1,0:T(8,128)S(1)}, f32[40,8,512]{2,1,0:T(8,128)}, u32[]{:S(2)}) copy-start(f32[40,8,512]{2,1,0:T(8,128)} %fusion.1) | copy-start | bytes 1966084
  98.1 3.4 %copy-start.15 = (f32[40,8,512]{2,1,0:T(8,128)S(1)}, f32[40,8,512]{2,1,0:T(8,128)}, u32[]{:S(2)}) copy-start(f32[40,8,512]{2,1,0:T(8,128)} %fusion) | copy-start | bytes 1966084
  98.1 3.4 %copy-start.16 = (f32[40,8,512]{2,1,0:T(8,128)S(1)}, f32[40,8,512]{2,1,0:T(8,128)}, u32[]{:S(2)}) copy-start(f32[40,8,512]{2,1,0:T(8,128)} %fusion.3) | copy-start | bytes 1966084
  98.1 3.4 %copy-start.27 = (f32[8]{0:T(128)S(1)}, f32[8]{0:T(128)}, u32[]{:S(2)}) copy-start(f32[8]{0:T(128)} %param.8) | copy-start | bytes 100
  105.3 72.5 %all-to-all-start.2 = ((bf16[256,8,512]{2,1,0:T(8,128)(2,1)}), bf16[256,8,512]{2,1,0:T(8,128)(2,1)}, u32[]{:S(2)}, u32[]{:S(2)}) async-start(bf16[256,8,512]{2,1,0:T(8,128)(2,1)} %gather_fusion.4), calls=%async_computation.2 | async-start | bytes 4194304 | tf_op jit(solution)/shard_map/all_to_all | solution.py:67
  125.8 23.9 %collective-permute-start.2 = (bf16[20,8,512]{2,1,0:T(8,128)(2,1)S(1)}, bf16[20,8,512]{2,1,0:T(8,128)(2,1)S(1)}, u32[]{:S(2)}, u32[]{:S(2)}) collective-permute-start(bf16[20,8,512]{2,1,0:T(8,128)(2,1)S(1)} %get-tuple-element.10), channel_id=1, source_target_pairs={{0,4},{4,8},{8,12},{12,16},{16,20},{20,24},{24,28},{28,32},{32,36}... | collective-permute-start | bytes 491528 | tf_op jit(solution)/shard_map/ppermute | solution.py:64
  129.3 28.2 %collective-permute-start.3 = (bf16[20,8,512]{2,1,0:T(8,128)(2,1)S(1)}, bf16[20,8,512]{2,1,0:T(8,128)(2,1)S(1)}, u32[]{:S(2)}, u32[]{:S(2)}) collective-permute-start(bf16[20,8,512]{2,1,0:T(8,128)(2,1)S(1)} %get-tuple-element.11), channel_id=1, source_target_pairs={{4,0},{8,4},{12,8},{16,12},{20,16},{24,20},{28,24},{32,28},{36,32}... | collective-permute-start | bytes 491528 | tf_op jit(solution)/shard_map/ppermute | solution.py:65
  157.6 3.0 %copy-start.24 = (f32[40,2,512]{2,1,0:T(2,128)S(1)}, f32[40,2,512]{2,1,0:T(2,128)}, u32[]{:S(2)}) copy-start(f32[40,2,512]{2,1,0:T(2,128)} %copy-done.23) | copy-start | bytes 491524
  157.6 5.7 %copy-start.20 = (f32[40,2,512]{2,1,0:T(2,128)S(1)}, f32[40,2,512]{2,1,0:T(2,128)}, u32[]{:S(2)}) copy-start(f32[40,2,512]{2,1,0:T(2,128)} %copy-done.19) | copy-start | bytes 491524
  160.6 2.6 %copy-start.3 = (bf16[320,8,512]{2,1,0:T(8,128)(2,1)S(1)}, bf16[320,8,512]{2,1,0:T(8,128)(2,1)}, u32[]{:S(2)}) copy-start(bf16[320,8,512]{2,1,0:T(8,128)(2,1)} %gather_fusion.3) | copy-start | bytes 7864324
  160.6 4.0 %copy-start.18 = (f32[40,2,512]{2,1,0:T(2,128)S(1)}, f32[40,2,512]{2,1,0:T(2,128)}, u32[]{:S(2)}) copy-start(f32[40,2,512]{2,1,0:T(2,128)} %copy-done.17) | copy-start | bytes 491524
  163.3 2.7 %copy-start.22 = (f32[40,2,512]{2,1,0:T(2,128)S(1)}, f32[40,2,512]{2,1,0:T(2,128)}, u32[]{:S(2)}) copy-start(f32[40,2,512]{2,1,0:T(2,128)} %copy-done.21) | copy-start | bytes 491524
  180.2 3.0 %copy-start.8 = (f32[40,512]{1,0:T(8,128)S(1)}, f32[40,512]{1,0:T(8,128)}, u32[]{:S(2)}) copy-start(f32[40,512]{1,0:T(8,128)} %get-tuple-element.12) | copy-start | bytes 245764
  180.2 3.0 %copy-start.9 = (f32[40,8,512]{2,1,0:T(8,128)S(1)}, f32[40,8,512]{2,1,0:T(8,128)}, u32[]{:S(2)}) copy-start(f32[40,8,512]{2,1,0:T(8,128)} %fusion.6) | copy-start | bytes 1966084
  180.2 3.0 %copy-start.10 = (f32[40,8,512]{2,1,0:T(8,128)S(1)}, f32[40,8,512]{2,1,0:T(8,128)}, u32[]{:S(2)}) copy-start(f32[40,8,512]{2,1,0:T(8,128)} %fusion.5) | copy-start | bytes 1966084
  180.3 3.0 %copy-start.11 = (f32[40,8,512]{2,1,0:T(8,128)S(1)}, f32[40,8,512]{2,1,0:T(8,128)}, u32[]{:S(2)}) copy-start(f32[40,8,512]{2,1,0:T(8,128)} %fusion.4) | copy-start | bytes 1966084
  180.3 3.0 %copy-start.12 = (f32[40,8,512]{2,1,0:T(8,128)S(1)}, f32[40,8,512]{2,1,0:T(8,128)}, u32[]{:S(2)}) copy-start(f32[40,8,512]{2,1,0:T(8,128)} %fusion.7) | copy-start | bytes 1966084

commit v2 on v1

v2 whole, which is shorter than its diff:
```python
import functools

import jax
import jax.numpy as jnp
from jax import lax
from jax.experimental import pallas as pl
from jax.experimental.pallas import tpu as pltpu
from jax.sharding import PartitionSpec as P

NEAR = 8
ITERS = 2
VMEM_LIMIT = 48 * 1024 * 1024


def pack_blocks(asked, tilted, out):
    def body(j, carry):
        out[j] = tilted[asked[j]]
        return carry

    lax.fori_loop(0, out.shape[0], body, 0, unroll=8)


def mapped_sum(index, source, kernels, rates, gathered, slots, first):
    kinds, size = kernels.shape[0], kernels.shape[1]
    rows = rates.shape[1]
    tilts = source.shape[1]
    total = None
    for slot in range(slots):

        def gather(pair, carry, slot=slot):
            low = source[index[2 * pair * slots + slot]]
            high = source[index[(2 * pair + 1) * slots + slot]]
            both = jnp.concatenate([low, high], axis=0)
            gathered[pl.ds(pl.multiple_of(pair * 2 * tilts, 2 * tilts), 2 * tilts), :] = both
            return carry

        lax.fori_loop(0, rows // 2, gather, 0, unroll=True)
        product = jnp.dot(
            gathered[...], kernels[slot % kinds], preferred_element_type=jnp.float32
        ).reshape(rows, tilts, size)
        term = product * rates[first + slot][:, None, :]
        total = term if total is None else total + term
    return total


def near_kernel(index, extended, kernels, rates, out, gathered):
    out[...] = mapped_sum(index, extended, kernels, rates, gathered, NEAR, 0)


def far_kernel(index, asked, arrived, kernels, rates, near, factor, tilted, outgoing, squares, gathered):
    slots = rates.shape[0] - NEAR
    total = mapped_sum(index, arrived, kernels, rates, gathered, slots, NEAR) + near[...]
    squares[...] = jnp.sum(total * total, axis=0)
    tilted[...] = (factor[...] * total).astype(jnp.bfloat16)
    pack_blocks(asked, tilted, outgoing)


def last_kernel(index, arrived, kernels, rates, near, mapped, squares, gathered):
    slots = rates.shape[0] - NEAR
    total = mapped_sum(index, arrived, kernels, rates, gathered, slots, NEAR) + near[...]
    squares[...] = jnp.sum(total * total, axis=0)
    for row in range(total.shape[0]):
        mapped[:, row * total.shape[2] : (row + 1) * total.shape[2]] = total[row]


def call(kernel, out_shape, scalars, arrays, scratch, flops):
    moved = sum(a.size * a.dtype.itemsize for a in (*arrays, *jax.tree.leaves(out_shape)))
    return pl.pallas_call(
        kernel,
        out_shape=out_shape,
        in_specs=[pl.BlockSpec(memory_space=pltpu.SMEM)] * len(scalars)
        + [pl.BlockSpec(memory_space=pltpu.VMEM)] * len(arrays),
        out_specs=jax.tree.map(lambda _: pl.BlockSpec(memory_space=pltpu.VMEM), out_shape),
        scratch_shapes=scratch,
        compiler_params=pltpu.CompilerParams(vmem_limit_bytes=VMEM_LIMIT),
        cost_estimate=pl.CostEstimate(flops=flops, bytes_accessed=moved, transcendentals=0),
    )(*scalars, *arrays)


def on_device(start, reward, theta, kernels, rates, pattern):
    tilt_count = start.shape[0]
    blocks_here, slot_count = pattern.shape
    block_size = kernels.shape[1]
    peer_count = lax.axis_size("rows")
    position = lax.axis_index("rows")
    total_blocks = blocks_here * peer_count
    far_count = slot_count - NEAR
    half_span = blocks_here // 2
    capacity = max(2, blocks_here * far_count // peer_count)

    far_cols = pattern[:, NEAR:].reshape(-1)
    owners = far_cols // blocks_here
    within = far_cols % blocks_here
    order_ids = jnp.arange(far_cols.shape[0], dtype=jnp.int32)
    earlier = order_ids[None, :] < order_ids[:, None]
    slot_rank = jnp.sum((owners[:, None] == owners[None, :]) & earlier, axis=1)
    peers = jnp.arange(peer_count, dtype=jnp.int32)
    places = jnp.arange(capacity, dtype=jnp.int32)
    asks = (owners[:, None, None] == peers[None, :, None]) & (
        slot_rank[:, None, None] == places[None, None, :]
    )
    requests = jnp.sum(jnp.where(asks, within[:, None, None], 0), axis=0)
    asked = lax.all_to_all(requests, "rows", split_axis=0, concat_axis=0, tiled=True).reshape(-1)
    far_index = owners * capacity + slot_rank

    local_rows = jnp.arange(blocks_here, dtype=jnp.int32)
    global_rows = position * blocks_here + local_rows
    shifts = (pattern[:, :NEAR] - global_rows[:, None] + half_span) % total_blocks - half_span
    near_index = (local_rows[:, None] + shifts + half_span).reshape(-1)

    up = [(i, (i + 1) % peer_count) for i in range(peer_count)]
    down = [(j, i) for i, j in up]
    rate_full = rates.transpose(1, 0, 2).astype(jnp.float32)
    factor = jnp.exp(theta[None, :, None] * reward.reshape(blocks_here, 1, block_size))

    block = (tilt_count, block_size)
    arrived_blocks = peer_count * capacity
    scratch = [pltpu.VMEM((blocks_here * tilt_count, block_size), jnp.bfloat16)]
    product_flops = 2 * blocks_here * tilt_count * block_size * block_size
    own_shape = jax.ShapeDtypeStruct((blocks_here, *block), jnp.float32)
    tilted_shape = jax.ShapeDtypeStruct((blocks_here, *block), jnp.bfloat16)
    outgoing_shape = jax.ShapeDtypeStruct((arrived_blocks, *block), jnp.bfloat16)
    squares_shape = jax.ShapeDtypeStruct(block, jnp.float32)
    mapped_shape = jax.ShapeDtypeStruct(start.shape, jnp.float32)

    tilted = factor * start.reshape(tilt_count, blocks_here, block_size).transpose(1, 0, 2)
    tilted = tilted.astype(jnp.bfloat16)
    squares = []
    for iteration in range(ITERS):
        before = lax.ppermute(tilted[blocks_here - half_span :], "rows", up)
        after = lax.ppermute(tilted[:half_span], "rows", down)
        if iteration == 0:
            before, after, asked = lax.optimization_barrier((before, after, asked))
            outgoing = call(pack_blocks, outgoing_shape, [asked], [tilted], [], 0)
        else:
            before, after, outgoing = lax.optimization_barrier((before, after, outgoing))
        arrived = lax.all_to_all(outgoing, "rows", split_axis=0, concat_axis=0, tiled=True)
        extended = jnp.concatenate([before, tilted, after], axis=0)
        near = call(
            near_kernel, own_shape, [near_index], [extended, kernels, rate_full], scratch, NEAR * product_flops
        )
        if iteration < ITERS - 1:
            tilted, outgoing, square = call(
                far_kernel,
                (tilted_shape, outgoing_shape, squares_shape),
                [far_index, asked],
                [arrived, kernels, rate_full, near, factor],
                scratch,
                far_count * product_flops,
            )
        else:
            mapped, square = call(
                last_kernel,
                (mapped_shape, squares_shape),
                [far_index],
                [arrived, kernels, rate_full, near],
                scratch,
                far_count * product_flops,
            )
        squares.append(jnp.sum(square, axis=1))

    partial = jnp.concatenate(squares)
    spread = jnp.broadcast_to(partial, (peer_count, partial.shape[0]))
    gathered = lax.all_to_all(spread, "rows", split_axis=0, concat_axis=0, tiled=True)
    totals = jnp.sum(gathered, axis=0).reshape(ITERS, tilt_count)
    states = total_blocks * block_size
    product = jnp.ones((tilt_count,), jnp.float32)
    growth = []
    for j in range(ITERS):
        scale = jnp.sqrt(totals[j] / product / product / states + 1e-06)
        product = product * scale
        growth.append(jnp.log(scale))
    return (mapped / product[:, None], jnp.stack(growth))


def solution(mesh):
    placed = (P("tilt", "rows"), P("rows"), P("tilt"), P(), P("rows", None, None), P("rows", None))
    return jax.shard_map(
        on_device,
        mesh=mesh,
        in_specs=placed,
        out_specs=(P("tilt", "rows"), P(None, "tilt")),
        check_vma=False,
    )
```

time: 218 us -> 211 us (0.968)
  matrix products: 22.7 us -> 0 us
  starting transfers between devices: 56.7 us -> 36.1 us
  waiting for transfers between devices: 78.2 us -> 95.9 us
  blocking collectives: 29.7 us -> 45.3 us
  Pallas kernels: 0 us -> 13.8 us
  local copies, waits for them, and re-layouts: 21.9 us -> 9.48 us
    all_to_all x2, waiting for transfers between devices: 22 us -> 93.6 us  [on_device(): lax.all_to_all(outgoing, 'rows', split_axis=0, concat_axis=0, tiled=True)]
    ppermute x2, waiting for transfers between devices: 34.9 us -> 1.18 us  [on_device(): before = lax.ppermute(tilted[blocks_here - half_span:], 'rows', up)]
    all_to_all x0 -> x1, blocking collectives: none -> 26.2 us  [on_device(): lax.all_to_all(requests, 'rows', split_axis=0, concat_axis=0, tiled=True)]
    dot_general x16 -> x0, matrix products: 22.7 us -> none  [apply(): jnp.einsum('lmtb,ba->lmta', columns[:, :, kind], kernels[kind], preferred...]
    all_to_all x1 -> x0, starting transfers between devices: 18.4 us -> none  [on_device(): lax.all_to_all(requests, 'rows', split_axis=0, concat_axis=0, tiled=True)]
    gather x6 -> x0, local copies, waits for them, and re-layouts: 15.2 us -> none  [the longest x2 6.05 us: on_device(): near_sum = apply(extended[near_index], rate_split[:, :NEAR])]
    pallas_call x0 -> x5, Pallas kernels: none -> 13.8 us  [call(): pl.pallas_call(kernel, out_shape=out_shape, in_specs=[pl.BlockSpec(memory...]
    ppermute x2, waiting for transfers between devices: 12.2 us -> 1.06 us  [on_device(): after = lax.ppermute(tilted[:half_span], 'rows', down)]
  transfers between devices with their start and end apart: 7 -> 6, of which waited for: 7 -> 4; matrix products, arithmetic and copies ran while one was open for 12% -> 3% of each run, Pallas kernels for 0% -> 2%
where the time goes in v2:
time: 211 us; the launch traced here: 210 us
  waiting for transfers between devices  95.9 us (45%)
  blocking collectives  45.3 us (21%)
  starting transfers between devices  36.1 us (17%)
  Pallas kernels  13.8 us (7%)
  local copies, waits for them, and re-layouts  9.48 us (4%)
  other arithmetic  8.95 us (4%)
    all_to_all x2, waiting for transfers between devices, on_device(): lax.all_to_all(outgoing, 'rows', split_axis=0, concat_axis=0, tiled=True)  93.6 us
    all_to_all x1, blocking collectives, on_device(): lax.all_to_all(requests, 'rows', split_axis=0, concat_axis=0, tiled=True)  26.2 us
    all_to_all x1, blocking collectives, on_device(): lax.all_to_all(spread, 'rows', split_axis=0, concat_axis=0, tiled=True)  19.1 us
    all_to_all x2, starting transfers between devices, on_device(): lax.all_to_all(outgoing, 'rows', split_axis=0, concat_axis=0, tiled=True)  19.1 us
    pallas_call x5, Pallas kernels, call(): pl.pallas_call(kernel, out_shape=out_shape, in_specs=[pl.BlockSpec(memory...  13.8 us
    ppermute x2, starting transfers between devices, on_device(): after = lax.ppermute(tilted[:half_span], 'rows', down)  11.4 us
    unnamed x26, local copies, waits for them, and re-layouts  6.95 us
    ppermute x2, starting transfers between devices, on_device(): before = lax.ppermute(tilted[blocks_here - half_span:], 'rows', up)  5.68 us
  transfers between devices with their start and end apart: 6, of which 4 were waited for; matrix products, arithmetic and copies ran while one was open for 3% of the time, Pallas kernels for 2%

profile of v2, /device:TPU:1, one launch (start us, length us, event | category | flops | bytes accessed | tf_op | source)
XLA Modules:
  0.0 210.4 jit_solution(9931933184612947720)
XLA Ops:
  0.6 0.9 mul.35
  1.6 2.2 %multiply_exponential_fusion = (f32[40,8,512]{2,1,0:T(8,128)}, bf16[40,8,512]{2,1,0:T(8,128)(2,1)S(1)}) fusion(f32[40,512]{1,0:T(8,128)S(1)} %mul.35, f32[8]{0:T(128)} %param.8, f32[40,8,512]{2,1,0:T(8,128)} %bitcast.10), kind=kLoop, calls=%fused_computation.4 | loop fusion | flops 491520 | bytes 1720352 | tf_op jit(solution)/shard_map/exp | solution.py:114
  3.7 8.8 %collective-permute-start.1 = (bf16[20,8,512]{2,1,0:T(8,128)(2,1)S(1)}, bf16[20,8,512]{2,1,0:T(8,128)(2,1)S(1)}, u32[]{:S(2)}, u32[]{:S(2)}) collective-permute-start(bf16[20,8,512]{2,1,0:T(8,128)(2,1)S(1)} %get-tuple-element.28), channel_id=1, source_target_pairs={{4,0},{8,4},{12,8},{16,12},{20,16},{24,20},{28,24},{32,28},{36,32}... | collective-permute-start | bytes 491528 | tf_op jit(solution)/shard_map/ppermute | solution.py:131
  12.5 1.9 collective-permute-start
  14.5 0.1 copy.21
  14.6 0.1 ne.66
  14.7 0.1 copy.22
  14.8 0.1 rem.42
  14.9 0.1 copy.23
  15.0 0.1 div.46
  15.1 0.2 convert_reduce_fusion
  15.3 0.1 iota_compare_fusion.1
  15.4 0.1 select_reduce_fusion
  15.6 0.1 copy.24
  15.7 26.2 %all_to_all.25 = s32[128,1,2]{2,1,0:T(1,128)S(1)} all-to-all(s32[128,1,2]{2,1,0:T(1,128)S(1)} %copy.24), channel_id=1, replica_groups=mesh['rows'=128,'tilt'=4] {'rows'}, dimensions={0} | all-to-all | bytes 2048 | tf_op jit(solution)/shard_map/all_to_all | solution.py:103
  41.9 0.5 broadcast.187
  42.4 0.8 reduce.4
  43.2 0.1 reshape.173.asked
  43.4 2.3 %shard_map.77 = bf16[256,8,512]{2,1,0:T(8,128)(2,1)} custom-call(s32[256]{0:T(256)S(1)} %reshape.173.asked, bf16[40,8,512]{2,1,0:T(8,128)(2,1)S(1)} %get-tuple-element.31.tilted), custom_call_target="tpu_custom_call" | custom-call | bytes 2424832 | tf_op jit(solution)/shard_map/pallas_call | solution.py:68
  45.7 6.8 %all-to-all-start.1 = ((bf16[256,8,512]{2,1,0:T(8,128)(2,1)}), bf16[256,8,512]{2,1,0:T(8,128)(2,1)}, u32[]{:S(2)}, u32[]{:S(2)}) async-start(bf16[256,8,512]{2,1,0:T(8,128)(2,1)} %shard_map.77), calls=%async_computation.1 | async-start | bytes 4194304 | tf_op jit(solution)/shard_map/all_to_all | solution.py:137
  52.6 0.1 reshape.174.index
  52.7 1.3 convert_bitcast_fusion.rates
  54.0 1.1 pad_maximum_fusion.extended
  55.1 2.3 %shard_map.78.near = f32[40,8,512]{2,1,0:T(8,128)S(1)} custom-call(s32[320]{0:T(512)S(1)} %reshape.174.index, bf16[80,8,512]{2,1,0:T(8,128)(2,1)S(1)} %pad_maximum_fusion.extended, bf16[4,512,512]{2,1,0:T(8,128)(2,1)S(1)} %copy-done, f32[12,40,512]{2,1,0:T(8,128)S(1)} %convert_bitcast_fusion.rates), custom_call_target="tpu_custom_call" | custom-call | flops 1342177280 | bytes 4390912 | tf_op jit(solution)/shard_map/pallas_call | solution.py:68
  57.4 0.8 copy-done.4
  58.2 46.2 %all-to-all-done.1.arrived = bf16[256,8,512]{2,1,0:T(8,128)(2,1)} async-done(((bf16[256,8,512]{2,1,0:T(8,128)(2,1)}), bf16[256,8,512]{2,1,0:T(8,128)(2,1)}, u32[]{:S(2)}, u32[]{:S(2)}) %all-to-all-start.1) | async-done | bytes 2097184 | tf_op jit(solution)/shard_map/all_to_all | solution.py:137
  104.4 1.1 copy-done.2
  105.5 1.1 copy-done.5
  106.6 3.7 %shard_map.79 = (bf16[40,8,512]{2,1,0:T(8,128)(2,1)S(1)}, bf16[256,8,512]{2,1,0:T(8,128)(2,1)S(1)}, f32[8,512]{1,0:T(8,128)S(1)}) custom-call(s32[160]{0:T(256)S(1)} %multiply_add_fusion.index, s32[256]{0:T(256)S(1)} %reshape.173.asked, bf16[256,8,512]{2,1,0:T(8,128)(2,1)} %all-to-all-done.1.arrived, bf16[4,512,512]{2,1,0:T(8,128)(2,1)} %kernels.7, ...), custom_call_target="tpu_custom_call" | custom-call | flops 671088640 | bytes 8929280 | tf_op jit(solution)/shard_map/pallas_call | solution.py:68
  110.3 1.3 copy-done.3
  111.6 2.6 %collective-permute-start.3 = (bf16[20,8,512]{2,1,0:T(8,128)(2,1)S(1)}, bf16[20,8,512]{2,1,0:T(8,128)(2,1)S(1)}, u32[]{:S(2)}, u32[]{:S(2)}) collective-permute-start(bf16[20,8,512]{2,1,0:T(8,128)(2,1)S(1)} %get-tuple-element.26), channel_id=1, source_target_pairs={{4,0},{8,4},{12,8},{16,12},{20,16},{24,20},{28,24},{32,28},{36,32}... | collective-permute-start | bytes 491528 | tf_op jit(solution)/shard_map/ppermute | solution.py:131
  114.3 3.8 %collective-permute-start.2 = (bf16[20,8,512]{2,1,0:T(8,128)(2,1)S(1)}, bf16[20,8,512]{2,1,0:T(8,128)(2,1)S(1)}, u32[]{:S(2)}, u32[]{:S(2)}) collective-permute-start(bf16[20,8,512]{2,1,0:T(8,128)(2,1)S(1)} %get-tuple-element.27), channel_id=1, source_target_pairs={{0,4},{4,8},{8,12},{12,16},{16,20},{20,24},{24,28},{28,32},{32,36}... | collective-permute-start | bytes 491528 | tf_op jit(solution)/shard_map/ppermute | solution.py:130
  118.0 1.1 collective-permute-done.3
  119.1 1.2 collective-permute-done.2
  120.3 0.7 copy-done.11
  120.9 12.2 %all-to-all-start.2 = ((bf16[256,8,512]{2,1,0:T(8,128)(2,1)}), bf16[256,8,512]{2,1,0:T(8,128)(2,1)}, u32[]{:S(2)}, u32[]{:S(2)}) async-start(bf16[256,8,512]{2,1,0:T(8,128)(2,1)} %copy-done.3), calls=%async_computation.2 | async-start | bytes 4194304 | tf_op jit(solution)/shard_map/all_to_all | solution.py:137
  133.2 0.1 reduce_sum.47
  133.3 1.1 pad_maximum_fusion.1.extended
  134.4 2.3 %shard_map.80.near = f32[40,8,512]{2,1,0:T(8,128)S(1)} custom-call(s32[320]{0:T(512)S(1)} %reshape.174.index, bf16[80,8,512]{2,1,0:T(8,128)(2,1)S(1)} %pad_maximum_fusion.1.extended, bf16[4,512,512]{2,1,0:T(8,128)(2,1)S(1)} %copy-done.1, f32[12,40,512]{2,1,0:T(8,128)S(1)} %convert_bitcast_fusion.rates), custom_call_target="tpu_custom_call" | custom-call | flops 1342177280 | bytes 4390912 | tf_op jit(solution)/shard_map/pallas_call | solution.py:68
  136.7 0.8 copy-done.6
  137.5 47.4 %all-to-all-done.2.arrived = bf16[256,8,512]{2,1,0:T(8,128)(2,1)} async-done(((bf16[256,8,512]{2,1,0:T(8,128)(2,1)}), bf16[256,8,512]{2,1,0:T(8,128)(2,1)}, u32[]{:S(2)}, u32[]{:S(2)}) %all-to-all-start.2) | async-done | bytes 2097184 | tf_op jit(solution)/shard_map/all_to_all | solution.py:137
  185.0 1.1 copy-done.7
  186.1 3.2 %shard_map.81 = (f32[8,20480]{1,0:T(8,128)S(1)}, f32[8,512]{1,0:T(8,128)S(1)}) custom-call(s32[160]{0:T(256)S(1)} %multiply_add_fusion.index, bf16[256,8,512]{2,1,0:T(8,128)(2,1)} %all-to-all-done.2.arrived, bf16[4,512,512]{2,1,0:T(8,128)(2,1)} %kernels.7, f32[12,40,512]{2,1,0:T(8,128)S(1)} %convert_bitcast_fusion.rates, f32[40,8,512]{2,1,0:T(8,128)S(1)} %copy-done.7), custom_call_target="tpu_custom_call" | custom-call | flops 671088640 | bytes 6504448 | tf_op jit(solution)/shard_map/pallas_call | solution.py:68
  189.3 0.1 reduce_sum.48
  189.5 19.1 %all_to_all.26 = f32[128,1,16]{2,1,0:T(1,128)S(1)} all-to-all(f32[128,1,16]{2,1,0:T(1,128)S(1)} %broadcast_in_dim.12), channel_id=1, replica_groups=mesh['rows'=128,'tilt'=4] {'rows'}, dimensions={0} | all-to-all | bytes 16384 | tf_op jit(solution)/shard_map/all_to_all | solution.py:164
  208.7 0.2 reduce_sum.49
  208.9 0.6 pad_maximum_fusion.2
  209.5 1.0 broadcast_divide_fusion
  (35 shorter events, 0.4 us)
Async XLA Ops:
  0.6 13.8 %copy-start.12 = (s32[40,12]{0,1:T(8,128)S(1)}, s32[40,12]{0,1:T(8,128)}, u32[]{:S(2)}) copy-start(s32[40,12]{0,1:T(8,128)} %param.11) | copy-start | bytes 5764
  3.7 39.6 %collective-permute-start.1 = (bf16[20,8,512]{2,1,0:T(8,128)(2,1)S(1)}, bf16[20,8,512]{2,1,0:T(8,128)(2,1)S(1)}, u32[]{:S(2)}, u32[]{:S(2)}) collective-permute-start(bf16[20,8,512]{2,1,0:T(8,128)(2,1)S(1)} %get-tuple-element.28), channel_id=1, source_target_pairs={{4,0},{8,4},{12,8},{16,12},{20,16},{24,20},{28,24},{32,28},{36,32}... | collective-permute-start | bytes 491528 | tf_op jit(solution)/shard_map/ppermute | solution.py:131
  12.5 30.8 %collective-permute-start = (bf16[20,8,512]{2,1,0:T(8,128)(2,1)S(1)}, bf16[20,8,512]{2,1,0:T(8,128)(2,1)S(1)}, u32[]{:S(2)}, u32[]{:S(2)}) collective-permute-start(bf16[20,8,512]{2,1,0:T(8,128)(2,1)S(1)} %get-tuple-element.29), channel_id=1, source_target_pairs={{0,4},{4,8},{8,12},{12,16},{16,20},{20,24},{24,28},{28,32},{32,36}... | collective-permute-start | bytes 491528 | tf_op jit(solution)/shard_map/ppermute | solution.py:130
  43.3 2.3 %copy-start.8 = (bf16[20,8,512]{2,1,0:T(8,128)(2,1)}, bf16[20,8,512]{2,1,0:T(8,128)(2,1)S(1)}, u32[]{:S(2)}) copy-start(bf16[20,8,512]{2,1,0:T(8,128)(2,1)S(1)} %collective-permute-done.1) | copy-start | bytes 491524
  43.3 9.4 %copy-start.9 = (bf16[20,8,512]{2,1,0:T(8,128)(2,1)}, bf16[20,8,512]{2,1,0:T(8,128)(2,1)S(1)}, u32[]{:S(2)}) copy-start(bf16[20,8,512]{2,1,0:T(8,128)(2,1)S(1)} %collective-permute-done) | copy-start | bytes 491524
  45.7 58.7 %all-to-all-start.1 = ((bf16[256,8,512]{2,1,0:T(8,128)(2,1)}), bf16[256,8,512]{2,1,0:T(8,128)(2,1)}, u32[]{:S(2)}, u32[]{:S(2)}) async-start(bf16[256,8,512]{2,1,0:T(8,128)(2,1)} %shard_map.77), calls=%async_computation.1 | async-start | bytes 4194304 | tf_op jit(solution)/shard_map/all_to_all | solution.py:137
  52.5 2.6 %copy-start = (bf16[4,512,512]{2,1,0:T(8,128)(2,1)S(1)}, bf16[4,512,512]{2,1,0:T(8,128)(2,1)}, u32[]{:S(2)}) copy-start(bf16[4,512,512]{2,1,0:T(8,128)(2,1)} %kernels.7) | copy-start | bytes 6291460
  57.4 0.8 copy-start.4
  104.4 1.1 copy-start.2
  105.5 1.1 copy-start.5
  110.3 1.3 copy-start.3
  111.6 7.4 %collective-permute-start.3 = (bf16[20,8,512]{2,1,0:T(8,128)(2,1)S(1)}, bf16[20,8,512]{2,1,0:T(8,128)(2,1)S(1)}, u32[]{:S(2)}, u32[]{:S(2)}) collective-permute-start(bf16[20,8,512]{2,1,0:T(8,128)(2,1)S(1)} %get-tuple-element.26), channel_id=1, source_target_pairs={{4,0},{8,4},{12,8},{16,12},{20,16},{24,20},{28,24},{32,28},{36,32}... | collective-permute-start | bytes 491528 | tf_op jit(solution)/shard_map/ppermute | solution.py:131
  114.3 6.0 %collective-permute-start.2 = (bf16[20,8,512]{2,1,0:T(8,128)(2,1)S(1)}, bf16[20,8,512]{2,1,0:T(8,128)(2,1)S(1)}, u32[]{:S(2)}, u32[]{:S(2)}) collective-permute-start(bf16[20,8,512]{2,1,0:T(8,128)(2,1)S(1)} %get-tuple-element.27), channel_id=1, source_target_pairs={{0,4},{4,8},{8,12},{12,16},{16,20},{20,24},{24,28},{28,32},{32,36}... | collective-permute-start | bytes 491528 | tf_op jit(solution)/shard_map/ppermute | solution.py:130
  119.1 1.2 copy-start.10
  120.3 0.7 copy-start.11
  120.9 13.5 %copy-start.1 = (bf16[4,512,512]{2,1,0:T(8,128)(2,1)S(1)}, bf16[4,512,512]{2,1,0:T(8,128)(2,1)}, u32[]{:S(2)}) copy-start(bf16[4,512,512]{2,1,0:T(8,128)(2,1)} %kernels.7) | copy-start | bytes 6291460
  120.9 64.0 %all-to-all-start.2 = ((bf16[256,8,512]{2,1,0:T(8,128)(2,1)}), bf16[256,8,512]{2,1,0:T(8,128)(2,1)}, u32[]{:S(2)}, u32[]{:S(2)}) async-start(bf16[256,8,512]{2,1,0:T(8,128)(2,1)} %copy-done.3), calls=%async_computation.2 | async-start | bytes 4194304 | tf_op jit(solution)/shard_map/all_to_all | solution.py:137
  136.7 0.8 copy-start.6
  185.0 1.1 copy-start.7

commit v3 on v2

v3 whole, which is shorter than its diff:
```python
import jax
import jax.numpy as jnp
from jax import lax
from jax.experimental import pallas as pl
from jax.experimental.pallas import tpu as pltpu
from jax.sharding import PartitionSpec as P

NEAR = 8
ITERS = 2
PACK_CHUNKS = 8
VMEM_LIMIT = 40 * 1024 * 1024


def pack_blocks(asked, tilted, staged, outgoing, sems):
    chunk = outgoing.shape[0] // PACK_CHUNKS
    copies = []
    for part in range(PACK_CHUNKS):

        def body(j, carry, part=part):
            staged[part * chunk + j] = tilted[asked[part * chunk + j]]
            return carry

        lax.fori_loop(0, chunk, body, 0, unroll=8)
        span = pl.ds(part * chunk, chunk)
        copies.append(pltpu.make_async_copy(staged.at[span], outgoing.at[span], sems.at[part]))
        copies[-1].start()
    for copy in copies:
        copy.wait()


def pack_kernel(asked, tilted, outgoing, staged, sems):
    pack_blocks(asked, tilted, staged, outgoing, sems)


def weighted(index, stride, slots, source, weights, rates, gathered):
    rows, size = rates.shape[1], rates.shape[2]
    tilts = source.shape[1]
    span = rows * tilts
    for n, slot in enumerate(slots):

        def gather(pair, carry, slot=slot, n=n):
            low = source[index[2 * pair * stride + slot]]
            high = source[index[(2 * pair + 1) * stride + slot]]
            at = pl.multiple_of(n * span + pair * 2 * tilts, 2 * tilts)
            gathered[pl.ds(at, 2 * tilts), :] = jnp.concatenate([low, high], axis=0)
            return carry

        lax.fori_loop(0, rows // 2, gather, 0, unroll=True)
    taken = gathered[: len(slots) * span, :]
    product = jnp.dot(taken, weights, preferred_element_type=jnp.float32)
    return product.reshape(len(slots), rows, tilts, size)


def map_blocks(near_index, far_index, before, own, after, arrived, kernels, rates, scratch):
    extended, far_blocks, weights, rate_buf, gathered, sems = scratch
    kinds = kernels.shape[0]
    rows, half = own.shape[0], before.shape[0]
    slot_count = rates.shape[0]
    far_count = slot_count - NEAR

    def fetch(src, dst, sem):
        copy = pltpu.make_async_copy(src, dst, sems.at[sem])
        copy.start()
        return copy

    pieces = [
        fetch(before, extended.at[pl.ds(0, half)], 0),
        fetch(own, extended.at[pl.ds(half, rows)], 1),
        fetch(after, extended.at[pl.ds(half + rows, half)], 2),
    ]
    kernel_copies = [fetch(kernels.at[0], weights.at[0], 3)]
    rate_copy = fetch(rates, rate_buf, 3 + kinds)
    kernel_copies += [fetch(kernels.at[k], weights.at[k], 3 + k) for k in range(1, kinds)]
    far_copy = fetch(arrived, far_blocks, 4 + kinds)
    for piece in pieces:
        piece.wait()

    total = None
    for kind in range(kinds):
        slots = range(kind, NEAR, kinds)
        kernel_copies[kind].wait()
        if kind == 0:
            rate_copy.wait()
        product = weighted(near_index, NEAR, slots, extended, weights[kind], rate_buf, gathered.at[kind % 2])
        for n, slot in enumerate(slots):
            term = product[n] * rate_buf[slot].astype(jnp.float32)[:, None, :]
            total = term if total is None else total + term
    far_copy.wait()
    for kind in range(kinds):
        slots = range(kind, far_count, kinds)
        product = weighted(far_index, far_count, slots, far_blocks, weights[kind], rate_buf, gathered.at[kind % 2])
        for n, slot in enumerate(slots):
            total = total + product[n] * rate_buf[NEAR + slot].astype(jnp.float32)[:, None, :]
    return total


def step_kernel(
    near_index, far_index, asked, before, own, after, arrived, kernels, rates, factor,
    tilted, outgoing, squares, staged, pack_sems, *scratch,
):
    total = map_blocks(near_index, far_index, before, own, after, arrived, kernels, rates, scratch)
    squares[...] = jnp.sum(total * total, axis=0)
    tilted[...] = (factor[...] * total).astype(jnp.bfloat16)
    pack_blocks(asked, tilted, staged, outgoing, pack_sems)


def last_kernel(
    near_index, far_index, before, own, after, arrived, kernels, rates, mapped, squares, *scratch
):
    total = map_blocks(near_index, far_index, before, own, after, arrived, kernels, rates, scratch)
    squares[...] = jnp.sum(total * total, axis=0)
    for row in range(total.shape[0]):
        mapped[:, row * total.shape[2] : (row + 1) * total.shape[2]] = total[row]


def call(kernel, outs, scalars, arrays, scratch, flops):
    place = {True: pl.BlockSpec(memory_space=pl.ANY), False: pl.BlockSpec(memory_space=pltpu.VMEM)}
    moved = sum(a.size * a.dtype.itemsize for a, _ in (*arrays, *outs))
    return pl.pallas_call(
        kernel,
        out_shape=[shape for shape, _ in outs],
        in_specs=[pl.BlockSpec(memory_space=pltpu.SMEM)] * len(scalars) + [place[far] for _, far in arrays],
        out_specs=[place[far] for _, far in outs],
        scratch_shapes=scratch,
        compiler_params=pltpu.CompilerParams(vmem_limit_bytes=VMEM_LIMIT),
        cost_estimate=pl.CostEstimate(flops=flops, bytes_accessed=moved, transcendentals=0),
    )(*scalars, *[array for array, _ in arrays])


def on_device(start, reward, theta, kernels, rates, pattern):
    tilt_count = start.shape[0]
    blocks_here, slot_count = pattern.shape
    block_size = kernels.shape[1]
    peer_count = lax.axis_size("rows")
    position = lax.axis_index("rows")
    total_blocks = blocks_here * peer_count
    far_count = slot_count - NEAR
    half_span = blocks_here // 2
    capacity = max(2, blocks_here * far_count // peer_count)

    far_cols = pattern[:, NEAR:].reshape(-1)
    owners = far_cols // blocks_here
    within = far_cols % blocks_here
    order_ids = jnp.arange(far_cols.shape[0], dtype=jnp.int32)
    earlier = order_ids[None, :] < order_ids[:, None]
    slot_rank = jnp.sum((owners[:, None] == owners[None, :]) & earlier, axis=1)
    peers = jnp.arange(peer_count, dtype=jnp.int32)
    places = jnp.arange(capacity, dtype=jnp.int32)
    asks = (owners[:, None, None] == peers[None, :, None]) & (
        slot_rank[:, None, None] == places[None, None, :]
    )
    requests = jnp.sum(jnp.where(asks, within[:, None, None], 0), axis=0)
    asked = lax.all_to_all(requests, "rows", split_axis=0, concat_axis=0, tiled=True).reshape(-1)
    far_index = owners * capacity + slot_rank

    local_rows = jnp.arange(blocks_here, dtype=jnp.int32)
    global_rows = position * blocks_here + local_rows
    shifts = (pattern[:, :NEAR] - global_rows[:, None] + half_span) % total_blocks - half_span
    near_index = (local_rows[:, None] + shifts + half_span).reshape(-1)

    up = [(i, (i + 1) % peer_count) for i in range(peer_count)]
    down = [(j, i) for i, j in up]
    rates_by_slot = rates.transpose(1, 0, 2)
    factor = jnp.exp(theta[None, :, None] * reward.reshape(blocks_here, 1, block_size))

    block = (tilt_count, block_size)
    arrived_blocks = peer_count * capacity
    tilted_shape = jax.ShapeDtypeStruct((blocks_here, *block), jnp.bfloat16)
    outgoing_shape = jax.ShapeDtypeStruct((arrived_blocks, *block), jnp.bfloat16)
    squares_shape = jax.ShapeDtypeStruct(block, jnp.float32)
    mapped_shape = jax.ShapeDtypeStruct(start.shape, jnp.float32)
    staging = [pltpu.VMEM(outgoing_shape.shape, jnp.bfloat16), pltpu.SemaphoreType.DMA((PACK_CHUNKS,))]
    kind_count = kernels.shape[0]
    gather_rows = max(NEAR, far_count) // kind_count * blocks_here * tilt_count
    scratch = [
        pltpu.VMEM((blocks_here + 2 * half_span, *block), jnp.bfloat16),
        pltpu.VMEM(outgoing_shape.shape, jnp.bfloat16),
        pltpu.VMEM(kernels.shape, jnp.bfloat16),
        pltpu.VMEM(rates_by_slot.shape, jnp.bfloat16),
        pltpu.VMEM((2, gather_rows, block_size), jnp.bfloat16),
        pltpu.SemaphoreType.DMA((5 + kind_count,)),
    ]
    map_flops = 2 * slot_count * blocks_here * tilt_count * block_size * block_size

    tilted = factor * start.reshape(tilt_count, blocks_here, block_size).transpose(1, 0, 2)
    tilted = tilted.astype(jnp.bfloat16)
    (outgoing,) = call(pack_kernel, [(outgoing_shape, True)], [asked], [(tilted, False)], staging, 0)
    squares = []
    for iteration in range(ITERS):
        arrived = lax.all_to_all(outgoing, "rows", split_axis=0, concat_axis=0, tiled=True)
        before = lax.ppermute(tilted[blocks_here - half_span :], "rows", up)
        after = lax.ppermute(tilted[:half_span], "rows", down)
        pieces = [(a, True) for a in (before, tilted, after, arrived, kernels, rates_by_slot)]
        if iteration < ITERS - 1:
            tilted, outgoing, square = call(
                step_kernel,
                [(tilted_shape, False), (outgoing_shape, True), (squares_shape, False)],
                [near_index, far_index, asked],
                [*pieces, (factor, False)],
                staging + scratch,
                map_flops,
            )
        else:
            mapped, square = call(
                last_kernel,
                [(mapped_shape, False), (squares_shape, False)],
                [near_index, far_index],
                pieces,
                scratch,
                map_flops,
            )
        squares.append(jnp.sum(square, axis=1))

    partial = jnp.concatenate(squares)
    spread = jnp.broadcast_to(partial, (peer_count, partial.shape[0]))
    gathered = lax.all_to_all(spread, "rows", split_axis=0, concat_axis=0, tiled=True)
    totals = jnp.sum(gathered, axis=0).reshape(ITERS, tilt_count)
    states = total_blocks * block_size
    product = jnp.ones((tilt_count,), jnp.float32)
    growth = []
    for j in range(ITERS):
        scale = jnp.sqrt(totals[j] / product / product / states + 1e-06)
        product = product * scale
        growth.append(jnp.log(scale))
    return (mapped / product[:, None], jnp.stack(growth))


def solution(mesh):
    placed = (P("tilt", "rows"), P("rows"), P("tilt"), P(), P("rows", None, None), P("rows", None))
    return jax.shard_map(
        on_device,
        mesh=mesh,
        in_specs=placed,
        out_specs=(P("tilt", "rows"), P(None, "tilt")),
        check_vma=False,
    )
```

time: 211 us -> 201 us (0.953)
  blocking collectives: 45.3 us -> 20.6 us
  starting transfers between devices: 36.1 us -> 45.1 us
  local copies, waits for them, and re-layouts: 9.48 us -> 15.2 us
  waiting for transfers between devices: 95.9 us -> 99.7 us
  other arithmetic: 8.95 us -> 6.03 us
    all_to_all x2, waiting for transfers between devices: 93.6 us -> 23.5 us  [on_device(): lax.all_to_all(outgoing, 'rows', split_axis=0, concat_axis=0, tiled=True)]
    ppermute x2, waiting for transfers between devices: 1.06 us -> 49.5 us  [on_device(): after = lax.ppermute(tilted[:half_span], 'rows', down)]
    all_to_all x1 -> x0, blocking collectives: 26.2 us -> none  [on_device(): lax.all_to_all(requests, 'rows', split_axis=0, concat_axis=0, tiled=True)]
    all_to_all x0 -> x1, starting transfers between devices: none -> 18.4 us  [on_device(): lax.all_to_all(requests, 'rows', split_axis=0, concat_axis=0, tiled=True)]
    ppermute x2, waiting for transfers between devices: 1.18 us -> 17.5 us  [on_device(): before = lax.ppermute(tilted[blocks_here - half_span:], 'rows', up)]
    all_to_all x0 -> x1, waiting for transfers between devices: none -> 9.25 us  [on_device(): lax.all_to_all(requests, 'rows', split_axis=0, concat_axis=0, tiled=True)]
    ppermute x2, starting transfers between devices: 11.4 us -> 5.7 us  [on_device(): after = lax.ppermute(tilted[:half_span], 'rows', down)]
    unnamed x26 -> x24, local copies, waits for them, and re-layouts: 6.95 us -> 11.3 us
  transfers between devices with their start and end apart: 6 -> 7, of which waited for: 4 -> 7; matrix products, arithmetic and copies ran while one was open for 3% -> 2% of each run, Pallas kernels for 2% -> 0%
where the time goes in v3:
time: 201 us; the launch traced here: 200 us
  waiting for transfers between devices  99.7 us (50%)
  starting transfers between devices  45.1 us (22%)
  blocking collectives  20.6 us (10%)
  local copies, waits for them, and re-layouts  15.2 us (8%)
  Pallas kernels  12.5 us (6%)
  other arithmetic  6.03 us (3%)
    ppermute x2, waiting for transfers between devices, on_device(): after = lax.ppermute(tilted[:half_span], 'rows', down)  49.5 us
    all_to_all x2, waiting for transfers between devices, on_device(): lax.all_to_all(outgoing, 'rows', split_axis=0, concat_axis=0, tiled=True)  23.5 us
    all_to_all x1, blocking collectives, on_device(): lax.all_to_all(spread, 'rows', split_axis=0, concat_axis=0, tiled=True)  20.6 us
    all_to_all x1, starting transfers between devices, on_device(): lax.all_to_all(requests, 'rows', split_axis=0, concat_axis=0, tiled=True)  18.4 us
    ppermute x2, waiting for transfers between devices, on_device(): before = lax.ppermute(tilted[blocks_here - half_span:], 'rows', up)  17.5 us
    all_to_all x2, starting transfers between devices, on_device(): lax.all_to_all(outgoing, 'rows', split_axis=0, concat_axis=0, tiled=True)  15.4 us
    pallas_call x3, Pallas kernels, call(): pl.pallas_call(kernel, out_shape=[shape for shape, _ in outs], in_specs=[...  12.5 us
    unnamed x24, local copies, waits for them, and re-layouts  11.3 us
  transfers between devices with their start and end apart: 7, of which 7 were waited for; matrix products, arithmetic and copies ran while one was open for 2% of the time, Pallas kernels for 0%

profile of v3, /device:TPU:1, one launch (start us, length us, event | category | flops | bytes accessed | tf_op | source)
XLA Modules:
  0.0 200.0 jit_solution(3781623174433560496)
XLA Ops:
  0.6 0.7 sign_compare_fusion
  1.3 0.7 slice_remainder_fusion
  2.0 0.1 copy.22
  2.1 0.1 ne.67
  2.3 0.1 rem.44
  2.7 0.2 convert_reduce_fusion
  3.0 0.1 select_reduce_fusion
  3.1 0.7 copy.25
  3.9 18.4 %all-to-all-start = ((s32[128,1,2]{2,1,0:T(1,128)}), s32[128,1,2]{2,1,0:T(1,128)S(1)}, u32[]{:S(2)}, u32[]{:S(2)}) async-start(s32[128,1,2]{2,1,0:T(1,128)} %copy.25), calls=%async_computation | async-start | bytes 131072 | tf_op jit(solution)/shard_map/all_to_all | solution.py:153
  22.3 0.9 mul.36
  23.2 1.3 multiply_exponential_fusion
  24.5 9.3 %all-to-all-done = s32[128,1,2]{2,1,0:T(1,128)S(1)} async-done(((s32[128,1,2]{2,1,0:T(1,128)}), s32[128,1,2]{2,1,0:T(1,128)S(1)}, u32[]{:S(2)}, u32[]{:S(2)}) %all-to-all-start) | async-done | bytes 1056 | tf_op jit(solution)/shard_map/all_to_all | solution.py:153
  33.7 0.5 broadcast.187
  34.2 0.8 reduce.4
  35.1 0.1 reshape.173.asked
  35.2 2.0 %shard_map.77 = bf16[256,8,512]{2,1,0:T(8,128)(2,1)} custom-call(s32[256]{0:T(256)S(1)} %reshape.173.asked, bf16[40,8,512]{2,1,0:T(8,128)(2,1)S(1)} %get-tuple-element.19.tilted.own), custom_call_target="tpu_custom_call" | custom-call | bytes 2424832 | tf_op jit(solution)/shard_map/pallas_call | solution.py:119
  37.2 5.8 %all-to-all-start.1 = ((bf16[256,8,512]{2,1,0:T(8,128)(2,1)}), bf16[256,8,512]{2,1,0:T(8,128)(2,1)S(1)}, u32[]{:S(2)}, u32[]{:S(2)}) async-start(bf16[256,8,512]{2,1,0:T(8,128)(2,1)} %shard_map.77), calls=%async_computation.1 | async-start | bytes 4194304 | tf_op jit(solution)/shard_map/all_to_all | solution.py:190
  43.0 0.7 fusion.5
  43.7 2.9 %collective-permute-start.1 = (bf16[20,8,512]{2,1,0:T(8,128)(2,1)}, bf16[20,8,512]{2,1,0:T(8,128)(2,1)S(1)}, u32[]{:S(2)}, u32[]{:S(2)}) collective-permute-start(bf16[20,8,512]{2,1,0:T(8,128)(2,1)} %get-tuple-element.16), channel_id=1, source_target_pairs={{4,0},{8,4},{12,8},{16,12},{20,16},{24,20},{28,24},{32,28},{36,32}... | collective-permute-start | bytes 491528 | tf_op jit(solution)/shard_map/ppermute | solution.py:192
  46.6 2.6 %collective-permute-start = (bf16[20,8,512]{2,1,0:T(8,128)(2,1)}, bf16[20,8,512]{2,1,0:T(8,128)(2,1)S(1)}, u32[]{:S(2)}, u32[]{:S(2)}) collective-permute-start(bf16[20,8,512]{2,1,0:T(8,128)(2,1)} %get-tuple-element.17), channel_id=1, source_target_pairs={{0,4},{4,8},{8,12},{12,16},{16,20},{20,24},{24,28},{28,32},{32,36}... | collective-permute-start | bytes 491528 | tf_op jit(solution)/shard_map/ppermute | solution.py:191
  49.5 23.7 %collective-permute-done.1.after = bf16[20,8,512]{2,1,0:T(8,128)(2,1)S(1)} collective-permute-done((bf16[20,8,512]{2,1,0:T(8,128)(2,1)}, bf16[20,8,512]{2,1,0:T(8,128)(2,1)S(1)}, u32[]{:S(2)}, u32[]{:S(2)}) %collective-permute-start.1) | collective-permute-done | bytes 163872 | tf_op jit(solution)/shard_map/ppermute | solution.py:192
  73.2 0.7 copy-done.5
  73.8 9.4 %collective-permute-done.before = bf16[20,8,512]{2,1,0:T(8,128)(2,1)S(1)} collective-permute-done((bf16[20,8,512]{2,1,0:T(8,128)(2,1)}, bf16[20,8,512]{2,1,0:T(8,128)(2,1)S(1)}, u32[]{:S(2)}, u32[]{:S(2)}) %collective-permute-start) | collective-permute-done | bytes 163872 | tf_op jit(solution)/shard_map/ppermute | solution.py:191
  83.2 0.7 copy-done.7
  83.9 11.6 %all-to-all-done.1.arrived = bf16[256,8,512]{2,1,0:T(8,128)(2,1)S(1)} async-done(((bf16[256,8,512]{2,1,0:T(8,128)(2,1)}), bf16[256,8,512]{2,1,0:T(8,128)(2,1)S(1)}, u32[]{:S(2)}, u32[]{:S(2)}) %all-to-all-start.1) | async-done | bytes 2097184 | tf_op jit(solution)/shard_map/all_to_all | solution.py:190
  95.5 1.6 copy-done.1
  97.1 1.0 copy-done.3
  98.1 0.9 copy-done.6
  99.0 0.9 copy-done.8
  99.9 5.7 %shard_map.78 = (bf16[40,8,512]{2,1,0:T(8,128)(2,1)S(1)}, bf16[256,8,512]{2,1,0:T(8,128)(2,1)S(1)}, f32[8,512]{1,0:T(8,128)S(1)}) custom-call(s32[320]{0:T(512)S(1)} %reshape.172.near_index, s32[160]{0:T(256)S(1)} %multiply_add_fusion.far_index, s32[256]{0:T(256)S(1)} %reshape.173.asked, bf16[20,8,512]{2,1,0:T(8,128)(2,1)S(1)} %copy-done.8, ...), custom_call_target="tpu_custom_call" | custom-call | flops 2013265920 | bytes 8437760 | tf_op jit(solution)/shard_map/pallas_call | solution.py:119
  105.6 1.3 copy-done
  106.9 9.6 %all-to-all-start.2 = ((bf16[256,8,512]{2,1,0:T(8,128)(2,1)}), bf16[256,8,512]{2,1,0:T(8,128)(2,1)S(1)}, u32[]{:S(2)}, u32[]{:S(2)}) async-start(bf16[256,8,512]{2,1,0:T(8,128)(2,1)} %copy-done), calls=%async_computation.2 | async-start | bytes 4194304 | tf_op jit(solution)/shard_map/all_to_all | solution.py:190
  116.6 2.8 %collective-permute-start.3 = (bf16[20,8,512]{2,1,0:T(8,128)(2,1)S(1)}, bf16[20,8,512]{2,1,0:T(8,128)(2,1)S(1)}, u32[]{:S(2)}, u32[]{:S(2)}) collective-permute-start(bf16[20,8,512]{2,1,0:T(8,128)(2,1)S(1)} %get-tuple-element.14), channel_id=1, source_target_pairs={{4,0},{8,4},{12,8},{16,12},{20,16},{24,20},{28,24},{32,28},{36,32}... | collective-permute-start | bytes 491528 | tf_op jit(solution)/shard_map/ppermute | solution.py:192
  119.4 2.9 %collective-permute-start.2 = (bf16[20,8,512]{2,1,0:T(8,128)(2,1)S(1)}, bf16[20,8,512]{2,1,0:T(8,128)(2,1)S(1)}, u32[]{:S(2)}, u32[]{:S(2)}) collective-permute-start(bf16[20,8,512]{2,1,0:T(8,128)(2,1)S(1)} %get-tuple-element.15), channel_id=1, source_target_pairs={{0,4},{4,8},{8,12},{12,16},{16,20},{20,24},{24,28},{28,32},{32,36}... | collective-permute-start | bytes 491528 | tf_op jit(solution)/shard_map/ppermute | solution.py:191
  122.4 0.1 reduce_sum.47
  122.5 25.8 %collective-permute-done.3.after = bf16[20,8,512]{2,1,0:T(8,128)(2,1)S(1)} collective-permute-done((bf16[20,8,512]{2,1,0:T(8,128)(2,1)S(1)}, bf16[20,8,512]{2,1,0:T(8,128)(2,1)S(1)}, u32[]{:S(2)}, u32[]{:S(2)}) %collective-permute-start.3) | collective-permute-done | bytes 163872 | tf_op jit(solution)/shard_map/ppermute | solution.py:192
  148.3 8.1 %collective-permute-done.2.before = bf16[20,8,512]{2,1,0:T(8,128)(2,1)S(1)} collective-permute-done((bf16[20,8,512]{2,1,0:T(8,128)(2,1)S(1)}, bf16[20,8,512]{2,1,0:T(8,128)(2,1)S(1)}, u32[]{:S(2)}, u32[]{:S(2)}) %collective-permute-start.2) | collective-permute-done | bytes 163872 | tf_op jit(solution)/shard_map/ppermute | solution.py:191
  156.4 0.7 copy-done.9
  157.1 11.9 %all-to-all-done.2.arrived = bf16[256,8,512]{2,1,0:T(8,128)(2,1)S(1)} async-done(((bf16[256,8,512]{2,1,0:T(8,128)(2,1)}), bf16[256,8,512]{2,1,0:T(8,128)(2,1)S(1)}, u32[]{:S(2)}, u32[]{:S(2)}) %all-to-all-start.2) | async-done | bytes 2097184 | tf_op jit(solution)/shard_map/all_to_all | solution.py:190
  168.9 1.6 copy-done.2
  170.5 1.0 copy-done.4
  171.6 0.9 copy-done.10
  172.5 4.9 %shard_map.79 = (f32[8,20480]{1,0:T(8,128)S(1)}, f32[8,512]{1,0:T(8,128)S(1)}) custom-call(s32[320]{0:T(512)S(1)} %reshape.172.near_index, s32[160]{0:T(256)S(1)} %multiply_add_fusion.far_index, bf16[20,8,512]{2,1,0:T(8,128)(2,1)S(1)} %copy-done.10, bf16[40,8,512]{2,1,0:T(8,128)(2,1)S(1)} %get-tuple-element.7.own, ...), custom_call_target="tpu_custom_call" | custom-call | flops 2013265920 | bytes 6012928 | tf_op jit(solution)/shard_map/pallas_call | solution.py:119
  177.4 0.1 reduce_sum.48
  177.6 20.6 %all_to_all.25 = f32[128,1,16]{2,1,0:T(1,128)S(1)} all-to-all(f32[128,1,16]{2,1,0:T(1,128)S(1)} %broadcast_in_dim.12), channel_id=1, replica_groups=mesh['rows'=128,'tilt'=4] {'rows'}, dimensions={0} | all-to-all | bytes 16384 | tf_op jit(solution)/shard_map/all_to_all | solution.py:216
  198.2 0.2 reduce_sum.49
  198.5 0.6 pad_maximum_fusion
  199.0 1.0 broadcast_divide_fusion
  (29 shorter events, 0.8 us)
Async XLA Ops:
  3.9 29.9 %all-to-all-start = ((s32[128,1,2]{2,1,0:T(1,128)}), s32[128,1,2]{2,1,0:T(1,128)S(1)}, u32[]{:S(2)}, u32[]{:S(2)}) async-start(s32[128,1,2]{2,1,0:T(1,128)} %copy.25), calls=%async_computation | async-start | bytes 131072 | tf_op jit(solution)/shard_map/all_to_all | solution.py:153
  37.2 12.1 %copy-start.11 = (s32[40,12]{0,1:T(8,128)S(1)}, s32[40,12]{0,1:T(8,128)}, u32[]{:S(2)}) copy-start(s32[40,12]{0,1:T(8,128)} %param.11) | copy-start | bytes 5764
  37.2 58.3 %all-to-all-start.1 = ((bf16[256,8,512]{2,1,0:T(8,128)(2,1)}), bf16[256,8,512]{2,1,0:T(8,128)(2,1)S(1)}, u32[]{:S(2)}, u32[]{:S(2)}) async-start(bf16[256,8,512]{2,1,0:T(8,128)(2,1)} %shard_map.77), calls=%async_computation.1 | async-start | bytes 4194304 | tf_op jit(solution)/shard_map/all_to_all | solution.py:190
  43.7 29.4 %collective-permute-start.1 = (bf16[20,8,512]{2,1,0:T(8,128)(2,1)}, bf16[20,8,512]{2,1,0:T(8,128)(2,1)S(1)}, u32[]{:S(2)}, u32[]{:S(2)}) collective-permute-start(bf16[20,8,512]{2,1,0:T(8,128)(2,1)} %get-tuple-element.16), channel_id=1, source_target_pairs={{4,0},{8,4},{12,8},{16,12},{20,16},{24,20},{28,24},{32,28},{36,32}... | collective-permute-start | bytes 491528 | tf_op jit(solution)/shard_map/ppermute | solution.py:192
  46.6 36.6 %collective-permute-start = (bf16[20,8,512]{2,1,0:T(8,128)(2,1)}, bf16[20,8,512]{2,1,0:T(8,128)(2,1)S(1)}, u32[]{:S(2)}, u32[]{:S(2)}) collective-permute-start(bf16[20,8,512]{2,1,0:T(8,128)(2,1)} %get-tuple-element.17), channel_id=1, source_target_pairs={{0,4},{4,8},{8,12},{12,16},{16,20},{20,24},{24,28},{28,32},{32,36}... | collective-permute-start | bytes 491528 | tf_op jit(solution)/shard_map/ppermute | solution.py:191
  73.2 0.7 copy-start.5
  83.2 0.7 copy-start.7
  95.5 1.6 copy-start.1
  97.1 1.0 copy-start.3
  98.1 0.9 copy-start.6
  99.0 0.9 copy-start.8
  105.6 1.3 copy-start
  106.9 62.0 %all-to-all-start.2 = ((bf16[256,8,512]{2,1,0:T(8,128)(2,1)}), bf16[256,8,512]{2,1,0:T(8,128)(2,1)S(1)}, u32[]{:S(2)}, u32[]{:S(2)}) async-start(bf16[256,8,512]{2,1,0:T(8,128)(2,1)} %copy-done), calls=%async_computation.2 | async-start | bytes 4194304 | tf_op jit(solution)/shard_map/all_to_all | solution.py:190
  116.6 31.7 %collective-permute-start.3 = (bf16[20,8,512]{2,1,0:T(8,128)(2,1)S(1)}, bf16[20,8,512]{2,1,0:T(8,128)(2,1)S(1)}, u32[]{:S(2)}, u32[]{:S(2)}) collective-permute-start(bf16[20,8,512]{2,1,0:T(8,128)(2,1)S(1)} %get-tuple-element.14), channel_id=1, source_target_pairs={{4,0},{8,4},{12,8},{16,12},{20,16},{24,20},{28,24},{32,28},{36,32}... | collective-permute-start | bytes 491528 | tf_op jit(solution)/shard_map/ppermute | solution.py:192
  119.4 37.0 %collective-permute-start.2 = (bf16[20,8,512]{2,1,0:T(8,128)(2,1)S(1)}, bf16[20,8,512]{2,1,0:T(8,128)(2,1)S(1)}, u32[]{:S(2)}, u32[]{:S(2)}) collective-permute-start(bf16[20,8,512]{2,1,0:T(8,128)(2,1)S(1)} %get-tuple-element.15), channel_id=1, source_target_pairs={{0,4},{4,8},{8,12},{12,16},{16,20},{20,24},{24,28},{28,32},{32,36}... | collective-permute-start | bytes 491528 | tf_op jit(solution)/shard_map/ppermute | solution.py:191
  156.4 0.7 copy-start.9
  168.9 1.6 copy-start.2
  170.5 1.0 copy-start.4
  171.6 0.9 copy-start.10

commit v4 on v3

v4 whole, which is shorter than its diff:
```python
import jax
import jax.numpy as jnp
from jax import lax
from jax.experimental import pallas as pl
from jax.experimental.pallas import tpu as pltpu
from jax.sharding import PartitionSpec as P

NEAR = 8
ITERS = 2
PACK_CHUNKS = 8
HALF_WORD = 1 << 16
VMEM_LIMIT = 62 * 1024 * 1024
SMALL_LIMIT = 48 * 1024 * 1024


def request_kernel(blocks_here, pattern, codes):
    peers = codes.shape[0]
    slots, rows = pattern.shape
    base = lax.broadcasted_iota(jnp.int32, (peers, rows), 0) * blocks_here
    low = jnp.full((peers, rows), blocks_here, jnp.int32)
    high = jnp.full((peers, rows), -1, jnp.int32)
    for slot in range(NEAR, slots):
        within = pattern[slot : slot + 1, :] - base
        named = (within >= 0) & (within < blocks_here)
        low = jnp.minimum(low, jnp.where(named, within, blocks_here))
        high = jnp.maximum(high, jnp.where(named, within, -1))
    low = jnp.min(low, axis=1, keepdims=True)
    high = jnp.max(high, axis=1, keepdims=True)
    code = jnp.where(high >= 0, high * HALF_WORD + low, 0)
    codes[...] = jnp.broadcast_to(code, codes.shape)


def start_copy(src, dst, sem):
    copy = pltpu.make_async_copy(src, dst, sem)
    copy.start()
    return copy


def pack_blocks(asked, tilted, staged, outgoing, sems):
    chunk = outgoing.shape[0] // PACK_CHUNKS
    copies = []
    for part in range(PACK_CHUNKS):

        def body(j, carry, part=part):
            code = asked[0, part * (chunk // 2) + j]
            staged[part * chunk + 2 * j] = tilted[lax.rem(code, HALF_WORD)]
            staged[part * chunk + 2 * j + 1] = tilted[lax.div(code, HALF_WORD)]
            return carry

        lax.fori_loop(0, chunk // 2, body, 0, unroll=8)
        span = pl.ds(part * chunk, chunk)
        copies.append(start_copy(staged.at[span], outgoing.at[span], sems.at[part]))
    return copies


def pack_kernel(codes, tilted, asked, outgoing, line, asked_smem, staged, line_sem, sems):
    peers = codes.shape[0]
    same = lax.broadcasted_iota(jnp.int32, (peers, peers), 0) == lax.broadcasted_iota(
        jnp.int32, (peers, peers), 1
    )
    words = jnp.sum(jnp.where(same, codes[:, :peers], 0), axis=0, keepdims=True)
    line[...] = words
    asked[...] = words
    start_copy(line, asked_smem, line_sem).wait()
    for copy in pack_blocks(asked_smem, tilted, staged, outgoing, sems):
        copy.wait()


def weighted(index, stride, slots, source, weights, gathered, rows, tilts):
    span = rows * tilts
    for n, slot in enumerate(slots):

        def gather(pair, carry, slot=slot, n=n):
            low = source[index[2 * pair * stride + slot]]
            high = source[index[(2 * pair + 1) * stride + slot]]
            at = pl.multiple_of(n * span + pair * 2 * tilts, 2 * tilts)
            gathered[pl.ds(at, 2 * tilts), :] = jnp.concatenate([low, high], axis=0)
            return carry

        lax.fori_loop(0, rows // 2, gather, 0, unroll=True)
    taken = gathered[: len(slots) * span, :]
    product = jnp.dot(taken, weights, preferred_element_type=jnp.float32)
    return product.reshape(len(slots), rows, tilts, weights.shape[1])


def map_blocks(operands, scratch):
    near_index, far_index, before, own, after, arrived, kernels, rates = operands
    near_smem, far_smem, extended, far_blocks, weights, rate_buf, gathered, sems = scratch
    kinds = kernels.shape[0]
    (rows, tilts, _), half = own.shape, before.shape[0]
    far_count = rates.shape[0] - NEAR

    first = [
        start_copy(near_index, near_smem, sems.at[0]),
        start_copy(before, extended.at[pl.ds(0, half)], sems.at[1]),
        start_copy(own, extended.at[pl.ds(half, rows)], sems.at[2]),
        start_copy(after, extended.at[pl.ds(half + rows, half)], sems.at[3]),
    ]
    kernel_copies = [start_copy(kernels.at[0], weights.at[0], sems.at[4])]
    rate_copy = start_copy(rates, rate_buf, sems.at[4 + kinds])
    kernel_copies += [
        start_copy(kernels.at[k], weights.at[k], sems.at[4 + k]) for k in range(1, kinds)
    ]
    late = [
        start_copy(far_index, far_smem, sems.at[5 + kinds]),
        start_copy(arrived, far_blocks, sems.at[6 + kinds]),
    ]
    for copy in first:
        copy.wait()

    total = None
    for kind in range(kinds):
        slots = range(kind, NEAR, kinds)
        kernel_copies[kind].wait()
        if kind == 0:
            rate_copy.wait()
        product = weighted(
            near_smem, NEAR, slots, extended, weights[kind], gathered.at[kind % 2], rows, tilts
        )
        for n, slot in enumerate(slots):
            term = product[n] * rate_buf[slot].astype(jnp.float32)[:, None, :]
            total = term if total is None else total + term
    for copy in late:
        copy.wait()
    for kind in range(kinds):
        slots = range(kind, far_count, kinds)
        product = weighted(
            far_smem, far_count, slots, far_blocks, weights[kind], gathered.at[kind % 2], rows, tilts
        )
        for n, slot in enumerate(slots):
            total = total + product[n] * rate_buf[NEAR + slot].astype(jnp.float32)[:, None, :]
    return total


def step_kernel(asked, factor, *refs):
    operands, (tilted, outgoing, squares) = refs[:8], refs[8:11]
    asked_smem, factor_buf, tilted_buf, staged, squares_buf, pack_sems, sems = refs[11:18]
    asked_copy = start_copy(asked, asked_smem, sems.at[0])
    factor_copy = start_copy(factor, factor_buf, sems.at[1])
    total = map_blocks(operands, refs[18:])
    factor_copy.wait()
    tilted_buf[...] = (factor_buf[...] * total).astype(jnp.bfloat16)
    copies = [start_copy(tilted_buf, tilted, sems.at[2])]
    asked_copy.wait()
    copies += pack_blocks(asked_smem, tilted_buf, staged, outgoing, pack_sems)
    squares_buf[...] = jnp.sum(total * total, axis=0)
    copies.append(start_copy(squares_buf, squares, sems.at[3]))
    for copy in copies:
        copy.wait()


def last_kernel(*refs):
    operands, (mapped, squares) = refs[:8], refs[8:10]
    mapped_buf, squares_buf, sems = refs[10:13]
    total = map_blocks(operands, refs[13:])
    for row in range(total.shape[0]):
        mapped_buf[:, row * total.shape[2] : (row + 1) * total.shape[2]] = total[row]
    copies = [start_copy(mapped_buf, mapped, sems.at[0])]
    squares_buf[...] = jnp.sum(total * total, axis=0)
    copies.append(start_copy(squares_buf, squares, sems.at[1]))
    for copy in copies:
        copy.wait()


def call(kernel, outs, arrays, scratch, flops, in_vmem=(), limit=VMEM_LIMIT):
    spec = [pl.BlockSpec(memory_space=pltpu.VMEM), pl.BlockSpec(memory_space=pl.ANY)]
    moved = sum(a.size * a.dtype.itemsize for a in (*arrays, *outs))
    return pl.pallas_call(
        kernel,
        out_shape=outs,
        in_specs=[spec[n not in in_vmem] for n in range(len(arrays))],
        out_specs=[spec[len(arrays) + n not in in_vmem] for n in range(len(outs))],
        scratch_shapes=scratch,
        compiler_params=pltpu.CompilerParams(vmem_limit_bytes=limit),
        cost_estimate=pl.CostEstimate(flops=flops, bytes_accessed=moved, transcendentals=0),
    )(*arrays)


def on_device(start, reward, theta, kernels, rates, pattern):
    tilt_count = start.shape[0]
    blocks_here, slot_count = pattern.shape
    kind_count, block_size = kernels.shape[:2]
    peer_count = lax.axis_size("rows")
    position = lax.axis_index("rows")
    total_blocks = blocks_here * peer_count
    far_count = slot_count - NEAR
    half_span = blocks_here // 2
    capacity = 2
    shape = jax.ShapeDtypeStruct
    sem = pltpu.SemaphoreType.DMA

    pattern_by_slot = pattern.T
    (codes,) = call(
        lambda *refs: request_kernel(blocks_here, *refs),
        [shape((peer_count, 128), jnp.int32)],
        [pattern_by_slot],
        [],
        0,
        in_vmem=(0, 1),
        limit=SMALL_LIMIT,
    )
    codes = lax.all_to_all(codes, "rows", split_axis=0, concat_axis=0, tiled=True)

    far_cols = pattern[:, NEAR:].reshape(-1)
    owners = lax.div(far_cols, blocks_here)
    smaller = (owners[:, None] == owners[None, :]) & (far_cols[None, :] < far_cols[:, None])
    far_index = owners * capacity + jnp.any(smaller, axis=1).astype(jnp.int32)
    local_rows = jnp.arange(blocks_here, dtype=jnp.int32)
    global_rows = position * blocks_here + local_rows
    shifts = (pattern[:, :NEAR] - global_rows[:, None] + half_span) % total_blocks - half_span
    near_index = (local_rows[:, None] + shifts + half_span).reshape(-1)

    up = [(i, (i + 1) % peer_count) for i in range(peer_count)]
    down = [(j, i) for i, j in up]
    rates_by_slot = rates.transpose(1, 0, 2)
    factor = jnp.exp(theta[None, :, None] * reward.reshape(blocks_here, 1, block_size))

    block = (tilt_count, block_size)
    asked_shape = shape((1, peer_count), jnp.int32)
    tilted_shape = shape((blocks_here, *block), jnp.bfloat16)
    outgoing_shape = shape((peer_count * capacity, *block), jnp.bfloat16)
    squares_shape = shape(block, jnp.float32)
    mapped_shape = shape(start.shape, jnp.float32)
    asked_smem = pltpu.SMEM(asked_shape.shape, jnp.int32)
    staged = pltpu.VMEM(outgoing_shape.shape, jnp.bfloat16)
    gather_rows = max(NEAR, far_count) // kind_count * blocks_here * tilt_count
    map_scratch = [
        pltpu.SMEM(near_index.shape, jnp.int32),
        pltpu.SMEM(far_index.shape, jnp.int32),
        pltpu.VMEM((blocks_here + 2 * half_span, *block), jnp.bfloat16),
        pltpu.VMEM(outgoing_shape.shape, jnp.bfloat16),
        pltpu.VMEM(kernels.shape, jnp.bfloat16),
        pltpu.VMEM(rates_by_slot.shape, jnp.bfloat16),
        pltpu.VMEM((2, gather_rows, block_size), jnp.bfloat16),
        sem((7 + kind_count,)),
    ]
    map_flops = 2 * slot_count * blocks_here * tilt_count * block_size * block_size

    tilted = factor * start.reshape(tilt_count, blocks_here, block_size).transpose(1, 0, 2)
    tilted = tilted.astype(jnp.bfloat16)
    asked, outgoing = call(
        pack_kernel,
        [asked_shape, outgoing_shape],
        [codes, tilted],
        [pltpu.VMEM(asked_shape.shape, jnp.int32), asked_smem, staged, sem, sem((PACK_CHUNKS,))],
        0,
        in_vmem=(0, 1, 2),
        limit=SMALL_LIMIT,
    )
    squares = []
    for iteration in range(ITERS):
        arrived = lax.all_to_all(outgoing, "rows", split_axis=0, concat_axis=0, tiled=True)
        before = lax.ppermute(tilted[blocks_here - half_span :], "rows", up)
        after = lax.ppermute(tilted[:half_span], "rows", down)
        operands = [near_index, far_index, before, tilted, after, arrived, kernels, rates_by_slot]
        if iteration < ITERS - 1:
            step_scratch = [
                asked_smem,
                pltpu.VMEM(tilted_shape.shape, jnp.float32),
                pltpu.VMEM(tilted_shape.shape, jnp.bfloat16),
                staged,
                pltpu.VMEM(block, jnp.float32),
                sem((PACK_CHUNKS,)),
                sem((4,)),
            ]
            tilted, outgoing, square = call(
                step_kernel,
                [tilted_shape, outgoing_shape, squares_shape],
                [asked, factor, *operands],
                step_scratch + map_scratch,
                map_flops,
            )
        else:
            last_scratch = [pltpu.VMEM(start.shape, jnp.float32), pltpu.VMEM(block, jnp.float32), sem((2,))]
            mapped, square = call(
                last_kernel,
                [mapped_shape, squares_shape],
                operands,
                last_scratch + map_scratch,
                map_flops,
            )
        squares.append(jnp.sum(square, axis=1))

    partial = jnp.concatenate(squares)
    spread = jnp.broadcast_to(partial, (peer_count, partial.shape[0]))
    gathered = lax.all_to_all(spread, "rows", split_axis=0, concat_axis=0, tiled=True)
    totals = jnp.sum(gathered, axis=0).reshape(ITERS, tilt_count)
    states = total_blocks * block_size
    product = jnp.ones((tilt_count,), jnp.float32)
    growth = []
    for j in range(ITERS):
        scale = jnp.sqrt(totals[j] / product / product / states + 1e-06)
        product = product * scale
        growth.append(jnp.log(scale))
    return (mapped / product[:, None], jnp.stack(growth))


def solution(mesh):
    placed = (P("tilt", "rows"), P("rows"), P("tilt"), P(), P("rows", None, None), P("rows", None))
    return jax.shard_map(
        on_device,
        mesh=mesh,
        in_specs=placed,
        out_specs=(P("tilt", "rows"), P(None, "tilt")),
        check_vma=False,
    )
```

time: 201 us -> 193 us (0.960)
  local copies, waits for them, and re-layouts: 15.2 us -> 3.18 us
  Pallas kernels: 12.5 us -> 14.7 us
    unnamed x24 -> x20, local copies, waits for them, and re-layouts: 11.3 us -> 1.25 us
    pallas_call x3 -> x4, Pallas kernels: 12.5 us -> 14.7 us  [call(): pl.pallas_call(kernel, out_shape=outs, in_specs=[spec[n not in in_vmem] f...]
  transfers between devices with their start and end apart: 7 -> 7, of which waited for: 7 -> 7; matrix products, arithmetic and copies ran while one was open for 2% -> 3% of each run, Pallas kernels for 0% -> 0%
where the time goes in v4:
time: 193 us; the launch traced here: 192 us
  waiting for transfers between devices  99.3 us (51%)
  starting transfers between devices  46.4 us (24%)
  blocking collectives  20.5 us (11%)
  Pallas kernels  14.7 us (8%)
  other arithmetic  6.86 us (4%)
  local copies, waits for them, and re-layouts  3.18 us (2%)
    ppermute x2, waiting for transfers between devices, on_device(): after = lax.ppermute(tilted[:half_span], 'rows', down)  48.2 us
    all_to_all x2, waiting for transfers between devices, on_device(): lax.all_to_all(outgoing, 'rows', split_axis=0, concat_axis=0, tiled=True)  24.7 us
    all_to_all x1, blocking collectives, on_device(): lax.all_to_all(spread, 'rows', split_axis=0, concat_axis=0, tiled=True)  20.5 us
    all_to_all x1, starting transfers between devices, on_device(): lax.all_to_all(codes, 'rows', split_axis=0, concat_axis=0, tiled=True)  18.4 us
    ppermute x2, waiting for transfers between devices, on_device(): before = lax.ppermute(tilted[blocks_here - half_span:], 'rows', up)  18 us
    all_to_all x2, starting transfers between devices, on_device(): lax.all_to_all(outgoing, 'rows', split_axis=0, concat_axis=0, tiled=True)  16.7 us
    pallas_call x4, Pallas kernels, call(): pl.pallas_call(kernel, out_shape=outs, in_specs=[spec[n not in in_vmem] f...  14.7 us
    all_to_all x1, waiting for transfers between devices, on_device(): lax.all_to_all(codes, 'rows', split_axis=0, concat_axis=0, tiled=True)  8.5 us
  transfers between devices with their start and end apart: 7, of which 7 were waited for; matrix products, arithmetic and copies ran while one was open for 3% of the time, Pallas kernels for 0%

profile of v4, /device:TPU:1, one launch (start us, length us, event | category | flops | bytes accessed | tf_op | source)
XLA Modules:
  0.0 191.8 jit_solution(13636313168638918011)
XLA Ops:
  0.6 0.0 copy-start.1
  0.6 0.7 copy-done.1
  1.3 0.9 shard_map.77
  2.2 18.4 %all-to-all-start = ((s32[128,1,128]{2,1,0:T(1,128)}), s32[128,1,128]{2,1,0:T(1,128)S(1)}, u32[]{:S(2)}, u32[]{:S(2)}) async-start(s32[128,1,128]{2,1,0:T(1,128)} %bitcast.2), calls=%async_computation | async-start | bytes 131072 | tf_op jit(solution)/shard_map/all_to_all | solution.py:202
  20.7 0.9 mul.36
  21.6 2.1 %multiply_exponential_fusion = (f32[40,8,512]{2,1,0:T(8,128)}, bf16[40,8,512]{2,1,0:T(8,128)(2,1)S(1)}) fusion(f32[40,512]{1,0:T(8,128)S(1)} %mul.36, f32[8]{0:T(128)} %param.8, f32[40,8,512]{2,1,0:T(8,128)} %bitcast.15), kind=kLoop, calls=%fused_computation.1 | loop fusion | flops 491520 | bytes 1720352 | tf_op jit(solution)/shard_map/exp | solution.py:216
  23.7 8.5 %all-to-all-done = s32[128,1,128]{2,1,0:T(1,128)S(1)} async-done(((s32[128,1,128]{2,1,0:T(1,128)}), s32[128,1,128]{2,1,0:T(1,128)S(1)}, u32[]{:S(2)}, u32[]{:S(2)}) %all-to-all-start) | async-done | bytes 65568 | tf_op jit(solution)/shard_map/all_to_all | solution.py:202
  32.2 2.0 %shard_map.78 = (s32[1,128]{1,0:T(1,128)S(1)}, bf16[256,8,512]{2,1,0:T(8,128)(2,1)}) custom-call(s32[128,128]{1,0:T(8,128)S(1)} %bitcast.13, bf16[40,8,512]{2,1,0:T(8,128)(2,1)S(1)} %get-tuple-element.23.tilted.refs_3_), custom_call_target="tpu_custom_call" | custom-call | bytes 2490880 | tf_op jit(solution)/shard_map/pallas_call | solution.py:168
  34.3 0.0 copy-start.3
  34.3 0.5 copy-done.3
  34.8 7.0 %all-to-all-start.1 = ((bf16[256,8,512]{2,1,0:T(8,128)(2,1)}), bf16[256,8,512]{2,1,0:T(8,128)(2,1)}, u32[]{:S(2)}, u32[]{:S(2)}) async-start(bf16[256,8,512]{2,1,0:T(8,128)(2,1)} %get-tuple-element.10), calls=%async_computation.1 | async-start | bytes 4194304 | tf_op jit(solution)/shard_map/all_to_all | solution.py:252
  41.7 0.0 copy-done
  41.8 3.0 %collective-permute-start.1 = (bf16[20,8,512]{2,1,0:T(8,128)(2,1)S(1)}, bf16[20,8,512]{2,1,0:T(8,128)(2,1)S(1)}, u32[]{:S(2)}, u32[]{:S(2)}) collective-permute-start(bf16[20,8,512]{2,1,0:T(8,128)(2,1)S(1)} %get-tuple-element.20), channel_id=1, source_target_pairs={{4,0},{8,4},{12,8},{16,12},{20,16},{24,20},{28,24},{32,28},{36,32}... | collective-permute-start | bytes 491528 | tf_op jit(solution)/shard_map/ppermute | solution.py:254
  44.8 2.6 %collective-permute-start = (bf16[20,8,512]{2,1,0:T(8,128)(2,1)S(1)}, bf16[20,8,512]{2,1,0:T(8,128)(2,1)S(1)}, u32[]{:S(2)}, u32[]{:S(2)}) collective-permute-start(bf16[20,8,512]{2,1,0:T(8,128)(2,1)S(1)} %get-tuple-element.21), channel_id=1, source_target_pairs={{0,4},{4,8},{8,12},{12,16},{16,20},{20,24},{24,28},{28,32},{32,36}... | collective-permute-start | bytes 491528 | tf_op jit(solution)/shard_map/ppermute | solution.py:253
  47.4 0.0 copy-done.2
  47.4 0.1 copy.16
  47.5 0.7 reshape.69.refs_0_
  48.2 0.1 copy.17
  48.3 0.1 reshape.70
  48.4 0.2 and_reduce_fusion
  48.6 0.6 convert_add_fusion.refs_1_
  49.2 22.4 %collective-permute-done.1.refs_4_ = bf16[20,8,512]{2,1,0:T(8,128)(2,1)S(1)} collective-permute-done((bf16[20,8,512]{2,1,0:T(8,128)(2,1)S(1)}, bf16[20,8,512]{2,1,0:T(8,128)(2,1)S(1)}, u32[]{:S(2)}, u32[]{:S(2)}) %collective-permute-start.1) | collective-permute-done | bytes 163872 | tf_op jit(solution)/shard_map/ppermute | solution.py:254
  71.5 10.0 %collective-permute-done.refs_2_ = bf16[20,8,512]{2,1,0:T(8,128)(2,1)S(1)} collective-permute-done((bf16[20,8,512]{2,1,0:T(8,128)(2,1)S(1)}, bf16[20,8,512]{2,1,0:T(8,128)(2,1)S(1)}, u32[]{:S(2)}, u32[]{:S(2)}) %collective-permute-start) | collective-permute-done | bytes 163872 | tf_op jit(solution)/shard_map/ppermute | solution.py:253
  81.6 12.3 %all-to-all-done.1.refs_5_ = bf16[256,8,512]{2,1,0:T(8,128)(2,1)} async-done(((bf16[256,8,512]{2,1,0:T(8,128)(2,1)}), bf16[256,8,512]{2,1,0:T(8,128)(2,1)}, u32[]{:S(2)}, u32[]{:S(2)}) %all-to-all-start.1) | async-done | bytes 2097184 | tf_op jit(solution)/shard_map/all_to_all | solution.py:252
  93.9 0.0 copy-done.6
  93.9 0.0 copy-done.7
  93.9 6.2 %shard_map.79 = (bf16[40,8,512]{2,1,0:T(8,128)(2,1)}, bf16[256,8,512]{2,1,0:T(8,128)(2,1)}, f32[8,512]{1,0:T(8,128)}) custom-call(s32[1,128]{1,0:T(1,128)} %copy-done.3, f32[40,8,512]{2,1,0:T(8,128)} %get-tuple-element.22.factor, s32[320]{0:T(512)} %reshape.69.refs_0_, s32[160]{0:T(256)} %convert_add_fusion.refs_1_, bf16[20,8,512]{2,1,0:T(8,128)(2,1)} %copy-done.7, ...), custom_call_target="tpu_custom_call" | custom-call | flops 2013265920 | bytes 8440192 | tf_op jit(solution)/shard_map/pallas_call | solution.py:168
  100.1 0.0 copy-start.4
  100.2 0.0 copy-start.5
  100.2 9.7 %all-to-all-start.2 = ((bf16[256,8,512]{2,1,0:T(8,128)(2,1)}), bf16[256,8,512]{2,1,0:T(8,128)(2,1)}, u32[]{:S(2)}, u32[]{:S(2)}) async-start(bf16[256,8,512]{2,1,0:T(8,128)(2,1)} %get-tuple-element.12), calls=%async_computation.2 | async-start | bytes 4194304 | tf_op jit(solution)/shard_map/all_to_all | solution.py:252
  109.9 0.0 copy-done.4
  109.9 2.9 %collective-permute-start.3 = (bf16[20,8,512]{2,1,0:T(8,128)(2,1)S(1)}, bf16[20,8,512]{2,1,0:T(8,128)(2,1)S(1)}, u32[]{:S(2)}, u32[]{:S(2)}) collective-permute-start(bf16[20,8,512]{2,1,0:T(8,128)(2,1)S(1)} %get-tuple-element.18), channel_id=1, source_target_pairs={{4,0},{8,4},{12,8},{16,12},{20,16},{24,20},{28,24},{32,28},{36,32}... | collective-permute-start | bytes 491528 | tf_op jit(solution)/shard_map/ppermute | solution.py:254
  112.8 2.9 %collective-permute-start.2 = (bf16[20,8,512]{2,1,0:T(8,128)(2,1)S(1)}, bf16[20,8,512]{2,1,0:T(8,128)(2,1)S(1)}, u32[]{:S(2)}, u32[]{:S(2)}) collective-permute-start(bf16[20,8,512]{2,1,0:T(8,128)(2,1)S(1)} %get-tuple-element.19), channel_id=1, source_target_pairs={{0,4},{4,8},{8,12},{12,16},{16,20},{20,24},{24,28},{28,32},{32,36}... | collective-permute-start | bytes 491528 | tf_op jit(solution)/shard_map/ppermute | solution.py:253
  115.7 0.0 copy-done.5
  115.7 0.1 reduce_sum.27
  115.8 25.8 %collective-permute-done.3.refs_4_ = bf16[20,8,512]{2,1,0:T(8,128)(2,1)S(1)} collective-permute-done((bf16[20,8,512]{2,1,0:T(8,128)(2,1)S(1)}, bf16[20,8,512]{2,1,0:T(8,128)(2,1)S(1)}, u32[]{:S(2)}, u32[]{:S(2)}) %collective-permute-start.3) | collective-permute-done | bytes 163872 | tf_op jit(solution)/shard_map/ppermute | solution.py:254
  141.6 8.0 %collective-permute-done.2.refs_2_ = bf16[20,8,512]{2,1,0:T(8,128)(2,1)S(1)} collective-permute-done((bf16[20,8,512]{2,1,0:T(8,128)(2,1)S(1)}, bf16[20,8,512]{2,1,0:T(8,128)(2,1)S(1)}, u32[]{:S(2)}, u32[]{:S(2)}) %collective-permute-start.2) | collective-permute-done | bytes 163872 | tf_op jit(solution)/shard_map/ppermute | solution.py:253
  149.6 12.3 %all-to-all-done.2.refs_5_ = bf16[256,8,512]{2,1,0:T(8,128)(2,1)} async-done(((bf16[256,8,512]{2,1,0:T(8,128)(2,1)}), bf16[256,8,512]{2,1,0:T(8,128)(2,1)}, u32[]{:S(2)}, u32[]{:S(2)}) %all-to-all-start.2) | async-done | bytes 2097184 | tf_op jit(solution)/shard_map/all_to_all | solution.py:252
  161.9 0.0 copy-done.8
  161.9 0.0 copy-done.9
  161.9 5.5 %shard_map.80 = (f32[8,20480]{1,0:T(8,128)}, f32[8,512]{1,0:T(8,128)}) custom-call(s32[320]{0:T(512)} %reshape.69.refs_0_, s32[160]{0:T(256)} %convert_add_fusion.refs_1_, bf16[20,8,512]{2,1,0:T(8,128)(2,1)} %copy-done.9, bf16[40,8,512]{2,1,0:T(8,128)(2,1)} %get-tuple-element.11.refs_3_, bf16[20,8,512]{2,1,0:T(8,128)(2,1)} %copy-done.8, ...), custom_call_target="tpu_custom_call" | custom-call | flops 2013265920 | bytes 6014848 | tf_op jit(solution)/shard_map/pallas_call | solution.py:168
  167.5 0.8 reduce_sum.28
  168.3 0.1 pad_maximum_fusion.1
  168.4 20.5 %all_to_all.27 = f32[128,1,16]{2,1,0:T(1,128)S(1)} all-to-all(f32[128,1,16]{2,1,0:T(1,128)S(1)} %broadcast_in_dim.2), channel_id=1, replica_groups=mesh['rows'=128,'tilt'=4] {'rows'}, dimensions={0} | all-to-all | bytes 16384 | tf_op jit(solution)/shard_map/all_to_all | solution.py:286
  188.9 0.2 reduce_sum.29
  189.1 0.1 multiply_bitcast_fusion
  189.2 0.6 pad_maximum_fusion
  189.7 2.0 %broadcast_divide_fusion = f32[8,20480]{1,0:T(8,128)} fusion(f32[8,20480]{1,0:T(8,128)} %get-tuple-element.13, f32[8]{0:T(128)S(1)} %get-tuple-element.25), kind=kLoop, calls=%fused_computation.2 | loop fusion | flops 163840 | bytes 1310752 | tf_op jit(solution)/shard_map/div | solution.py:295
  (14 shorter events, 0.1 us)
Async XLA Ops:
  0.6 0.7 copy-start.1
  2.2 30.0 %all-to-all-start = ((s32[128,1,128]{2,1,0:T(1,128)}), s32[128,1,128]{2,1,0:T(1,128)S(1)}, u32[]{:S(2)}, u32[]{:S(2)}) async-start(s32[128,1,128]{2,1,0:T(1,128)} %bitcast.2), calls=%async_computation | async-start | bytes 131072 | tf_op jit(solution)/shard_map/all_to_all | solution.py:202
  23.7 18.0 %copy-start = (bf16[40,8,512]{2,1,0:T(8,128)(2,1)}, bf16[40,8,512]{2,1,0:T(8,128)(2,1)S(1)}, u32[]{:S(2)}) copy-start(bf16[40,8,512]{2,1,0:T(8,128)(2,1)S(1)} %get-tuple-element.23.tilted.refs_3_) | copy-start | bytes 983044
  34.3 0.5 copy-start.3
  34.8 12.6 %copy-start.2 = (s32[40,12]{0,1:T(8,128)S(1)}, s32[40,12]{0,1:T(8,128)}, u32[]{:S(2)}) copy-start(s32[40,12]{0,1:T(8,128)} %param.11) | copy-start | bytes 5764
  34.8 59.1 %all-to-all-start.1 = ((bf16[256,8,512]{2,1,0:T(8,128)(2,1)}), bf16[256,8,512]{2,1,0:T(8,128)(2,1)}, u32[]{:S(2)}, u32[]{:S(2)}) async-start(bf16[256,8,512]{2,1,0:T(8,128)(2,1)} %get-tuple-element.10), calls=%async_computation.1 | async-start | bytes 4194304 | tf_op jit(solution)/shard_map/all_to_all | solution.py:252
  41.8 29.7 %collective-permute-start.1 = (bf16[20,8,512]{2,1,0:T(8,128)(2,1)S(1)}, bf16[20,8,512]{2,1,0:T(8,128)(2,1)S(1)}, u32[]{:S(2)}, u32[]{:S(2)}) collective-permute-start(bf16[20,8,512]{2,1,0:T(8,128)(2,1)S(1)} %get-tuple-element.20), channel_id=1, source_target_pairs={{4,0},{8,4},{12,8},{16,12},{20,16},{24,20},{28,24},{32,28},{36,32}... | collective-permute-start | bytes 491528 | tf_op jit(solution)/shard_map/ppermute | solution.py:254
  44.8 36.8 %collective-permute-start = (bf16[20,8,512]{2,1,0:T(8,128)(2,1)S(1)}, bf16[20,8,512]{2,1,0:T(8,128)(2,1)S(1)}, u32[]{:S(2)}, u32[]{:S(2)}) collective-permute-start(bf16[20,8,512]{2,1,0:T(8,128)(2,1)S(1)} %get-tuple-element.21), channel_id=1, source_target_pairs={{0,4},{4,8},{8,12},{12,16},{16,20},{20,24},{24,28},{28,32},{32,36}... | collective-permute-start | bytes 491528 | tf_op jit(solution)/shard_map/ppermute | solution.py:253
  71.5 22.4 %copy-start.6 = (bf16[20,8,512]{2,1,0:T(8,128)(2,1)}, bf16[20,8,512]{2,1,0:T(8,128)(2,1)S(1)}, u32[]{:S(2)}) copy-start(bf16[20,8,512]{2,1,0:T(8,128)(2,1)S(1)} %collective-permute-done.1.refs_4_) | copy-start | bytes 491524
  81.6 12.3 %copy-start.7 = (bf16[20,8,512]{2,1,0:T(8,128)(2,1)}, bf16[20,8,512]{2,1,0:T(8,128)(2,1)S(1)}, u32[]{:S(2)}) copy-start(bf16[20,8,512]{2,1,0:T(8,128)(2,1)S(1)} %collective-permute-done.refs_2_) | copy-start | bytes 491524
  100.1 9.8 %copy-start.4 = (bf16[40,8,512]{2,1,0:T(8,128)(2,1)S(1)}, bf16[40,8,512]{2,1,0:T(8,128)(2,1)}, u32[]{:S(2)}) copy-start(bf16[40,8,512]{2,1,0:T(8,128)(2,1)} %get-tuple-element.11.refs_3_) | copy-start | bytes 983044
  100.2 15.5 %copy-start.5 = (f32[8,512]{1,0:T(8,128)S(1)}, f32[8,512]{1,0:T(8,128)}, u32[]{:S(2)}) copy-start(f32[8,512]{1,0:T(8,128)} %get-tuple-element.14) | copy-start | bytes 49156
  100.2 61.8 %all-to-all-start.2 = ((bf16[256,8,512]{2,1,0:T(8,128)(2,1)}), bf16[256,8,512]{2,1,0:T(8,128)(2,1)}, u32[]{:S(2)}, u32[]{:S(2)}) async-start(bf16[256,8,512]{2,1,0:T(8,128)(2,1)} %get-tuple-element.12), calls=%async_computation.2 | async-start | bytes 4194304 | tf_op jit(solution)/shard_map/all_to_all | solution.py:252
  109.9 31.7 %collective-permute-start.3 = (bf16[20,8,512]{2,1,0:T(8,128)(2,1)S(1)}, bf16[20,8,512]{2,1,0:T(8,128)(2,1)S(1)}, u32[]{:S(2)}, u32[]{:S(2)}) collective-permute-start(bf16[20,8,512]{2,1,0:T(8,128)(2,1)S(1)} %get-tuple-element.18), channel_id=1, source_target_pairs={{4,0},{8,4},{12,8},{16,12},{20,16},{24,20},{28,24},{32,28},{36,32}... | collective-permute-start | bytes 491528 | tf_op jit(solution)/shard_map/ppermute | solution.py:254
  112.8 36.8 %collective-permute-start.2 = (bf16[20,8,512]{2,1,0:T(8,128)(2,1)S(1)}, bf16[20,8,512]{2,1,0:T(8,128)(2,1)S(1)}, u32[]{:S(2)}, u32[]{:S(2)}) collective-permute-start(bf16[20,8,512]{2,1,0:T(8,128)(2,1)S(1)} %get-tuple-element.19), channel_id=1, source_target_pairs={{0,4},{4,8},{8,12},{12,16},{16,20},{20,24},{24,28},{28,32},{32,36}... | collective-permute-start | bytes 491528 | tf_op jit(solution)/shard_map/ppermute | solution.py:253
  141.6 20.3 %copy-start.8 = (bf16[20,8,512]{2,1,0:T(8,128)(2,1)}, bf16[20,8,512]{2,1,0:T(8,128)(2,1)S(1)}, u32[]{:S(2)}) copy-start(bf16[20,8,512]{2,1,0:T(8,128)(2,1)S(1)} %collective-permute-done.3.refs_4_) | copy-start | bytes 491524
  149.6 12.3 %copy-start.9 = (bf16[20,8,512]{2,1,0:T(8,128)(2,1)}, bf16[20,8,512]{2,1,0:T(8,128)(2,1)S(1)}, u32[]{:S(2)}) copy-start(bf16[20,8,512]{2,1,0:T(8,128)(2,1)S(1)} %collective-permute-done.2.refs_2_) | copy-start | bytes 491524

commit v5 on v4

--- a/solution.py
+++ b/solution.py
@@ -26,8 +26,7 @@
         high = jnp.maximum(high, jnp.where(named, within, -1))
     low = jnp.min(low, axis=1, keepdims=True)
     high = jnp.max(high, axis=1, keepdims=True)
-    code = jnp.where(high >= 0, high * HALF_WORD + low, 0)
-    codes[...] = jnp.broadcast_to(code, codes.shape)
+    codes[...] = jnp.where(high >= 0, high * HALF_WORD + low, 0)
 
 
 def start_copy(src, dst, sem):
@@ -36,15 +35,23 @@
     return copy
 
 
-def pack_blocks(asked, tilted, staged, outgoing, sems):
+def read_words(codes, line, words, sem):
+    peers = codes.shape[0]
+    across = lax.broadcasted_iota(jnp.int32, (peers, peers), 1)
+    same = lax.broadcasted_iota(jnp.int32, (peers, peers), 0) == across
+    line[...] = jnp.sum(jnp.where(same, codes[...], 0), axis=0, keepdims=True)
+    return start_copy(line, words, sem)
+
+
+def pack_blocks(words, tilted, staged, outgoing, sems):
     chunk = outgoing.shape[0] // PACK_CHUNKS
     copies = []
     for part in range(PACK_CHUNKS):
 
         def body(j, carry, part=part):
-            code = asked[0, part * (chunk // 2) + j]
-            staged[part * chunk + 2 * j] = tilted[lax.rem(code, HALF_WORD)]
-            staged[part * chunk + 2 * j + 1] = tilted[lax.div(code, HALF_WORD)]
+            word = words[0, part * (chunk // 2) + j]
+            staged[part * chunk + 2 * j] = tilted[lax.rem(word, HALF_WORD)]
+            staged[part * chunk + 2 * j + 1] = tilted[lax.div(word, HALF_WORD)]
             return carry
 
         lax.fori_loop(0, chunk // 2, body, 0, unroll=8)
@@ -53,16 +60,9 @@
     return copies
 
 
-def pack_kernel(codes, tilted, asked, outgoing, line, asked_smem, staged, line_sem, sems):
-    peers = codes.shape[0]
-    same = lax.broadcasted_iota(jnp.int32, (peers, peers), 0) == lax.broadcasted_iota(
-        jnp.int32, (peers, peers), 1
-    )
-    words = jnp.sum(jnp.where(same, codes[:, :peers], 0), axis=0, keepdims=True)
-    line[...] = words
-    asked[...] = words
-    start_copy(line, asked_smem, line_sem).wait()
-    for copy in pack_blocks(asked_smem, tilted, staged, outgoing, sems):
+def pack_kernel(codes, tilted, outgoing, line, words, staged, word_sem, sems):
+    read_words(codes, line, words, word_sem).wait()
+    for copy in pack_blocks(words, tilted, staged, outgoing, sems):
         copy.wait()
 
 
@@ -132,34 +132,47 @@
     return total
 
 
-def step_kernel(asked, factor, *refs):
+def sum_of_squares(total):
+    return jnp.sum(jnp.sum(total * total, axis=0), axis=1, keepdims=True)
+
+
+def step_kernel(codes, reward, theta, *refs):
     operands, (tilted, outgoing, squares) = refs[:8], refs[8:11]
-    asked_smem, factor_buf, tilted_buf, staged, squares_buf, pack_sems, sems = refs[11:18]
-    asked_copy = start_copy(asked, asked_smem, sems.at[0])
-    factor_copy = start_copy(factor, factor_buf, sems.at[1])
-    total = map_blocks(operands, refs[18:])
-    factor_copy.wait()
-    tilted_buf[...] = (factor_buf[...] * total).astype(jnp.bfloat16)
-    copies = [start_copy(tilted_buf, tilted, sems.at[2])]
-    asked_copy.wait()
-    copies += pack_blocks(asked_smem, tilted_buf, staged, outgoing, pack_sems)
-    squares_buf[...] = jnp.sum(total * total, axis=0)
-    copies.append(start_copy(squares_buf, squares, sems.at[3]))
+    codes_buf, line, words, reward_buf, theta_smem, tilted_buf, staged, pack_sems, sems = refs[11:20]
+    codes_copy = start_copy(codes, codes_buf, sems.at[0])
+    reward_copy = start_copy(reward, reward_buf, sems.at[1])
+    theta_copy = start_copy(theta, theta_smem, sems.at[4])
+    total = map_blocks(operands, refs[20:])
+    reward_copy.wait()
+    theta_copy.wait()
+    codes_copy.wait()
+    words_copy = read_words(codes_buf, line, words, sems.at[2])
+    tilt = lax.broadcasted_iota(jnp.int32, total.shape[1:], 0)
+    thetas = jnp.zeros(total.shape[1:], jnp.float32)
+    for t in range(total.shape[1]):
+        thetas = jnp.where(tilt == t, theta_smem[t], thetas)
+    factor = jnp.exp(thetas[None] * reward_buf[...][:, None, :])
+    tilted_buf[...] = (factor * total).astype(jnp.bfloat16)
+    copies = [start_copy(tilted_buf, tilted, sems.at[3])]
+    words_copy.wait()
+    copies += pack_blocks(words, tilted_buf, staged, outgoing, pack_sems)
+    squares[...] = jnp.broadcast_to(sum_of_squares(total), squares.shape)
     for copy in copies:
         copy.wait()
 
 
-def last_kernel(*refs):
-    operands, (mapped, squares) = refs[:8], refs[8:10]
-    mapped_buf, squares_buf, sems = refs[10:13]
-    total = map_blocks(operands, refs[13:])
+def last_kernel(first_squares, *refs):
+    operands, (mapped, sums) = refs[:8], refs[8:10]
+    total = map_blocks(operands, refs[10:])
     for row in range(total.shape[0]):
-        mapped_buf[:, row * total.shape[2] : (row + 1) * total.shape[2]] = total[row]
-    copies = [start_copy(mapped_buf, mapped, sems.at[0])]
-    squares_buf[...] = jnp.sum(total * total, axis=0)
-    copies.append(start_copy(squares_buf, squares, sems.at[1]))
-    for copy in copies:
-        copy.wait()
+        mapped[:, row * total.shape[2] : (row + 1) * total.shape[2]] = total[row]
+    tilts = total.shape[1]
+    across = lax.broadcasted_iota(jnp.int32, (tilts, sums.shape[1]), 1)
+    tilt = lax.broadcasted_iota(jnp.int32, (tilts, sums.shape[1]), 0)
+    both = jnp.where(across == tilt, first_squares[:, :1], 0.0) + jnp.where(
+        across == tilt + tilts, sum_of_squares(total), 0.0
+    )
+    sums[...] = jnp.broadcast_to(jnp.sum(both, axis=0, keepdims=True), sums.shape)
 
 
 def call(kernel, outs, arrays, scratch, flops, in_vmem=(), limit=VMEM_LIMIT):
@@ -192,12 +205,11 @@
     pattern_by_slot = pattern.T
     (codes,) = call(
         lambda *refs: request_kernel(blocks_here, *refs),
-        [shape((peer_count, 128), jnp.int32)],
+        [shape((peer_count, 1), jnp.int32)],
         [pattern_by_slot],
         [],
         0,
         in_vmem=(0, 1),
-        limit=SMALL_LIMIT,
     )
     codes = lax.all_to_all(codes, "rows", split_axis=0, concat_axis=0, tiled=True)
 
@@ -213,15 +225,15 @@
     up = [(i, (i + 1) % peer_count) for i in range(peer_count)]
     down = [(j, i) for i, j in up]
     rates_by_slot = rates.transpose(1, 0, 2)
-    factor = jnp.exp(theta[None, :, None] * reward.reshape(blocks_here, 1, block_size))
+    reward = reward.reshape(blocks_here, block_size)
 
     block = (tilt_count, block_size)
-    asked_shape = shape((1, peer_count), jnp.int32)
     tilted_shape = shape((blocks_here, *block), jnp.bfloat16)
     outgoing_shape = shape((peer_count * capacity, *block), jnp.bfloat16)
-    squares_shape = shape(block, jnp.float32)
+    squares_shape = shape((tilt_count, 128), jnp.float32)
+    sums_shape = shape((peer_count, ITERS * tilt_count), jnp.float32)
     mapped_shape = shape(start.shape, jnp.float32)
-    asked_smem = pltpu.SMEM(asked_shape.shape, jnp.int32)
+    word_buffers = [pltpu.VMEM((1, peer_count), jnp.int32), pltpu.SMEM((1, peer_count), jnp.int32)]
     staged = pltpu.VMEM(outgoing_shape.shape, jnp.bfloat16)
     gather_rows = max(NEAR, far_count) // kind_count * blocks_here * tilt_count
     map_scratch = [
@@ -236,18 +248,18 @@
     ]
     map_flops = 2 * slot_count * blocks_here * tilt_count * block_size * block_size
 
+    factor = jnp.exp(theta[None, :, None] * reward[:, None, :])
     tilted = factor * start.reshape(tilt_count, blocks_here, block_size).transpose(1, 0, 2)
     tilted = tilted.astype(jnp.bfloat16)
-    asked, outgoing = call(
+    (outgoing,) = call(
         pack_kernel,
-        [asked_shape, outgoing_shape],
+        [outgoing_shape],
         [codes, tilted],
-        [pltpu.VMEM(asked_shape.shape, jnp.int32), asked_smem, staged, sem, sem((PACK_CHUNKS,))],
+        [*word_buffers, staged, sem, sem((PACK_CHUNKS,))],
         0,
-        in_vmem=(0, 1, 2),
+        in_vmem=(0, 1),
         limit=SMALL_LIMIT,
     )
-    squares = []
     for iteration in range(ITERS):
         arrived = lax.all_to_all(outgoing, "rows", split_axis=0, concat_axis=0, tiled=True)
         before = lax.ppermute(tilted[blocks_here - half_span :], "rows", up)
@@ -255,35 +267,34 @@
         operands = [near_index, far_index, before, tilted, after, arrived, kernels, rates_by_slot]
         if iteration < ITERS - 1:
             step_scratch = [
-                asked_smem,
-                pltpu.VMEM(tilted_shape.shape, jnp.float32),
+                pltpu.VMEM(codes.shape, jnp.int32),
+                *word_buffers,
+                pltpu.VMEM(reward.shape, jnp.float32),
+                pltpu.SMEM(theta.shape, jnp.float32),
                 pltpu.VMEM(tilted_shape.shape, jnp.bfloat16),
                 staged,
-                pltpu.VMEM(block, jnp.float32),
                 sem((PACK_CHUNKS,)),
-                sem((4,)),
+                sem((5,)),
             ]
-            tilted, outgoing, square = call(
+            tilted, outgoing, squares = call(
                 step_kernel,
                 [tilted_shape, outgoing_shape, squares_shape],
-                [asked, factor, *operands],
+                [codes, reward, theta, *operands],
                 step_scratch + map_scratch,
                 map_flops,
+                in_vmem=(13,),
             )
         else:
-            last_scratch = [pltpu.VMEM(start.shape, jnp.float32), pltpu.VMEM(block, jnp.float32), sem((2,))]
-            mapped, square = call(
+            mapped, sums = call(
                 last_kernel,
-                [mapped_shape, squares_shape],
-                operands,
-                last_scratch + map_scratch,
+                [mapped_shape, sums_shape],
+                [squares, *operands],
+                map_scratch,
                 map_flops,
+                in_vmem=(0, 9, 10),
             )
-        squares.append(jnp.sum(square, axis=1))
-
-    partial = jnp.concatenate(squares)
-    spread = jnp.broadcast_to(partial, (peer_count, partial.shape[0]))
-    gathered = lax.all_to_all(spread, "rows", split_axis=0, concat_axis=0, tiled=True)
+
+    gathered = lax.all_to_all(sums, "rows", split_axis=0, concat_axis=0, tiled=True)
     totals = jnp.sum(gathered, axis=0).reshape(ITERS, tilt_count)
     states = total_blocks * block_size
     product = jnp.ones((tilt_count,), jnp.float32)

time: 193 us -> 193 us (level)
  Pallas kernels: 14.7 us -> 17.3 us
    pallas_call x4, Pallas kernels: 14.7 us -> 17.3 us  [call(): pl.pallas_call(kernel, out_shape=outs, in_specs=[spec[n not in in_vmem] f...]
    exp x1 -> x0, other arithmetic: 2.14 us -> none  [on_device(): jnp.exp(theta[None, :, None] * reward.reshape(blocks_here, 1, block_size))]
  transfers between devices with their start and end apart: 7 -> 7, of which waited for: 7 -> 7; matrix products, arithmetic and copies ran while one was open for 3% -> 2% of each run, Pallas kernels for 0% -> 0%
where the time goes in v5:
time: 193 us; the launch traced here: 192 us
  waiting for transfers between devices  100 us (52%)
  starting transfers between devices  46.3 us (24%)
  blocking collectives  20.7 us (11%)
  Pallas kernels  17.3 us (9%)
  other arithmetic  4.98 us (3%)
  local copies, waits for them, and re-layouts  1.94 us (1%)
    ppermute x2, waiting for transfers between devices, on_device(): after = lax.ppermute(tilted[:half_span], 'rows', down)  48.3 us
    all_to_all x2, waiting for transfers between devices, on_device(): lax.all_to_all(outgoing, 'rows', split_axis=0, concat_axis=0, tiled=True)  24.7 us
    all_to_all x1, blocking collectives, on_device(): lax.all_to_all(sums, 'rows', split_axis=0, concat_axis=0, tiled=True)  20.7 us
    all_to_all x1, starting transfers between devices, on_device(): lax.all_to_all(codes, 'rows', split_axis=0, concat_axis=0, tiled=True)  18.4 us
    ppermute x2, waiting for transfers between devices, on_device(): before = lax.ppermute(tilted[blocks_here - half_span:], 'rows', up)  18 us
    pallas_call x4, Pallas kernels, call(): pl.pallas_call(kernel, out_shape=outs, in_specs=[spec[n not in in_vmem] f...  17.3 us
    all_to_all x2, starting transfers between devices, on_device(): lax.all_to_all(outgoing, 'rows', split_axis=0, concat_axis=0, tiled=True)  16.6 us
    all_to_all x1, waiting for transfers between devices, on_device(): lax.all_to_all(codes, 'rows', split_axis=0, concat_axis=0, tiled=True)  9.32 us
  transfers between devices with their start and end apart: 7, of which 7 were waited for; matrix products, arithmetic and copies ran while one was open for 2% of the time, Pallas kernels for 0%

profile of v5, /device:TPU:1, one launch (start us, length us, event | category | flops | bytes accessed | tf_op | source)
XLA Modules:
  0.0 192.3 jit_solution(7373256040889746489)
XLA Ops:
  0.6 1.6 shard_map.77
  2.2 18.4 %all-to-all-start = ((s32[128,1,1]{2,1,0:T(1,128)}), s32[128,1,1]{2,1,0:T(1,128)S(1)}, u32[]{:S(2)}, u32[]{:S(2)}) async-start(s32[128,1,1]{2,1,0:T(1,128)} %bitcast.17), calls=%async_computation | async-start | bytes 131072 | tf_op jit(solution)/shard_map/all_to_all | solution.py:214
  20.7 0.9 reshape.69.reward
  21.6 0.0 copy-start.3
  21.6 1.3 multiply_convert_fusion.tilted.refs_3_
  22.9 0.0 copy-start
  22.9 9.3 %all-to-all-done = s32[128,1,1]{2,1,0:T(1,128)S(1)} async-done(((s32[128,1,1]{2,1,0:T(1,128)}), s32[128,1,1]{2,1,0:T(1,128)S(1)}, u32[]{:S(2)}, u32[]{:S(2)}) %all-to-all-start) | async-done | bytes 544 | tf_op jit(solution)/shard_map/all_to_all | solution.py:214
  32.2 0.0 copy-start.1
  32.2 2.1 %shard_map.78 = bf16[256,8,512]{2,1,0:T(8,128)(2,1)} custom-call(s32[128,1]{1,0:T(8,128)S(1)} %bitcast.14, bf16[40,8,512]{2,1,0:T(8,128)(2,1)S(1)} %multiply_convert_fusion.tilted.refs_3_), custom_call_target="tpu_custom_call" | custom-call | bytes 2425344 | tf_op jit(solution)/shard_map/pallas_call | solution.py:181
  34.3 0.0 copy-start.4
  34.4 0.0 copy-done.3
  34.4 0.0 copy-done.1
  34.4 6.8 %all-to-all-start.1 = ((bf16[256,8,512]{2,1,0:T(8,128)(2,1)}), bf16[256,8,512]{2,1,0:T(8,128)(2,1)}, u32[]{:S(2)}, u32[]{:S(2)}) async-start(bf16[256,8,512]{2,1,0:T(8,128)(2,1)} %shard_map.78), calls=%async_computation.1 | async-start | bytes 4194304 | tf_op jit(solution)/shard_map/all_to_all | solution.py:264
  41.2 0.0 copy-done
  41.2 3.0 %collective-permute-start.1 = (bf16[20,8,512]{2,1,0:T(8,128)(2,1)S(1)}, bf16[20,8,512]{2,1,0:T(8,128)(2,1)S(1)}, u32[]{:S(2)}, u32[]{:S(2)}) collective-permute-start(bf16[20,8,512]{2,1,0:T(8,128)(2,1)S(1)} %get-tuple-element.16), channel_id=1, source_target_pairs={{4,0},{8,4},{12,8},{16,12},{20,16},{24,20},{28,24},{32,28},{36,32}... | collective-permute-start | bytes 491528 | tf_op jit(solution)/shard_map/ppermute | solution.py:266
  44.2 2.6 %collective-permute-start = (bf16[20,8,512]{2,1,0:T(8,128)(2,1)S(1)}, bf16[20,8,512]{2,1,0:T(8,128)(2,1)S(1)}, u32[]{:S(2)}, u32[]{:S(2)}) collective-permute-start(bf16[20,8,512]{2,1,0:T(8,128)(2,1)S(1)} %get-tuple-element.17), channel_id=1, source_target_pairs={{0,4},{4,8},{8,12},{12,16},{16,20},{20,24},{24,28},{28,32},{32,36}... | collective-permute-start | bytes 491528 | tf_op jit(solution)/shard_map/ppermute | solution.py:265
  46.8 0.0 copy-done.4
  46.9 0.1 copy.27
  47.0 0.7 reshape.70.refs_0_
  47.6 0.1 copy.28
  47.7 0.1 reshape.71
  47.8 0.2 and_reduce_fusion
  48.1 0.6 convert_add_fusion.refs_1_
  48.6 22.3 %collective-permute-done.1.refs_4_ = bf16[20,8,512]{2,1,0:T(8,128)(2,1)S(1)} collective-permute-done((bf16[20,8,512]{2,1,0:T(8,128)(2,1)S(1)}, bf16[20,8,512]{2,1,0:T(8,128)(2,1)S(1)}, u32[]{:S(2)}, u32[]{:S(2)}) %collective-permute-start.1) | collective-permute-done | bytes 163872 | tf_op jit(solution)/shard_map/ppermute | solution.py:266
  71.0 0.0 copy-start.5
  71.0 10.0 %collective-permute-done.refs_2_ = bf16[20,8,512]{2,1,0:T(8,128)(2,1)S(1)} collective-permute-done((bf16[20,8,512]{2,1,0:T(8,128)(2,1)S(1)}, bf16[20,8,512]{2,1,0:T(8,128)(2,1)S(1)}, u32[]{:S(2)}, u32[]{:S(2)}) %collective-permute-start) | collective-permute-done | bytes 163872 | tf_op jit(solution)/shard_map/ppermute | solution.py:265
  81.0 0.0 copy-start.6
  81.0 12.3 %all-to-all-done.1.refs_5_ = bf16[256,8,512]{2,1,0:T(8,128)(2,1)} async-done(((bf16[256,8,512]{2,1,0:T(8,128)(2,1)}), bf16[256,8,512]{2,1,0:T(8,128)(2,1)}, u32[]{:S(2)}, u32[]{:S(2)}) %all-to-all-start.1) | async-done | bytes 2097184 | tf_op jit(solution)/shard_map/all_to_all | solution.py:264
  93.3 0.0 copy-done.5
  93.3 0.0 copy-done.6
  93.3 7.4 %shard_map.79 = (bf16[40,8,512]{2,1,0:T(8,128)(2,1)}, bf16[256,8,512]{2,1,0:T(8,128)(2,1)}, f32[8,128]{1,0:T(8,128)}) custom-call(s32[128,1]{1,0:T(8,128)} %bitcast.15, f32[40,512]{1,0:T(8,128)} %copy-done.3, f32[8]{0:T(128)} %theta.1, s32[320]{0:T(512)} %reshape.70.refs_0_, s32[160]{0:T(256)} %convert_add_fusion.refs_1_, bf16[20,8,512]{2,1,0:T(8,128)(2,1)} %copy-done.6, ...), custom_call_target="tpu_custom_call" | custom-call | flops 2013265920 | bytes 7854496 | tf_op jit(solution)/shard_map/pallas_call | solution.py:181
  100.8 0.0 copy-start.2
  100.8 9.7 %all-to-all-start.2 = ((bf16[256,8,512]{2,1,0:T(8,128)(2,1)}), bf16[256,8,512]{2,1,0:T(8,128)(2,1)}, u32[]{:S(2)}, u32[]{:S(2)}) async-start(bf16[256,8,512]{2,1,0:T(8,128)(2,1)} %get-tuple-element.9), calls=%async_computation.2 | async-start | bytes 4194304 | tf_op jit(solution)/shard_map/all_to_all | solution.py:264
  110.5 0.0 copy-done.2
  110.6 2.9 %collective-permute-start.3 = (bf16[20,8,512]{2,1,0:T(8,128)(2,1)S(1)}, bf16[20,8,512]{2,1,0:T(8,128)(2,1)S(1)}, u32[]{:S(2)}, u32[]{:S(2)}) collective-permute-start(bf16[20,8,512]{2,1,0:T(8,128)(2,1)S(1)} %get-tuple-element.14), channel_id=1, source_target_pairs={{4,0},{8,4},{12,8},{16,12},{20,16},{24,20},{28,24},{32,28},{36,32}... | collective-permute-start | bytes 491528 | tf_op jit(solution)/shard_map/ppermute | solution.py:266
  113.4 2.9 %collective-permute-start.2 = (bf16[20,8,512]{2,1,0:T(8,128)(2,1)S(1)}, bf16[20,8,512]{2,1,0:T(8,128)(2,1)S(1)}, u32[]{:S(2)}, u32[]{:S(2)}) collective-permute-start(bf16[20,8,512]{2,1,0:T(8,128)(2,1)S(1)} %get-tuple-element.15), channel_id=1, source_target_pairs={{0,4},{4,8},{8,12},{12,16},{16,20},{20,24},{24,28},{28,32},{32,36}... | collective-permute-start | bytes 491528 | tf_op jit(solution)/shard_map/ppermute | solution.py:265
  116.3 25.9 %collective-permute-done.3.refs_4_ = bf16[20,8,512]{2,1,0:T(8,128)(2,1)S(1)} collective-permute-done((bf16[20,8,512]{2,1,0:T(8,128)(2,1)S(1)}, bf16[20,8,512]{2,1,0:T(8,128)(2,1)S(1)}, u32[]{:S(2)}, u32[]{:S(2)}) %collective-permute-start.3) | collective-permute-done | bytes 163872 | tf_op jit(solution)/shard_map/ppermute | solution.py:266
  142.3 0.0 copy-start.7
  142.3 8.0 %collective-permute-done.2.refs_2_ = bf16[20,8,512]{2,1,0:T(8,128)(2,1)S(1)} collective-permute-done((bf16[20,8,512]{2,1,0:T(8,128)(2,1)S(1)}, bf16[20,8,512]{2,1,0:T(8,128)(2,1)S(1)}, u32[]{:S(2)}, u32[]{:S(2)}) %collective-permute-start.2) | collective-permute-done | bytes 163872 | tf_op jit(solution)/shard_map/ppermute | solution.py:265
  150.2 12.3 %all-to-all-done.2.refs_5_ = bf16[256,8,512]{2,1,0:T(8,128)(2,1)} async-done(((bf16[256,8,512]{2,1,0:T(8,128)(2,1)}), bf16[256,8,512]{2,1,0:T(8,128)(2,1)}, u32[]{:S(2)}, u32[]{:S(2)}) %all-to-all-start.2) | async-done | bytes 2097184 | tf_op jit(solution)/shard_map/all_to_all | solution.py:264
  162.5 0.0 copy-done.7
  162.5 0.0 copy-done.8
  162.6 6.2 %shard_map.80 = (f32[8,20480]{1,0:T(8,128)}, f32[128,16]{1,0:T(8,128)}) custom-call(f32[8,128]{1,0:T(8,128)} %get-tuple-element.7.first_squares, s32[320]{0:T(512)} %reshape.70.refs_0_, s32[160]{0:T(256)} %convert_add_fusion.refs_1_, bf16[20,8,512]{2,1,0:T(8,128)(2,1)} %copy-done.8, bf16[40,8,512]{2,1,0:T(8,128)(2,1)} %get-tuple-element.8.refs_3_, ...), custom_call_target="tpu_custom_call" | custom-call | flops 2013265920 | bytes 6010752 | tf_op jit(solution)/shard_map/pallas_call | solution.py:181
  168.7 20.7 %all_to_all.30 = f32[128,1,16]{2,1,0:T(1,128)S(1)} all-to-all(f32[128,1,16]{2,1,0:T(1,128)} %bitcast.18), channel_id=1, replica_groups=mesh['rows'=128,'tilt'=4] {'rows'}, dimensions={0} | all-to-all | bytes 16384 | tf_op jit(solution)/shard_map/all_to_all | solution.py:297
  189.5 0.2 reduce_sum.9
  189.6 0.1 multiply_bitcast_fusion
  189.7 0.6 pad_maximum_fusion
  190.3 2.0 %broadcast_divide_fusion = f32[8,20480]{1,0:T(8,128)} fusion(f32[8,20480]{1,0:T(8,128)} %get-tuple-element.10, f32[8]{0:T(128)S(1)} %get-tuple-element.19), kind=kLoop, calls=%fused_computation.1 | loop fusion | flops 163840 | bytes 1310752 | tf_op jit(solution)/shard_map/div | solution.py:306
  (8 shorter events, 0.1 us)
Async XLA Ops:
  2.2 30.0 %all-to-all-start = ((s32[128,1,1]{2,1,0:T(1,128)}), s32[128,1,1]{2,1,0:T(1,128)S(1)}, u32[]{:S(2)}, u32[]{:S(2)}) async-start(s32[128,1,1]{2,1,0:T(1,128)} %bitcast.17), calls=%async_computation | async-start | bytes 131072 | tf_op jit(solution)/shard_map/all_to_all | solution.py:214
  21.6 12.8 %copy-start.3 = (f32[40,512]{1,0:T(8,128)}, f32[40,512]{1,0:T(8,128)S(1)}, u32[]{:S(2)}) copy-start(f32[40,512]{1,0:T(8,128)S(1)} %reshape.69.reward) | copy-start | bytes 245764
  22.9 18.3 %copy-start = (bf16[40,8,512]{2,1,0:T(8,128)(2,1)}, bf16[40,8,512]{2,1,0:T(8,128)(2,1)S(1)}, u32[]{:S(2)}) copy-start(bf16[40,8,512]{2,1,0:T(8,128)(2,1)S(1)} %multiply_convert_fusion.tilted.refs_3_) | copy-start | bytes 983044
  32.2 2.2 %copy-start.1 = (s32[128,1,1]{2,1,0:T(1,128)}, s32[128,1,1]{2,1,0:T(1,128)S(1)}, u32[]{:S(2)}) copy-start(s32[128,1,1]{2,1,0:T(1,128)S(1)} %all-to-all-done) | copy-start | bytes 1540
  34.3 12.5 %copy-start.4 = (s32[40,12]{0,1:T(8,128)S(1)}, s32[40,12]{0,1:T(8,128)}, u32[]{:S(2)}) copy-start(s32[40,12]{0,1:T(8,128)} %param.11) | copy-start | bytes 5764
  34.4 59.0 %all-to-all-start.1 = ((bf16[256,8,512]{2,1,0:T(8,128)(2,1)}), bf16[256,8,512]{2,1,0:T(8,128)(2,1)}, u32[]{:S(2)}, u32[]{:S(2)}) async-start(bf16[256,8,512]{2,1,0:T(8,128)(2,1)} %shard_map.78), calls=%async_computation.1 | async-start | bytes 4194304 | tf_op jit(solution)/shard_map/all_to_all | solution.py:264
  41.2 29.7 %collective-permute-start.1 = (bf16[20,8,512]{2,1,0:T(8,128)(2,1)S(1)}, bf16[20,8,512]{2,1,0:T(8,128)(2,1)S(1)}, u32[]{:S(2)}, u32[]{:S(2)}) collective-permute-start(bf16[20,8,512]{2,1,0:T(8,128)(2,1)S(1)} %get-tuple-element.16), channel_id=1, source_target_pairs={{4,0},{8,4},{12,8},{16,12},{20,16},{24,20},{28,24},{32,28},{36,32}... | collective-permute-start | bytes 491528 | tf_op jit(solution)/shard_map/ppermute | solution.py:266
  44.2 36.8 %collective-permute-start = (bf16[20,8,512]{2,1,0:T(8,128)(2,1)S(1)}, bf16[20,8,512]{2,1,0:T(8,128)(2,1)S(1)}, u32[]{:S(2)}, u32[]{:S(2)}) collective-permute-start(bf16[20,8,512]{2,1,0:T(8,128)(2,1)S(1)} %get-tuple-element.17), channel_id=1, source_target_pairs={{0,4},{4,8},{8,12},{12,16},{16,20},{20,24},{24,28},{28,32},{32,36}... | collective-permute-start | bytes 491528 | tf_op jit(solution)/shard_map/ppermute | solution.py:265
  71.0 22.4 %copy-start.5 = (bf16[20,8,512]{2,1,0:T(8,128)(2,1)}, bf16[20,8,512]{2,1,0:T(8,128)(2,1)S(1)}, u32[]{:S(2)}) copy-start(bf16[20,8,512]{2,1,0:T(8,128)(2,1)S(1)} %collective-permute-done.1.refs_4_) | copy-start | bytes 491524
  81.0 12.3 %copy-start.6 = (bf16[20,8,512]{2,1,0:T(8,128)(2,1)}, bf16[20,8,512]{2,1,0:T(8,128)(2,1)S(1)}, u32[]{:S(2)}) copy-start(bf16[20,8,512]{2,1,0:T(8,128)(2,1)S(1)} %collective-permute-done.refs_2_) | copy-start | bytes 491524
  100.8 9.8 %copy-start.2 = (bf16[40,8,512]{2,1,0:T(8,128)(2,1)S(1)}, bf16[40,8,512]{2,1,0:T(8,128)(2,1)}, u32[]{:S(2)}) copy-start(bf16[40,8,512]{2,1,0:T(8,128)(2,1)} %get-tuple-element.8.refs_3_) | copy-start | bytes 983044
  100.8 61.8 %all-to-all-start.2 = ((bf16[256,8,512]{2,1,0:T(8,128)(2,1)}), bf16[256,8,512]{2,1,0:T(8,128)(2,1)}, u32[]{:S(2)}, u32[]{:S(2)}) async-start(bf16[256,8,512]{2,1,0:T(8,128)(2,1)} %get-tuple-element.9), calls=%async_computation.2 | async-start | bytes 4194304 | tf_op jit(solution)/shard_map/all_to_all | solution.py:264
  110.6 31.7 %collective-permute-start.3 = (bf16[20,8,512]{2,1,0:T(8,128)(2,1)S(1)}, bf16[20,8,512]{2,1,0:T(8,128)(2,1)S(1)}, u32[]{:S(2)}, u32[]{:S(2)}) collective-permute-start(bf16[20,8,512]{2,1,0:T(8,128)(2,1)S(1)} %get-tuple-element.14), channel_id=1, source_target_pairs={{4,0},{8,4},{12,8},{16,12},{20,16},{24,20},{28,24},{32,28},{36,32}... | collective-permute-start | bytes 491528 | tf_op jit(solution)/shard_map/ppermute | solution.py:266
  113.4 36.8 %collective-permute-start.2 = (bf16[20,8,512]{2,1,0:T(8,128)(2,1)S(1)}, bf16[20,8,512]{2,1,0:T(8,128)(2,1)S(1)}, u32[]{:S(2)}, u32[]{:S(2)}) collective-permute-start(bf16[20,8,512]{2,1,0:T(8,128)(2,1)S(1)} %get-tuple-element.15), channel_id=1, source_target_pairs={{0,4},{4,8},{8,12},{12,16},{16,20},{20,24},{24,28},{28,32},{32,36}... | collective-permute-start | bytes 491528 | tf_op jit(solution)/shard_map/ppermute | solution.py:265
  142.3 20.3 %copy-start.7 = (bf16[20,8,512]{2,1,0:T(8,128)(2,1)}, bf16[20,8,512]{2,1,0:T(8,128)(2,1)S(1)}, u32[]{:S(2)}) copy-start(bf16[20,8,512]{2,1,0:T(8,128)(2,1)S(1)} %collective-permute-done.3.refs_4_) | copy-start | bytes 491524
  150.2 12.3 %copy-start.8 = (bf16[20,8,512]{2,1,0:T(8,128)(2,1)}, bf16[20,8,512]{2,1,0:T(8,128)(2,1)S(1)}, u32[]{:S(2)}) copy-start(bf16[20,8,512]{2,1,0:T(8,128)(2,1)S(1)} %collective-permute-done.2.refs_2_) | copy-start | bytes 491524

commit v6 on v5

--- a/solution.py
+++ b/solution.py
@@ -11,6 +11,8 @@
 HALF_WORD = 1 << 16
 VMEM_LIMIT = 62 * 1024 * 1024
 SMALL_LIMIT = 48 * 1024 * 1024
+STEP_LIMIT = 51 * 1024 * 1024
+LAST_LIMIT = 50 * 1024 * 1024
 
 
 def request_kernel(blocks_here, pattern, codes):
@@ -50,8 +52,8 @@
 
         def body(j, carry, part=part):
             word = words[0, part * (chunk // 2) + j]
-            staged[part * chunk + 2 * j] = tilted[lax.rem(word, HALF_WORD)]
-            staged[part * chunk + 2 * j + 1] = tilted[lax.div(word, HALF_WORD)]
+            staged[part * chunk + 2 * j] = tilted[word & (HALF_WORD - 1)]
+            staged[part * chunk + 2 * j + 1] = tilted[lax.shift_right_logical(word, 16)]
             return carry
 
         lax.fori_loop(0, chunk // 2, body, 0, unroll=8)
@@ -85,7 +87,7 @@
 
 def map_blocks(operands, scratch):
     near_index, far_index, before, own, after, arrived, kernels, rates = operands
-    near_smem, far_smem, extended, far_blocks, weights, rate_buf, gathered, sems = scratch
+    near_smem, far_smem, extended, weights, rate_buf, gathered, sems, *far_buf = scratch
     kinds = kernels.shape[0]
     (rows, tilts, _), half = own.shape, before.shape[0]
     far_count = rates.shape[0] - NEAR
@@ -101,10 +103,10 @@
     kernel_copies += [
         start_copy(kernels.at[k], weights.at[k], sems.at[4 + k]) for k in range(1, kinds)
     ]
-    late = [
-        start_copy(far_index, far_smem, sems.at[5 + kinds]),
-        start_copy(arrived, far_blocks, sems.at[6 + kinds]),
-    ]
+    late = [start_copy(far_index, far_smem, sems.at[5 + kinds])]
+    if far_buf:
+        late.append(start_copy(arrived, far_buf[0], sems.at[6 + kinds]))
+        arrived = far_buf[0]
     for copy in first:
         copy.wait()
 
@@ -125,7 +127,7 @@
     for kind in range(kinds):
         slots = range(kind, far_count, kinds)
         product = weighted(
-            far_smem, far_count, slots, far_blocks, weights[kind], gathered.at[kind % 2], rows, tilts
+            far_smem, far_count, slots, arrived, weights[kind], gathered.at[kind % 2], rows, tilts
         )
         for n, slot in enumerate(slots):
             total = total + product[n] * rate_buf[NEAR + slot].astype(jnp.float32)[:, None, :]
@@ -136,27 +138,20 @@
     return jnp.sum(jnp.sum(total * total, axis=0), axis=1, keepdims=True)
 
 
-def step_kernel(codes, reward, theta, *refs):
+def step_kernel(codes, factor, *refs):
     operands, (tilted, outgoing, squares) = refs[:8], refs[8:11]
-    codes_buf, line, words, reward_buf, theta_smem, tilted_buf, staged, pack_sems, sems = refs[11:20]
+    codes_buf, line, words, factor_buf, tilted_buf, staged, pack_sems, sems = refs[11:19]
     codes_copy = start_copy(codes, codes_buf, sems.at[0])
-    reward_copy = start_copy(reward, reward_buf, sems.at[1])
-    theta_copy = start_copy(theta, theta_smem, sems.at[4])
-    total = map_blocks(operands, refs[20:])
-    reward_copy.wait()
-    theta_copy.wait()
+    factor_copy = start_copy(factor, factor_buf, sems.at[1])
+    total = map_blocks(operands, refs[19:])
     codes_copy.wait()
     words_copy = read_words(codes_buf, line, words, sems.at[2])
-    tilt = lax.broadcasted_iota(jnp.int32, total.shape[1:], 0)
-    thetas = jnp.zeros(total.shape[1:], jnp.float32)
-    for t in range(total.shape[1]):
-        thetas = jnp.where(tilt == t, theta_smem[t], thetas)
-    factor = jnp.exp(thetas[None] * reward_buf[...][:, None, :])
-    tilted_buf[...] = (factor * total).astype(jnp.bfloat16)
+    factor_copy.wait()
+    tilted_buf[...] = (factor_buf[...] * total).astype(jnp.bfloat16)
     copies = [start_copy(tilted_buf, tilted, sems.at[3])]
     words_copy.wait()
     copies += pack_blocks(words, tilted_buf, staged, outgoing, pack_sems)
-    squares[...] = jnp.broadcast_to(sum_of_squares(total), squares.shape)
+    squares[...] = jnp.sum(total * total, axis=0)
     for copy in copies:
         copy.wait()
 
@@ -169,7 +164,8 @@
     tilts = total.shape[1]
     across = lax.broadcasted_iota(jnp.int32, (tilts, sums.shape[1]), 1)
     tilt = lax.broadcasted_iota(jnp.int32, (tilts, sums.shape[1]), 0)
-    both = jnp.where(across == tilt, first_squares[:, :1], 0.0) + jnp.where(
+    first = jnp.sum(first_squares[...], axis=1, keepdims=True)
+    both = jnp.where(across == tilt, first, 0.0) + jnp.where(
         across == tilt + tilts, sum_of_squares(total), 0.0
     )
     sums[...] = jnp.broadcast_to(jnp.sum(both, axis=0, keepdims=True), sums.shape)
@@ -230,7 +226,7 @@
     block = (tilt_count, block_size)
     tilted_shape = shape((blocks_here, *block), jnp.bfloat16)
     outgoing_shape = shape((peer_count * capacity, *block), jnp.bfloat16)
-    squares_shape = shape((tilt_count, 128), jnp.float32)
+    squares_shape = shape(block, jnp.float32)
     sums_shape = shape((peer_count, ITERS * tilt_count), jnp.float32)
     mapped_shape = shape(start.shape, jnp.float32)
     word_buffers = [pltpu.VMEM((1, peer_count), jnp.int32), pltpu.SMEM((1, peer_count), jnp.int32)]
@@ -240,7 +236,6 @@
         pltpu.SMEM(near_index.shape, jnp.int32),
         pltpu.SMEM(far_index.shape, jnp.int32),
         pltpu.VMEM((blocks_here + 2 * half_span, *block), jnp.bfloat16),
-        pltpu.VMEM(outgoing_shape.shape, jnp.bfloat16),
         pltpu.VMEM(kernels.shape, jnp.bfloat16),
         pltpu.VMEM(rates_by_slot.shape, jnp.bfloat16),
         pltpu.VMEM((2, gather_rows, block_size), jnp.bfloat16),
@@ -269,20 +264,20 @@
             step_scratch = [
                 pltpu.VMEM(codes.shape, jnp.int32),
                 *word_buffers,
-                pltpu.VMEM(reward.shape, jnp.float32),
-                pltpu.SMEM(theta.shape, jnp.float32),
+                pltpu.VMEM(tilted_shape.shape, jnp.float32),
                 pltpu.VMEM(tilted_shape.shape, jnp.bfloat16),
                 staged,
                 sem((PACK_CHUNKS,)),
-                sem((5,)),
+                sem((4,)),
             ]
             tilted, outgoing, squares = call(
                 step_kernel,
                 [tilted_shape, outgoing_shape, squares_shape],
-                [codes, reward, theta, *operands],
-                step_scratch + map_scratch,
+                [codes, factor, *operands],
+                [*step_scratch, *map_scratch, staged],
                 map_flops,
-                in_vmem=(13,),
+                in_vmem=(12,),
+                limit=STEP_LIMIT,
             )
         else:
             mapped, sums = call(
@@ -291,7 +286,8 @@
                 [squares, *operands],
                 map_scratch,
                 map_flops,
-                in_vmem=(0, 9, 10),
+                in_vmem=(0, 6, 9, 10),
+                limit=LAST_LIMIT,
             )
 
     gathered = lax.all_to_all(sums, "rows", split_axis=0, concat_axis=0, tiled=True)

time: 193 us -> 190 us (0.984)
  waiting for transfers between devices: 100 us -> 102 us
where the time goes in v6:
time: 190 us; the launch traced here: 189 us
  waiting for transfers between devices  102 us (54%)
  starting transfers between devices  45.2 us (24%)
  blocking collectives  19.9 us (10%)
  Pallas kernels  15.6 us (8%)
  other arithmetic  3.3 us (2%)
  local copies, waits for them, and re-layouts  2.36 us (1%)
    ppermute x2, waiting for transfers between devices, on_device(): after = lax.ppermute(tilted[:half_span], 'rows', down)  49.5 us
    all_to_all x2, waiting for transfers between devices, on_device(): lax.all_to_all(outgoing, 'rows', split_axis=0, concat_axis=0, tiled=True)  24.9 us
    all_to_all x1, blocking collectives, on_device(): lax.all_to_all(sums, 'rows', split_axis=0, concat_axis=0, tiled=True)  19.9 us
    all_to_all x1, starting transfers between devices, on_device(): lax.all_to_all(codes, 'rows', split_axis=0, concat_axis=0, tiled=True)  18.4 us
    ppermute x2, waiting for transfers between devices, on_device(): before = lax.ppermute(tilted[blocks_here - half_span:], 'rows', up)  18.1 us
    pallas_call x4, Pallas kernels, call(): pl.pallas_call(kernel, out_shape=outs, in_specs=[spec[n not in in_vmem] f...  15.6 us
    all_to_all x2, starting transfers between devices, on_device(): lax.all_to_all(outgoing, 'rows', split_axis=0, concat_axis=0, tiled=True)  15.5 us
    all_to_all x1, waiting for transfers between devices, on_device(): lax.all_to_all(codes, 'rows', split_axis=0, concat_axis=0, tiled=True)  9.26 us
  transfers between devices with their start and end apart: 7, of which 7 were waited for; matrix products, arithmetic and copies ran while one was open for 2% of the time, Pallas kernels for 0%

profile of v6, /device:TPU:1, one launch (start us, length us, event | category | flops | bytes accessed | tf_op | source)
XLA Modules:
  0.0 188.9 jit_solution(12321020273157522993)
XLA Ops:
  0.6 1.6 shard_map.77
  2.2 18.4 %all-to-all-start = ((s32[128,1,1]{2,1,0:T(1,128)}), s32[128,1,1]{2,1,0:T(1,128)S(1)}, u32[]{:S(2)}, u32[]{:S(2)}) async-start(s32[128,1,1]{2,1,0:T(1,128)} %bitcast.20), calls=%async_computation | async-start | bytes 131072 | tf_op jit(solution)/shard_map/all_to_all | solution.py:210
  20.7 0.9 mul.33
  21.6 1.3 multiply_convert_fusion
  22.8 9.3 %all-to-all-done = s32[128,1,1]{2,1,0:T(1,128)S(1)} async-done(((s32[128,1,1]{2,1,0:T(1,128)}), s32[128,1,1]{2,1,0:T(1,128)S(1)}, u32[]{:S(2)}, u32[]{:S(2)}) %all-to-all-start) | async-done | bytes 544 | tf_op jit(solution)/shard_map/all_to_all | solution.py:210
  32.1 2.1 %shard_map.78 = bf16[256,8,512]{2,1,0:T(8,128)(2,1)} custom-call(s32[128,1]{1,0:T(8,128)S(1)} %bitcast.14, bf16[40,8,512]{2,1,0:T(8,128)(2,1)S(1)} %get-tuple-element.18.tilted.refs_3_), custom_call_target="tpu_custom_call" | custom-call | bytes 2425344 | tf_op jit(solution)/shard_map/pallas_call | solution.py:177
  34.2 0.0 copy-start.2
  34.2 0.0 copy-start
  34.2 7.0 %all-to-all-start.1 = ((bf16[256,8,512]{2,1,0:T(8,128)(2,1)}), bf16[256,8,512]{2,1,0:T(8,128)(2,1)}, u32[]{:S(2)}, u32[]{:S(2)}) async-start(bf16[256,8,512]{2,1,0:T(8,128)(2,1)} %shard_map.78), calls=%async_computation.1 | async-start | bytes 4194304 | tf_op jit(solution)/shard_map/all_to_all | solution.py:259
  41.2 3.0 %collective-permute-start.1 = (bf16[20,8,512]{2,1,0:T(8,128)(2,1)S(1)}, bf16[20,8,512]{2,1,0:T(8,128)(2,1)S(1)}, u32[]{:S(2)}, u32[]{:S(2)}) collective-permute-start(bf16[20,8,512]{2,1,0:T(8,128)(2,1)S(1)} %get-tuple-element.16), channel_id=1, source_target_pairs={{4,0},{8,4},{12,8},{16,12},{20,16},{24,20},{28,24},{32,28},{36,32}... | collective-permute-start | bytes 491528 | tf_op jit(solution)/shard_map/ppermute | solution.py:261
  44.2 2.6 %collective-permute-start = (bf16[20,8,512]{2,1,0:T(8,128)(2,1)S(1)}, bf16[20,8,512]{2,1,0:T(8,128)(2,1)S(1)}, u32[]{:S(2)}, u32[]{:S(2)}) collective-permute-start(bf16[20,8,512]{2,1,0:T(8,128)(2,1)S(1)} %get-tuple-element.17), channel_id=1, source_target_pairs={{0,4},{4,8},{8,12},{12,16},{16,20},{20,24},{24,28},{28,32},{32,36}... | collective-permute-start | bytes 491528 | tf_op jit(solution)/shard_map/ppermute | solution.py:260
  46.8 0.0 copy-done.2
  46.9 0.1 copy.27
  46.9 0.1 reshape.66.refs_0_
  47.0 0.1 copy.28
  47.1 0.1 reshape.67
  47.2 0.2 and_reduce_fusion
  47.5 23.5 %collective-permute-done.1.refs_4_ = bf16[20,8,512]{2,1,0:T(8,128)(2,1)S(1)} collective-permute-done((bf16[20,8,512]{2,1,0:T(8,128)(2,1)S(1)}, bf16[20,8,512]{2,1,0:T(8,128)(2,1)S(1)}, u32[]{:S(2)}, u32[]{:S(2)}) %collective-permute-start.1) | collective-permute-done | bytes 163872 | tf_op jit(solution)/shard_map/ppermute | solution.py:261
  71.0 10.0 %collective-permute-done.refs_2_ = bf16[20,8,512]{2,1,0:T(8,128)(2,1)S(1)} collective-permute-done((bf16[20,8,512]{2,1,0:T(8,128)(2,1)S(1)}, bf16[20,8,512]{2,1,0:T(8,128)(2,1)S(1)}, u32[]{:S(2)}, u32[]{:S(2)}) %collective-permute-start) | collective-permute-done | bytes 163872 | tf_op jit(solution)/shard_map/ppermute | solution.py:260
  81.0 12.3 %all-to-all-done.1.refs_5_ = bf16[256,8,512]{2,1,0:T(8,128)(2,1)} async-done(((bf16[256,8,512]{2,1,0:T(8,128)(2,1)}), bf16[256,8,512]{2,1,0:T(8,128)(2,1)}, u32[]{:S(2)}, u32[]{:S(2)}) %all-to-all-start.1) | async-done | bytes 2097184 | tf_op jit(solution)/shard_map/all_to_all | solution.py:259
  93.3 0.0 copy-done
  93.3 7.1 %shard_map.79 = (bf16[40,8,512]{2,1,0:T(8,128)(2,1)S(1)}, bf16[256,8,512]{2,1,0:T(8,128)(2,1)}, f32[8,512]{1,0:T(8,128)S(1)}) custom-call(s32[128,1]{1,0:T(8,128)S(1)} %bitcast.15, f32[40,8,512]{2,1,0:T(8,128)S(1)} %get-tuple-element.19.factor, s32[320]{0:T(512)S(1)} %reshape.66.refs_0_, s32[160]{0:T(256)S(1)} %convert_add_fusion.refs_1_, ...), custom_call_target="tpu_custom_call" | custom-call | flops 2013265920 | bytes 8440192 | tf_op jit(solution)/shard_map/pallas_call | solution.py:177
  100.5 8.5 %all-to-all-start.2 = ((bf16[256,8,512]{2,1,0:T(8,128)(2,1)}), bf16[256,8,512]{2,1,0:T(8,128)(2,1)S(1)}, u32[]{:S(2)}, u32[]{:S(2)}) async-start(bf16[256,8,512]{2,1,0:T(8,128)(2,1)} %get-tuple-element.9), calls=%async_computation.2 | async-start | bytes 4194304 | tf_op jit(solution)/shard_map/all_to_all | solution.py:259
  109.0 2.8 %collective-permute-start.3 = (bf16[20,8,512]{2,1,0:T(8,128)(2,1)S(1)}, bf16[20,8,512]{2,1,0:T(8,128)(2,1)S(1)}, u32[]{:S(2)}, u32[]{:S(2)}) collective-permute-start(bf16[20,8,512]{2,1,0:T(8,128)(2,1)S(1)} %get-tuple-element.14), channel_id=1, source_target_pairs={{4,0},{8,4},{12,8},{16,12},{20,16},{24,20},{28,24},{32,28},{36,32}... | collective-permute-start | bytes 491528 | tf_op jit(solution)/shard_map/ppermute | solution.py:261
  111.8 2.9 %collective-permute-start.2 = (bf16[20,8,512]{2,1,0:T(8,128)(2,1)S(1)}, bf16[20,8,512]{2,1,0:T(8,128)(2,1)S(1)}, u32[]{:S(2)}, u32[]{:S(2)}) collective-permute-start(bf16[20,8,512]{2,1,0:T(8,128)(2,1)S(1)} %get-tuple-element.15), channel_id=1, source_target_pairs={{0,4},{4,8},{8,12},{12,16},{16,20},{20,24},{24,28},{28,32},{32,36}... | collective-permute-start | bytes 491528 | tf_op jit(solution)/shard_map/ppermute | solution.py:260
  114.8 26.0 %collective-permute-done.3.refs_4_ = bf16[20,8,512]{2,1,0:T(8,128)(2,1)S(1)} collective-permute-done((bf16[20,8,512]{2,1,0:T(8,128)(2,1)S(1)}, bf16[20,8,512]{2,1,0:T(8,128)(2,1)S(1)}, u32[]{:S(2)}, u32[]{:S(2)}) %collective-permute-start.3) | collective-permute-done | bytes 163872 | tf_op jit(solution)/shard_map/ppermute | solution.py:261
  140.7 8.1 %collective-permute-done.2.refs_2_ = bf16[20,8,512]{2,1,0:T(8,128)(2,1)S(1)} collective-permute-done((bf16[20,8,512]{2,1,0:T(8,128)(2,1)S(1)}, bf16[20,8,512]{2,1,0:T(8,128)(2,1)S(1)}, u32[]{:S(2)}, u32[]{:S(2)}) %collective-permute-start.2) | collective-permute-done | bytes 163872 | tf_op jit(solution)/shard_map/ppermute | solution.py:260
  148.8 12.5 %all-to-all-done.2.refs_5_ = bf16[256,8,512]{2,1,0:T(8,128)(2,1)S(1)} async-done(((bf16[256,8,512]{2,1,0:T(8,128)(2,1)}), bf16[256,8,512]{2,1,0:T(8,128)(2,1)S(1)}, u32[]{:S(2)}, u32[]{:S(2)}) %all-to-all-start.2) | async-done | bytes 2097184 | tf_op jit(solution)/shard_map/all_to_all | solution.py:259
  161.3 0.0 copy-start.1
  161.3 1.0 copy-done.1
  162.4 4.8 %shard_map.80 = (f32[8,20480]{1,0:T(8,128)S(1)}, f32[128,16]{1,0:T(8,128)S(1)}) custom-call(f32[8,512]{1,0:T(8,128)S(1)} %get-tuple-element.7.first_squares, s32[320]{0:T(512)S(1)} %reshape.66.refs_0_, s32[160]{0:T(256)S(1)} %convert_add_fusion.refs_1_, bf16[20,8,512]{2,1,0:T(8,128)(2,1)S(1)} %collective-permute-done.2.refs_2_, ...), custom_call_target="tpu_custom_call" | custom-call | flops 2013265920 | bytes 6023040 | tf_op jit(solution)/shard_map/pallas_call | solution.py:177
  167.2 19.9 %all_to_all.30 = f32[128,1,16]{2,1,0:T(1,128)S(1)} all-to-all(f32[128,1,16]{2,1,0:T(1,128)S(1)} %bitcast.16), channel_id=1, replica_groups=mesh['rows'=128,'tilt'=4] {'rows'}, dimensions={0} | all-to-all | bytes 16384 | tf_op jit(solution)/shard_map/all_to_all | solution.py:293
  187.2 0.2 reduce_sum.9
  187.3 0.1 multiply_bitcast_fusion
  187.4 0.6 pad_maximum_fusion
  188.0 1.0 broadcast_divide_fusion
  (8 shorter events, 0.1 us)
Async XLA Ops:
  2.2 29.9 %all-to-all-start = ((s32[128,1,1]{2,1,0:T(1,128)}), s32[128,1,1]{2,1,0:T(1,128)S(1)}, u32[]{:S(2)}, u32[]{:S(2)}) async-start(s32[128,1,1]{2,1,0:T(1,128)} %bitcast.20), calls=%async_computation | async-start | bytes 131072 | tf_op jit(solution)/shard_map/all_to_all | solution.py:210
  34.2 12.6 %copy-start.2 = (s32[40,12]{0,1:T(8,128)S(1)}, s32[40,12]{0,1:T(8,128)}, u32[]{:S(2)}) copy-start(s32[40,12]{0,1:T(8,128)} %param.11) | copy-start | bytes 5764
  34.2 59.1 %copy-start = (bf16[40,12,512]{2,0,1:T(8,128)(2,1)S(1)}, bf16[40,12,512]{2,0,1:T(8,128)(2,1)}, u32[]{:S(2)}) copy-start(bf16[40,12,512]{2,0,1:T(8,128)(2,1)} %param.10) | copy-start | bytes 1474564
  34.2 59.1 %all-to-all-start.1 = ((bf16[256,8,512]{2,1,0:T(8,128)(2,1)}), bf16[256,8,512]{2,1,0:T(8,128)(2,1)}, u32[]{:S(2)}, u32[]{:S(2)}) async-start(bf16[256,8,512]{2,1,0:T(8,128)(2,1)} %shard_map.78), calls=%async_computation.1 | async-start | bytes 4194304 | tf_op jit(solution)/shard_map/all_to_all | solution.py:259
  41.2 29.8 %collective-permute-start.1 = (bf16[20,8,512]{2,1,0:T(8,128)(2,1)S(1)}, bf16[20,8,512]{2,1,0:T(8,128)(2,1)S(1)}, u32[]{:S(2)}, u32[]{:S(2)}) collective-permute-start(bf16[20,8,512]{2,1,0:T(8,128)(2,1)S(1)} %get-tuple-element.16), channel_id=1, source_target_pairs={{4,0},{8,4},{12,8},{16,12},{20,16},{24,20},{28,24},{32,28},{36,32}... | collective-permute-start | bytes 491528 | tf_op jit(solution)/shard_map/ppermute | solution.py:261
  44.2 36.8 %collective-permute-start = (bf16[20,8,512]{2,1,0:T(8,128)(2,1)S(1)}, bf16[20,8,512]{2,1,0:T(8,128)(2,1)S(1)}, u32[]{:S(2)}, u32[]{:S(2)}) collective-permute-start(bf16[20,8,512]{2,1,0:T(8,128)(2,1)S(1)} %get-tuple-element.17), channel_id=1, source_target_pairs={{0,4},{4,8},{8,12},{12,16},{16,20},{20,24},{24,28},{28,32},{32,36}... | collective-permute-start | bytes 491528 | tf_op jit(solution)/shard_map/ppermute | solution.py:260
  100.5 60.9 %all-to-all-start.2 = ((bf16[256,8,512]{2,1,0:T(8,128)(2,1)}), bf16[256,8,512]{2,1,0:T(8,128)(2,1)S(1)}, u32[]{:S(2)}, u32[]{:S(2)}) async-start(bf16[256,8,512]{2,1,0:T(8,128)(2,1)} %get-tuple-element.9), calls=%async_computation.2 | async-start | bytes 4194304 | tf_op jit(solution)/shard_map/all_to_all | solution.py:259
  109.0 31.7 %collective-permute-start.3 = (bf16[20,8,512]{2,1,0:T(8,128)(2,1)S(1)}, bf16[20,8,512]{2,1,0:T(8,128)(2,1)S(1)}, u32[]{:S(2)}, u32[]{:S(2)}) collective-permute-start(bf16[20,8,512]{2,1,0:T(8,128)(2,1)S(1)} %get-tuple-element.14), channel_id=1, source_target_pairs={{4,0},{8,4},{12,8},{16,12},{20,16},{24,20},{28,24},{32,28},{36,32}... | collective-permute-start | bytes 491528 | tf_op jit(solution)/shard_map/ppermute | solution.py:261
  111.8 37.0 %collective-permute-start.2 = (bf16[20,8,512]{2,1,0:T(8,128)(2,1)S(1)}, bf16[20,8,512]{2,1,0:T(8,128)(2,1)S(1)}, u32[]{:S(2)}, u32[]{:S(2)}) collective-permute-start(bf16[20,8,512]{2,1,0:T(8,128)(2,1)S(1)} %get-tuple-element.15), channel_id=1, source_target_pairs={{0,4},{4,8},{8,12},{12,16},{16,20},{20,24},{24,28},{28,32},{32,36}... | collective-permute-start | bytes 491528 | tf_op jit(solution)/shard_map/ppermute | solution.py:260
  161.3 1.0 copy-start.1

commit v7 on v6

--- a/solution.py
+++ b/solution.py
@@ -9,10 +9,9 @@
 ITERS = 2
 PACK_CHUNKS = 8
 HALF_WORD = 1 << 16
-VMEM_LIMIT = 62 * 1024 * 1024
-SMALL_LIMIT = 48 * 1024 * 1024
-STEP_LIMIT = 51 * 1024 * 1024
-LAST_LIMIT = 50 * 1024 * 1024
+REQUEST_LIMIT = 62 * 1024 * 1024
+PACK_LIMIT = 48 * 1024 * 1024
+MAP_LIMIT = 51 * 1024 * 1024
 
 
 def request_kernel(blocks_here, pattern, codes):
@@ -85,9 +84,9 @@
     return product.reshape(len(slots), rows, tilts, weights.shape[1])
 
 
-def map_blocks(operands, scratch):
+def map_blocks(operands, scratch, meanwhile=None):
     near_index, far_index, before, own, after, arrived, kernels, rates = operands
-    near_smem, far_smem, extended, weights, rate_buf, gathered, sems, *far_buf = scratch
+    near_smem, far_smem, extended, far_blocks, weights, rate_buf, gathered, sems = scratch
     kinds = kernels.shape[0]
     (rows, tilts, _), half = own.shape, before.shape[0]
     far_count = rates.shape[0] - NEAR
@@ -103,10 +102,12 @@
     kernel_copies += [
         start_copy(kernels.at[k], weights.at[k], sems.at[4 + k]) for k in range(1, kinds)
     ]
-    late = [start_copy(far_index, far_smem, sems.at[5 + kinds])]
-    if far_buf:
-        late.append(start_copy(arrived, far_buf[0], sems.at[6 + kinds]))
-        arrived = far_buf[0]
+    late = [
+        start_copy(far_index, far_smem, sems.at[5 + kinds]),
+        start_copy(arrived, far_blocks, sems.at[6 + kinds]),
+    ]
+    if meanwhile is not None:
+        meanwhile()
     for copy in first:
         copy.wait()
 
@@ -127,7 +128,7 @@
     for kind in range(kinds):
         slots = range(kind, far_count, kinds)
         product = weighted(
-            far_smem, far_count, slots, arrived, weights[kind], gathered.at[kind % 2], rows, tilts
+            far_smem, far_count, slots, far_blocks, weights[kind], gathered.at[kind % 2], rows, tilts
         )
         for n, slot in enumerate(slots):
             total = total + product[n] * rate_buf[NEAR + slot].astype(jnp.float32)[:, None, :]
@@ -142,10 +143,15 @@
     operands, (tilted, outgoing, squares) = refs[:8], refs[8:11]
     codes_buf, line, words, factor_buf, tilted_buf, staged, pack_sems, sems = refs[11:19]
     codes_copy = start_copy(codes, codes_buf, sems.at[0])
-    factor_copy = start_copy(factor, factor_buf, sems.at[1])
-    total = map_blocks(operands, refs[19:])
-    codes_copy.wait()
-    words_copy = read_words(codes_buf, line, words, sems.at[2])
+    waits = []
+
+    def decode():
+        waits.append(start_copy(factor, factor_buf, sems.at[1]))
+        codes_copy.wait()
+        waits.append(read_words(codes_buf, line, words, sems.at[2]))
+
+    total = map_blocks(operands, refs[19:], decode)
+    factor_copy, words_copy = waits
     factor_copy.wait()
     tilted_buf[...] = (factor_buf[...] * total).astype(jnp.bfloat16)
     copies = [start_copy(tilted_buf, tilted, sems.at[3])]
@@ -171,7 +177,7 @@
     sums[...] = jnp.broadcast_to(jnp.sum(both, axis=0, keepdims=True), sums.shape)
 
 
-def call(kernel, outs, arrays, scratch, flops, in_vmem=(), limit=VMEM_LIMIT):
+def call(kernel, outs, arrays, scratch, flops, limit, in_vmem=()):
     spec = [pl.BlockSpec(memory_space=pltpu.VMEM), pl.BlockSpec(memory_space=pl.ANY)]
     moved = sum(a.size * a.dtype.itemsize for a in (*arrays, *outs))
     return pl.pallas_call(
@@ -205,6 +211,7 @@
         [pattern_by_slot],
         [],
         0,
+        REQUEST_LIMIT,
         in_vmem=(0, 1),
     )
     codes = lax.all_to_all(codes, "rows", split_axis=0, concat_axis=0, tiled=True)
@@ -236,6 +243,7 @@
         pltpu.SMEM(near_index.shape, jnp.int32),
         pltpu.SMEM(far_index.shape, jnp.int32),
         pltpu.VMEM((blocks_here + 2 * half_span, *block), jnp.bfloat16),
+        staged,
         pltpu.VMEM(kernels.shape, jnp.bfloat16),
         pltpu.VMEM(rates_by_slot.shape, jnp.bfloat16),
         pltpu.VMEM((2, gather_rows, block_size), jnp.bfloat16),
@@ -252,8 +260,8 @@
         [codes, tilted],
         [*word_buffers, staged, sem, sem((PACK_CHUNKS,))],
         0,
+        PACK_LIMIT,
         in_vmem=(0, 1),
-        limit=SMALL_LIMIT,
     )
     for iteration in range(ITERS):
         arrived = lax.all_to_all(outgoing, "rows", split_axis=0, concat_axis=0, tiled=True)
@@ -274,10 +282,10 @@
                 step_kernel,
                 [tilted_shape, outgoing_shape, squares_shape],
                 [codes, factor, *operands],
-                [*step_scratch, *map_scratch, staged],
+                step_scratch + map_scratch,
                 map_flops,
+                MAP_LIMIT,
                 in_vmem=(12,),
-                limit=STEP_LIMIT,
             )
         else:
             mapped, sums = call(
@@ -286,8 +294,8 @@
                 [squares, *operands],
                 map_scratch,
                 map_flops,
-                in_vmem=(0, 6, 9, 10),
-                limit=LAST_LIMIT,
+                MAP_LIMIT,
+                in_vmem=(0, 9, 10),
             )
 
     gathered = lax.all_to_all(sums, "rows", split_axis=0, concat_axis=0, tiled=True)

time: 190 us -> 188 us (0.989)
  no operation moved by 1% of the time
where the time goes in v7:
time: 188 us; the launch traced here: 187 us
  waiting for transfers between devices  101 us (54%)
  starting transfers between devices  45.6 us (24%)
  blocking collectives  19.8 us (11%)
  Pallas kernels  15 us (8%)
  other arithmetic  3.3 us (2%)
    ppermute x2, waiting for transfers between devices, on_device(): after = lax.ppermute(tilted[:half_span], 'rows', down)  49.5 us
    all_to_all x2, waiting for transfers between devices, on_device(): lax.all_to_all(outgoing, 'rows', split_axis=0, concat_axis=0, tiled=True)  24.7 us
    all_to_all x1, blocking collectives, on_device(): lax.all_to_all(sums, 'rows', split_axis=0, concat_axis=0, tiled=True)  19.8 us
    all_to_all x1, starting transfers between devices, on_device(): lax.all_to_all(codes, 'rows', split_axis=0, concat_axis=0, tiled=True)  18.4 us
    ppermute x2, waiting for transfers between devices, on_device(): before = lax.ppermute(tilted[blocks_here - half_span:], 'rows', up)  18 us
    all_to_all x2, starting transfers between devices, on_device(): lax.all_to_all(outgoing, 'rows', split_axis=0, concat_axis=0, tiled=True)  15.9 us
    pallas_call x4, Pallas kernels, call(): pl.pallas_call(kernel, out_shape=outs, in_specs=[spec[n not in in_vmem] f...  15 us
    all_to_all x1, waiting for transfers between devices, on_device(): lax.all_to_all(codes, 'rows', split_axis=0, concat_axis=0, tiled=True)  9.26 us
  transfers between devices with their start and end apart: 7, of which 7 were waited for; matrix products, arithmetic and copies ran while one was open for 2% of the time, Pallas kernels for 0%

profile of v7, /device:TPU:1, one launch (start us, length us, event | category | flops | bytes accessed | tf_op | source)
XLA Modules:
  0.0 187.3 jit_solution(16905848515462374992)
XLA Ops:
  0.6 1.6 shard_map.77
  2.2 18.4 %all-to-all-start = ((s32[128,1,1]{2,1,0:T(1,128)}), s32[128,1,1]{2,1,0:T(1,128)S(1)}, u32[]{:S(2)}, u32[]{:S(2)}) async-start(s32[128,1,1]{2,1,0:T(1,128)} %bitcast.20), calls=%async_computation | async-start | bytes 131072 | tf_op jit(solution)/shard_map/all_to_all | solution.py:217
  20.7 0.9 mul.33
  21.6 1.3 multiply_convert_fusion
  22.8 9.3 %all-to-all-done = s32[128,1,1]{2,1,0:T(1,128)S(1)} async-done(((s32[128,1,1]{2,1,0:T(1,128)}), s32[128,1,1]{2,1,0:T(1,128)S(1)}, u32[]{:S(2)}, u32[]{:S(2)}) %all-to-all-start) | async-done | bytes 544 | tf_op jit(solution)/shard_map/all_to_all | solution.py:217
  32.1 2.1 %shard_map.78 = bf16[256,8,512]{2,1,0:T(8,128)(2,1)} custom-call(s32[128,1]{1,0:T(8,128)S(1)} %bitcast.14, bf16[40,8,512]{2,1,0:T(8,128)(2,1)S(1)} %get-tuple-element.18.tilted.refs_3_), custom_call_target="tpu_custom_call" | custom-call | bytes 2425344 | tf_op jit(solution)/shard_map/pallas_call | solution.py:183
  34.2 0.0 copy-start.1
  34.2 0.0 copy-start
  34.2 7.0 %all-to-all-start.1 = ((bf16[256,8,512]{2,1,0:T(8,128)(2,1)}), bf16[256,8,512]{2,1,0:T(8,128)(2,1)}, u32[]{:S(2)}, u32[]{:S(2)}) async-start(bf16[256,8,512]{2,1,0:T(8,128)(2,1)} %shard_map.78), calls=%async_computation.1 | async-start | bytes 4194304 | tf_op jit(solution)/shard_map/all_to_all | solution.py:267
  41.2 3.0 %collective-permute-start.1 = (bf16[20,8,512]{2,1,0:T(8,128)(2,1)S(1)}, bf16[20,8,512]{2,1,0:T(8,128)(2,1)S(1)}, u32[]{:S(2)}, u32[]{:S(2)}) collective-permute-start(bf16[20,8,512]{2,1,0:T(8,128)(2,1)S(1)} %get-tuple-element.16), channel_id=1, source_target_pairs={{4,0},{8,4},{12,8},{16,12},{20,16},{24,20},{28,24},{32,28},{36,32}... | collective-permute-start | bytes 491528 | tf_op jit(solution)/shard_map/ppermute | solution.py:269
  44.2 2.6 %collective-permute-start = (bf16[20,8,512]{2,1,0:T(8,128)(2,1)S(1)}, bf16[20,8,512]{2,1,0:T(8,128)(2,1)S(1)}, u32[]{:S(2)}, u32[]{:S(2)}) collective-permute-start(bf16[20,8,512]{2,1,0:T(8,128)(2,1)S(1)} %get-tuple-element.17), channel_id=1, source_target_pairs={{0,4},{4,8},{8,12},{12,16},{16,20},{20,24},{24,28},{28,32},{32,36}... | collective-permute-start | bytes 491528 | tf_op jit(solution)/shard_map/ppermute | solution.py:268
  46.8 0.0 copy-done.1
  46.8 0.1 copy.27
  46.9 0.1 reshape.66.refs_0_
  47.0 0.1 copy.28
  47.1 0.1 reshape.67
  47.2 0.2 and_reduce_fusion
  47.5 23.5 %collective-permute-done.1.refs_4_ = bf16[20,8,512]{2,1,0:T(8,128)(2,1)S(1)} collective-permute-done((bf16[20,8,512]{2,1,0:T(8,128)(2,1)S(1)}, bf16[20,8,512]{2,1,0:T(8,128)(2,1)S(1)}, u32[]{:S(2)}, u32[]{:S(2)}) %collective-permute-start.1) | collective-permute-done | bytes 163872 | tf_op jit(solution)/shard_map/ppermute | solution.py:269
  71.0 10.0 %collective-permute-done.refs_2_ = bf16[20,8,512]{2,1,0:T(8,128)(2,1)S(1)} collective-permute-done((bf16[20,8,512]{2,1,0:T(8,128)(2,1)S(1)}, bf16[20,8,512]{2,1,0:T(8,128)(2,1)S(1)}, u32[]{:S(2)}, u32[]{:S(2)}) %collective-permute-start) | collective-permute-done | bytes 163872 | tf_op jit(solution)/shard_map/ppermute | solution.py:268
  81.0 12.3 %all-to-all-done.1.refs_5_ = bf16[256,8,512]{2,1,0:T(8,128)(2,1)} async-done(((bf16[256,8,512]{2,1,0:T(8,128)(2,1)}), bf16[256,8,512]{2,1,0:T(8,128)(2,1)}, u32[]{:S(2)}, u32[]{:S(2)}) %all-to-all-start.1) | async-done | bytes 2097184 | tf_op jit(solution)/shard_map/all_to_all | solution.py:267
  93.3 0.0 copy-done
  93.3 6.5 %shard_map.79 = (bf16[40,8,512]{2,1,0:T(8,128)(2,1)S(1)}, bf16[256,8,512]{2,1,0:T(8,128)(2,1)}, f32[8,512]{1,0:T(8,128)S(1)}) custom-call(s32[128,1]{1,0:T(8,128)S(1)} %bitcast.15, f32[40,8,512]{2,1,0:T(8,128)S(1)} %get-tuple-element.19.factor, s32[320]{0:T(512)S(1)} %reshape.66.refs_0_, s32[160]{0:T(256)S(1)} %convert_add_fusion.refs_1_, ...), custom_call_target="tpu_custom_call" | custom-call | flops 2013265920 | bytes 8440192 | tf_op jit(solution)/shard_map/pallas_call | solution.py:183
  99.8 9.0 %all-to-all-start.2 = ((bf16[256,8,512]{2,1,0:T(8,128)(2,1)}), bf16[256,8,512]{2,1,0:T(8,128)(2,1)}, u32[]{:S(2)}, u32[]{:S(2)}) async-start(bf16[256,8,512]{2,1,0:T(8,128)(2,1)} %get-tuple-element.9), calls=%async_computation.2 | async-start | bytes 4194304 | tf_op jit(solution)/shard_map/all_to_all | solution.py:267
  108.8 2.9 %collective-permute-start.3 = (bf16[20,8,512]{2,1,0:T(8,128)(2,1)S(1)}, bf16[20,8,512]{2,1,0:T(8,128)(2,1)S(1)}, u32[]{:S(2)}, u32[]{:S(2)}) collective-permute-start(bf16[20,8,512]{2,1,0:T(8,128)(2,1)S(1)} %get-tuple-element.14), channel_id=1, source_target_pairs={{4,0},{8,4},{12,8},{16,12},{20,16},{24,20},{28,24},{32,28},{36,32}... | collective-permute-start | bytes 491528 | tf_op jit(solution)/shard_map/ppermute | solution.py:269
  111.7 2.9 %collective-permute-start.2 = (bf16[20,8,512]{2,1,0:T(8,128)(2,1)S(1)}, bf16[20,8,512]{2,1,0:T(8,128)(2,1)S(1)}, u32[]{:S(2)}, u32[]{:S(2)}) collective-permute-start(bf16[20,8,512]{2,1,0:T(8,128)(2,1)S(1)} %get-tuple-element.15), channel_id=1, source_target_pairs={{0,4},{4,8},{8,12},{12,16},{16,20},{20,24},{24,28},{28,32},{32,36}... | collective-permute-start | bytes 491528 | tf_op jit(solution)/shard_map/ppermute | solution.py:268
  114.5 26.0 %collective-permute-done.3.refs_4_ = bf16[20,8,512]{2,1,0:T(8,128)(2,1)S(1)} collective-permute-done((bf16[20,8,512]{2,1,0:T(8,128)(2,1)S(1)}, bf16[20,8,512]{2,1,0:T(8,128)(2,1)S(1)}, u32[]{:S(2)}, u32[]{:S(2)}) %collective-permute-start.3) | collective-permute-done | bytes 163872 | tf_op jit(solution)/shard_map/ppermute | solution.py:269
  140.5 8.0 %collective-permute-done.2.refs_2_ = bf16[20,8,512]{2,1,0:T(8,128)(2,1)S(1)} collective-permute-done((bf16[20,8,512]{2,1,0:T(8,128)(2,1)S(1)}, bf16[20,8,512]{2,1,0:T(8,128)(2,1)S(1)}, u32[]{:S(2)}, u32[]{:S(2)}) %collective-permute-start.2) | collective-permute-done | bytes 163872 | tf_op jit(solution)/shard_map/ppermute | solution.py:268
  148.4 12.3 %all-to-all-done.2.refs_5_ = bf16[256,8,512]{2,1,0:T(8,128)(2,1)} async-done(((bf16[256,8,512]{2,1,0:T(8,128)(2,1)}), bf16[256,8,512]{2,1,0:T(8,128)(2,1)}, u32[]{:S(2)}, u32[]{:S(2)}) %all-to-all-start.2) | async-done | bytes 2097184 | tf_op jit(solution)/shard_map/all_to_all | solution.py:267
  160.8 4.9 %shard_map.80 = (f32[8,20480]{1,0:T(8,128)S(1)}, f32[128,16]{1,0:T(8,128)S(1)}) custom-call(f32[8,512]{1,0:T(8,128)S(1)} %get-tuple-element.7.first_squares, s32[320]{0:T(512)S(1)} %reshape.66.refs_0_, s32[160]{0:T(256)S(1)} %convert_add_fusion.refs_1_, bf16[20,8,512]{2,1,0:T(8,128)(2,1)S(1)} %collective-permute-done.2.refs_2_, ...), custom_call_target="tpu_custom_call" | custom-call | flops 2013265920 | bytes 6023040 | tf_op jit(solution)/shard_map/pallas_call | solution.py:183
  165.6 19.8 %all_to_all.30 = f32[128,1,16]{2,1,0:T(1,128)S(1)} all-to-all(f32[128,1,16]{2,1,0:T(1,128)S(1)} %bitcast.16), channel_id=1, replica_groups=mesh['rows'=128,'tilt'=4] {'rows'}, dimensions={0} | all-to-all | bytes 16384 | tf_op jit(solution)/shard_map/all_to_all | solution.py:301
  185.5 0.2 reduce_sum.9
  185.6 0.1 multiply_bitcast_fusion
  185.7 0.6 pad_maximum_fusion
  186.3 1.0 broadcast_divide_fusion
  (8 shorter events, 0.1 us)
Async XLA Ops:
  2.2 29.9 %all-to-all-start = ((s32[128,1,1]{2,1,0:T(1,128)}), s32[128,1,1]{2,1,0:T(1,128)S(1)}, u32[]{:S(2)}, u32[]{:S(2)}) async-start(s32[128,1,1]{2,1,0:T(1,128)} %bitcast.20), calls=%async_computation | async-start | bytes 131072 | tf_op jit(solution)/shard_map/all_to_all | solution.py:217
  34.2 12.6 %copy-start.1 = (s32[40,12]{0,1:T(8,128)S(1)}, s32[40,12]{0,1:T(8,128)}, u32[]{:S(2)}) copy-start(s32[40,12]{0,1:T(8,128)} %param.11) | copy-start | bytes 5764
  34.2 59.1 %copy-start = (bf16[40,12,512]{2,0,1:T(8,128)(2,1)S(1)}, bf16[40,12,512]{2,0,1:T(8,128)(2,1)}, u32[]{:S(2)}) copy-start(bf16[40,12,512]{2,0,1:T(8,128)(2,1)} %param.10) | copy-start | bytes 1474564
  34.2 59.1 %all-to-all-start.1 = ((bf16[256,8,512]{2,1,0:T(8,128)(2,1)}), bf16[256,8,512]{2,1,0:T(8,128)(2,1)}, u32[]{:S(2)}, u32[]{:S(2)}) async-start(bf16[256,8,512]{2,1,0:T(8,128)(2,1)} %shard_map.78), calls=%async_computation.1 | async-start | bytes 4194304 | tf_op jit(solution)/shard_map/all_to_all | solution.py:267
  41.2 29.8 %collective-permute-start.1 = (bf16[20,8,512]{2,1,0:T(8,128)(2,1)S(1)}, bf16[20,8,512]{2,1,0:T(8,128)(2,1)S(1)}, u32[]{:S(2)}, u32[]{:S(2)}) collective-permute-start(bf16[20,8,512]{2,1,0:T(8,128)(2,1)S(1)} %get-tuple-element.16), channel_id=1, source_target_pairs={{4,0},{8,4},{12,8},{16,12},{20,16},{24,20},{28,24},{32,28},{36,32}... | collective-permute-start | bytes 491528 | tf_op jit(solution)/shard_map/ppermute | solution.py:269
  44.2 36.8 %collective-permute-start = (bf16[20,8,512]{2,1,0:T(8,128)(2,1)S(1)}, bf16[20,8,512]{2,1,0:T(8,128)(2,1)S(1)}, u32[]{:S(2)}, u32[]{:S(2)}) collective-permute-start(bf16[20,8,512]{2,1,0:T(8,128)(2,1)S(1)} %get-tuple-element.17), channel_id=1, source_target_pairs={{0,4},{4,8},{8,12},{12,16},{16,20},{20,24},{24,28},{28,32},{32,36}... | collective-permute-start | bytes 491528 | tf_op jit(solution)/shard_map/ppermute | solution.py:268
  99.8 61.0 %all-to-all-start.2 = ((bf16[256,8,512]{2,1,0:T(8,128)(2,1)}), bf16[256,8,512]{2,1,0:T(8,128)(2,1)}, u32[]{:S(2)}, u32[]{:S(2)}) async-start(bf16[256,8,512]{2,1,0:T(8,128)(2,1)} %get-tuple-element.9), calls=%async_computation.2 | async-start | bytes 4194304 | tf_op jit(solution)/shard_map/all_to_all | solution.py:267
  108.8 31.7 %collective-permute-start.3 = (bf16[20,8,512]{2,1,0:T(8,128)(2,1)S(1)}, bf16[20,8,512]{2,1,0:T(8,128)(2,1)S(1)}, u32[]{:S(2)}, u32[]{:S(2)}) collective-permute-start(bf16[20,8,512]{2,1,0:T(8,128)(2,1)S(1)} %get-tuple-element.14), channel_id=1, source_target_pairs={{4,0},{8,4},{12,8},{16,12},{20,16},{24,20},{28,24},{32,28},{36,32}... | collective-permute-start | bytes 491528 | tf_op jit(solution)/shard_map/ppermute | solution.py:269
  111.7 36.8 %collective-permute-start.2 = (bf16[20,8,512]{2,1,0:T(8,128)(2,1)S(1)}, bf16[20,8,512]{2,1,0:T(8,128)(2,1)S(1)}, u32[]{:S(2)}, u32[]{:S(2)}) collective-permute-start(bf16[20,8,512]{2,1,0:T(8,128)(2,1)S(1)} %get-tuple-element.15), channel_id=1, source_target_pairs={{0,4},{4,8},{8,12},{12,16},{16,20},{20,24},{24,28},{28,32},{32,36}... | collective-permute-start | bytes 491528 | tf_op jit(solution)/shard_map/ppermute | solution.py:268

commit v8 on v7

--- a/solution.py
+++ b/solution.py
@@ -1,3 +1,5 @@
+import math
+
 import jax
 import jax.numpy as jnp
 from jax import lax
@@ -11,7 +13,7 @@
 HALF_WORD = 1 << 16
 REQUEST_LIMIT = 62 * 1024 * 1024
 PACK_LIMIT = 48 * 1024 * 1024
-MAP_LIMIT = 51 * 1024 * 1024
+MAP_LIMIT = 44 * 1024 * 1024
 
 
 def request_kernel(blocks_here, pattern, codes):
@@ -86,7 +88,7 @@
 
 def map_blocks(operands, scratch, meanwhile=None):
     near_index, far_index, before, own, after, arrived, kernels, rates = operands
-    near_smem, far_smem, extended, far_blocks, weights, rate_buf, gathered, sems = scratch
+    near_smem, far_smem, extended, far_blocks, rate_buf, gathered, sems = scratch
     kinds = kernels.shape[0]
     (rows, tilts, _), half = own.shape, before.shape[0]
     far_count = rates.shape[0] - NEAR
@@ -97,14 +99,10 @@
         start_copy(own, extended.at[pl.ds(half, rows)], sems.at[2]),
         start_copy(after, extended.at[pl.ds(half + rows, half)], sems.at[3]),
     ]
-    kernel_copies = [start_copy(kernels.at[0], weights.at[0], sems.at[4])]
-    rate_copy = start_copy(rates, rate_buf, sems.at[4 + kinds])
-    kernel_copies += [
-        start_copy(kernels.at[k], weights.at[k], sems.at[4 + k]) for k in range(1, kinds)
-    ]
+    first.append(start_copy(rates, rate_buf, sems.at[4]))
     late = [
-        start_copy(far_index, far_smem, sems.at[5 + kinds]),
-        start_copy(arrived, far_blocks, sems.at[6 + kinds]),
+        start_copy(far_index, far_smem, sems.at[5]),
+        start_copy(arrived, far_blocks, sems.at[6]),
     ]
     if meanwhile is not None:
         meanwhile()
@@ -114,11 +112,8 @@
     total = None
     for kind in range(kinds):
         slots = range(kind, NEAR, kinds)
-        kernel_copies[kind].wait()
-        if kind == 0:
-            rate_copy.wait()
         product = weighted(
-            near_smem, NEAR, slots, extended, weights[kind], gathered.at[kind % 2], rows, tilts
+            near_smem, NEAR, slots, extended, kernels[kind], gathered.at[kind % 2], rows, tilts
         )
         for n, slot in enumerate(slots):
             term = product[n] * rate_buf[slot].astype(jnp.float32)[:, None, :]
@@ -128,7 +123,7 @@
     for kind in range(kinds):
         slots = range(kind, far_count, kinds)
         product = weighted(
-            far_smem, far_count, slots, far_blocks, weights[kind], gathered.at[kind % 2], rows, tilts
+            far_smem, far_count, slots, far_blocks, kernels[kind], gathered.at[kind % 2], rows, tilts
         )
         for n, slot in enumerate(slots):
             total = total + product[n] * rate_buf[NEAR + slot].astype(jnp.float32)[:, None, :]
@@ -141,21 +136,18 @@
 
 def step_kernel(codes, factor, *refs):
     operands, (tilted, outgoing, squares) = refs[:8], refs[8:11]
-    codes_buf, line, words, factor_buf, tilted_buf, staged, pack_sems, sems = refs[11:19]
+    codes_buf, line, words, tilted_buf, staged, pack_sems, sems = refs[11:18]
     codes_copy = start_copy(codes, codes_buf, sems.at[0])
-    waits = []
+    decoded = []
 
     def decode():
-        waits.append(start_copy(factor, factor_buf, sems.at[1]))
         codes_copy.wait()
-        waits.append(read_words(codes_buf, line, words, sems.at[2]))
-
-    total = map_blocks(operands, refs[19:], decode)
-    factor_copy, words_copy = waits
-    factor_copy.wait()
-    tilted_buf[...] = (factor_buf[...] * total).astype(jnp.bfloat16)
-    copies = [start_copy(tilted_buf, tilted, sems.at[3])]
-    words_copy.wait()
+        decoded.append(read_words(codes_buf, line, words, sems.at[1]))
+
+    total = map_blocks(operands, refs[18:], decode)
+    tilted_buf[...] = (factor[...] * total).astype(jnp.bfloat16)
+    copies = [start_copy(tilted_buf, tilted, sems.at[2])]
+    decoded[0].wait()
     copies += pack_blocks(words, tilted_buf, staged, outgoing, pack_sems)
     squares[...] = jnp.sum(total * total, axis=0)
     for copy in copies:
@@ -179,7 +171,7 @@
 
 def call(kernel, outs, arrays, scratch, flops, limit, in_vmem=()):
     spec = [pl.BlockSpec(memory_space=pltpu.VMEM), pl.BlockSpec(memory_space=pl.ANY)]
-    moved = sum(a.size * a.dtype.itemsize for a in (*arrays, *outs))
+    moved = sum(math.prod(a.shape) * a.dtype.itemsize for a in (*arrays, *outs))
     return pl.pallas_call(
         kernel,
         out_shape=outs,
@@ -244,10 +236,9 @@
         pltpu.SMEM(far_index.shape, jnp.int32),
         pltpu.VMEM((blocks_here + 2 * half_span, *block), jnp.bfloat16),
         staged,
-        pltpu.VMEM(kernels.shape, jnp.bfloat16),
         pltpu.VMEM(rates_by_slot.shape, jnp.bfloat16),
         pltpu.VMEM((2, gather_rows, block_size), jnp.bfloat16),
-        sem((7 + kind_count,)),
+        sem((7,)),
     ]
     map_flops = 2 * slot_count * blocks_here * tilt_count * block_size * block_size
 
@@ -256,7 +247,7 @@
     tilted = tilted.astype(jnp.bfloat16)
     (outgoing,) = call(
         pack_kernel,
-        [outgoing_shape],
+        [pltpu.HBM(outgoing_shape.shape, outgoing_shape.dtype)],
         [codes, tilted],
         [*word_buffers, staged, sem, sem((PACK_CHUNKS,))],
         0,
@@ -267,25 +258,29 @@
         arrived = lax.all_to_all(outgoing, "rows", split_axis=0, concat_axis=0, tiled=True)
         before = lax.ppermute(tilted[blocks_here - half_span :], "rows", up)
         after = lax.ppermute(tilted[:half_span], "rows", down)
-        operands = [near_index, far_index, before, tilted, after, arrived, kernels, rates_by_slot]
+        arrived = pltpu.with_memory_space_constraint(arrived, pltpu.HBM)
+        rates_hbm = pltpu.with_memory_space_constraint(rates_by_slot, pltpu.HBM)
+        if iteration < ITERS - 1:
+            before = pltpu.with_memory_space_constraint(before, pltpu.HBM)
+            after = pltpu.with_memory_space_constraint(after, pltpu.HBM)
+        operands = [near_index, far_index, before, tilted, after, arrived, kernels, rates_hbm]
         if iteration < ITERS - 1:
             step_scratch = [
                 pltpu.VMEM(codes.shape, jnp.int32),
                 *word_buffers,
-                pltpu.VMEM(tilted_shape.shape, jnp.float32),
                 pltpu.VMEM(tilted_shape.shape, jnp.bfloat16),
                 staged,
                 sem((PACK_CHUNKS,)),
-                sem((4,)),
+                sem((3,)),
             ]
             tilted, outgoing, squares = call(
                 step_kernel,
-                [tilted_shape, outgoing_shape, squares_shape],
+                [tilted_shape, pltpu.HBM(outgoing_shape.shape, outgoing_shape.dtype), squares_shape],
                 [codes, factor, *operands],
                 step_scratch + map_scratch,
                 map_flops,
                 MAP_LIMIT,
-                in_vmem=(12,),
+                in_vmem=(1, 8, 12),
             )
         else:
             mapped, sums = call(
@@ -295,7 +290,7 @@
                 map_scratch,
                 map_flops,
                 MAP_LIMIT,
-                in_vmem=(0, 9, 10),
+                in_vmem=(0, 7, 9, 10),
             )
 
     gathered = lax.all_to_all(sums, "rows", split_axis=0, concat_axis=0, tiled=True)

time: 188 us -> 187 us (level)
  no operation moved by 1% of the time
where the time goes in v8:
time: 187 us; the launch traced here: 186 us
  waiting for transfers between devices  101 us (54%)
  starting transfers between devices  45.8 us (24%)
  blocking collectives  19.8 us (11%)
  Pallas kernels  13.7 us (7%)
  other arithmetic  3.3 us (2%)
    ppermute x2, waiting for transfers between devices, on_device(): after = lax.ppermute(tilted[:half_span], 'rows', down)  49.5 us
    all_to_all x2, waiting for transfers between devices, on_device(): lax.all_to_all(outgoing, 'rows', split_axis=0, concat_axis=0, tiled=True)  24.7 us
    all_to_all x1, blocking collectives, on_device(): lax.all_to_all(sums, 'rows', split_axis=0, concat_axis=0, tiled=True)  19.8 us
    all_to_all x1, starting transfers between devices, on_device(): lax.all_to_all(codes, 'rows', split_axis=0, concat_axis=0, tiled=True)  18.4 us
    ppermute x2, waiting for transfers between devices, on_device(): before = lax.ppermute(tilted[blocks_here - half_span:], 'rows', up)  18 us
    all_to_all x2, starting transfers between devices, on_device(): lax.all_to_all(outgoing, 'rows', split_axis=0, concat_axis=0, tiled=True)  16 us
    pallas_call x4, Pallas kernels, call(): pl.pallas_call(kernel, out_shape=outs, in_specs=[spec[n not in in_vmem] f...  13.7 us
    all_to_all x1, waiting for transfers between devices, on_device(): lax.all_to_all(codes, 'rows', split_axis=0, concat_axis=0, tiled=True)  9.26 us
  transfers between devices with their start and end apart: 7, of which 7 were waited for; matrix products, arithmetic and copies ran while one was open for 2% of the time, Pallas kernels for 0%

profile of v8, /device:TPU:1, one launch (start us, length us, event | category | flops | bytes accessed | tf_op | source)
XLA Modules:
  0.0 186.1 jit_solution(17337260896632736514)
XLA Ops:
  0.6 1.6 shard_map.77
  2.2 18.4 %all-to-all-start = ((s32[128,1,1]{2,1,0:T(1,128)}), s32[128,1,1]{2,1,0:T(1,128)S(1)}, u32[]{:S(2)}, u32[]{:S(2)}) async-start(s32[128,1,1]{2,1,0:T(1,128)} %bitcast.18), calls=%async_computation | async-start | bytes 131072 | tf_op jit(solution)/shard_map/all_to_all | solution.py:209
  20.7 0.9 mul.33
  21.6 1.3 multiply_convert_fusion
  22.8 9.3 %all-to-all-done = s32[128,1,1]{2,1,0:T(1,128)S(1)} async-done(((s32[128,1,1]{2,1,0:T(1,128)}), s32[128,1,1]{2,1,0:T(1,128)S(1)}, u32[]{:S(2)}, u32[]{:S(2)}) %all-to-all-start) | async-done | bytes 544 | tf_op jit(solution)/shard_map/all_to_all | solution.py:209
  32.1 2.1 %shard_map.78 = bf16[256,8,512]{2,1,0:T(8,128)(2,1)} custom-call(s32[128,1]{1,0:T(8,128)S(1)} %bitcast.14, bf16[40,8,512]{2,1,0:T(8,128)(2,1)S(1)} %get-tuple-element.18.tilted.refs_3_), custom_call_target="tpu_custom_call" | custom-call | bytes 2425344 | tf_op jit(solution)/shard_map/pallas_call | solution.py:175
  34.2 0.0 copy-start.1
  34.2 0.0 copy-start
  34.2 7.0 %all-to-all-start.1 = ((bf16[256,8,512]{2,1,0:T(8,128)(2,1)}), bf16[256,8,512]{2,1,0:T(8,128)(2,1)}, u32[]{:S(2)}, u32[]{:S(2)}) async-start(bf16[256,8,512]{2,1,0:T(8,128)(2,1)} %shard_map.78), calls=%async_computation.1 | async-start | bytes 4194304 | tf_op jit(solution)/shard_map/all_to_all | solution.py:258
  41.2 3.0 %collective-permute-start.1 = (bf16[20,8,512]{2,1,0:T(8,128)(2,1)S(1)}, bf16[20,8,512]{2,1,0:T(8,128)(2,1)}, u32[]{:S(2)}, u32[]{:S(2)}) collective-permute-start(bf16[20,8,512]{2,1,0:T(8,128)(2,1)S(1)} %get-tuple-element.16), channel_id=1, source_target_pairs={{4,0},{8,4},{12,8},{16,12},{20,16},{24,20},{28,24},{32,28},{36,32}... | collective-permute-start | bytes 491528 | tf_op jit(solution)/shard_map/ppermute | solution.py:260
  44.2 2.6 %collective-permute-start = (bf16[20,8,512]{2,1,0:T(8,128)(2,1)S(1)}, bf16[20,8,512]{2,1,0:T(8,128)(2,1)}, u32[]{:S(2)}, u32[]{:S(2)}) collective-permute-start(bf16[20,8,512]{2,1,0:T(8,128)(2,1)S(1)} %get-tuple-element.17), channel_id=1, source_target_pairs={{0,4},{4,8},{8,12},{12,16},{16,20},{20,24},{24,28},{28,32},{32,36}... | collective-permute-start | bytes 491528 | tf_op jit(solution)/shard_map/ppermute | solution.py:259
  46.8 0.0 copy-done.1
  46.9 0.1 copy.27
  46.9 0.1 reshape.66.refs_0_
  47.0 0.1 copy.28
  47.1 0.1 reshape.67
  47.2 0.2 and_reduce_fusion
  47.5 23.5 %collective-permute-done.1.refs_4_ = bf16[20,8,512]{2,1,0:T(8,128)(2,1)} collective-permute-done((bf16[20,8,512]{2,1,0:T(8,128)(2,1)S(1)}, bf16[20,8,512]{2,1,0:T(8,128)(2,1)}, u32[]{:S(2)}, u32[]{:S(2)}) %collective-permute-start.1) | collective-permute-done | bytes 163872 | tf_op jit(solution)/shard_map/ppermute | solution.py:260
  71.0 10.0 %collective-permute-done.refs_2_ = bf16[20,8,512]{2,1,0:T(8,128)(2,1)} collective-permute-done((bf16[20,8,512]{2,1,0:T(8,128)(2,1)S(1)}, bf16[20,8,512]{2,1,0:T(8,128)(2,1)}, u32[]{:S(2)}, u32[]{:S(2)}) %collective-permute-start) | collective-permute-done | bytes 163872 | tf_op jit(solution)/shard_map/ppermute | solution.py:259
  81.0 12.3 %all-to-all-done.1.refs_5_ = bf16[256,8,512]{2,1,0:T(8,128)(2,1)} async-done(((bf16[256,8,512]{2,1,0:T(8,128)(2,1)}), bf16[256,8,512]{2,1,0:T(8,128)(2,1)}, u32[]{:S(2)}, u32[]{:S(2)}) %all-to-all-start.1) | async-done | bytes 2097184 | tf_op jit(solution)/shard_map/all_to_all | solution.py:258
  93.3 0.0 copy-done
  93.3 5.6 %shard_map.79 = (bf16[40,8,512]{2,1,0:T(8,128)(2,1)S(1)}, bf16[256,8,512]{2,1,0:T(8,128)(2,1)}, f32[8,512]{1,0:T(8,128)S(1)}) custom-call(s32[128,1]{1,0:T(8,128)S(1)} %bitcast.15, f32[40,8,512]{2,1,0:T(8,128)S(1)} %get-tuple-element.19.factor, s32[320]{0:T(512)S(1)} %reshape.66.refs_0_, s32[160]{0:T(256)S(1)} %convert_add_fusion.refs_1_, ...), custom_call_target="tpu_custom_call" | custom-call | flops 2013265920 | bytes 8440192 | tf_op jit(solution)/shard_map/pallas_call | solution.py:175
  99.0 9.1 %all-to-all-start.2 = ((bf16[256,8,512]{2,1,0:T(8,128)(2,1)}), bf16[256,8,512]{2,1,0:T(8,128)(2,1)}, u32[]{:S(2)}, u32[]{:S(2)}) async-start(bf16[256,8,512]{2,1,0:T(8,128)(2,1)} %get-tuple-element.9), calls=%async_computation.2 | async-start | bytes 4194304 | tf_op jit(solution)/shard_map/all_to_all | solution.py:258
  108.1 2.9 %collective-permute-start.3 = (bf16[20,8,512]{2,1,0:T(8,128)(2,1)S(1)}, bf16[20,8,512]{2,1,0:T(8,128)(2,1)S(1)}, u32[]{:S(2)}, u32[]{:S(2)}) collective-permute-start(bf16[20,8,512]{2,1,0:T(8,128)(2,1)S(1)} %get-tuple-element.14), channel_id=1, source_target_pairs={{4,0},{8,4},{12,8},{16,12},{20,16},{24,20},{28,24},{32,28},{36,32}... | collective-permute-start | bytes 491528 | tf_op jit(solution)/shard_map/ppermute | solution.py:260
  111.0 2.9 %collective-permute-start.2 = (bf16[20,8,512]{2,1,0:T(8,128)(2,1)S(1)}, bf16[20,8,512]{2,1,0:T(8,128)(2,1)S(1)}, u32[]{:S(2)}, u32[]{:S(2)}) collective-permute-start(bf16[20,8,512]{2,1,0:T(8,128)(2,1)S(1)} %get-tuple-element.15), channel_id=1, source_target_pairs={{0,4},{4,8},{8,12},{12,16},{16,20},{20,24},{24,28},{28,32},{32,36}... | collective-permute-start | bytes 491528 | tf_op jit(solution)/shard_map/ppermute | solution.py:259
  113.8 26.0 %collective-permute-done.3.refs_4_ = bf16[20,8,512]{2,1,0:T(8,128)(2,1)S(1)} collective-permute-done((bf16[20,8,512]{2,1,0:T(8,128)(2,1)S(1)}, bf16[20,8,512]{2,1,0:T(8,128)(2,1)S(1)}, u32[]{:S(2)}, u32[]{:S(2)}) %collective-permute-start.3) | collective-permute-done | bytes 163872 | tf_op jit(solution)/shard_map/ppermute | solution.py:260
  139.8 8.0 %collective-permute-done.2.refs_2_ = bf16[20,8,512]{2,1,0:T(8,128)(2,1)S(1)} collective-permute-done((bf16[20,8,512]{2,1,0:T(8,128)(2,1)S(1)}, bf16[20,8,512]{2,1,0:T(8,128)(2,1)S(1)}, u32[]{:S(2)}, u32[]{:S(2)}) %collective-permute-start.2) | collective-permute-done | bytes 163872 | tf_op jit(solution)/shard_map/ppermute | solution.py:259
  147.7 12.3 %all-to-all-done.2.refs_5_ = bf16[256,8,512]{2,1,0:T(8,128)(2,1)} async-done(((bf16[256,8,512]{2,1,0:T(8,128)(2,1)}), bf16[256,8,512]{2,1,0:T(8,128)(2,1)}, u32[]{:S(2)}, u32[]{:S(2)}) %all-to-all-start.2) | async-done | bytes 2097184 | tf_op jit(solution)/shard_map/all_to_all | solution.py:258
  160.1 4.4 %shard_map.80 = (f32[8,20480]{1,0:T(8,128)S(1)}, f32[128,16]{1,0:T(8,128)S(1)}) custom-call(f32[8,512]{1,0:T(8,128)S(1)} %get-tuple-element.7.first_squares, s32[320]{0:T(512)S(1)} %reshape.66.refs_0_, s32[160]{0:T(256)S(1)} %convert_add_fusion.refs_1_, bf16[20,8,512]{2,1,0:T(8,128)(2,1)S(1)} %collective-permute-done.2.refs_2_, ...), custom_call_target="tpu_custom_call" | custom-call | flops 2013265920 | bytes 6023040 | tf_op jit(solution)/shard_map/pallas_call | solution.py:175
  164.4 19.8 %all_to_all.30 = f32[128,1,16]{2,1,0:T(1,128)S(1)} all-to-all(f32[128,1,16]{2,1,0:T(1,128)S(1)} %bitcast.16), channel_id=1, replica_groups=mesh['rows'=128,'tilt'=4] {'rows'}, dimensions={0} | all-to-all | bytes 16384 | tf_op jit(solution)/shard_map/all_to_all | solution.py:296
  184.3 0.2 reduce_sum.9
  184.4 0.1 multiply_bitcast_fusion
  184.5 0.6 pad_maximum_fusion
  185.1 1.0 broadcast_divide_fusion
  (8 shorter events, 0.1 us)
Async XLA Ops:
  2.2 29.9 %all-to-all-start = ((s32[128,1,1]{2,1,0:T(1,128)}), s32[128,1,1]{2,1,0:T(1,128)S(1)}, u32[]{:S(2)}, u32[]{:S(2)}) async-start(s32[128,1,1]{2,1,0:T(1,128)} %bitcast.18), calls=%async_computation | async-start | bytes 131072 | tf_op jit(solution)/shard_map/all_to_all | solution.py:209
  34.2 12.6 %copy-start.1 = (s32[40,12]{0,1:T(8,128)S(1)}, s32[40,12]{0,1:T(8,128)}, u32[]{:S(2)}) copy-start(s32[40,12]{0,1:T(8,128)} %param.11) | copy-start | bytes 5764
  34.2 59.1 %copy-start = (bf16[4,512,512]{2,1,0:T(8,128)(2,1)S(1)}, bf16[4,512,512]{2,1,0:T(8,128)(2,1)}, u32[]{:S(2)}) copy-start(bf16[4,512,512]{2,1,0:T(8,128)(2,1)} %refs_6_.3) | copy-start | bytes 6291460
  34.2 59.1 %all-to-all-start.1 = ((bf16[256,8,512]{2,1,0:T(8,128)(2,1)}), bf16[256,8,512]{2,1,0:T(8,128)(2,1)}, u32[]{:S(2)}, u32[]{:S(2)}) async-start(bf16[256,8,512]{2,1,0:T(8,128)(2,1)} %shard_map.78), calls=%async_computation.1 | async-start | bytes 4194304 | tf_op jit(solution)/shard_map/all_to_all | solution.py:258
  41.2 29.8 %collective-permute-start.1 = (bf16[20,8,512]{2,1,0:T(8,128)(2,1)S(1)}, bf16[20,8,512]{2,1,0:T(8,128)(2,1)}, u32[]{:S(2)}, u32[]{:S(2)}) collective-permute-start(bf16[20,8,512]{2,1,0:T(8,128)(2,1)S(1)} %get-tuple-element.16), channel_id=1, source_target_pairs={{4,0},{8,4},{12,8},{16,12},{20,16},{24,20},{28,24},{32,28},{36,32}... | collective-permute-start | bytes 491528 | tf_op jit(solution)/shard_map/ppermute | solution.py:260
  44.2 36.8 %collective-permute-start = (bf16[20,8,512]{2,1,0:T(8,128)(2,1)S(1)}, bf16[20,8,512]{2,1,0:T(8,128)(2,1)}, u32[]{:S(2)}, u32[]{:S(2)}) collective-permute-start(bf16[20,8,512]{2,1,0:T(8,128)(2,1)S(1)} %get-tuple-element.17), channel_id=1, source_target_pairs={{0,4},{4,8},{8,12},{12,16},{16,20},{20,24},{24,28},{28,32},{32,36}... | collective-permute-start | bytes 491528 | tf_op jit(solution)/shard_map/ppermute | solution.py:259
  99.0 61.1 %all-to-all-start.2 = ((bf16[256,8,512]{2,1,0:T(8,128)(2,1)}), bf16[256,8,512]{2,1,0:T(8,128)(2,1)}, u32[]{:S(2)}, u32[]{:S(2)}) async-start(bf16[256,8,512]{2,1,0:T(8,128)(2,1)} %get-tuple-element.9), calls=%async_computation.2 | async-start | bytes 4194304 | tf_op jit(solution)/shard_map/all_to_all | solution.py:258
  108.1 31.7 %collective-permute-start.3 = (bf16[20,8,512]{2,1,0:T(8,128)(2,1)S(1)}, bf16[20,8,512]{2,1,0:T(8,128)(2,1)S(1)}, u32[]{:S(2)}, u32[]{:S(2)}) collective-permute-start(bf16[20,8,512]{2,1,0:T(8,128)(2,1)S(1)} %get-tuple-element.14), channel_id=1, source_target_pairs={{4,0},{8,4},{12,8},{16,12},{20,16},{24,20},{28,24},{32,28},{36,32}... | collective-permute-start | bytes 491528 | tf_op jit(solution)/shard_map/ppermute | solution.py:260
  111.0 36.8 %collective-permute-start.2 = (bf16[20,8,512]{2,1,0:T(8,128)(2,1)S(1)}, bf16[20,8,512]{2,1,0:T(8,128)(2,1)S(1)}, u32[]{:S(2)}, u32[]{:S(2)}) collective-permute-start(bf16[20,8,512]{2,1,0:T(8,128)(2,1)S(1)} %get-tuple-element.15), channel_id=1, source_target_pairs={{0,4},{4,8},{8,12},{12,16},{16,20},{20,24},{24,28},{28,32},{32,36}... | collective-permute-start | bytes 491528 | tf_op jit(solution)/shard_map/ppermute | solution.py:259

commit v9 on v8

--- a/solution.py
+++ b/solution.py
@@ -10,6 +10,7 @@
 NEAR = 8
 ITERS = 2
 PACK_CHUNKS = 8
+END_CHUNKS = 4
 HALF_WORD = 1 << 16
 REQUEST_LIMIT = 62 * 1024 * 1024
 PACK_LIMIT = 48 * 1024 * 1024
@@ -99,7 +100,7 @@
         start_copy(own, extended.at[pl.ds(half, rows)], sems.at[2]),
         start_copy(after, extended.at[pl.ds(half + rows, half)], sems.at[3]),
     ]
-    first.append(start_copy(rates, rate_buf, sems.at[4]))
+    rate_copy = start_copy(rates, rate_buf, sems.at[4])
     late = [
         start_copy(far_index, far_smem, sems.at[5]),
         start_copy(arrived, far_blocks, sems.at[6]),
@@ -115,6 +116,8 @@
         product = weighted(
             near_smem, NEAR, slots, extended, kernels[kind], gathered.at[kind % 2], rows, tilts
         )
+        if kind == 0:
+            rate_copy.wait()
         for n, slot in enumerate(slots):
             term = product[n] * rate_buf[slot].astype(jnp.float32)[:, None, :]
             total = term if total is None else total + term
@@ -136,17 +139,15 @@
 
 def step_kernel(codes, factor, *refs):
     operands, (tilted, outgoing, squares) = refs[:8], refs[8:11]
-    codes_buf, line, words, tilted_buf, staged, pack_sems, sems = refs[11:18]
-    codes_copy = start_copy(codes, codes_buf, sems.at[0])
+    line, words, tilted_buf, staged, pack_sems, sems = refs[11:17]
     decoded = []
 
     def decode():
-        codes_copy.wait()
-        decoded.append(read_words(codes_buf, line, words, sems.at[1]))
-
-    total = map_blocks(operands, refs[18:], decode)
+        decoded.append(read_words(codes, line, words, sems.at[0]))
+
+    total = map_blocks(operands, refs[17:], decode)
     tilted_buf[...] = (factor[...] * total).astype(jnp.bfloat16)
-    copies = [start_copy(tilted_buf, tilted, sems.at[2])]
+    copies = [start_copy(tilted_buf, tilted, sems.at[1])]
     decoded[0].wait()
     copies += pack_blocks(words, tilted_buf, staged, outgoing, pack_sems)
     squares[...] = jnp.sum(total * total, axis=0)
@@ -167,6 +168,33 @@
         across == tilt + tilts, sum_of_squares(total), 0.0
     )
     sums[...] = jnp.broadcast_to(jnp.sum(both, axis=0, keepdims=True), sums.shape)
+
+
+def end_kernel(states, sums, mapped, iterate, growth, scaled, sems):
+    tilts = mapped.shape[0]
+    totals = jnp.sum(sums[...], axis=0, keepdims=True)
+    across = lax.broadcasted_iota(jnp.int32, (tilts, sums.shape[1]), 1)
+    tilt = lax.broadcasted_iota(jnp.int32, (tilts, sums.shape[1]), 0)
+    diagonal = lax.broadcasted_iota(jnp.int32, (tilts, tilts), 0) == lax.broadcasted_iota(
+        jnp.int32, (tilts, tilts), 1
+    )
+    product = jnp.ones((tilts, 1), jnp.float32)
+    for j in range(ITERS):
+        total = jnp.sum(jnp.where(across == tilt + j * tilts, totals, 0.0), axis=1, keepdims=True)
+        scale = jnp.sqrt(total / product / product / states + 1e-06)
+        product = product * scale
+        growth[j : j + 1, :] = jnp.sum(
+            jnp.where(diagonal, jnp.log(scale), 0.0), axis=0, keepdims=True
+        )
+    inverse = 1.0 / product
+    width = mapped.shape[1] // END_CHUNKS
+    copies = []
+    for part in range(END_CHUNKS):
+        span = pl.ds(part * width, width)
+        scaled[:, span] = mapped[:, span] * inverse
+        copies.append(start_copy(scaled.at[:, span], iterate.at[:, span], sems.at[part]))
+    for copy in copies:
+        copy.wait()
 
 
 def call(kernel, outs, arrays, scratch, flops, limit, in_vmem=()):
@@ -266,12 +294,11 @@
         operands = [near_index, far_index, before, tilted, after, arrived, kernels, rates_hbm]
         if iteration < ITERS - 1:
             step_scratch = [
-                pltpu.VMEM(codes.shape, jnp.int32),
                 *word_buffers,
                 pltpu.VMEM(tilted_shape.shape, jnp.bfloat16),
                 staged,
                 sem((PACK_CHUNKS,)),
-                sem((3,)),
+                sem((2,)),
             ]
             tilted, outgoing, squares = call(
                 step_kernel,
@@ -280,7 +307,7 @@
                 step_scratch + map_scratch,
                 map_flops,
                 MAP_LIMIT,
-                in_vmem=(1, 8, 12),
+                in_vmem=(0, 1, 8, 12),
             )
         else:
             mapped, sums = call(
@@ -294,15 +321,16 @@
             )
 
     gathered = lax.all_to_all(sums, "rows", split_axis=0, concat_axis=0, tiled=True)
-    totals = jnp.sum(gathered, axis=0).reshape(ITERS, tilt_count)
     states = total_blocks * block_size
-    product = jnp.ones((tilt_count,), jnp.float32)
-    growth = []
-    for j in range(ITERS):
-        scale = jnp.sqrt(totals[j] / product / product / states + 1e-06)
-        product = product * scale
-        growth.append(jnp.log(scale))
-    return (mapped / product[:, None], jnp.stack(growth))
+    return call(
+        lambda *refs: end_kernel(states, *refs),
+        [mapped_shape, shape((ITERS, tilt_count), jnp.float32)],
+        [gathered, mapped],
+        [pltpu.VMEM(start.shape, jnp.float32), sem((END_CHUNKS,))],
+        0,
+        MAP_LIMIT,
+        in_vmem=(0, 1, 3),
+    )
 
 
 def solution(mesh):

time: 187 us -> 186 us (level)
    pallas_call x4 -> x5, Pallas kernels: 13.7 us -> 14.8 us  [call(): pl.pallas_call(kernel, out_shape=outs, in_specs=[spec[n not in in_vmem] f...]
where the time goes in v9:
time: 186 us
  waiting for transfers between devices  101 us (54%)
  starting transfers between devices  45.7 us (25%)
  blocking collectives  19.8 us (11%)
  Pallas kernels  14.8 us (8%)
    ppermute x2, waiting for transfers between devices, on_device(): after = lax.ppermute(tilted[:half_span], 'rows', down)  49.5 us
    all_to_all x2, waiting for transfers between devices, on_device(): lax.all_to_all(outgoing, 'rows', split_axis=0, concat_axis=0, tiled=True)  24.7 us
    all_to_all x1, blocking collectives, on_device(): lax.all_to_all(sums, 'rows', split_axis=0, concat_axis=0, tiled=True)  19.8 us
    all_to_all x1, starting transfers between devices, on_device(): lax.all_to_all(codes, 'rows', split_axis=0, concat_axis=0, tiled=True)  18.4 us
    ppermute x2, waiting for transfers between devices, on_device(): before = lax.ppermute(tilted[blocks_here - half_span:], 'rows', up)  18 us
    all_to_all x2, starting transfers between devices, on_device(): lax.all_to_all(outgoing, 'rows', split_axis=0, concat_axis=0, tiled=True)  16 us
    pallas_call x5, Pallas kernels, call(): pl.pallas_call(kernel, out_shape=outs, in_specs=[spec[n not in in_vmem] f...  14.8 us
    all_to_all x1, waiting for transfers between devices, on_device(): lax.all_to_all(codes, 'rows', split_axis=0, concat_axis=0, tiled=True)  9.26 us
  transfers between devices with their start and end apart: 7, of which 7 were waited for; matrix products, arithmetic and copies ran while one was open for 2% of the time, Pallas kernels for 0%

profile of v9, /device:TPU:1, one launch (start us, length us, event | category | flops | bytes accessed | tf_op | source)
XLA Modules:
  0.0 185.5 jit_solution(208978653561061503)
XLA Ops:
  0.6 1.6 shard_map.77
  2.2 18.4 %all-to-all-start = ((s32[128,1,1]{2,1,0:T(1,128)}), s32[128,1,1]{2,1,0:T(1,128)S(1)}, u32[]{:S(2)}, u32[]{:S(2)}) async-start(s32[128,1,1]{2,1,0:T(1,128)} %bitcast.16), calls=%async_computation | async-start | bytes 131072 | tf_op jit(solution)/shard_map/all_to_all | solution.py:237
  20.7 0.9 mul.28
  21.6 1.3 multiply_convert_fusion
  22.8 9.3 %all-to-all-done = s32[128,1,1]{2,1,0:T(1,128)S(1)} async-done(((s32[128,1,1]{2,1,0:T(1,128)}), s32[128,1,1]{2,1,0:T(1,128)S(1)}, u32[]{:S(2)}, u32[]{:S(2)}) %all-to-all-start) | async-done | bytes 544 | tf_op jit(solution)/shard_map/all_to_all | solution.py:237
  32.1 2.1 %shard_map.78 = bf16[256,8,512]{2,1,0:T(8,128)(2,1)} custom-call(s32[128,1]{1,0:T(8,128)S(1)} %bitcast.11, bf16[40,8,512]{2,1,0:T(8,128)(2,1)S(1)} %get-tuple-element.16.tilted.refs_3_), custom_call_target="tpu_custom_call" | custom-call | bytes 2425344 | tf_op jit(solution)/shard_map/pallas_call | solution.py:203
  34.2 0.0 copy-start.1
  34.2 0.0 copy-start
  34.2 7.0 %all-to-all-start.1 = ((bf16[256,8,512]{2,1,0:T(8,128)(2,1)}), bf16[256,8,512]{2,1,0:T(8,128)(2,1)}, u32[]{:S(2)}, u32[]{:S(2)}) async-start(bf16[256,8,512]{2,1,0:T(8,128)(2,1)} %shard_map.78), calls=%async_computation.1 | async-start | bytes 4194304 | tf_op jit(solution)/shard_map/all_to_all | solution.py:286
  41.2 3.0 %collective-permute-start.1 = (bf16[20,8,512]{2,1,0:T(8,128)(2,1)S(1)}, bf16[20,8,512]{2,1,0:T(8,128)(2,1)}, u32[]{:S(2)}, u32[]{:S(2)}) collective-permute-start(bf16[20,8,512]{2,1,0:T(8,128)(2,1)S(1)} %get-tuple-element.14), channel_id=1, source_target_pairs={{4,0},{8,4},{12,8},{16,12},{20,16},{24,20},{28,24},{32,28},{36,32}... | collective-permute-start | bytes 491528 | tf_op jit(solution)/shard_map/ppermute | solution.py:288
  44.2 2.6 %collective-permute-start = (bf16[20,8,512]{2,1,0:T(8,128)(2,1)S(1)}, bf16[20,8,512]{2,1,0:T(8,128)(2,1)}, u32[]{:S(2)}, u32[]{:S(2)}) collective-permute-start(bf16[20,8,512]{2,1,0:T(8,128)(2,1)S(1)} %get-tuple-element.15), channel_id=1, source_target_pairs={{0,4},{4,8},{8,12},{12,16},{16,20},{20,24},{24,28},{28,32},{32,36}... | collective-permute-start | bytes 491528 | tf_op jit(solution)/shard_map/ppermute | solution.py:287
  46.8 0.0 copy-done.1
  46.9 0.1 copy.27
  46.9 0.1 reshape.35.refs_0_
  47.0 0.1 copy.28
  47.1 0.1 reshape.36
  47.2 0.2 and_reduce_fusion
  47.5 23.5 %collective-permute-done.1.refs_4_ = bf16[20,8,512]{2,1,0:T(8,128)(2,1)} collective-permute-done((bf16[20,8,512]{2,1,0:T(8,128)(2,1)S(1)}, bf16[20,8,512]{2,1,0:T(8,128)(2,1)}, u32[]{:S(2)}, u32[]{:S(2)}) %collective-permute-start.1) | collective-permute-done | bytes 163872 | tf_op jit(solution)/shard_map/ppermute | solution.py:288
  71.0 10.0 %collective-permute-done.refs_2_ = bf16[20,8,512]{2,1,0:T(8,128)(2,1)} collective-permute-done((bf16[20,8,512]{2,1,0:T(8,128)(2,1)S(1)}, bf16[20,8,512]{2,1,0:T(8,128)(2,1)}, u32[]{:S(2)}, u32[]{:S(2)}) %collective-permute-start) | collective-permute-done | bytes 163872 | tf_op jit(solution)/shard_map/ppermute | solution.py:287
  81.0 12.3 %all-to-all-done.1.refs_5_ = bf16[256,8,512]{2,1,0:T(8,128)(2,1)} async-done(((bf16[256,8,512]{2,1,0:T(8,128)(2,1)}), bf16[256,8,512]{2,1,0:T(8,128)(2,1)}, u32[]{:S(2)}, u32[]{:S(2)}) %all-to-all-start.1) | async-done | bytes 2097184 | tf_op jit(solution)/shard_map/all_to_all | solution.py:286
  93.3 0.0 copy-done
  93.3 5.6 %shard_map.79 = (bf16[40,8,512]{2,1,0:T(8,128)(2,1)S(1)}, bf16[256,8,512]{2,1,0:T(8,128)(2,1)}, f32[8,512]{1,0:T(8,128)S(1)}) custom-call(s32[128,1]{1,0:T(8,128)S(1)} %bitcast.12, f32[40,8,512]{2,1,0:T(8,128)S(1)} %get-tuple-element.17.factor, s32[320]{0:T(512)S(1)} %reshape.35.refs_0_, s32[160]{0:T(256)S(1)} %convert_add_fusion.refs_1_, ...), custom_call_target="tpu_custom_call" | custom-call | flops 2013265920 | bytes 8440192 | tf_op jit(solution)/shard_map/pallas_call | solution.py:203
  98.9 9.0 %all-to-all-start.2 = ((bf16[256,8,512]{2,1,0:T(8,128)(2,1)}), bf16[256,8,512]{2,1,0:T(8,128)(2,1)}, u32[]{:S(2)}, u32[]{:S(2)}) async-start(bf16[256,8,512]{2,1,0:T(8,128)(2,1)} %get-tuple-element.9), calls=%async_computation.2 | async-start | bytes 4194304 | tf_op jit(solution)/shard_map/all_to_all | solution.py:286
  108.0 2.9 %collective-permute-start.3 = (bf16[20,8,512]{2,1,0:T(8,128)(2,1)S(1)}, bf16[20,8,512]{2,1,0:T(8,128)(2,1)S(1)}, u32[]{:S(2)}, u32[]{:S(2)}) collective-permute-start(bf16[20,8,512]{2,1,0:T(8,128)(2,1)S(1)} %get-tuple-element.12), channel_id=1, source_target_pairs={{4,0},{8,4},{12,8},{16,12},{20,16},{24,20},{28,24},{32,28},{36,32}... | collective-permute-start | bytes 491528 | tf_op jit(solution)/shard_map/ppermute | solution.py:288
  110.8 2.9 %collective-permute-start.2 = (bf16[20,8,512]{2,1,0:T(8,128)(2,1)S(1)}, bf16[20,8,512]{2,1,0:T(8,128)(2,1)S(1)}, u32[]{:S(2)}, u32[]{:S(2)}) collective-permute-start(bf16[20,8,512]{2,1,0:T(8,128)(2,1)S(1)} %get-tuple-element.13), channel_id=1, source_target_pairs={{0,4},{4,8},{8,12},{12,16},{16,20},{20,24},{24,28},{28,32},{32,36}... | collective-permute-start | bytes 491528 | tf_op jit(solution)/shard_map/ppermute | solution.py:287
  113.7 26.0 %collective-permute-done.3.refs_4_ = bf16[20,8,512]{2,1,0:T(8,128)(2,1)S(1)} collective-permute-done((bf16[20,8,512]{2,1,0:T(8,128)(2,1)S(1)}, bf16[20,8,512]{2,1,0:T(8,128)(2,1)S(1)}, u32[]{:S(2)}, u32[]{:S(2)}) %collective-permute-start.3) | collective-permute-done | bytes 163872 | tf_op jit(solution)/shard_map/ppermute | solution.py:288
  139.7 8.0 %collective-permute-done.2.refs_2_ = bf16[20,8,512]{2,1,0:T(8,128)(2,1)S(1)} collective-permute-done((bf16[20,8,512]{2,1,0:T(8,128)(2,1)S(1)}, bf16[20,8,512]{2,1,0:T(8,128)(2,1)S(1)}, u32[]{:S(2)}, u32[]{:S(2)}) %collective-permute-start.2) | collective-permute-done | bytes 163872 | tf_op jit(solution)/shard_map/ppermute | solution.py:287
  147.6 12.3 %all-to-all-done.2.refs_5_ = bf16[256,8,512]{2,1,0:T(8,128)(2,1)} async-done(((bf16[256,8,512]{2,1,0:T(8,128)(2,1)}), bf16[256,8,512]{2,1,0:T(8,128)(2,1)}, u32[]{:S(2)}, u32[]{:S(2)}) %all-to-all-start.2) | async-done | bytes 2097184 | tf_op jit(solution)/shard_map/all_to_all | solution.py:286
  159.9 4.0 %shard_map.80 = (f32[8,20480]{1,0:T(8,128)S(1)}, f32[128,16]{1,0:T(8,128)S(1)}) custom-call(f32[8,512]{1,0:T(8,128)S(1)} %get-tuple-element.7.first_squares, s32[320]{0:T(512)S(1)} %reshape.35.refs_0_, s32[160]{0:T(256)S(1)} %convert_add_fusion.refs_1_, bf16[20,8,512]{2,1,0:T(8,128)(2,1)S(1)} %collective-permute-done.2.refs_2_, ...), custom_call_target="tpu_custom_call" | custom-call | flops 2013265920 | bytes 6023040 | tf_op jit(solution)/shard_map/pallas_call | solution.py:203
  164.0 19.8 %all_to_all.32 = f32[128,1,16]{2,1,0:T(1,128)S(1)} all-to-all(f32[128,1,16]{2,1,0:T(1,128)S(1)} %bitcast.14), channel_id=1, replica_groups=mesh['rows'=128,'tilt'=4] {'rows'}, dimensions={0} | all-to-all | bytes 16384 | tf_op jit(solution)/shard_map/all_to_all | solution.py:323
  183.8 1.6 shard_map.81
  (7 shorter events, 0.1 us)
Async XLA Ops:
  2.2 29.9 %all-to-all-start = ((s32[128,1,1]{2,1,0:T(1,128)}), s32[128,1,1]{2,1,0:T(1,128)S(1)}, u32[]{:S(2)}, u32[]{:S(2)}) async-start(s32[128,1,1]{2,1,0:T(1,128)} %bitcast.16), calls=%async_computation | async-start | bytes 131072 | tf_op jit(solution)/shard_map/all_to_all | solution.py:237
  34.2 12.6 %copy-start.1 = (s32[40,12]{0,1:T(8,128)S(1)}, s32[40,12]{0,1:T(8,128)}, u32[]{:S(2)}) copy-start(s32[40,12]{0,1:T(8,128)} %param.11) | copy-start | bytes 5764
  34.2 59.1 %copy-start = (bf16[4,512,512]{2,1,0:T(8,128)(2,1)S(1)}, bf16[4,512,512]{2,1,0:T(8,128)(2,1)}, u32[]{:S(2)}) copy-start(bf16[4,512,512]{2,1,0:T(8,128)(2,1)} %refs_6_.3) | copy-start | bytes 6291460
  34.2 59.1 %all-to-all-start.1 = ((bf16[256,8,512]{2,1,0:T(8,128)(2,1)}), bf16[256,8,512]{2,1,0:T(8,128)(2,1)}, u32[]{:S(2)}, u32[]{:S(2)}) async-start(bf16[256,8,512]{2,1,0:T(8,128)(2,1)} %shard_map.78), calls=%async_computation.1 | async-start | bytes 4194304 | tf_op jit(solution)/shard_map/all_to_all | solution.py:286
  41.2 29.8 %collective-permute-start.1 = (bf16[20,8,512]{2,1,0:T(8,128)(2,1)S(1)}, bf16[20,8,512]{2,1,0:T(8,128)(2,1)}, u32[]{:S(2)}, u32[]{:S(2)}) collective-permute-start(bf16[20,8,512]{2,1,0:T(8,128)(2,1)S(1)} %get-tuple-element.14), channel_id=1, source_target_pairs={{4,0},{8,4},{12,8},{16,12},{20,16},{24,20},{28,24},{32,28},{36,32}... | collective-permute-start | bytes 491528 | tf_op jit(solution)/shard_map/ppermute | solution.py:288
  44.2 36.8 %collective-permute-start = (bf16[20,8,512]{2,1,0:T(8,128)(2,1)S(1)}, bf16[20,8,512]{2,1,0:T(8,128)(2,1)}, u32[]{:S(2)}, u32[]{:S(2)}) collective-permute-start(bf16[20,8,512]{2,1,0:T(8,128)(2,1)S(1)} %get-tuple-element.15), channel_id=1, source_target_pairs={{0,4},{4,8},{8,12},{12,16},{16,20},{20,24},{24,28},{28,32},{32,36}... | collective-permute-start | bytes 491528 | tf_op jit(solution)/shard_map/ppermute | solution.py:287
  98.9 61.1 %all-to-all-start.2 = ((bf16[256,8,512]{2,1,0:T(8,128)(2,1)}), bf16[256,8,512]{2,1,0:T(8,128)(2,1)}, u32[]{:S(2)}, u32[]{:S(2)}) async-start(bf16[256,8,512]{2,1,0:T(8,128)(2,1)} %get-tuple-element.9), calls=%async_computation.2 | async-start | bytes 4194304 | tf_op jit(solution)/shard_map/all_to_all | solution.py:286
  108.0 31.7 %collective-permute-start.3 = (bf16[20,8,512]{2,1,0:T(8,128)(2,1)S(1)}, bf16[20,8,512]{2,1,0:T(8,128)(2,1)S(1)}, u32[]{:S(2)}, u32[]{:S(2)}) collective-permute-start(bf16[20,8,512]{2,1,0:T(8,128)(2,1)S(1)} %get-tuple-element.12), channel_id=1, source_target_pairs={{4,0},{8,4},{12,8},{16,12},{20,16},{24,20},{28,24},{32,28},{36,32}... | collective-permute-start | bytes 491528 | tf_op jit(solution)/shard_map/ppermute | solution.py:288
  110.8 36.8 %collective-permute-start.2 = (bf16[20,8,512]{2,1,0:T(8,128)(2,1)S(1)}, bf16[20,8,512]{2,1,0:T(8,128)(2,1)S(1)}, u32[]{:S(2)}, u32[]{:S(2)}) collective-permute-start(bf16[20,8,512]{2,1,0:T(8,128)(2,1)S(1)} %get-tuple-element.13), channel_id=1, source_target_pairs={{0,4},{4,8},{8,12},{12,16},{16,20},{20,24},{24,28},{28,32},{32,36}... | collective-permute-start | bytes 491528 | tf_op jit(solution)/shard_map/ppermute | solution.py:287

commit v10 on v9

--- a/solution.py
+++ b/solution.py
@@ -87,9 +87,43 @@
     return product.reshape(len(slots), rows, tilts, weights.shape[1])
 
 
+def near_sum(index, first_row, source, kernels, rates, gathered, rows, before_first_use=None):
+    kinds, tilts = kernels.shape[0], source.shape[1]
+    total = None
+    for kind in range(kinds):
+        slots = range(kind, NEAR, kinds)
+        product = weighted(
+            index, NEAR, slots, source, kernels[kind], gathered.at[kind % 2], rows, tilts
+        )
+        if kind == 0 and before_first_use is not None:
+            before_first_use.wait()
+        for n, slot in enumerate(slots):
+            rate = rates[slot, first_row : first_row + rows, :].astype(jnp.float32)
+            term = product[n] * rate[:, None, :]
+            total = term if total is None else total + term
+    return total
+
+
+def upper_kernel(index, own, after, kernels, rates, out, *scratch):
+    index_smem, extended, rate_buf, out_buf, gathered, sems = scratch
+    rows, half = own.shape[0], after.shape[0]
+    copies = [
+        start_copy(index, index_smem, sems.at[0]),
+        start_copy(own, extended.at[pl.ds(0, rows)], sems.at[1]),
+        start_copy(after, extended.at[pl.ds(rows, half)], sems.at[2]),
+    ]
+    rate_copy = start_copy(rates.at[pl.ds(0, NEAR)], rate_buf, sems.at[3])
+    for copy in copies:
+        copy.wait()
+    out_buf[...] = near_sum(
+        index_smem, rows - half, extended, kernels, rate_buf, gathered, half, rate_copy
+    )
+    start_copy(out_buf, out, sems.at[4]).wait()
+
+
 def map_blocks(operands, scratch, meanwhile=None):
-    near_index, far_index, before, own, after, arrived, kernels, rates = operands
-    near_smem, far_smem, extended, far_blocks, rate_buf, gathered, sems = scratch
+    near_index, far_index, before, own, upper, arrived, kernels, rates = operands
+    near_smem, far_smem, extended, far_blocks, rate_buf, upper_buf, gathered, sems = scratch
     kinds = kernels.shape[0]
     (rows, tilts, _), half = own.shape, before.shape[0]
     far_count = rates.shape[0] - NEAR
@@ -98,11 +132,11 @@
         start_copy(near_index, near_smem, sems.at[0]),
         start_copy(before, extended.at[pl.ds(0, half)], sems.at[1]),
         start_copy(own, extended.at[pl.ds(half, rows)], sems.at[2]),
-        start_copy(after, extended.at[pl.ds(half + rows, half)], sems.at[3]),
-    ]
-    rate_copy = start_copy(rates, rate_buf, sems.at[4])
+    ]
+    rate_copy = start_copy(rates, rate_buf, sems.at[3])
     late = [
-        start_copy(far_index, far_smem, sems.at[5]),
+        start_copy(far_index, far_smem, sems.at[4]),
+        start_copy(upper, upper_buf, sems.at[5]),
         start_copy(arrived, far_blocks, sems.at[6]),
     ]
     if meanwhile is not None:
@@ -110,19 +144,10 @@
     for copy in first:
         copy.wait()
 
-    total = None
-    for kind in range(kinds):
-        slots = range(kind, NEAR, kinds)
-        product = weighted(
-            near_smem, NEAR, slots, extended, kernels[kind], gathered.at[kind % 2], rows, tilts
-        )
-        if kind == 0:
-            rate_copy.wait()
-        for n, slot in enumerate(slots):
-            term = product[n] * rate_buf[slot].astype(jnp.float32)[:, None, :]
-            total = term if total is None else total + term
+    lower = near_sum(near_smem, 0, extended, kernels, rate_buf, gathered, half, rate_copy)
     for copy in late:
         copy.wait()
+    total = jnp.concatenate([lower, upper_buf[...]], axis=0)
     for kind in range(kinds):
         slots = range(kind, far_count, kinds)
         product = weighted(
@@ -243,7 +268,9 @@
     local_rows = jnp.arange(blocks_here, dtype=jnp.int32)
     global_rows = position * blocks_here + local_rows
     shifts = (pattern[:, :NEAR] - global_rows[:, None] + half_span) % total_blocks - half_span
-    near_index = (local_rows[:, None] + shifts + half_span).reshape(-1)
+    near_index = local_rows[:, None] + shifts + half_span
+    lower_index = near_index[:half_span].reshape(-1)
+    upper_index = near_index[half_span:].reshape(-1) - half_span
 
     up = [(i, (i + 1) % peer_count) for i in range(peer_count)]
     down = [(j, i) for i, j in up]
@@ -258,17 +285,32 @@
     mapped_shape = shape(start.shape, jnp.float32)
     word_buffers = [pltpu.VMEM((1, peer_count), jnp.int32), pltpu.SMEM((1, peer_count), jnp.int32)]
     staged = pltpu.VMEM(outgoing_shape.shape, jnp.bfloat16)
-    gather_rows = max(NEAR, far_count) // kind_count * blocks_here * tilt_count
+    upper_shape = shape((half_span, *block), jnp.float32)
+    reach = pltpu.VMEM((blocks_here + half_span, *block), jnp.bfloat16)
+    near_rows = NEAR // kind_count * half_span * tilt_count
+    far_rows = far_count // kind_count * blocks_here * tilt_count
+    gathered = pltpu.VMEM((2, max(near_rows, far_rows), block_size), jnp.bfloat16)
+    upper_scratch = [
+        pltpu.SMEM(upper_index.shape, jnp.int32),
+        reach,
+        pltpu.VMEM((NEAR, blocks_here, block_size), jnp.bfloat16),
+        pltpu.VMEM(upper_shape.shape, jnp.float32),
+        gathered,
+        sem((5,)),
+    ]
     map_scratch = [
-        pltpu.SMEM(near_index.shape, jnp.int32),
+        pltpu.SMEM(lower_index.shape, jnp.int32),
         pltpu.SMEM(far_index.shape, jnp.int32),
-        pltpu.VMEM((blocks_here + 2 * half_span, *block), jnp.bfloat16),
+        reach,
         staged,
         pltpu.VMEM(rates_by_slot.shape, jnp.bfloat16),
-        pltpu.VMEM((2, gather_rows, block_size), jnp.bfloat16),
+        pltpu.VMEM(upper_shape.shape, jnp.float32),
+        gathered,
         sem((7,)),
     ]
-    map_flops = 2 * slot_count * blocks_here * tilt_count * block_size * block_size
+    slot_flops = 2 * blocks_here * tilt_count * block_size * block_size
+    upper_flops = NEAR * slot_flops // 2
+    map_flops = slot_count * slot_flops - upper_flops
 
     factor = jnp.exp(theta[None, :, None] * reward[:, None, :])
     tilted = factor * start.reshape(tilt_count, blocks_here, block_size).transpose(1, 0, 2)
@@ -290,8 +332,17 @@
         rates_hbm = pltpu.with_memory_space_constraint(rates_by_slot, pltpu.HBM)
         if iteration < ITERS - 1:
             before = pltpu.with_memory_space_constraint(before, pltpu.HBM)
-            after = pltpu.with_memory_space_constraint(after, pltpu.HBM)
-        operands = [near_index, far_index, before, tilted, after, arrived, kernels, rates_hbm]
+        (upper,) = call(
+            upper_kernel,
+            [pltpu.HBM(upper_shape.shape, upper_shape.dtype)],
+            [upper_index, tilted, after, kernels, rates_hbm],
+            upper_scratch,
+            upper_flops,
+            MAP_LIMIT,
+            in_vmem=(3,),
+        )
+        upper = pltpu.with_memory_space_constraint(upper, pltpu.HBM)
+        operands = [lower_index, far_index, before, tilted, upper, arrived, kernels, rates_hbm]
         if iteration < ITERS - 1:
             step_scratch = [
                 *word_buffers,

time: 186 us -> 190 us (1.022)
  waiting for transfers between devices: 101 us -> 94.8 us
  Pallas kernels: 14.8 us -> 18.6 us
  starting transfers between devices: 45.7 us -> 48.8 us
  blocking collectives: 19.8 us -> 22.4 us
    ppermute x2, waiting for transfers between devices: 18 us -> 12.6 us  [on_device(): before = lax.ppermute(tilted[blocks_here - half_span:], 'rows', up)]
    pallas_call x5 -> x7, Pallas kernels: 14.8 us -> 18.6 us  [call(): pl.pallas_call(kernel, out_shape=outs, in_specs=[spec[n not in in_vmem] f...]
    all_to_all x2, starting transfers between devices: 16 us -> 19.1 us  [on_device(): lax.all_to_all(outgoing, 'rows', split_axis=0, concat_axis=0, tiled=True)]
    all_to_all x1, blocking collectives: 19.8 us -> 22.4 us  [on_device(): lax.all_to_all(sums, 'rows', split_axis=0, concat_axis=0, tiled=True)]
  transfers between devices with their start and end apart: 7 -> 7, of which waited for: 7 -> 7; matrix products, arithmetic and copies ran while one was open for 2% -> 2% of each run, Pallas kernels for 0% -> 3%
where the time goes in v10:
time: 190 us; the launch traced here: 189 us
  waiting for transfers between devices  94.8 us (50%)
  starting transfers between devices  48.8 us (26%)
  blocking collectives  22.4 us (12%)
  Pallas kernels  18.6 us (10%)
  local copies, waits for them, and re-layouts  2.23 us (1%)
    ppermute x2, waiting for transfers between devices, on_device(): after = lax.ppermute(tilted[:half_span], 'rows', down)  48.5 us
    all_to_all x2, waiting for transfers between devices, on_device(): lax.all_to_all(outgoing, 'rows', split_axis=0, concat_axis=0, tiled=True)  24.5 us
    all_to_all x1, blocking collectives, on_device(): lax.all_to_all(sums, 'rows', split_axis=0, concat_axis=0, tiled=True)  22.4 us
    all_to_all x2, starting transfers between devices, on_device(): lax.all_to_all(outgoing, 'rows', split_axis=0, concat_axis=0, tiled=True)  19.1 us
    pallas_call x7, Pallas kernels, call(): pl.pallas_call(kernel, out_shape=outs, in_specs=[spec[n not in in_vmem] f...  18.6 us
    all_to_all x1, starting transfers between devices, on_device(): lax.all_to_all(codes, 'rows', split_axis=0, concat_axis=0, tiled=True)  18.4 us
    ppermute x2, waiting for transfers between devices, on_device(): before = lax.ppermute(tilted[blocks_here - half_span:], 'rows', up)  12.6 us
    all_to_all x1, waiting for transfers between devices, on_device(): lax.all_to_all(codes, 'rows', split_axis=0, concat_axis=0, tiled=True)  9.26 us
  transfers between devices with their start and end apart: 7, of which 7 were waited for; matrix products, arithmetic and copies ran while one was open for 2% of the time, Pallas kernels for 3%

profile of v10, /device:TPU:1, one launch (start us, length us, event | category | flops | bytes accessed | tf_op | source)
XLA Modules:
  0.0 189.4 jit_solution(5647327134714319523)
XLA Ops:
  0.6 1.6 shard_map.77
  2.2 18.4 %all-to-all-start = ((s32[128,1,1]{2,1,0:T(1,128)}), s32[128,1,1]{2,1,0:T(1,128)S(1)}, u32[]{:S(2)}, u32[]{:S(2)}) async-start(s32[128,1,1]{2,1,0:T(1,128)} %bitcast.20), calls=%async_computation | async-start | bytes 131072 | tf_op jit(solution)/shard_map/all_to_all | solution.py:262
  20.7 0.9 mul.28
  21.6 1.3 multiply_convert_fusion
  22.8 9.3 %all-to-all-done = s32[128,1,1]{2,1,0:T(1,128)S(1)} async-done(((s32[128,1,1]{2,1,0:T(1,128)}), s32[128,1,1]{2,1,0:T(1,128)S(1)}, u32[]{:S(2)}, u32[]{:S(2)}) %all-to-all-start) | async-done | bytes 544 | tf_op jit(solution)/shard_map/all_to_all | solution.py:262
  32.1 2.1 %shard_map.79 = bf16[256,8,512]{2,1,0:T(8,128)(2,1)} custom-call(s32[128,1]{1,0:T(8,128)S(1)} %bitcast.11, bf16[40,8,512]{2,1,0:T(8,128)(2,1)S(1)} %get-tuple-element.16.own.tilted.refs_3_), custom_call_target="tpu_custom_call" | custom-call | bytes 2425344 | tf_op jit(solution)/shard_map/pallas_call | solution.py:228
  34.2 0.0 copy-start.2
  34.2 0.0 copy-start
  34.2 7.0 %all-to-all-start.1 = ((bf16[256,8,512]{2,1,0:T(8,128)(2,1)}), bf16[256,8,512]{2,1,0:T(8,128)(2,1)}, u32[]{:S(2)}, u32[]{:S(2)}) async-start(bf16[256,8,512]{2,1,0:T(8,128)(2,1)} %shard_map.79), calls=%async_computation.1 | async-start | bytes 4194304 | tf_op jit(solution)/shard_map/all_to_all | solution.py:328
  41.2 0.7 fusion.4
  41.9 3.0 %collective-permute-start.1 = (bf16[20,8,512]{2,1,0:T(8,128)(2,1)}, bf16[20,8,512]{2,1,0:T(8,128)(2,1)S(1)}, u32[]{:S(2)}, u32[]{:S(2)}) collective-permute-start(bf16[20,8,512]{2,1,0:T(8,128)(2,1)} %get-tuple-element.14), channel_id=1, source_target_pairs={{4,0},{8,4},{12,8},{16,12},{20,16},{24,20},{28,24},{32,28},{36,32}... | collective-permute-start | bytes 491528 | tf_op jit(solution)/shard_map/ppermute | solution.py:330
  44.9 2.6 %collective-permute-start = (bf16[20,8,512]{2,1,0:T(8,128)(2,1)}, bf16[20,8,512]{2,1,0:T(8,128)(2,1)S(1)}, u32[]{:S(2)}, u32[]{:S(2)}) collective-permute-start(bf16[20,8,512]{2,1,0:T(8,128)(2,1)} %get-tuple-element.15), channel_id=1, source_target_pairs={{0,4},{4,8},{8,12},{12,16},{16,20},{20,24},{24,28},{28,32},{32,36}... | collective-permute-start | bytes 491528 | tf_op jit(solution)/shard_map/ppermute | solution.py:329
  47.5 0.0 copy-done.2
  47.5 0.1 copy.31
  47.6 0.1 reshape.39
  47.8 0.2 and_reduce_fusion
  48.0 0.1 slice_add_fusion
  48.1 0.1 copy.32
  48.2 0.1 sub.21.index
  48.3 0.1 copy.30
  48.3 0.1 reshape.38.refs_0_
  48.4 22.5 %collective-permute-done.1.after = bf16[20,8,512]{2,1,0:T(8,128)(2,1)S(1)} collective-permute-done((bf16[20,8,512]{2,1,0:T(8,128)(2,1)}, bf16[20,8,512]{2,1,0:T(8,128)(2,1)S(1)}, u32[]{:S(2)}, u32[]{:S(2)}) %collective-permute-start.1) | collective-permute-done | bytes 163872 | tf_op jit(solution)/shard_map/ppermute | solution.py:330
  71.0 0.0 copy-done
  71.0 2.8 %shard_map.78.refs_4_ = f32[20,8,512]{2,1,0:T(8,128)} custom-call(s32[160]{0:T(256)S(1)} %sub.21.index, bf16[40,8,512]{2,1,0:T(8,128)(2,1)S(1)} %get-tuple-element.16.own.tilted.refs_3_, bf16[20,8,512]{2,1,0:T(8,128)(2,1)S(1)} %collective-permute-done.1.after, bf16[4,512,512]{2,1,0:T(8,128)(2,1)S(1)} %copy-done, bf16[12,40,512]{2,1,0:T(8,128)(2,1)} %bitcast.15), custom_call_target="tpu_custom_call" | custom-call | flops 671088640 | bytes 3408512 | tf_op jit(solution)/shard_map/pallas_call | solution.py:228
  73.8 7.4 %collective-permute-done.refs_2_ = bf16[20,8,512]{2,1,0:T(8,128)(2,1)S(1)} collective-permute-done((bf16[20,8,512]{2,1,0:T(8,128)(2,1)}, bf16[20,8,512]{2,1,0:T(8,128)(2,1)S(1)}, u32[]{:S(2)}, u32[]{:S(2)}) %collective-permute-start) | collective-permute-done | bytes 163872 | tf_op jit(solution)/shard_map/ppermute | solution.py:329
  81.1 0.0 copy-start.1
  81.1 12.2 %all-to-all-done.1.refs_5_ = bf16[256,8,512]{2,1,0:T(8,128)(2,1)} async-done(((bf16[256,8,512]{2,1,0:T(8,128)(2,1)}), bf16[256,8,512]{2,1,0:T(8,128)(2,1)}, u32[]{:S(2)}, u32[]{:S(2)}) %all-to-all-start.1) | async-done | bytes 2097184 | tf_op jit(solution)/shard_map/all_to_all | solution.py:328
  93.3 0.0 copy-done.1
  93.3 4.6 %shard_map.80 = (bf16[40,8,512]{2,1,0:T(8,128)(2,1)S(1)}, bf16[256,8,512]{2,1,0:T(8,128)(2,1)}, f32[8,512]{1,0:T(8,128)S(1)}) custom-call(s32[128,1]{1,0:T(8,128)S(1)} %bitcast.12, f32[40,8,512]{2,1,0:T(8,128)S(1)} %get-tuple-element.17.factor, s32[160]{0:T(256)S(1)} %reshape.38.refs_0_, s32[160]{0:T(256)S(1)} %convert_add_fusion.refs_1_, ...), custom_call_target="tpu_custom_call" | custom-call | flops 1342177280 | bytes 8603392 | tf_op jit(solution)/shard_map/pallas_call | solution.py:228
  97.9 12.1 %all-to-all-start.2 = ((bf16[256,8,512]{2,1,0:T(8,128)(2,1)}), bf16[256,8,512]{2,1,0:T(8,128)(2,1)}, u32[]{:S(2)}, u32[]{:S(2)}) async-start(bf16[256,8,512]{2,1,0:T(8,128)(2,1)} %get-tuple-element.9), calls=%async_computation.2 | async-start | bytes 4194304 | tf_op jit(solution)/shard_map/all_to_all | solution.py:328
  110.1 2.9 %collective-permute-start.3 = (bf16[20,8,512]{2,1,0:T(8,128)(2,1)S(1)}, bf16[20,8,512]{2,1,0:T(8,128)(2,1)S(1)}, u32[]{:S(2)}, u32[]{:S(2)}) collective-permute-start(bf16[20,8,512]{2,1,0:T(8,128)(2,1)S(1)} %get-tuple-element.12), channel_id=1, source_target_pairs={{4,0},{8,4},{12,8},{16,12},{20,16},{24,20},{28,24},{32,28},{36,32}... | collective-permute-start | bytes 491528 | tf_op jit(solution)/shard_map/ppermute | solution.py:330
  113.0 2.9 %collective-permute-start.2 = (bf16[20,8,512]{2,1,0:T(8,128)(2,1)S(1)}, bf16[20,8,512]{2,1,0:T(8,128)(2,1)S(1)}, u32[]{:S(2)}, u32[]{:S(2)}) collective-permute-start(bf16[20,8,512]{2,1,0:T(8,128)(2,1)S(1)} %get-tuple-element.13), channel_id=1, source_target_pairs={{0,4},{4,8},{8,12},{12,16},{16,20},{20,24},{24,28},{28,32},{32,36}... | collective-permute-start | bytes 491528 | tf_op jit(solution)/shard_map/ppermute | solution.py:329
  115.9 26.0 %collective-permute-done.3.after = bf16[20,8,512]{2,1,0:T(8,128)(2,1)S(1)} collective-permute-done((bf16[20,8,512]{2,1,0:T(8,128)(2,1)S(1)}, bf16[20,8,512]{2,1,0:T(8,128)(2,1)S(1)}, u32[]{:S(2)}, u32[]{:S(2)}) %collective-permute-start.3) | collective-permute-done | bytes 163872 | tf_op jit(solution)/shard_map/ppermute | solution.py:330
  141.8 2.8 %shard_map.81.refs_4_ = f32[20,8,512]{2,1,0:T(8,128)} custom-call(s32[160]{0:T(256)S(1)} %sub.21.index, bf16[40,8,512]{2,1,0:T(8,128)(2,1)S(1)} %get-tuple-element.8.own.refs_3_, bf16[20,8,512]{2,1,0:T(8,128)(2,1)S(1)} %collective-permute-done.3.after, bf16[4,512,512]{2,1,0:T(8,128)(2,1)S(1)} %copy-done, bf16[12,40,512]{2,1,0:T(8,128)(2,1)} %bitcast.17), custom_call_target="tpu_custom_call" | custom-call | flops 671088640 | bytes 3408512 | tf_op jit(solution)/shard_map/pallas_call | solution.py:228
  144.6 5.2 %collective-permute-done.2.refs_2_ = bf16[20,8,512]{2,1,0:T(8,128)(2,1)S(1)} collective-permute-done((bf16[20,8,512]{2,1,0:T(8,128)(2,1)S(1)}, bf16[20,8,512]{2,1,0:T(8,128)(2,1)S(1)}, u32[]{:S(2)}, u32[]{:S(2)}) %collective-permute-start.2) | collective-permute-done | bytes 163872 | tf_op jit(solution)/shard_map/ppermute | solution.py:329
  149.8 12.3 %all-to-all-done.2.refs_5_ = bf16[256,8,512]{2,1,0:T(8,128)(2,1)} async-done(((bf16[256,8,512]{2,1,0:T(8,128)(2,1)}), bf16[256,8,512]{2,1,0:T(8,128)(2,1)}, u32[]{:S(2)}, u32[]{:S(2)}) %all-to-all-start.2) | async-done | bytes 2097184 | tf_op jit(solution)/shard_map/all_to_all | solution.py:328
  162.1 3.2 %shard_map.82 = (f32[8,20480]{1,0:T(8,128)S(1)}, f32[128,16]{1,0:T(8,128)S(1)}) custom-call(f32[8,512]{1,0:T(8,128)S(1)} %get-tuple-element.7.first_squares, s32[160]{0:T(256)S(1)} %reshape.38.refs_0_, s32[160]{0:T(256)S(1)} %convert_add_fusion.refs_1_, bf16[20,8,512]{2,1,0:T(8,128)(2,1)S(1)} %collective-permute-done.2.refs_2_, ...), custom_call_target="tpu_custom_call" | custom-call | flops 1342177280 | bytes 6186240 | tf_op jit(solution)/shard_map/pallas_call | solution.py:228
  165.3 22.4 %all_to_all.32 = f32[128,1,16]{2,1,0:T(1,128)S(1)} all-to-all(f32[128,1,16]{2,1,0:T(1,128)S(1)} %bitcast.14), channel_id=1, replica_groups=mesh['rows'=128,'tilt'=4] {'rows'}, dimensions={0} | all-to-all | bytes 16384 | tf_op jit(solution)/shard_map/all_to_all | solution.py:374
  187.7 1.6 shard_map.83
  (6 shorter events, 0.1 us)
Async XLA Ops:
  2.2 29.9 %all-to-all-start = ((s32[128,1,1]{2,1,0:T(1,128)}), s32[128,1,1]{2,1,0:T(1,128)S(1)}, u32[]{:S(2)}, u32[]{:S(2)}) async-start(s32[128,1,1]{2,1,0:T(1,128)} %bitcast.20), calls=%async_computation | async-start | bytes 131072 | tf_op jit(solution)/shard_map/all_to_all | solution.py:262
  34.2 13.3 %copy-start.2 = (s32[40,12]{0,1:T(8,128)S(1)}, s32[40,12]{0,1:T(8,128)}, u32[]{:S(2)}) copy-start(s32[40,12]{0,1:T(8,128)} %param.11) | copy-start | bytes 5764
  34.2 36.8 %copy-start = (bf16[4,512,512]{2,1,0:T(8,128)(2,1)S(1)}, bf16[4,512,512]{2,1,0:T(8,128)(2,1)}, u32[]{:S(2)}) copy-start(bf16[4,512,512]{2,1,0:T(8,128)(2,1)} %refs_6_.3) | copy-start | bytes 6291460
  34.2 59.1 %all-to-all-start.1 = ((bf16[256,8,512]{2,1,0:T(8,128)(2,1)}), bf16[256,8,512]{2,1,0:T(8,128)(2,1)}, u32[]{:S(2)}, u32[]{:S(2)}) async-start(bf16[256,8,512]{2,1,0:T(8,128)(2,1)} %shard_map.79), calls=%async_computation.1 | async-start | bytes 4194304 | tf_op jit(solution)/shard_map/all_to_all | solution.py:328
  41.9 29.0 %collective-permute-start.1 = (bf16[20,8,512]{2,1,0:T(8,128)(2,1)}, bf16[20,8,512]{2,1,0:T(8,128)(2,1)S(1)}, u32[]{:S(2)}, u32[]{:S(2)}) collective-permute-start(bf16[20,8,512]{2,1,0:T(8,128)(2,1)} %get-tuple-element.14), channel_id=1, source_target_pairs={{4,0},{8,4},{12,8},{16,12},{20,16},{24,20},{28,24},{32,28},{36,32}... | collective-permute-start | bytes 491528 | tf_op jit(solution)/shard_map/ppermute | solution.py:330
  44.9 36.2 %collective-permute-start = (bf16[20,8,512]{2,1,0:T(8,128)(2,1)}, bf16[20,8,512]{2,1,0:T(8,128)(2,1)S(1)}, u32[]{:S(2)}, u32[]{:S(2)}) collective-permute-start(bf16[20,8,512]{2,1,0:T(8,128)(2,1)} %get-tuple-element.15), channel_id=1, source_target_pairs={{0,4},{4,8},{8,12},{12,16},{16,20},{20,24},{24,28},{28,32},{32,36}... | collective-permute-start | bytes 491528 | tf_op jit(solution)/shard_map/ppermute | solution.py:329
  81.1 12.2 %copy-start.1 = (bf16[20,8,512]{2,1,0:T(8,128)(2,1)}, bf16[20,8,512]{2,1,0:T(8,128)(2,1)S(1)}, u32[]{:S(2)}) copy-start(bf16[20,8,512]{2,1,0:T(8,128)(2,1)S(1)} %collective-permute-done.refs_2_) | copy-start | bytes 491524
  97.9 64.2 %all-to-all-start.2 = ((bf16[256,8,512]{2,1,0:T(8,128)(2,1)}), bf16[256,8,512]{2,1,0:T(8,128)(2,1)}, u32[]{:S(2)}, u32[]{:S(2)}) async-start(bf16[256,8,512]{2,1,0:T(8,128)(2,1)} %get-tuple-element.9), calls=%async_computation.2 | async-start | bytes 4194304 | tf_op jit(solution)/shard_map/all_to_all | solution.py:328
  110.1 31.7 %collective-permute-start.3 = (bf16[20,8,512]{2,1,0:T(8,128)(2,1)S(1)}, bf16[20,8,512]{2,1,0:T(8,128)(2,1)S(1)}, u32[]{:S(2)}, u32[]{:S(2)}) collective-permute-start(bf16[20,8,512]{2,1,0:T(8,128)(2,1)S(1)} %get-tuple-element.12), channel_id=1, source_target_pairs={{4,0},{8,4},{12,8},{16,12},{20,16},{24,20},{28,24},{32,28},{36,32}... | collective-permute-start | bytes 491528 | tf_op jit(solution)/shard_map/ppermute | solution.py:330
  113.0 36.8 %collective-permute-start.2 = (bf16[20,8,512]{2,1,0:T(8,128)(2,1)S(1)}, bf16[20,8,512]{2,1,0:T(8,128)(2,1)S(1)}, u32[]{:S(2)}, u32[]{:S(2)}) collective-permute-start(bf16[20,8,512]{2,1,0:T(8,128)(2,1)S(1)} %get-tuple-element.13), channel_id=1, source_target_pairs={{0,4},{4,8},{8,12},{12,16},{16,20},{20,24},{24,28},{28,32},{32,36}... | collective-permute-start | bytes 491528 | tf_op jit(solution)/shard_map/ppermute | solution.py:329

commit v11 on v10

--- a/solution.py
+++ b/solution.py
@@ -87,8 +87,9 @@
     return product.reshape(len(slots), rows, tilts, weights.shape[1])
 
 
-def near_sum(index, first_row, source, kernels, rates, gathered, rows, before_first_use=None):
-    kinds, tilts = kernels.shape[0], source.shape[1]
+def near_sum(index, source, kernels, rates, gathered, rows, before_first_use=None):
+    kinds, tilts, size = kernels.shape[0], source.shape[1], source.shape[2]
+    upper = jnp.full((rows, size), index[rows * NEAR]) > 0
     total = None
     for kind in range(kinds):
         slots = range(kind, NEAR, kinds)
@@ -98,45 +99,44 @@
         if kind == 0 and before_first_use is not None:
             before_first_use.wait()
         for n, slot in enumerate(slots):
-            rate = rates[slot, first_row : first_row + rows, :].astype(jnp.float32)
+            rate = rates[slot].astype(jnp.float32)
+            rate = jnp.where(upper, rate[rows:], rate[:rows])
             term = product[n] * rate[:, None, :]
             total = term if total is None else total + term
     return total
 
 
-def upper_kernel(index, own, after, kernels, rates, out, *scratch):
+def early_kernel(index, own, halo, kernels, rates, out, *scratch):
     index_smem, extended, rate_buf, out_buf, gathered, sems = scratch
-    rows, half = own.shape[0], after.shape[0]
+    rows, half = own.shape[0], halo.shape[0]
     copies = [
         start_copy(index, index_smem, sems.at[0]),
         start_copy(own, extended.at[pl.ds(0, rows)], sems.at[1]),
-        start_copy(after, extended.at[pl.ds(rows, half)], sems.at[2]),
+        start_copy(halo, extended.at[pl.ds(rows, half)], sems.at[2]),
     ]
     rate_copy = start_copy(rates.at[pl.ds(0, NEAR)], rate_buf, sems.at[3])
     for copy in copies:
         copy.wait()
-    out_buf[...] = near_sum(
-        index_smem, rows - half, extended, kernels, rate_buf, gathered, half, rate_copy
-    )
+    out_buf[...] = near_sum(index_smem, extended, kernels, rate_buf, gathered, half, rate_copy)
     start_copy(out_buf, out, sems.at[4]).wait()
 
 
 def map_blocks(operands, scratch, meanwhile=None):
-    near_index, far_index, before, own, upper, arrived, kernels, rates = operands
-    near_smem, far_smem, extended, far_blocks, rate_buf, upper_buf, gathered, sems = scratch
+    near_index, far_index, halo, own, early, arrived, kernels, rates = operands
+    near_smem, far_smem, extended, far_blocks, rate_buf, early_buf, gathered, sems = scratch
     kinds = kernels.shape[0]
-    (rows, tilts, _), half = own.shape, before.shape[0]
+    (rows, tilts, size), half = own.shape, halo.shape[0]
     far_count = rates.shape[0] - NEAR
 
     first = [
         start_copy(near_index, near_smem, sems.at[0]),
-        start_copy(before, extended.at[pl.ds(0, half)], sems.at[1]),
-        start_copy(own, extended.at[pl.ds(half, rows)], sems.at[2]),
+        start_copy(own, extended.at[pl.ds(0, rows)], sems.at[1]),
+        start_copy(halo, extended.at[pl.ds(rows, half)], sems.at[2]),
     ]
     rate_copy = start_copy(rates, rate_buf, sems.at[3])
     late = [
         start_copy(far_index, far_smem, sems.at[4]),
-        start_copy(upper, upper_buf, sems.at[5]),
+        start_copy(early, early_buf, sems.at[5]),
         start_copy(arrived, far_blocks, sems.at[6]),
     ]
     if meanwhile is not None:
@@ -144,10 +144,12 @@
     for copy in first:
         copy.wait()
 
-    lower = near_sum(near_smem, 0, extended, kernels, rate_buf, gathered, half, rate_copy)
+    here = near_sum(near_smem, extended, kernels, rate_buf, gathered, half, rate_copy)
     for copy in late:
         copy.wait()
-    total = jnp.concatenate([lower, upper_buf[...]], axis=0)
+    upper = jnp.full((half, tilts, size), near_smem[half * NEAR]) > 0
+    other = early_buf[...]
+    total = jnp.concatenate([jnp.where(upper, other, here), jnp.where(upper, here, other)], axis=0)
     for kind in range(kinds):
         slots = range(kind, far_count, kinds)
         product = weighted(
@@ -268,12 +270,20 @@
     local_rows = jnp.arange(blocks_here, dtype=jnp.int32)
     global_rows = position * blocks_here + local_rows
     shifts = (pattern[:, :NEAR] - global_rows[:, None] + half_span) % total_blocks - half_span
-    near_index = local_rows[:, None] + shifts + half_span
-    lower_index = near_index[:half_span].reshape(-1)
-    upper_index = near_index[half_span:].reshape(-1) - half_span
-
-    up = [(i, (i + 1) % peer_count) for i in range(peer_count)]
-    down = [(j, i) for i, j in up]
+    reached = local_rows[:, None] + shifts
+    reached = jnp.where(reached < 0, reached + blocks_here + half_span, reached)
+
+    odd = position % 2
+    early_first = half_span * (1 - odd)
+
+    def half_index(start_row):
+        entries = lax.dynamic_slice(reached, (start_row, 0), (half_span, NEAR)).reshape(-1)
+        return jnp.concatenate([entries, start_row[None]])
+
+    early_index = half_index(early_first)
+    late_index = half_index(half_span - early_first)
+    on_chip = [(i, i + 1 - 2 * (i % 2)) for i in range(peer_count)]
+    off_chip = [(i, (i - 1 + 2 * (i % 2)) % peer_count) for i in range(peer_count)]
     rates_by_slot = rates.transpose(1, 0, 2)
     reward = reward.reshape(blocks_here, block_size)
 
@@ -285,32 +295,32 @@
     mapped_shape = shape(start.shape, jnp.float32)
     word_buffers = [pltpu.VMEM((1, peer_count), jnp.int32), pltpu.SMEM((1, peer_count), jnp.int32)]
     staged = pltpu.VMEM(outgoing_shape.shape, jnp.bfloat16)
-    upper_shape = shape((half_span, *block), jnp.float32)
+    early_shape = shape((half_span, *block), jnp.float32)
     reach = pltpu.VMEM((blocks_here + half_span, *block), jnp.bfloat16)
     near_rows = NEAR // kind_count * half_span * tilt_count
     far_rows = far_count // kind_count * blocks_here * tilt_count
     gathered = pltpu.VMEM((2, max(near_rows, far_rows), block_size), jnp.bfloat16)
-    upper_scratch = [
-        pltpu.SMEM(upper_index.shape, jnp.int32),
+    early_scratch = [
+        pltpu.SMEM(early_index.shape, jnp.int32),
         reach,
         pltpu.VMEM((NEAR, blocks_here, block_size), jnp.bfloat16),
-        pltpu.VMEM(upper_shape.shape, jnp.float32),
+        pltpu.VMEM(early_shape.shape, jnp.float32),
         gathered,
         sem((5,)),
     ]
     map_scratch = [
-        pltpu.SMEM(lower_index.shape, jnp.int32),
+        pltpu.SMEM(late_index.shape, jnp.int32),
         pltpu.SMEM(far_index.shape, jnp.int32),
         reach,
         staged,
         pltpu.VMEM(rates_by_slot.shape, jnp.bfloat16),
-        pltpu.VMEM(upper_shape.shape, jnp.float32),
+        pltpu.VMEM(early_shape.shape, jnp.float32),
         gathered,
         sem((7,)),
     ]
     slot_flops = 2 * blocks_here * tilt_count * block_size * block_size
-    upper_flops = NEAR * slot_flops // 2
-    map_flops = slot_count * slot_flops - upper_flops
+    early_flops = NEAR * slot_flops // 2
+    map_flops = slot_count * slot_flops - early_flops
 
     factor = jnp.exp(theta[None, :, None] * reward[:, None, :])
     tilted = factor * start.reshape(tilt_count, blocks_here, block_size).transpose(1, 0, 2)
@@ -326,23 +336,24 @@
     )
     for iteration in range(ITERS):
         arrived = lax.all_to_all(outgoing, "rows", split_axis=0, concat_axis=0, tiled=True)
-        before = lax.ppermute(tilted[blocks_here - half_span :], "rows", up)
-        after = lax.ppermute(tilted[:half_span], "rows", down)
+        head, tail = tilted[:half_span], tilted[blocks_here - half_span :]
+        near_halo = lax.ppermute(jnp.where(odd, head, tail), "rows", on_chip)
+        far_halo = lax.ppermute(jnp.where(odd, tail, head), "rows", off_chip)
         arrived = pltpu.with_memory_space_constraint(arrived, pltpu.HBM)
         rates_hbm = pltpu.with_memory_space_constraint(rates_by_slot, pltpu.HBM)
         if iteration < ITERS - 1:
-            before = pltpu.with_memory_space_constraint(before, pltpu.HBM)
-        (upper,) = call(
-            upper_kernel,
-            [pltpu.HBM(upper_shape.shape, upper_shape.dtype)],
-            [upper_index, tilted, after, kernels, rates_hbm],
-            upper_scratch,
-            upper_flops,
+            far_halo = pltpu.with_memory_space_constraint(far_halo, pltpu.HBM)
+        (early,) = call(
+            early_kernel,
+            [pltpu.HBM(early_shape.shape, early_shape.dtype)],
+            [early_index, tilted, near_halo, kernels, rates_hbm],
+            early_scratch,
+            early_flops,
             MAP_LIMIT,
             in_vmem=(3,),
         )
-        upper = pltpu.with_memory_space_constraint(upper, pltpu.HBM)
-        operands = [lower_index, far_index, before, tilted, upper, arrived, kernels, rates_hbm]
+        early = pltpu.with_memory_space_constraint(early, pltpu.HBM)
+        operands = [late_index, far_index, far_halo, tilted, early, arrived, kernels, rates_hbm]
         if iteration < ITERS - 1:
             step_scratch = [
                 *word_buffers,

time: 190 us -> 185 us (0.974)
  blocking collectives: 22.4 us -> 19.8 us
  starting transfers between devices: 48.8 us -> 46.3 us
    all_to_all x1, blocking collectives: 22.4 us -> 19.8 us  [on_device(): lax.all_to_all(sums, 'rows', split_axis=0, concat_axis=0, tiled=True)]
    all_to_all x2, starting transfers between devices: 19.1 us -> 16.6 us  [on_device(): lax.all_to_all(outgoing, 'rows', split_axis=0, concat_axis=0, tiled=True)]
  transfers between devices with their start and end apart: 7 -> 7, of which waited for: 7 -> 5; matrix products, arithmetic and copies ran while one was open for 2% -> 2% of each run, Pallas kernels for 3% -> 3%
where the time goes in v11:
time: 185 us
  waiting for transfers between devices  94.4 us (51%)
  starting transfers between devices  46.3 us (25%)
  blocking collectives  19.8 us (11%)
  Pallas kernels  19 us (10%)
  other arithmetic  2.47 us (1%)
    ppermute x2, waiting for transfers between devices, on_device(): far_halo = lax.ppermute(jnp.where(odd, tail, head), 'rows', off_chip)  60.6 us
    all_to_all x2, waiting for transfers between devices, on_device(): lax.all_to_all(outgoing, 'rows', split_axis=0, concat_axis=0, tiled=True)  24.5 us
    all_to_all x1, blocking collectives, on_device(): lax.all_to_all(sums, 'rows', split_axis=0, concat_axis=0, tiled=True)  19.8 us
    pallas_call x7, Pallas kernels, call(): pl.pallas_call(kernel, out_shape=outs, in_specs=[spec[n not in in_vmem] f...  19 us
    all_to_all x1, starting transfers between devices, on_device(): lax.all_to_all(codes, 'rows', split_axis=0, concat_axis=0, tiled=True)  18.4 us
    all_to_all x2, starting transfers between devices, on_device(): lax.all_to_all(outgoing, 'rows', split_axis=0, concat_axis=0, tiled=True)  16.6 us
    all_to_all x1, waiting for transfers between devices, on_device(): lax.all_to_all(codes, 'rows', split_axis=0, concat_axis=0, tiled=True)  9.26 us
    ppermute x2, starting transfers between devices, on_device(): near_halo = lax.ppermute(jnp.where(odd, head, tail), 'rows', on_chip)  5.85 us
  transfers between devices with their start and end apart: 7, of which 5 were waited for; matrix products, arithmetic and copies ran while one was open for 2% of the time, Pallas kernels for 3%

profile of v11, /device:TPU:1, one launch (start us, length us, event | category | flops | bytes accessed | tf_op | source)
XLA Modules:
  0.0 184.6 jit_solution(11033075965869842757)
XLA Ops:
  0.6 1.6 shard_map.77
  2.2 18.4 %all-to-all-start = ((s32[128,1,1]{2,1,0:T(1,128)}), s32[128,1,1]{2,1,0:T(1,128)S(1)}, u32[]{:S(2)}, u32[]{:S(2)}) async-start(s32[128,1,1]{2,1,0:T(1,128)} %bitcast.22), calls=%async_computation | async-start | bytes 131072 | tf_op jit(solution)/shard_map/all_to_all | solution.py:264
  20.7 0.9 mul.31
  21.6 1.3 multiply_convert_fusion
  22.8 9.3 %all-to-all-done = s32[128,1,1]{2,1,0:T(1,128)S(1)} async-done(((s32[128,1,1]{2,1,0:T(1,128)}), s32[128,1,1]{2,1,0:T(1,128)S(1)}, u32[]{:S(2)}, u32[]{:S(2)}) %all-to-all-start) | async-done | bytes 544 | tf_op jit(solution)/shard_map/all_to_all | solution.py:264
  32.1 2.1 %shard_map.79 = bf16[256,8,512]{2,1,0:T(8,128)(2,1)} custom-call(s32[128,1]{1,0:T(8,128)S(1)} %bitcast.13, bf16[40,8,512]{2,1,0:T(8,128)(2,1)S(1)} %get-tuple-element.16.own.tilted.refs_3_), custom_call_target="tpu_custom_call" | custom-call | bytes 2425344 | tf_op jit(solution)/shard_map/pallas_call | solution.py:230
  34.2 0.0 copy-start.2
  34.2 0.0 copy-start
  34.2 7.0 %all-to-all-start.1 = ((bf16[256,8,512]{2,1,0:T(8,128)(2,1)}), bf16[256,8,512]{2,1,0:T(8,128)(2,1)}, u32[]{:S(2)}, u32[]{:S(2)}) async-start(bf16[256,8,512]{2,1,0:T(8,128)(2,1)} %shard_map.79), calls=%async_computation.1 | async-start | bytes 4194304 | tf_op jit(solution)/shard_map/all_to_all | solution.py:338
  41.2 0.7 broadcast_select_fusion.2
  42.0 3.0 %collective-permute-start.1 = (bf16[20,8,512]{2,1,0:T(8,128)(2,1)}, bf16[20,8,512]{2,1,0:T(8,128)(2,1)S(1)}, u32[]{:S(2)}, u32[]{:S(2)}) collective-permute-start(bf16[20,8,512]{2,1,0:T(8,128)(2,1)} %get-tuple-element.14), channel_id=1, source_target_pairs={{0,4},{4,0},{8,12},{12,8},{16,20},{20,16},{24,28},{28,24},{32,36},... | collective-permute-start | bytes 491528 | tf_op jit(solution)/shard_map/ppermute | solution.py:340
  44.9 2.6 %collective-permute-start = (bf16[20,8,512]{2,1,0:T(8,128)(2,1)}, bf16[20,8,512]{2,1,0:T(8,128)(2,1)S(1)}, u32[]{:S(2)}, u32[]{:S(2)}) collective-permute-start(bf16[20,8,512]{2,1,0:T(8,128)(2,1)} %get-tuple-element.15), channel_id=1, source_target_pairs={{0,508},{4,8},{8,4},{12,16},{16,12},{20,24},{24,20},{28,32},{32,28... | collective-permute-start | bytes 491528 | tf_op jit(solution)/shard_map/ppermute | solution.py:341
  47.6 0.0 copy-done.2
  47.6 0.1 constant_dynamic-slice_fusion
  47.7 0.1 copy.32
  47.8 0.1 reshape.41
  47.9 0.1 copy.31
  48.0 0.1 reshape.39
  48.1 0.2 and_reduce_fusion
  48.3 0.1 pad_add_fusion.1.index
  48.4 0.1 copy.30
  48.5 0.1 reshape.38
  48.6 0.1 pad_add_fusion.refs_0_
  48.7 0.0 collective-permute-done.1.halo
  48.7 0.0 copy-done
  48.7 2.8 %shard_map.78.refs_4_ = f32[20,8,512]{2,1,0:T(8,128)} custom-call(s32[161]{0:T(256)S(1)} %pad_add_fusion.1.index, bf16[40,8,512]{2,1,0:T(8,128)(2,1)S(1)} %get-tuple-element.16.own.tilted.refs_3_, bf16[20,8,512]{2,1,0:T(8,128)(2,1)S(1)} %collective-permute-done.1.halo, bf16[4,512,512]{2,1,0:T(8,128)(2,1)S(1)} %copy-done, bf16[12,40,512]{2,1,0:T(8,128)(2,1)} %bitcast.17), custom_call_target="tpu_custom_call" | custom-call | flops 671088640 | bytes 3408516 | tf_op jit(solution)/shard_map/pallas_call | solution.py:230
  51.5 29.6 %collective-permute-done.refs_2_ = bf16[20,8,512]{2,1,0:T(8,128)(2,1)S(1)} collective-permute-done((bf16[20,8,512]{2,1,0:T(8,128)(2,1)}, bf16[20,8,512]{2,1,0:T(8,128)(2,1)S(1)}, u32[]{:S(2)}, u32[]{:S(2)}) %collective-permute-start) | collective-permute-done | bytes 163872 | tf_op jit(solution)/shard_map/ppermute | solution.py:341
  81.1 0.0 copy-start.1
  81.1 12.2 %all-to-all-done.1.refs_5_ = bf16[256,8,512]{2,1,0:T(8,128)(2,1)} async-done(((bf16[256,8,512]{2,1,0:T(8,128)(2,1)}), bf16[256,8,512]{2,1,0:T(8,128)(2,1)}, u32[]{:S(2)}, u32[]{:S(2)}) %all-to-all-start.1) | async-done | bytes 2097184 | tf_op jit(solution)/shard_map/all_to_all | solution.py:338
  93.3 0.0 copy-done.1
  93.3 4.8 %shard_map.80 = (bf16[40,8,512]{2,1,0:T(8,128)(2,1)S(1)}, bf16[256,8,512]{2,1,0:T(8,128)(2,1)}, f32[8,512]{1,0:T(8,128)S(1)}) custom-call(s32[128,1]{1,0:T(8,128)S(1)} %bitcast.14, f32[40,8,512]{2,1,0:T(8,128)S(1)} %get-tuple-element.17.factor, s32[161]{0:T(256)S(1)} %pad_add_fusion.refs_0_, s32[160]{0:T(256)S(1)} %convert_add_fusion.refs_1_, ...), custom_call_target="tpu_custom_call" | custom-call | flops 1342177280 | bytes 8603396 | tf_op jit(solution)/shard_map/pallas_call | solution.py:230
  98.2 9.6 %all-to-all-start.2 = ((bf16[256,8,512]{2,1,0:T(8,128)(2,1)}), bf16[256,8,512]{2,1,0:T(8,128)(2,1)}, u32[]{:S(2)}, u32[]{:S(2)}) async-start(bf16[256,8,512]{2,1,0:T(8,128)(2,1)} %get-tuple-element.9), calls=%async_computation.2 | async-start | bytes 4194304 | tf_op jit(solution)/shard_map/all_to_all | solution.py:338
  107.8 2.9 %collective-permute-start.3 = (bf16[20,8,512]{2,1,0:T(8,128)(2,1)S(1)}, bf16[20,8,512]{2,1,0:T(8,128)(2,1)S(1)}, u32[]{:S(2)}, u32[]{:S(2)}) collective-permute-start(bf16[20,8,512]{2,1,0:T(8,128)(2,1)S(1)} %get-tuple-element.12), channel_id=1, source_target_pairs={{0,4},{4,0},{8,12},{12,8},{16,20},{20,16},{24,28},{28,24},{32,36},... | collective-permute-start | bytes 491528 | tf_op jit(solution)/shard_map/ppermute | solution.py:340
  110.7 2.9 %collective-permute-start.2 = (bf16[20,8,512]{2,1,0:T(8,128)(2,1)S(1)}, bf16[20,8,512]{2,1,0:T(8,128)(2,1)S(1)}, u32[]{:S(2)}, u32[]{:S(2)}) collective-permute-start(bf16[20,8,512]{2,1,0:T(8,128)(2,1)S(1)} %get-tuple-element.13), channel_id=1, source_target_pairs={{0,508},{4,8},{8,4},{12,16},{16,12},{20,24},{24,20},{28,32},{32,28... | collective-permute-start | bytes 491528 | tf_op jit(solution)/shard_map/ppermute | solution.py:341
  113.6 0.0 collective-permute-done.3.halo
  113.6 2.8 %shard_map.81.refs_4_ = f32[20,8,512]{2,1,0:T(8,128)} custom-call(s32[161]{0:T(256)S(1)} %pad_add_fusion.1.index, bf16[40,8,512]{2,1,0:T(8,128)(2,1)S(1)} %get-tuple-element.8.own.refs_3_, bf16[20,8,512]{2,1,0:T(8,128)(2,1)S(1)} %collective-permute-done.3.halo, bf16[4,512,512]{2,1,0:T(8,128)(2,1)S(1)} %copy-done, bf16[12,40,512]{2,1,0:T(8,128)(2,1)} %bitcast.19), custom_call_target="tpu_custom_call" | custom-call | flops 671088640 | bytes 3408516 | tf_op jit(solution)/shard_map/pallas_call | solution.py:230
  116.4 31.0 %collective-permute-done.2.refs_2_ = bf16[20,8,512]{2,1,0:T(8,128)(2,1)S(1)} collective-permute-done((bf16[20,8,512]{2,1,0:T(8,128)(2,1)S(1)}, bf16[20,8,512]{2,1,0:T(8,128)(2,1)S(1)}, u32[]{:S(2)}, u32[]{:S(2)}) %collective-permute-start.2) | collective-permute-done | bytes 163872 | tf_op jit(solution)/shard_map/ppermute | solution.py:341
  147.5 12.3 %all-to-all-done.2.refs_5_ = bf16[256,8,512]{2,1,0:T(8,128)(2,1)} async-done(((bf16[256,8,512]{2,1,0:T(8,128)(2,1)}), bf16[256,8,512]{2,1,0:T(8,128)(2,1)}, u32[]{:S(2)}, u32[]{:S(2)}) %all-to-all-start.2) | async-done | bytes 2097184 | tf_op jit(solution)/shard_map/all_to_all | solution.py:338
  159.8 3.3 %shard_map.82 = (f32[8,20480]{1,0:T(8,128)S(1)}, f32[128,16]{1,0:T(8,128)S(1)}) custom-call(f32[8,512]{1,0:T(8,128)S(1)} %get-tuple-element.7.first_squares, s32[161]{0:T(256)S(1)} %pad_add_fusion.refs_0_, s32[160]{0:T(256)S(1)} %convert_add_fusion.refs_1_, bf16[20,8,512]{2,1,0:T(8,128)(2,1)S(1)} %collective-permute-done.2.refs_2_, ...), custom_call_target="tpu_custom_call" | custom-call | flops 1342177280 | bytes 6186244 | tf_op jit(solution)/shard_map/pallas_call | solution.py:230
  163.1 19.8 %all_to_all.32 = f32[128,1,16]{2,1,0:T(1,128)S(1)} all-to-all(f32[128,1,16]{2,1,0:T(1,128)S(1)} %bitcast.16), channel_id=1, replica_groups=mesh['rows'=128,'tilt'=4] {'rows'}, dimensions={0} | all-to-all | bytes 16384 | tf_op jit(solution)/shard_map/all_to_all | solution.py:385
  182.9 1.6 shard_map.83
  (6 shorter events, 0.1 us)
Async XLA Ops:
  2.2 29.9 %all-to-all-start = ((s32[128,1,1]{2,1,0:T(1,128)}), s32[128,1,1]{2,1,0:T(1,128)S(1)}, u32[]{:S(2)}, u32[]{:S(2)}) async-start(s32[128,1,1]{2,1,0:T(1,128)} %bitcast.22), calls=%async_computation | async-start | bytes 131072 | tf_op jit(solution)/shard_map/all_to_all | solution.py:264
  34.2 13.4 %copy-start.2 = (s32[40,12]{0,1:T(8,128)S(1)}, s32[40,12]{0,1:T(8,128)}, u32[]{:S(2)}) copy-start(s32[40,12]{0,1:T(8,128)} %param.11) | copy-start | bytes 5764
  34.2 14.5 %copy-start = (bf16[4,512,512]{2,1,0:T(8,128)(2,1)S(1)}, bf16[4,512,512]{2,1,0:T(8,128)(2,1)}, u32[]{:S(2)}) copy-start(bf16[4,512,512]{2,1,0:T(8,128)(2,1)} %refs_6_.3) | copy-start | bytes 6291460
  34.2 59.1 %all-to-all-start.1 = ((bf16[256,8,512]{2,1,0:T(8,128)(2,1)}), bf16[256,8,512]{2,1,0:T(8,128)(2,1)}, u32[]{:S(2)}, u32[]{:S(2)}) async-start(bf16[256,8,512]{2,1,0:T(8,128)(2,1)} %shard_map.79), calls=%async_computation.1 | async-start | bytes 4194304 | tf_op jit(solution)/shard_map/all_to_all | solution.py:338
  42.0 6.7 %collective-permute-start.1 = (bf16[20,8,512]{2,1,0:T(8,128)(2,1)}, bf16[20,8,512]{2,1,0:T(8,128)(2,1)S(1)}, u32[]{:S(2)}, u32[]{:S(2)}) collective-permute-start(bf16[20,8,512]{2,1,0:T(8,128)(2,1)} %get-tuple-element.14), channel_id=1, source_target_pairs={{0,4},{4,0},{8,12},{12,8},{16,20},{20,16},{24,28},{28,24},{32,36},... | collective-permute-start | bytes 491528 | tf_op jit(solution)/shard_map/ppermute | solution.py:340
  44.9 36.2 %collective-permute-start = (bf16[20,8,512]{2,1,0:T(8,128)(2,1)}, bf16[20,8,512]{2,1,0:T(8,128)(2,1)S(1)}, u32[]{:S(2)}, u32[]{:S(2)}) collective-permute-start(bf16[20,8,512]{2,1,0:T(8,128)(2,1)} %get-tuple-element.15), channel_id=1, source_target_pairs={{0,508},{4,8},{8,4},{12,16},{16,12},{20,24},{24,20},{28,32},{32,28... | collective-permute-start | bytes 491528 | tf_op jit(solution)/shard_map/ppermute | solution.py:341
  81.1 12.2 %copy-start.1 = (bf16[20,8,512]{2,1,0:T(8,128)(2,1)}, bf16[20,8,512]{2,1,0:T(8,128)(2,1)S(1)}, u32[]{:S(2)}) copy-start(bf16[20,8,512]{2,1,0:T(8,128)(2,1)S(1)} %collective-permute-done.refs_2_) | copy-start | bytes 491524
  98.2 61.6 %all-to-all-start.2 = ((bf16[256,8,512]{2,1,0:T(8,128)(2,1)}), bf16[256,8,512]{2,1,0:T(8,128)(2,1)}, u32[]{:S(2)}, u32[]{:S(2)}) async-start(bf16[256,8,512]{2,1,0:T(8,128)(2,1)} %get-tuple-element.9), calls=%async_computation.2 | async-start | bytes 4194304 | tf_op jit(solution)/shard_map/all_to_all | solution.py:338
  107.8 5.8 %collective-permute-start.3 = (bf16[20,8,512]{2,1,0:T(8,128)(2,1)S(1)}, bf16[20,8,512]{2,1,0:T(8,128)(2,1)S(1)}, u32[]{:S(2)}, u32[]{:S(2)}) collective-permute-start(bf16[20,8,512]{2,1,0:T(8,128)(2,1)S(1)} %get-tuple-element.12), channel_id=1, source_target_pairs={{0,4},{4,0},{8,12},{12,8},{16,20},{20,16},{24,28},{28,24},{32,36},... | collective-permute-start | bytes 491528 | tf_op jit(solution)/shard_map/ppermute | solution.py:340
  110.7 36.8 %collective-permute-start.2 = (bf16[20,8,512]{2,1,0:T(8,128)(2,1)S(1)}, bf16[20,8,512]{2,1,0:T(8,128)(2,1)S(1)}, u32[]{:S(2)}, u32[]{:S(2)}) collective-permute-start(bf16[20,8,512]{2,1,0:T(8,128)(2,1)S(1)} %get-tuple-element.13), channel_id=1, source_target_pairs={{0,508},{4,8},{8,4},{12,16},{16,12},{20,24},{24,20},{28,32},{32,28... | collective-permute-start | bytes 491528 | tf_op jit(solution)/shard_map/ppermute | solution.py:341

commit v12 on v11

--- a/solution.py
+++ b/solution.py
@@ -166,16 +166,19 @@
 
 def step_kernel(codes, factor, *refs):
     operands, (tilted, outgoing, squares) = refs[:8], refs[8:11]
-    line, words, tilted_buf, staged, pack_sems, sems = refs[11:17]
-    decoded = []
-
-    def decode():
-        decoded.append(read_words(codes, line, words, sems.at[0]))
-
-    total = map_blocks(operands, refs[17:], decode)
-    tilted_buf[...] = (factor[...] * total).astype(jnp.bfloat16)
+    line, words, factor_buf, tilted_buf, staged, pack_sems, sems = refs[11:18]
+    started = []
+
+    def meanwhile():
+        started.append(read_words(codes, line, words, sems.at[0]))
+        started.append(start_copy(factor, factor_buf, sems.at[2]))
+
+    total = map_blocks(operands, refs[18:], meanwhile)
+    words_copy, factor_copy = started
+    factor_copy.wait()
+    tilted_buf[...] = (factor_buf[...] * total).astype(jnp.bfloat16)
     copies = [start_copy(tilted_buf, tilted, sems.at[1])]
-    decoded[0].wait()
+    words_copy.wait()
     copies += pack_blocks(words, tilted_buf, staged, outgoing, pack_sems)
     squares[...] = jnp.sum(total * total, axis=0)
     for copy in copies:
@@ -342,7 +345,7 @@
         arrived = pltpu.with_memory_space_constraint(arrived, pltpu.HBM)
         rates_hbm = pltpu.with_memory_space_constraint(rates_by_slot, pltpu.HBM)
         if iteration < ITERS - 1:
-            far_halo = pltpu.with_memory_space_constraint(far_halo, pltpu.HBM)
+            factor_hbm = pltpu.with_memory_space_constraint(factor, pltpu.HBM)
         (early,) = call(
             early_kernel,
             [pltpu.HBM(early_shape.shape, early_shape.dtype)],
@@ -357,19 +360,20 @@
         if iteration < ITERS - 1:
             step_scratch = [
                 *word_buffers,
+                pltpu.VMEM(tilted_shape.shape, jnp.float32),
                 pltpu.VMEM(tilted_shape.shape, jnp.bfloat16),
                 staged,
                 sem((PACK_CHUNKS,)),
-                sem((2,)),
+                sem((3,)),
             ]
             tilted, outgoing, squares = call(
                 step_kernel,
                 [tilted_shape, pltpu.HBM(outgoing_shape.shape, outgoing_shape.dtype), squares_shape],
-                [codes, factor, *operands],
+                [codes, factor_hbm, *operands],
                 step_scratch + map_scratch,
                 map_flops,
                 MAP_LIMIT,
-                in_vmem=(0, 1, 8, 12),
+                in_vmem=(0, 8, 12),
             )
         else:
             mapped, sums = call(

time: 185 us -> 185 us (level)
  no operation moved by 1% of the time
where the time goes in v12:
time: 185 us; the launch traced here: 184 us
  waiting for transfers between devices  94.3 us (51%)
  starting transfers between devices  45.7 us (25%)
  blocking collectives  19.8 us (11%)
  Pallas kernels  19 us (10%)
  other arithmetic  2.6 us (1%)
    ppermute x2, waiting for transfers between devices, on_device(): far_halo = lax.ppermute(jnp.where(odd, tail, head), 'rows', off_chip)  61.2 us
    all_to_all x2, waiting for transfers between devices, on_device(): lax.all_to_all(outgoing, 'rows', split_axis=0, concat_axis=0, tiled=True)  24.7 us
    all_to_all x1, blocking collectives, on_device(): lax.all_to_all(sums, 'rows', split_axis=0, concat_axis=0, tiled=True)  19.8 us
    pallas_call x7, Pallas kernels, call(): pl.pallas_call(kernel, out_shape=outs, in_specs=[spec[n not in in_vmem] f...  19 us
    all_to_all x1, starting transfers between devices, on_device(): lax.all_to_all(codes, 'rows', split_axis=0, concat_axis=0, tiled=True)  18.4 us
    all_to_all x2, starting transfers between devices, on_device(): lax.all_to_all(outgoing, 'rows', split_axis=0, concat_axis=0, tiled=True)  15.9 us
    all_to_all x1, waiting for transfers between devices, on_device(): lax.all_to_all(codes, 'rows', split_axis=0, concat_axis=0, tiled=True)  8.51 us
    ppermute x2, starting transfers between devices, on_device(): near_halo = lax.ppermute(jnp.where(odd, head, tail), 'rows', on_chip)  5.86 us
  transfers between devices with their start and end apart: 7, of which 5 were waited for; matrix products, arithmetic and copies ran while one was open for 2% of the time, Pallas kernels for 3%

profile of v12, /device:TPU:1, one launch (start us, length us, event | category | flops | bytes accessed | tf_op | source)
XLA Modules:
  0.0 184.0 jit_solution(15397343285344849155)
XLA Ops:
  0.6 1.6 shard_map.77
  2.2 18.4 %all-to-all-start = ((s32[128,1,1]{2,1,0:T(1,128)}), s32[128,1,1]{2,1,0:T(1,128)S(1)}, u32[]{:S(2)}, u32[]{:S(2)}) async-start(s32[128,1,1]{2,1,0:T(1,128)} %bitcast.22), calls=%async_computation | async-start | bytes 131072 | tf_op jit(solution)/shard_map/all_to_all | solution.py:267
  20.6 0.9 mul.31
  21.6 2.1 %multiply_convert_fusion = (bf16[40,8,512]{2,1,0:T(8,128)(2,1)S(1)}, f32[40,8,512]{2,1,0:T(8,128)}) fusion(f32[40,8,512]{2,1,0:T(8,128)} %bitcast.21, f32[40,512]{1,0:T(8,128)S(1)} %mul.31, f32[8]{0:T(128)} %param.8), kind=kLoop, calls=%fused_computation | loop fusion | flops 491520 | bytes 1720352 | tf_op jit(solution)/shard_map/convert_element_type | solution.py:330
  23.7 8.5 %all-to-all-done = s32[128,1,1]{2,1,0:T(1,128)S(1)} async-done(((s32[128,1,1]{2,1,0:T(1,128)}), s32[128,1,1]{2,1,0:T(1,128)S(1)}, u32[]{:S(2)}, u32[]{:S(2)}) %all-to-all-start) | async-done | bytes 544 | tf_op jit(solution)/shard_map/all_to_all | solution.py:267
  32.2 2.1 %shard_map.79 = bf16[256,8,512]{2,1,0:T(8,128)(2,1)} custom-call(s32[128,1]{1,0:T(8,128)S(1)} %bitcast.13, bf16[40,8,512]{2,1,0:T(8,128)(2,1)S(1)} %get-tuple-element.16.own.tilted.refs_3_), custom_call_target="tpu_custom_call" | custom-call | bytes 2425344 | tf_op jit(solution)/shard_map/pallas_call | solution.py:233
  34.3 0.0 copy-start.1
  34.3 0.0 copy-start
  34.3 6.9 %all-to-all-start.1 = ((bf16[256,8,512]{2,1,0:T(8,128)(2,1)}), bf16[256,8,512]{2,1,0:T(8,128)(2,1)}, u32[]{:S(2)}, u32[]{:S(2)}) async-start(bf16[256,8,512]{2,1,0:T(8,128)(2,1)} %shard_map.79), calls=%async_computation.1 | async-start | bytes 4194304 | tf_op jit(solution)/shard_map/all_to_all | solution.py:341
  41.3 3.0 %collective-permute-start.1 = (bf16[20,8,512]{2,1,0:T(8,128)(2,1)S(1)}, bf16[20,8,512]{2,1,0:T(8,128)(2,1)S(1)}, u32[]{:S(2)}, u32[]{:S(2)}) collective-permute-start(bf16[20,8,512]{2,1,0:T(8,128)(2,1)S(1)} %get-tuple-element.14), channel_id=1, source_target_pairs={{0,4},{4,0},{8,12},{12,8},{16,20},{20,16},{24,28},{28,24},{32,36},... | collective-permute-start | bytes 491528 | tf_op jit(solution)/shard_map/ppermute | solution.py:343
  44.3 2.6 %collective-permute-start = (bf16[20,8,512]{2,1,0:T(8,128)(2,1)S(1)}, bf16[20,8,512]{2,1,0:T(8,128)(2,1)S(1)}, u32[]{:S(2)}, u32[]{:S(2)}) collective-permute-start(bf16[20,8,512]{2,1,0:T(8,128)(2,1)S(1)} %get-tuple-element.15), channel_id=1, source_target_pairs={{0,508},{4,8},{8,4},{12,16},{16,12},{20,24},{24,20},{28,32},{32,28... | collective-permute-start | bytes 491528 | tf_op jit(solution)/shard_map/ppermute | solution.py:344
  46.9 0.0 copy-done.1
  47.0 0.1 constant_dynamic-slice_fusion
  47.1 0.1 copy.32
  47.2 0.1 reshape.41
  47.3 0.1 copy.31
  47.3 0.1 reshape.39
  47.5 0.2 and_reduce_fusion
  47.7 0.1 pad_add_fusion.1.index
  47.8 0.1 copy.30
  47.9 0.1 reshape.38
  48.0 0.1 pad_add_fusion.refs_0_
  48.0 0.0 collective-permute-done.1.halo
  48.0 0.0 copy-done
  48.0 2.8 %shard_map.78.refs_4_ = f32[20,8,512]{2,1,0:T(8,128)} custom-call(s32[161]{0:T(256)S(1)} %pad_add_fusion.1.index, bf16[40,8,512]{2,1,0:T(8,128)(2,1)S(1)} %get-tuple-element.16.own.tilted.refs_3_, bf16[20,8,512]{2,1,0:T(8,128)(2,1)S(1)} %collective-permute-done.1.halo, bf16[4,512,512]{2,1,0:T(8,128)(2,1)S(1)} %copy-done, bf16[12,40,512]{2,1,0:T(8,128)(2,1)} %bitcast.17), custom_call_target="tpu_custom_call" | custom-call | flops 671088640 | bytes 3408516 | tf_op jit(solution)/shard_map/pallas_call | solution.py:233
  50.9 30.2 %collective-permute-done.refs_2_ = bf16[20,8,512]{2,1,0:T(8,128)(2,1)S(1)} collective-permute-done((bf16[20,8,512]{2,1,0:T(8,128)(2,1)S(1)}, bf16[20,8,512]{2,1,0:T(8,128)(2,1)S(1)}, u32[]{:S(2)}, u32[]{:S(2)}) %collective-permute-start) | collective-permute-done | bytes 163872 | tf_op jit(solution)/shard_map/ppermute | solution.py:344
  81.1 12.3 %all-to-all-done.1.refs_5_ = bf16[256,8,512]{2,1,0:T(8,128)(2,1)} async-done(((bf16[256,8,512]{2,1,0:T(8,128)(2,1)}), bf16[256,8,512]{2,1,0:T(8,128)(2,1)}, u32[]{:S(2)}, u32[]{:S(2)}) %all-to-all-start.1) | async-done | bytes 2097184 | tf_op jit(solution)/shard_map/all_to_all | solution.py:341
  93.4 4.8 %shard_map.80 = (bf16[40,8,512]{2,1,0:T(8,128)(2,1)S(1)}, bf16[256,8,512]{2,1,0:T(8,128)(2,1)}, f32[8,512]{1,0:T(8,128)S(1)}) custom-call(s32[128,1]{1,0:T(8,128)S(1)} %bitcast.14, f32[40,8,512]{2,1,0:T(8,128)} %get-tuple-element.17.factor, s32[161]{0:T(256)S(1)} %pad_add_fusion.refs_0_, s32[160]{0:T(256)S(1)} %convert_add_fusion.refs_1_, ...), custom_call_target="tpu_custom_call" | custom-call | flops 1342177280 | bytes 8603396 | tf_op jit(solution)/shard_map/pallas_call | solution.py:233
  98.2 8.9 %all-to-all-start.2 = ((bf16[256,8,512]{2,1,0:T(8,128)(2,1)}), bf16[256,8,512]{2,1,0:T(8,128)(2,1)}, u32[]{:S(2)}, u32[]{:S(2)}) async-start(bf16[256,8,512]{2,1,0:T(8,128)(2,1)} %get-tuple-element.9), calls=%async_computation.2 | async-start | bytes 4194304 | tf_op jit(solution)/shard_map/all_to_all | solution.py:341
  107.2 2.9 %collective-permute-start.3 = (bf16[20,8,512]{2,1,0:T(8,128)(2,1)S(1)}, bf16[20,8,512]{2,1,0:T(8,128)(2,1)S(1)}, u32[]{:S(2)}, u32[]{:S(2)}) collective-permute-start(bf16[20,8,512]{2,1,0:T(8,128)(2,1)S(1)} %get-tuple-element.12), channel_id=1, source_target_pairs={{0,4},{4,0},{8,12},{12,8},{16,20},{20,16},{24,28},{28,24},{32,36},... | collective-permute-start | bytes 491528 | tf_op jit(solution)/shard_map/ppermute | solution.py:343
  110.1 2.9 %collective-permute-start.2 = (bf16[20,8,512]{2,1,0:T(8,128)(2,1)S(1)}, bf16[20,8,512]{2,1,0:T(8,128)(2,1)S(1)}, u32[]{:S(2)}, u32[]{:S(2)}) collective-permute-start(bf16[20,8,512]{2,1,0:T(8,128)(2,1)S(1)} %get-tuple-element.13), channel_id=1, source_target_pairs={{0,508},{4,8},{8,4},{12,16},{16,12},{20,24},{24,20},{28,32},{32,28... | collective-permute-start | bytes 491528 | tf_op jit(solution)/shard_map/ppermute | solution.py:344
  113.0 0.0 collective-permute-done.3.halo
  113.0 2.8 %shard_map.81.refs_4_ = f32[20,8,512]{2,1,0:T(8,128)} custom-call(s32[161]{0:T(256)S(1)} %pad_add_fusion.1.index, bf16[40,8,512]{2,1,0:T(8,128)(2,1)S(1)} %get-tuple-element.8.own.refs_3_, bf16[20,8,512]{2,1,0:T(8,128)(2,1)S(1)} %collective-permute-done.3.halo, bf16[4,512,512]{2,1,0:T(8,128)(2,1)S(1)} %copy-done, bf16[12,40,512]{2,1,0:T(8,128)(2,1)} %bitcast.19), custom_call_target="tpu_custom_call" | custom-call | flops 671088640 | bytes 3408516 | tf_op jit(solution)/shard_map/pallas_call | solution.py:233
  115.9 31.0 %collective-permute-done.2.refs_2_ = bf16[20,8,512]{2,1,0:T(8,128)(2,1)S(1)} collective-permute-done((bf16[20,8,512]{2,1,0:T(8,128)(2,1)S(1)}, bf16[20,8,512]{2,1,0:T(8,128)(2,1)S(1)}, u32[]{:S(2)}, u32[]{:S(2)}) %collective-permute-start.2) | collective-permute-done | bytes 163872 | tf_op jit(solution)/shard_map/ppermute | solution.py:344
  146.9 12.3 %all-to-all-done.2.refs_5_ = bf16[256,8,512]{2,1,0:T(8,128)(2,1)} async-done(((bf16[256,8,512]{2,1,0:T(8,128)(2,1)}), bf16[256,8,512]{2,1,0:T(8,128)(2,1)}, u32[]{:S(2)}, u32[]{:S(2)}) %all-to-all-start.2) | async-done | bytes 2097184 | tf_op jit(solution)/shard_map/all_to_all | solution.py:341
  159.2 3.3 %shard_map.82 = (f32[8,20480]{1,0:T(8,128)S(1)}, f32[128,16]{1,0:T(8,128)S(1)}) custom-call(f32[8,512]{1,0:T(8,128)S(1)} %get-tuple-element.7.first_squares, s32[161]{0:T(256)S(1)} %pad_add_fusion.refs_0_, s32[160]{0:T(256)S(1)} %convert_add_fusion.refs_1_, bf16[20,8,512]{2,1,0:T(8,128)(2,1)S(1)} %collective-permute-done.2.refs_2_, ...), custom_call_target="tpu_custom_call" | custom-call | flops 1342177280 | bytes 6186244 | tf_op jit(solution)/shard_map/pallas_call | solution.py:233
  162.5 19.8 %all_to_all.32 = f32[128,1,16]{2,1,0:T(1,128)S(1)} all-to-all(f32[128,1,16]{2,1,0:T(1,128)S(1)} %bitcast.16), channel_id=1, replica_groups=mesh['rows'=128,'tilt'=4] {'rows'}, dimensions={0} | all-to-all | bytes 16384 | tf_op jit(solution)/shard_map/all_to_all | solution.py:389
  182.3 1.6 shard_map.83
  (7 shorter events, 0.1 us)
Async XLA Ops:
  2.2 30.0 %all-to-all-start = ((s32[128,1,1]{2,1,0:T(1,128)}), s32[128,1,1]{2,1,0:T(1,128)S(1)}, u32[]{:S(2)}, u32[]{:S(2)}) async-start(s32[128,1,1]{2,1,0:T(1,128)} %bitcast.22), calls=%async_computation | async-start | bytes 131072 | tf_op jit(solution)/shard_map/all_to_all | solution.py:267
  34.3 12.7 %copy-start.1 = (s32[40,12]{0,1:T(8,128)S(1)}, s32[40,12]{0,1:T(8,128)}, u32[]{:S(2)}) copy-start(s32[40,12]{0,1:T(8,128)} %param.11) | copy-start | bytes 5764
  34.3 13.8 %copy-start = (bf16[4,512,512]{2,1,0:T(8,128)(2,1)S(1)}, bf16[4,512,512]{2,1,0:T(8,128)(2,1)}, u32[]{:S(2)}) copy-start(bf16[4,512,512]{2,1,0:T(8,128)(2,1)} %refs_6_.3) | copy-start | bytes 6291460
  34.3 59.1 %all-to-all-start.1 = ((bf16[256,8,512]{2,1,0:T(8,128)(2,1)}), bf16[256,8,512]{2,1,0:T(8,128)(2,1)}, u32[]{:S(2)}, u32[]{:S(2)}) async-start(bf16[256,8,512]{2,1,0:T(8,128)(2,1)} %shard_map.79), calls=%async_computation.1 | async-start | bytes 4194304 | tf_op jit(solution)/shard_map/all_to_all | solution.py:341
  41.3 6.7 %collective-permute-start.1 = (bf16[20,8,512]{2,1,0:T(8,128)(2,1)S(1)}, bf16[20,8,512]{2,1,0:T(8,128)(2,1)S(1)}, u32[]{:S(2)}, u32[]{:S(2)}) collective-permute-start(bf16[20,8,512]{2,1,0:T(8,128)(2,1)S(1)} %get-tuple-element.14), channel_id=1, source_target_pairs={{0,4},{4,0},{8,12},{12,8},{16,20},{20,16},{24,28},{28,24},{32,36},... | collective-permute-start | bytes 491528 | tf_op jit(solution)/shard_map/ppermute | solution.py:343
  44.3 36.8 %collective-permute-start = (bf16[20,8,512]{2,1,0:T(8,128)(2,1)S(1)}, bf16[20,8,512]{2,1,0:T(8,128)(2,1)S(1)}, u32[]{:S(2)}, u32[]{:S(2)}) collective-permute-start(bf16[20,8,512]{2,1,0:T(8,128)(2,1)S(1)} %get-tuple-element.15), channel_id=1, source_target_pairs={{0,508},{4,8},{8,4},{12,16},{16,12},{20,24},{24,20},{28,32},{32,28... | collective-permute-start | bytes 491528 | tf_op jit(solution)/shard_map/ppermute | solution.py:344
  98.2 61.0 %all-to-all-start.2 = ((bf16[256,8,512]{2,1,0:T(8,128)(2,1)}), bf16[256,8,512]{2,1,0:T(8,128)(2,1)}, u32[]{:S(2)}, u32[]{:S(2)}) async-start(bf16[256,8,512]{2,1,0:T(8,128)(2,1)} %get-tuple-element.9), calls=%async_computation.2 | async-start | bytes 4194304 | tf_op jit(solution)/shard_map/all_to_all | solution.py:341
  107.2 5.8 %collective-permute-start.3 = (bf16[20,8,512]{2,1,0:T(8,128)(2,1)S(1)}, bf16[20,8,512]{2,1,0:T(8,128)(2,1)S(1)}, u32[]{:S(2)}, u32[]{:S(2)}) collective-permute-start(bf16[20,8,512]{2,1,0:T(8,128)(2,1)S(1)} %get-tuple-element.12), channel_id=1, source_target_pairs={{0,4},{4,0},{8,12},{12,8},{16,20},{20,16},{24,28},{28,24},{32,36},... | collective-permute-start | bytes 491528 | tf_op jit(solution)/shard_map/ppermute | solution.py:343
  110.1 36.8 %collective-permute-start.2 = (bf16[20,8,512]{2,1,0:T(8,128)(2,1)S(1)}, bf16[20,8,512]{2,1,0:T(8,128)(2,1)S(1)}, u32[]{:S(2)}, u32[]{:S(2)}) collective-permute-start(bf16[20,8,512]{2,1,0:T(8,128)(2,1)S(1)} %get-tuple-element.13), channel_id=1, source_target_pairs={{0,508},{4,8},{8,4},{12,16},{16,12},{20,24},{24,20},{28,32},{32,28... | collective-permute-start | bytes 491528 | tf_op jit(solution)/shard_map/ppermute | solution.py:344

commit v13 on v12

--- a/solution.py
+++ b/solution.py
@@ -87,7 +87,7 @@
     return product.reshape(len(slots), rows, tilts, weights.shape[1])
 
 
-def near_sum(index, source, kernels, rates, gathered, rows, before_first_use=None):
+def near_sum(index, source, kernels, rates, gathered, rows):
     kinds, tilts, size = kernels.shape[0], source.shape[1], source.shape[2]
     upper = jnp.full((rows, size), index[rows * NEAR]) > 0
     total = None
@@ -96,8 +96,6 @@
         product = weighted(
             index, NEAR, slots, source, kernels[kind], gathered.at[kind % 2], rows, tilts
         )
-        if kind == 0 and before_first_use is not None:
-            before_first_use.wait()
         for n, slot in enumerate(slots):
             rate = rates[slot].astype(jnp.float32)
             rate = jnp.where(upper, rate[rows:], rate[:rows])
@@ -107,23 +105,22 @@
 
 
 def early_kernel(index, own, halo, kernels, rates, out, *scratch):
-    index_smem, extended, rate_buf, out_buf, gathered, sems = scratch
+    index_smem, extended, out_buf, gathered, sems = scratch
     rows, half = own.shape[0], halo.shape[0]
     copies = [
         start_copy(index, index_smem, sems.at[0]),
         start_copy(own, extended.at[pl.ds(0, rows)], sems.at[1]),
         start_copy(halo, extended.at[pl.ds(rows, half)], sems.at[2]),
     ]
-    rate_copy = start_copy(rates.at[pl.ds(0, NEAR)], rate_buf, sems.at[3])
     for copy in copies:
         copy.wait()
-    out_buf[...] = near_sum(index_smem, extended, kernels, rate_buf, gathered, half, rate_copy)
-    start_copy(out_buf, out, sems.at[4]).wait()
+    out_buf[...] = near_sum(index_smem, extended, kernels, rates, gathered, half)
+    start_copy(out_buf, out, sems.at[3]).wait()
 
 
 def map_blocks(operands, scratch, meanwhile=None):
     near_index, far_index, halo, own, early, arrived, kernels, rates = operands
-    near_smem, far_smem, extended, far_blocks, rate_buf, early_buf, gathered, sems = scratch
+    near_smem, far_smem, extended, far_blocks, early_buf, gathered, sems = scratch
     kinds = kernels.shape[0]
     (rows, tilts, size), half = own.shape, halo.shape[0]
     far_count = rates.shape[0] - NEAR
@@ -133,18 +130,17 @@
         start_copy(own, extended.at[pl.ds(0, rows)], sems.at[1]),
         start_copy(halo, extended.at[pl.ds(rows, half)], sems.at[2]),
     ]
-    rate_copy = start_copy(rates, rate_buf, sems.at[3])
     late = [
-        start_copy(far_index, far_smem, sems.at[4]),
-        start_copy(early, early_buf, sems.at[5]),
-        start_copy(arrived, far_blocks, sems.at[6]),
+        start_copy(far_index, far_smem, sems.at[3]),
+        start_copy(early, early_buf, sems.at[4]),
+        start_copy(arrived, far_blocks, sems.at[5]),
     ]
     if meanwhile is not None:
         meanwhile()
     for copy in first:
         copy.wait()
 
-    here = near_sum(near_smem, extended, kernels, rate_buf, gathered, half, rate_copy)
+    here = near_sum(near_smem, extended, kernels, rates, gathered, half)
     for copy in late:
         copy.wait()
     upper = jnp.full((half, tilts, size), near_smem[half * NEAR]) > 0
@@ -156,7 +152,7 @@
             far_smem, far_count, slots, far_blocks, kernels[kind], gathered.at[kind % 2], rows, tilts
         )
         for n, slot in enumerate(slots):
-            total = total + product[n] * rate_buf[NEAR + slot].astype(jnp.float32)[:, None, :]
+            total = total + product[n] * rates[NEAR + slot].astype(jnp.float32)[:, None, :]
     return total
 
 
@@ -306,20 +302,18 @@
     early_scratch = [
         pltpu.SMEM(early_index.shape, jnp.int32),
         reach,
-        pltpu.VMEM((NEAR, blocks_here, block_size), jnp.bfloat16),
         pltpu.VMEM(early_shape.shape, jnp.float32),
         gathered,
-        sem((5,)),
+        sem((4,)),
     ]
     map_scratch = [
         pltpu.SMEM(late_index.shape, jnp.int32),
         pltpu.SMEM(far_index.shape, jnp.int32),
         reach,
         staged,
-        pltpu.VMEM(rates_by_slot.shape, jnp.bfloat16),
         pltpu.VMEM(early_shape.shape, jnp.float32),
         gathered,
-        sem((7,)),
+        sem((6,)),
     ]
     slot_flops = 2 * blocks_here * tilt_count * block_size * block_size
     early_flops = NEAR * slot_flops // 2
@@ -343,20 +337,19 @@
         near_halo = lax.ppermute(jnp.where(odd, head, tail), "rows", on_chip)
         far_halo = lax.ppermute(jnp.where(odd, tail, head), "rows", off_chip)
         arrived = pltpu.with_memory_space_constraint(arrived, pltpu.HBM)
-        rates_hbm = pltpu.with_memory_space_constraint(rates_by_slot, pltpu.HBM)
         if iteration < ITERS - 1:
             factor_hbm = pltpu.with_memory_space_constraint(factor, pltpu.HBM)
         (early,) = call(
             early_kernel,
             [pltpu.HBM(early_shape.shape, early_shape.dtype)],
-            [early_index, tilted, near_halo, kernels, rates_hbm],
+            [early_index, tilted, near_halo, kernels, rates_by_slot],
             early_scratch,
             early_flops,
             MAP_LIMIT,
-            in_vmem=(3,),
+            in_vmem=(3, 4),
         )
         early = pltpu.with_memory_space_constraint(early, pltpu.HBM)
-        operands = [late_index, far_index, far_halo, tilted, early, arrived, kernels, rates_hbm]
+        operands = [late_index, far_index, far_halo, tilted, early, arrived, kernels, rates_by_slot]
         if iteration < ITERS - 1:
             step_scratch = [
                 *word_buffers,
@@ -373,7 +366,7 @@
                 step_scratch + map_scratch,
                 map_flops,
                 MAP_LIMIT,
-                in_vmem=(0, 8, 12),
+                in_vmem=(0, 8, 9, 12),
             )
         else:
             mapped, sums = call(
@@ -383,7 +376,7 @@
                 map_scratch,
                 map_flops,
                 MAP_LIMIT,
-                in_vmem=(0, 7, 9, 10),
+                in_vmem=(0, 7, 8, 9, 10),
             )
 
     gathered = lax.all_to_all(sums, "rows", split_axis=0, concat_axis=0, tiled=True)

time: 185 us -> 184 us (level)
  transfers between devices with their start and end apart: 7 -> 7, of which waited for: 5 -> 5; matrix products, arithmetic and copies ran while one was open for 2% -> 3% of each run, Pallas kernels for 3% -> 2%
where the time goes in v13:
time: 184 us
  waiting for transfers between devices  94.9 us (52%)
  starting transfers between devices  45.7 us (25%)
  blocking collectives  19.8 us (11%)
  Pallas kernels  17.5 us (10%)
  other arithmetic  3.26 us (2%)
    ppermute x2, waiting for transfers between devices, on_device(): far_halo = lax.ppermute(jnp.where(odd, tail, head), 'rows', off_chip)  61.7 us
    all_to_all x2, waiting for transfers between devices, on_device(): lax.all_to_all(outgoing, 'rows', split_axis=0, concat_axis=0, tiled=True)  24.7 us
    all_to_all x1, blocking collectives, on_device(): lax.all_to_all(sums, 'rows', split_axis=0, concat_axis=0, tiled=True)  19.8 us
    all_to_all x1, starting transfers between devices, on_device(): lax.all_to_all(codes, 'rows', split_axis=0, concat_axis=0, tiled=True)  18.4 us
    pallas_call x7, Pallas kernels, call(): pl.pallas_call(kernel, out_shape=outs, in_specs=[spec[n not in in_vmem] f...  17.5 us
    all_to_all x2, starting transfers between devices, on_device(): lax.all_to_all(outgoing, 'rows', split_axis=0, concat_axis=0, tiled=True)  15.9 us
    all_to_all x1, waiting for transfers between devices, on_device(): lax.all_to_all(codes, 'rows', split_axis=0, concat_axis=0, tiled=True)  8.52 us
    ppermute x2, starting transfers between devices, on_device(): near_halo = lax.ppermute(jnp.where(odd, head, tail), 'rows', on_chip)  5.85 us
  transfers between devices with their start and end apart: 7, of which 5 were waited for; matrix products, arithmetic and copies ran while one was open for 3% of the time, Pallas kernels for 2%

profile of v13, /device:TPU:1, one launch (start us, length us, event | category | flops | bytes accessed | tf_op | source)
XLA Modules:
  0.0 183.8 jit_solution(2781142948057450023)
XLA Ops:
  0.6 1.6 shard_map.77
  2.2 18.4 %all-to-all-start = ((s32[128,1,1]{2,1,0:T(1,128)}), s32[128,1,1]{2,1,0:T(1,128)S(1)}, u32[]{:S(2)}, u32[]{:S(2)}) async-start(s32[128,1,1]{2,1,0:T(1,128)} %bitcast.22), calls=%async_computation | async-start | bytes 131072 | tf_op jit(solution)/shard_map/all_to_all | solution.py:263
  20.7 0.9 mul.31
  21.6 2.1 %multiply_convert_fusion = (bf16[40,8,512]{2,1,0:T(8,128)(2,1)S(1)}, f32[40,8,512]{2,1,0:T(8,128)}) fusion(f32[40,8,512]{2,1,0:T(8,128)} %bitcast.21, f32[40,512]{1,0:T(8,128)S(1)} %mul.31, f32[8]{0:T(128)} %param.8), kind=kLoop, calls=%fused_computation | loop fusion | flops 491520 | bytes 1720352 | tf_op jit(solution)/shard_map/convert_element_type | solution.py:324
  23.7 8.5 %all-to-all-done = s32[128,1,1]{2,1,0:T(1,128)S(1)} async-done(((s32[128,1,1]{2,1,0:T(1,128)}), s32[128,1,1]{2,1,0:T(1,128)S(1)}, u32[]{:S(2)}, u32[]{:S(2)}) %all-to-all-start) | async-done | bytes 544 | tf_op jit(solution)/shard_map/all_to_all | solution.py:263
  32.2 2.1 %shard_map.79 = bf16[256,8,512]{2,1,0:T(8,128)(2,1)} custom-call(s32[128,1]{1,0:T(8,128)S(1)} %bitcast.17, bf16[40,8,512]{2,1,0:T(8,128)(2,1)S(1)} %get-tuple-element.16.own.tilted.refs_3_), custom_call_target="tpu_custom_call" | custom-call | bytes 2425344 | tf_op jit(solution)/shard_map/pallas_call | solution.py:229
  34.3 0.0 copy-start.2
  34.3 0.0 copy-start
  34.3 0.0 copy-start.1
  34.3 7.0 %all-to-all-start.1 = ((bf16[256,8,512]{2,1,0:T(8,128)(2,1)}), bf16[256,8,512]{2,1,0:T(8,128)(2,1)}, u32[]{:S(2)}, u32[]{:S(2)}) async-start(bf16[256,8,512]{2,1,0:T(8,128)(2,1)} %shard_map.79), calls=%async_computation.1 | async-start | bytes 4194304 | tf_op jit(solution)/shard_map/all_to_all | solution.py:335
  41.3 0.7 broadcast_select_fusion.2
  42.0 3.0 %collective-permute-start.1 = (bf16[20,8,512]{2,1,0:T(8,128)(2,1)}, bf16[20,8,512]{2,1,0:T(8,128)(2,1)S(1)}, u32[]{:S(2)}, u32[]{:S(2)}) collective-permute-start(bf16[20,8,512]{2,1,0:T(8,128)(2,1)} %get-tuple-element.14), channel_id=1, source_target_pairs={{0,4},{4,0},{8,12},{12,8},{16,20},{20,16},{24,28},{28,24},{32,36},... | collective-permute-start | bytes 491528 | tf_op jit(solution)/shard_map/ppermute | solution.py:337
  45.0 2.6 %collective-permute-start = (bf16[20,8,512]{2,1,0:T(8,128)(2,1)S(1)}, bf16[20,8,512]{2,1,0:T(8,128)(2,1)S(1)}, u32[]{:S(2)}, u32[]{:S(2)}) collective-permute-start(bf16[20,8,512]{2,1,0:T(8,128)(2,1)S(1)} %get-tuple-element.15), channel_id=1, source_target_pairs={{0,508},{4,8},{8,4},{12,16},{16,12},{20,24},{24,20},{28,32},{32,28... | collective-permute-start | bytes 491528 | tf_op jit(solution)/shard_map/ppermute | solution.py:338
  47.6 0.0 copy-done.2
  47.7 0.1 constant_dynamic-slice_fusion
  47.8 0.1 copy.32
  47.9 0.1 reshape.41
  48.0 0.1 copy.31
  48.0 0.1 reshape.39
  48.2 0.2 and_reduce_fusion
  48.4 0.1 pad_add_fusion.1.index
  48.5 0.1 copy.30
  48.6 0.1 reshape.38
  48.7 0.1 pad_add_fusion.refs_0_
  48.7 0.0 collective-permute-done.1.halo
  48.7 0.0 copy-done
  48.7 0.0 copy-done.1
  48.7 2.2 %shard_map.78.refs_4_ = f32[20,8,512]{2,1,0:T(8,128)} custom-call(s32[161]{0:T(256)S(1)} %pad_add_fusion.1.index, bf16[40,8,512]{2,1,0:T(8,128)(2,1)S(1)} %get-tuple-element.16.own.tilted.refs_3_, bf16[20,8,512]{2,1,0:T(8,128)(2,1)S(1)} %collective-permute-done.1.halo, bf16[4,512,512]{2,1,0:T(8,128)(2,1)S(1)} %copy-done, bf16[12,40,512]{2,1,0:T(8,128)(2,1)S(1)} %bitcast.13), custom_call_target="tpu_custom_call" | custom-call | flops 671088640 | bytes 3408516 | tf_op jit(solution)/shard_map/pallas_call | solution.py:229
  51.0 30.1 %collective-permute-done.refs_2_ = bf16[20,8,512]{2,1,0:T(8,128)(2,1)S(1)} collective-permute-done((bf16[20,8,512]{2,1,0:T(8,128)(2,1)S(1)}, bf16[20,8,512]{2,1,0:T(8,128)(2,1)S(1)}, u32[]{:S(2)}, u32[]{:S(2)}) %collective-permute-start) | collective-permute-done | bytes 163872 | tf_op jit(solution)/shard_map/ppermute | solution.py:338
  81.1 12.3 %all-to-all-done.1.refs_5_ = bf16[256,8,512]{2,1,0:T(8,128)(2,1)} async-done(((bf16[256,8,512]{2,1,0:T(8,128)(2,1)}), bf16[256,8,512]{2,1,0:T(8,128)(2,1)}, u32[]{:S(2)}, u32[]{:S(2)}) %all-to-all-start.1) | async-done | bytes 2097184 | tf_op jit(solution)/shard_map/all_to_all | solution.py:335
  93.4 4.7 %shard_map.80 = (bf16[40,8,512]{2,1,0:T(8,128)(2,1)S(1)}, bf16[256,8,512]{2,1,0:T(8,128)(2,1)}, f32[8,512]{1,0:T(8,128)S(1)}) custom-call(s32[128,1]{1,0:T(8,128)S(1)} %bitcast.18, f32[40,8,512]{2,1,0:T(8,128)} %get-tuple-element.17.factor, s32[161]{0:T(256)S(1)} %pad_add_fusion.refs_0_, s32[160]{0:T(256)S(1)} %convert_add_fusion.refs_1_, ...), custom_call_target="tpu_custom_call" | custom-call | flops 1342177280 | bytes 8603396 | tf_op jit(solution)/shard_map/pallas_call | solution.py:229
  98.1 8.9 %all-to-all-start.2 = ((bf16[256,8,512]{2,1,0:T(8,128)(2,1)}), bf16[256,8,512]{2,1,0:T(8,128)(2,1)}, u32[]{:S(2)}, u32[]{:S(2)}) async-start(bf16[256,8,512]{2,1,0:T(8,128)(2,1)} %get-tuple-element.9), calls=%async_computation.2 | async-start | bytes 4194304 | tf_op jit(solution)/shard_map/all_to_all | solution.py:335
  107.1 2.9 %collective-permute-start.3 = (bf16[20,8,512]{2,1,0:T(8,128)(2,1)S(1)}, bf16[20,8,512]{2,1,0:T(8,128)(2,1)S(1)}, u32[]{:S(2)}, u32[]{:S(2)}) collective-permute-start(bf16[20,8,512]{2,1,0:T(8,128)(2,1)S(1)} %get-tuple-element.12), channel_id=1, source_target_pairs={{0,4},{4,0},{8,12},{12,8},{16,20},{20,16},{24,28},{28,24},{32,36},... | collective-permute-start | bytes 491528 | tf_op jit(solution)/shard_map/ppermute | solution.py:337
  110.0 2.9 %collective-permute-start.2 = (bf16[20,8,512]{2,1,0:T(8,128)(2,1)S(1)}, bf16[20,8,512]{2,1,0:T(8,128)(2,1)S(1)}, u32[]{:S(2)}, u32[]{:S(2)}) collective-permute-start(bf16[20,8,512]{2,1,0:T(8,128)(2,1)S(1)} %get-tuple-element.13), channel_id=1, source_target_pairs={{0,508},{4,8},{8,4},{12,16},{16,12},{20,24},{24,20},{28,32},{32,28... | collective-permute-start | bytes 491528 | tf_op jit(solution)/shard_map/ppermute | solution.py:338
  112.9 0.0 collective-permute-done.3.halo
  112.9 2.2 %shard_map.81.refs_4_ = f32[20,8,512]{2,1,0:T(8,128)} custom-call(s32[161]{0:T(256)S(1)} %pad_add_fusion.1.index, bf16[40,8,512]{2,1,0:T(8,128)(2,1)S(1)} %get-tuple-element.8.own.refs_3_, bf16[20,8,512]{2,1,0:T(8,128)(2,1)S(1)} %collective-permute-done.3.halo, bf16[4,512,512]{2,1,0:T(8,128)(2,1)S(1)} %copy-done, bf16[12,40,512]{2,1,0:T(8,128)(2,1)S(1)} %bitcast.15), custom_call_target="tpu_custom_call" | custom-call | flops 671088640 | bytes 3408516 | tf_op jit(solution)/shard_map/pallas_call | solution.py:229
  115.1 31.6 %collective-permute-done.2.refs_2_ = bf16[20,8,512]{2,1,0:T(8,128)(2,1)S(1)} collective-permute-done((bf16[20,8,512]{2,1,0:T(8,128)(2,1)S(1)}, bf16[20,8,512]{2,1,0:T(8,128)(2,1)S(1)}, u32[]{:S(2)}, u32[]{:S(2)}) %collective-permute-start.2) | collective-permute-done | bytes 163872 | tf_op jit(solution)/shard_map/ppermute | solution.py:338
  146.8 12.3 %all-to-all-done.2.refs_5_ = bf16[256,8,512]{2,1,0:T(8,128)(2,1)} async-done(((bf16[256,8,512]{2,1,0:T(8,128)(2,1)}), bf16[256,8,512]{2,1,0:T(8,128)(2,1)}, u32[]{:S(2)}, u32[]{:S(2)}) %all-to-all-start.2) | async-done | bytes 2097184 | tf_op jit(solution)/shard_map/all_to_all | solution.py:335
  159.1 3.1 %shard_map.82 = (f32[8,20480]{1,0:T(8,128)S(1)}, f32[128,16]{1,0:T(8,128)S(1)}) custom-call(f32[8,512]{1,0:T(8,128)S(1)} %get-tuple-element.7.first_squares, s32[161]{0:T(256)S(1)} %pad_add_fusion.refs_0_, s32[160]{0:T(256)S(1)} %convert_add_fusion.refs_1_, bf16[20,8,512]{2,1,0:T(8,128)(2,1)S(1)} %collective-permute-done.2.refs_2_, ...), custom_call_target="tpu_custom_call" | custom-call | flops 1342177280 | bytes 6186244 | tf_op jit(solution)/shard_map/pallas_call | solution.py:229
  162.2 19.8 %all_to_all.32 = f32[128,1,16]{2,1,0:T(1,128)S(1)} all-to-all(f32[128,1,16]{2,1,0:T(1,128)S(1)} %bitcast.20), channel_id=1, replica_groups=mesh['rows'=128,'tilt'=4] {'rows'}, dimensions={0} | all-to-all | bytes 16384 | tf_op jit(solution)/shard_map/all_to_all | solution.py:382
  182.1 1.6 shard_map.83
  (6 shorter events, 0.1 us)
Async XLA Ops:
  2.2 30.0 %all-to-all-start = ((s32[128,1,1]{2,1,0:T(1,128)}), s32[128,1,1]{2,1,0:T(1,128)S(1)}, u32[]{:S(2)}, u32[]{:S(2)}) async-start(s32[128,1,1]{2,1,0:T(1,128)} %bitcast.22), calls=%async_computation | async-start | bytes 131072 | tf_op jit(solution)/shard_map/all_to_all | solution.py:263
  34.3 13.3 %copy-start.2 = (s32[40,12]{0,1:T(8,128)S(1)}, s32[40,12]{0,1:T(8,128)}, u32[]{:S(2)}) copy-start(s32[40,12]{0,1:T(8,128)} %param.11) | copy-start | bytes 5764
  34.3 14.4 %copy-start = (bf16[4,512,512]{2,1,0:T(8,128)(2,1)S(1)}, bf16[4,512,512]{2,1,0:T(8,128)(2,1)}, u32[]{:S(2)}) copy-start(bf16[4,512,512]{2,1,0:T(8,128)(2,1)} %refs_6_.3) | copy-start | bytes 6291460
  34.3 14.4 %copy-start.1 = (bf16[40,12,512]{2,0,1:T(8,128)(2,1)S(1)}, bf16[40,12,512]{2,0,1:T(8,128)(2,1)}, u32[]{:S(2)}) copy-start(bf16[40,12,512]{2,0,1:T(8,128)(2,1)} %param.10) | copy-start | bytes 1474564
  34.3 59.1 %all-to-all-start.1 = ((bf16[256,8,512]{2,1,0:T(8,128)(2,1)}), bf16[256,8,512]{2,1,0:T(8,128)(2,1)}, u32[]{:S(2)}, u32[]{:S(2)}) async-start(bf16[256,8,512]{2,1,0:T(8,128)(2,1)} %shard_map.79), calls=%async_computation.1 | async-start | bytes 4194304 | tf_op jit(solution)/shard_map/all_to_all | solution.py:335
  42.0 6.7 %collective-permute-start.1 = (bf16[20,8,512]{2,1,0:T(8,128)(2,1)}, bf16[20,8,512]{2,1,0:T(8,128)(2,1)S(1)}, u32[]{:S(2)}, u32[]{:S(2)}) collective-permute-start(bf16[20,8,512]{2,1,0:T(8,128)(2,1)} %get-tuple-element.14), channel_id=1, source_target_pairs={{0,4},{4,0},{8,12},{12,8},{16,20},{20,16},{24,28},{28,24},{32,36},... | collective-permute-start | bytes 491528 | tf_op jit(solution)/shard_map/ppermute | solution.py:337
  45.0 36.1 %collective-permute-start = (bf16[20,8,512]{2,1,0:T(8,128)(2,1)S(1)}, bf16[20,8,512]{2,1,0:T(8,128)(2,1)S(1)}, u32[]{:S(2)}, u32[]{:S(2)}) collective-permute-start(bf16[20,8,512]{2,1,0:T(8,128)(2,1)S(1)} %get-tuple-element.15), channel_id=1, source_target_pairs={{0,508},{4,8},{8,4},{12,16},{16,12},{20,24},{24,20},{28,32},{32,28... | collective-permute-start | bytes 491528 | tf_op jit(solution)/shard_map/ppermute | solution.py:338
  98.1 61.0 %all-to-all-start.2 = ((bf16[256,8,512]{2,1,0:T(8,128)(2,1)}), bf16[256,8,512]{2,1,0:T(8,128)(2,1)}, u32[]{:S(2)}, u32[]{:S(2)}) async-start(bf16[256,8,512]{2,1,0:T(8,128)(2,1)} %get-tuple-element.9), calls=%async_computation.2 | async-start | bytes 4194304 | tf_op jit(solution)/shard_map/all_to_all | solution.py:335
  107.1 5.8 %collective-permute-start.3 = (bf16[20,8,512]{2,1,0:T(8,128)(2,1)S(1)}, bf16[20,8,512]{2,1,0:T(8,128)(2,1)S(1)}, u32[]{:S(2)}, u32[]{:S(2)}) collective-permute-start(bf16[20,8,512]{2,1,0:T(8,128)(2,1)S(1)} %get-tuple-element.12), channel_id=1, source_target_pairs={{0,4},{4,0},{8,12},{12,8},{16,20},{20,16},{24,28},{28,24},{32,36},... | collective-permute-start | bytes 491528 | tf_op jit(solution)/shard_map/ppermute | solution.py:337
  110.0 36.8 %collective-permute-start.2 = (bf16[20,8,512]{2,1,0:T(8,128)(2,1)S(1)}, bf16[20,8,512]{2,1,0:T(8,128)(2,1)S(1)}, u32[]{:S(2)}, u32[]{:S(2)}) collective-permute-start(bf16[20,8,512]{2,1,0:T(8,128)(2,1)S(1)} %get-tuple-element.13), channel_id=1, source_target_pairs={{0,508},{4,8},{8,4},{12,16},{16,12},{20,24},{24,20},{28,32},{32,28... | collective-permute-start | bytes 491528 | tf_op jit(solution)/shard_map/ppermute | solution.py:338

commit v14 on v13

--- a/solution.py
+++ b/solution.py
@@ -205,13 +205,11 @@
         jnp.int32, (tilts, tilts), 1
     )
     product = jnp.ones((tilts, 1), jnp.float32)
+    scales = []
     for j in range(ITERS):
         total = jnp.sum(jnp.where(across == tilt + j * tilts, totals, 0.0), axis=1, keepdims=True)
-        scale = jnp.sqrt(total / product / product / states + 1e-06)
-        product = product * scale
-        growth[j : j + 1, :] = jnp.sum(
-            jnp.where(diagonal, jnp.log(scale), 0.0), axis=0, keepdims=True
-        )
+        scales.append(jnp.sqrt(total / product / product / states + 1e-06))
+        product = product * scales[-1]
     inverse = 1.0 / product
     width = mapped.shape[1] // END_CHUNKS
     copies = []
@@ -219,6 +217,10 @@
         span = pl.ds(part * width, width)
         scaled[:, span] = mapped[:, span] * inverse
         copies.append(start_copy(scaled.at[:, span], iterate.at[:, span], sems.at[part]))
+    for j, scale in enumerate(scales):
+        growth[j : j + 1, :] = jnp.sum(
+            jnp.where(diagonal, jnp.log(scale), 0.0), axis=0, keepdims=True
+        )
     for copy in copies:
         copy.wait()
 

time: 184 us -> 184 us (level)
  no operation moved by 1% of the time
where the time goes in v14:
time: 184 us
  waiting for transfers between devices  94.9 us (52%)
  starting transfers between devices  45.7 us (25%)
  blocking collectives  19.8 us (11%)
  Pallas kernels  17.5 us (10%)
  other arithmetic  3.26 us (2%)
    ppermute x2, waiting for transfers between devices, on_device(): far_halo = lax.ppermute(jnp.where(odd, tail, head), 'rows', off_chip)  61.7 us
    all_to_all x2, waiting for transfers between devices, on_device(): lax.all_to_all(outgoing, 'rows', split_axis=0, concat_axis=0, tiled=True)  24.7 us
    all_to_all x1, blocking collectives, on_device(): lax.all_to_all(sums, 'rows', split_axis=0, concat_axis=0, tiled=True)  19.8 us
    all_to_all x1, starting transfers between devices, on_device(): lax.all_to_all(codes, 'rows', split_axis=0, concat_axis=0, tiled=True)  18.4 us
    pallas_call x7, Pallas kernels, call(): pl.pallas_call(kernel, out_shape=outs, in_specs=[spec[n not in in_vmem] f...  17.5 us
    all_to_all x2, starting transfers between devices, on_device(): lax.all_to_all(outgoing, 'rows', split_axis=0, concat_axis=0, tiled=True)  15.9 us
    all_to_all x1, waiting for transfers between devices, on_device(): lax.all_to_all(codes, 'rows', split_axis=0, concat_axis=0, tiled=True)  8.52 us
    ppermute x2, starting transfers between devices, on_device(): near_halo = lax.ppermute(jnp.where(odd, head, tail), 'rows', on_chip)  5.85 us
  transfers between devices with their start and end apart: 7, of which 5 were waited for; matrix products, arithmetic and copies ran while one was open for 3% of the time, Pallas kernels for 2%

profile of v14, /device:TPU:1, one launch (start us, length us, event | category | flops | bytes accessed | tf_op | source)
XLA Modules:
  0.0 183.8 jit_solution(5582323586610202215)
XLA Ops:
  0.6 1.6 shard_map.77
  2.2 18.4 %all-to-all-start = ((s32[128,1,1]{2,1,0:T(1,128)}), s32[128,1,1]{2,1,0:T(1,128)S(1)}, u32[]{:S(2)}, u32[]{:S(2)}) async-start(s32[128,1,1]{2,1,0:T(1,128)} %bitcast.22), calls=%async_computation | async-start | bytes 131072 | tf_op jit(solution)/shard_map/all_to_all | solution.py:265
  20.7 0.9 mul.31
  21.6 2.1 %multiply_convert_fusion = (bf16[40,8,512]{2,1,0:T(8,128)(2,1)S(1)}, f32[40,8,512]{2,1,0:T(8,128)}) fusion(f32[40,8,512]{2,1,0:T(8,128)} %bitcast.21, f32[40,512]{1,0:T(8,128)S(1)} %mul.31, f32[8]{0:T(128)} %param.8), kind=kLoop, calls=%fused_computation | loop fusion | flops 491520 | bytes 1720352 | tf_op jit(solution)/shard_map/convert_element_type | solution.py:326
  23.7 8.5 %all-to-all-done = s32[128,1,1]{2,1,0:T(1,128)S(1)} async-done(((s32[128,1,1]{2,1,0:T(1,128)}), s32[128,1,1]{2,1,0:T(1,128)S(1)}, u32[]{:S(2)}, u32[]{:S(2)}) %all-to-all-start) | async-done | bytes 544 | tf_op jit(solution)/shard_map/all_to_all | solution.py:265
  32.2 2.1 %shard_map.79 = bf16[256,8,512]{2,1,0:T(8,128)(2,1)} custom-call(s32[128,1]{1,0:T(8,128)S(1)} %bitcast.17, bf16[40,8,512]{2,1,0:T(8,128)(2,1)S(1)} %get-tuple-element.16.own.tilted.refs_3_), custom_call_target="tpu_custom_call" | custom-call | bytes 2425344 | tf_op jit(solution)/shard_map/pallas_call | solution.py:231
  34.3 0.0 copy-start.2
  34.3 0.0 copy-start
  34.3 0.0 copy-start.1
  34.3 7.0 %all-to-all-start.1 = ((bf16[256,8,512]{2,1,0:T(8,128)(2,1)}), bf16[256,8,512]{2,1,0:T(8,128)(2,1)}, u32[]{:S(2)}, u32[]{:S(2)}) async-start(bf16[256,8,512]{2,1,0:T(8,128)(2,1)} %shard_map.79), calls=%async_computation.1 | async-start | bytes 4194304 | tf_op jit(solution)/shard_map/all_to_all | solution.py:337
  41.3 0.7 broadcast_select_fusion.2
  42.0 3.0 %collective-permute-start.1 = (bf16[20,8,512]{2,1,0:T(8,128)(2,1)}, bf16[20,8,512]{2,1,0:T(8,128)(2,1)S(1)}, u32[]{:S(2)}, u32[]{:S(2)}) collective-permute-start(bf16[20,8,512]{2,1,0:T(8,128)(2,1)} %get-tuple-element.14), channel_id=1, source_target_pairs={{0,4},{4,0},{8,12},{12,8},{16,20},{20,16},{24,28},{28,24},{32,36},... | collective-permute-start | bytes 491528 | tf_op jit(solution)/shard_map/ppermute | solution.py:339
  45.0 2.6 %collective-permute-start = (bf16[20,8,512]{2,1,0:T(8,128)(2,1)S(1)}, bf16[20,8,512]{2,1,0:T(8,128)(2,1)S(1)}, u32[]{:S(2)}, u32[]{:S(2)}) collective-permute-start(bf16[20,8,512]{2,1,0:T(8,128)(2,1)S(1)} %get-tuple-element.15), channel_id=1, source_target_pairs={{0,508},{4,8},{8,4},{12,16},{16,12},{20,24},{24,20},{28,32},{32,28... | collective-permute-start | bytes 491528 | tf_op jit(solution)/shard_map/ppermute | solution.py:340
  47.6 0.0 copy-done.2
  47.7 0.1 constant_dynamic-slice_fusion
  47.8 0.1 copy.32
  47.9 0.1 reshape.41
  48.0 0.1 copy.31
  48.0 0.1 reshape.39
  48.2 0.2 and_reduce_fusion
  48.4 0.1 pad_add_fusion.1.index
  48.5 0.1 copy.30
  48.6 0.1 reshape.38
  48.7 0.1 pad_add_fusion.refs_0_
  48.7 0.0 collective-permute-done.1.halo
  48.7 0.0 copy-done
  48.7 0.0 copy-done.1
  48.7 2.2 %shard_map.78.refs_4_ = f32[20,8,512]{2,1,0:T(8,128)} custom-call(s32[161]{0:T(256)S(1)} %pad_add_fusion.1.index, bf16[40,8,512]{2,1,0:T(8,128)(2,1)S(1)} %get-tuple-element.16.own.tilted.refs_3_, bf16[20,8,512]{2,1,0:T(8,128)(2,1)S(1)} %collective-permute-done.1.halo, bf16[4,512,512]{2,1,0:T(8,128)(2,1)S(1)} %copy-done, bf16[12,40,512]{2,1,0:T(8,128)(2,1)S(1)} %bitcast.13), custom_call_target="tpu_custom_call" | custom-call | flops 671088640 | bytes 3408516 | tf_op jit(solution)/shard_map/pallas_call | solution.py:231
  51.0 30.1 %collective-permute-done.refs_2_ = bf16[20,8,512]{2,1,0:T(8,128)(2,1)S(1)} collective-permute-done((bf16[20,8,512]{2,1,0:T(8,128)(2,1)S(1)}, bf16[20,8,512]{2,1,0:T(8,128)(2,1)S(1)}, u32[]{:S(2)}, u32[]{:S(2)}) %collective-permute-start) | collective-permute-done | bytes 163872 | tf_op jit(solution)/shard_map/ppermute | solution.py:340
  81.1 12.3 %all-to-all-done.1.refs_5_ = bf16[256,8,512]{2,1,0:T(8,128)(2,1)} async-done(((bf16[256,8,512]{2,1,0:T(8,128)(2,1)}), bf16[256,8,512]{2,1,0:T(8,128)(2,1)}, u32[]{:S(2)}, u32[]{:S(2)}) %all-to-all-start.1) | async-done | bytes 2097184 | tf_op jit(solution)/shard_map/all_to_all | solution.py:337
  93.4 4.7 %shard_map.80 = (bf16[40,8,512]{2,1,0:T(8,128)(2,1)S(1)}, bf16[256,8,512]{2,1,0:T(8,128)(2,1)}, f32[8,512]{1,0:T(8,128)S(1)}) custom-call(s32[128,1]{1,0:T(8,128)S(1)} %bitcast.18, f32[40,8,512]{2,1,0:T(8,128)} %get-tuple-element.17.factor, s32[161]{0:T(256)S(1)} %pad_add_fusion.refs_0_, s32[160]{0:T(256)S(1)} %convert_add_fusion.refs_1_, ...), custom_call_target="tpu_custom_call" | custom-call | flops 1342177280 | bytes 8603396 | tf_op jit(solution)/shard_map/pallas_call | solution.py:231
  98.1 8.9 %all-to-all-start.2 = ((bf16[256,8,512]{2,1,0:T(8,128)(2,1)}), bf16[256,8,512]{2,1,0:T(8,128)(2,1)}, u32[]{:S(2)}, u32[]{:S(2)}) async-start(bf16[256,8,512]{2,1,0:T(8,128)(2,1)} %get-tuple-element.9), calls=%async_computation.2 | async-start | bytes 4194304 | tf_op jit(solution)/shard_map/all_to_all | solution.py:337
  107.1 2.9 %collective-permute-start.3 = (bf16[20,8,512]{2,1,0:T(8,128)(2,1)S(1)}, bf16[20,8,512]{2,1,0:T(8,128)(2,1)S(1)}, u32[]{:S(2)}, u32[]{:S(2)}) collective-permute-start(bf16[20,8,512]{2,1,0:T(8,128)(2,1)S(1)} %get-tuple-element.12), channel_id=1, source_target_pairs={{0,4},{4,0},{8,12},{12,8},{16,20},{20,16},{24,28},{28,24},{32,36},... | collective-permute-start | bytes 491528 | tf_op jit(solution)/shard_map/ppermute | solution.py:339
  110.0 2.9 %collective-permute-start.2 = (bf16[20,8,512]{2,1,0:T(8,128)(2,1)S(1)}, bf16[20,8,512]{2,1,0:T(8,128)(2,1)S(1)}, u32[]{:S(2)}, u32[]{:S(2)}) collective-permute-start(bf16[20,8,512]{2,1,0:T(8,128)(2,1)S(1)} %get-tuple-element.13), channel_id=1, source_target_pairs={{0,508},{4,8},{8,4},{12,16},{16,12},{20,24},{24,20},{28,32},{32,28... | collective-permute-start | bytes 491528 | tf_op jit(solution)/shard_map/ppermute | solution.py:340
  112.9 0.0 collective-permute-done.3.halo
  112.9 2.2 %shard_map.81.refs_4_ = f32[20,8,512]{2,1,0:T(8,128)} custom-call(s32[161]{0:T(256)S(1)} %pad_add_fusion.1.index, bf16[40,8,512]{2,1,0:T(8,128)(2,1)S(1)} %get-tuple-element.8.own.refs_3_, bf16[20,8,512]{2,1,0:T(8,128)(2,1)S(1)} %collective-permute-done.3.halo, bf16[4,512,512]{2,1,0:T(8,128)(2,1)S(1)} %copy-done, bf16[12,40,512]{2,1,0:T(8,128)(2,1)S(1)} %bitcast.15), custom_call_target="tpu_custom_call" | custom-call | flops 671088640 | bytes 3408516 | tf_op jit(solution)/shard_map/pallas_call | solution.py:231
  115.1 31.6 %collective-permute-done.2.refs_2_ = bf16[20,8,512]{2,1,0:T(8,128)(2,1)S(1)} collective-permute-done((bf16[20,8,512]{2,1,0:T(8,128)(2,1)S(1)}, bf16[20,8,512]{2,1,0:T(8,128)(2,1)S(1)}, u32[]{:S(2)}, u32[]{:S(2)}) %collective-permute-start.2) | collective-permute-done | bytes 163872 | tf_op jit(solution)/shard_map/ppermute | solution.py:340
  146.8 12.3 %all-to-all-done.2.refs_5_ = bf16[256,8,512]{2,1,0:T(8,128)(2,1)} async-done(((bf16[256,8,512]{2,1,0:T(8,128)(2,1)}), bf16[256,8,512]{2,1,0:T(8,128)(2,1)}, u32[]{:S(2)}, u32[]{:S(2)}) %all-to-all-start.2) | async-done | bytes 2097184 | tf_op jit(solution)/shard_map/all_to_all | solution.py:337
  159.1 3.1 %shard_map.82 = (f32[8,20480]{1,0:T(8,128)S(1)}, f32[128,16]{1,0:T(8,128)S(1)}) custom-call(f32[8,512]{1,0:T(8,128)S(1)} %get-tuple-element.7.first_squares, s32[161]{0:T(256)S(1)} %pad_add_fusion.refs_0_, s32[160]{0:T(256)S(1)} %convert_add_fusion.refs_1_, bf16[20,8,512]{2,1,0:T(8,128)(2,1)S(1)} %collective-permute-done.2.refs_2_, ...), custom_call_target="tpu_custom_call" | custom-call | flops 1342177280 | bytes 6186244 | tf_op jit(solution)/shard_map/pallas_call | solution.py:231
  162.2 19.8 %all_to_all.32 = f32[128,1,16]{2,1,0:T(1,128)S(1)} all-to-all(f32[128,1,16]{2,1,0:T(1,128)S(1)} %bitcast.20), channel_id=1, replica_groups=mesh['rows'=128,'tilt'=4] {'rows'}, dimensions={0} | all-to-all | bytes 16384 | tf_op jit(solution)/shard_map/all_to_all | solution.py:384
  182.1 1.6 shard_map.83
  (6 shorter events, 0.1 us)
Async XLA Ops:
  2.2 30.0 %all-to-all-start = ((s32[128,1,1]{2,1,0:T(1,128)}), s32[128,1,1]{2,1,0:T(1,128)S(1)}, u32[]{:S(2)}, u32[]{:S(2)}) async-start(s32[128,1,1]{2,1,0:T(1,128)} %bitcast.22), calls=%async_computation | async-start | bytes 131072 | tf_op jit(solution)/shard_map/all_to_all | solution.py:265
  34.3 13.3 %copy-start.2 = (s32[40,12]{0,1:T(8,128)S(1)}, s32[40,12]{0,1:T(8,128)}, u32[]{:S(2)}) copy-start(s32[40,12]{0,1:T(8,128)} %param.11) | copy-start | bytes 5764
  34.3 14.4 %copy-start = (bf16[4,512,512]{2,1,0:T(8,128)(2,1)S(1)}, bf16[4,512,512]{2,1,0:T(8,128)(2,1)}, u32[]{:S(2)}) copy-start(bf16[4,512,512]{2,1,0:T(8,128)(2,1)} %refs_6_.3) | copy-start | bytes 6291460
  34.3 14.4 %copy-start.1 = (bf16[40,12,512]{2,0,1:T(8,128)(2,1)S(1)}, bf16[40,12,512]{2,0,1:T(8,128)(2,1)}, u32[]{:S(2)}) copy-start(bf16[40,12,512]{2,0,1:T(8,128)(2,1)} %param.10) | copy-start | bytes 1474564
  34.3 59.1 %all-to-all-start.1 = ((bf16[256,8,512]{2,1,0:T(8,128)(2,1)}), bf16[256,8,512]{2,1,0:T(8,128)(2,1)}, u32[]{:S(2)}, u32[]{:S(2)}) async-start(bf16[256,8,512]{2,1,0:T(8,128)(2,1)} %shard_map.79), calls=%async_computation.1 | async-start | bytes 4194304 | tf_op jit(solution)/shard_map/all_to_all | solution.py:337
  42.0 6.7 %collective-permute-start.1 = (bf16[20,8,512]{2,1,0:T(8,128)(2,1)}, bf16[20,8,512]{2,1,0:T(8,128)(2,1)S(1)}, u32[]{:S(2)}, u32[]{:S(2)}) collective-permute-start(bf16[20,8,512]{2,1,0:T(8,128)(2,1)} %get-tuple-element.14), channel_id=1, source_target_pairs={{0,4},{4,0},{8,12},{12,8},{16,20},{20,16},{24,28},{28,24},{32,36},... | collective-permute-start | bytes 491528 | tf_op jit(solution)/shard_map/ppermute | solution.py:339
  45.0 36.1 %collective-permute-start = (bf16[20,8,512]{2,1,0:T(8,128)(2,1)S(1)}, bf16[20,8,512]{2,1,0:T(8,128)(2,1)S(1)}, u32[]{:S(2)}, u32[]{:S(2)}) collective-permute-start(bf16[20,8,512]{2,1,0:T(8,128)(2,1)S(1)} %get-tuple-element.15), channel_id=1, source_target_pairs={{0,508},{4,8},{8,4},{12,16},{16,12},{20,24},{24,20},{28,32},{32,28... | collective-permute-start | bytes 491528 | tf_op jit(solution)/shard_map/ppermute | solution.py:340
  98.1 61.0 %all-to-all-start.2 = ((bf16[256,8,512]{2,1,0:T(8,128)(2,1)}), bf16[256,8,512]{2,1,0:T(8,128)(2,1)}, u32[]{:S(2)}, u32[]{:S(2)}) async-start(bf16[256,8,512]{2,1,0:T(8,128)(2,1)} %get-tuple-element.9), calls=%async_computation.2 | async-start | bytes 4194304 | tf_op jit(solution)/shard_map/all_to_all | solution.py:337
  107.1 5.8 %collective-permute-start.3 = (bf16[20,8,512]{2,1,0:T(8,128)(2,1)S(1)}, bf16[20,8,512]{2,1,0:T(8,128)(2,1)S(1)}, u32[]{:S(2)}, u32[]{:S(2)}) collective-permute-start(bf16[20,8,512]{2,1,0:T(8,128)(2,1)S(1)} %get-tuple-element.12), channel_id=1, source_target_pairs={{0,4},{4,0},{8,12},{12,8},{16,20},{20,16},{24,28},{28,24},{32,36},... | collective-permute-start | bytes 491528 | tf_op jit(solution)/shard_map/ppermute | solution.py:339
  110.0 36.8 %collective-permute-start.2 = (bf16[20,8,512]{2,1,0:T(8,128)(2,1)S(1)}, bf16[20,8,512]{2,1,0:T(8,128)(2,1)S(1)}, u32[]{:S(2)}, u32[]{:S(2)}) collective-permute-start(bf16[20,8,512]{2,1,0:T(8,128)(2,1)S(1)} %get-tuple-element.13), channel_id=1, source_target_pairs={{0,508},{4,8},{8,4},{12,16},{16,12},{20,24},{24,20},{28,32},{32,28... | collective-permute-start | bytes 491528 | tf_op jit(solution)/shard_map/ppermute | solution.py:340

commit v15 on v14

--- a/solution.py
+++ b/solution.py
@@ -9,7 +9,7 @@
 
 NEAR = 8
 ITERS = 2
-PACK_CHUNKS = 8
+PACK_CHUNKS = 4
 END_CHUNKS = 4
 HALF_WORD = 1 << 16
 REQUEST_LIMIT = 62 * 1024 * 1024

time: 184 us -> 184 us (level)
  no operation moved by 1% of the time
where the time goes in v15:
time: 184 us
  waiting for transfers between devices  94.9 us (52%)
  starting transfers between devices  45.7 us (25%)
  blocking collectives  19.8 us (11%)
  Pallas kernels  17.5 us (10%)
  other arithmetic  3.26 us (2%)
    ppermute x2, waiting for transfers between devices, on_device(): far_halo = lax.ppermute(jnp.where(odd, tail, head), 'rows', off_chip)  61.7 us
    all_to_all x2, waiting for transfers between devices, on_device(): lax.all_to_all(outgoing, 'rows', split_axis=0, concat_axis=0, tiled=True)  24.7 us
    all_to_all x1, blocking collectives, on_device(): lax.all_to_all(sums, 'rows', split_axis=0, concat_axis=0, tiled=True)  19.8 us
    all_to_all x1, starting transfers between devices, on_device(): lax.all_to_all(codes, 'rows', split_axis=0, concat_axis=0, tiled=True)  18.4 us
    pallas_call x7, Pallas kernels, call(): pl.pallas_call(kernel, out_shape=outs, in_specs=[spec[n not in in_vmem] f...  17.5 us
    all_to_all x2, starting transfers between devices, on_device(): lax.all_to_all(outgoing, 'rows', split_axis=0, concat_axis=0, tiled=True)  15.9 us
    all_to_all x1, waiting for transfers between devices, on_device(): lax.all_to_all(codes, 'rows', split_axis=0, concat_axis=0, tiled=True)  8.52 us
    ppermute x2, starting transfers between devices, on_device(): near_halo = lax.ppermute(jnp.where(odd, head, tail), 'rows', on_chip)  5.85 us
  transfers between devices with their start and end apart: 7, of which 5 were waited for; matrix products, arithmetic and copies ran while one was open for 3% of the time, Pallas kernels for 2%

profile of v15, /device:TPU:1, one launch (start us, length us, event | category | flops | bytes accessed | tf_op | source)
XLA Modules:
  0.0 183.8 jit_solution(13505760487394066373)
XLA Ops:
  0.6 1.6 shard_map.77
  2.2 18.4 %all-to-all-start = ((s32[128,1,1]{2,1,0:T(1,128)}), s32[128,1,1]{2,1,0:T(1,128)S(1)}, u32[]{:S(2)}, u32[]{:S(2)}) async-start(s32[128,1,1]{2,1,0:T(1,128)} %bitcast.22), calls=%async_computation | async-start | bytes 131072 | tf_op jit(solution)/shard_map/all_to_all | solution.py:265
  20.7 0.9 mul.31
  21.6 2.1 %multiply_convert_fusion = (bf16[40,8,512]{2,1,0:T(8,128)(2,1)S(1)}, f32[40,8,512]{2,1,0:T(8,128)}) fusion(f32[40,8,512]{2,1,0:T(8,128)} %bitcast.21, f32[40,512]{1,0:T(8,128)S(1)} %mul.31, f32[8]{0:T(128)} %param.8), kind=kLoop, calls=%fused_computation | loop fusion | flops 491520 | bytes 1720352 | tf_op jit(solution)/shard_map/convert_element_type | solution.py:326
  23.7 8.5 %all-to-all-done = s32[128,1,1]{2,1,0:T(1,128)S(1)} async-done(((s32[128,1,1]{2,1,0:T(1,128)}), s32[128,1,1]{2,1,0:T(1,128)S(1)}, u32[]{:S(2)}, u32[]{:S(2)}) %all-to-all-start) | async-done | bytes 544 | tf_op jit(solution)/shard_map/all_to_all | solution.py:265
  32.2 2.1 %shard_map.79 = bf16[256,8,512]{2,1,0:T(8,128)(2,1)} custom-call(s32[128,1]{1,0:T(8,128)S(1)} %bitcast.17, bf16[40,8,512]{2,1,0:T(8,128)(2,1)S(1)} %get-tuple-element.16.own.tilted.refs_3_), custom_call_target="tpu_custom_call" | custom-call | bytes 2425344 | tf_op jit(solution)/shard_map/pallas_call | solution.py:231
  34.3 0.0 copy-start.2
  34.3 0.0 copy-start
  34.3 0.0 copy-start.1
  34.3 7.0 %all-to-all-start.1 = ((bf16[256,8,512]{2,1,0:T(8,128)(2,1)}), bf16[256,8,512]{2,1,0:T(8,128)(2,1)}, u32[]{:S(2)}, u32[]{:S(2)}) async-start(bf16[256,8,512]{2,1,0:T(8,128)(2,1)} %shard_map.79), calls=%async_computation.1 | async-start | bytes 4194304 | tf_op jit(solution)/shard_map/all_to_all | solution.py:337
  41.3 0.7 broadcast_select_fusion.2
  42.0 3.0 %collective-permute-start.1 = (bf16[20,8,512]{2,1,0:T(8,128)(2,1)}, bf16[20,8,512]{2,1,0:T(8,128)(2,1)S(1)}, u32[]{:S(2)}, u32[]{:S(2)}) collective-permute-start(bf16[20,8,512]{2,1,0:T(8,128)(2,1)} %get-tuple-element.14), channel_id=1, source_target_pairs={{0,4},{4,0},{8,12},{12,8},{16,20},{20,16},{24,28},{28,24},{32,36},... | collective-permute-start | bytes 491528 | tf_op jit(solution)/shard_map/ppermute | solution.py:339
  45.0 2.6 %collective-permute-start = (bf16[20,8,512]{2,1,0:T(8,128)(2,1)S(1)}, bf16[20,8,512]{2,1,0:T(8,128)(2,1)S(1)}, u32[]{:S(2)}, u32[]{:S(2)}) collective-permute-start(bf16[20,8,512]{2,1,0:T(8,128)(2,1)S(1)} %get-tuple-element.15), channel_id=1, source_target_pairs={{0,508},{4,8},{8,4},{12,16},{16,12},{20,24},{24,20},{28,32},{32,28... | collective-permute-start | bytes 491528 | tf_op jit(solution)/shard_map/ppermute | solution.py:340
  47.6 0.0 copy-done.2
  47.7 0.1 constant_dynamic-slice_fusion
  47.8 0.1 copy.32
  47.9 0.1 reshape.41
  48.0 0.1 copy.31
  48.1 0.1 reshape.39
  48.2 0.2 and_reduce_fusion
  48.4 0.1 pad_add_fusion.1.index
  48.5 0.1 copy.30
  48.6 0.1 reshape.38
  48.7 0.1 pad_add_fusion.refs_0_
  48.7 0.0 collective-permute-done.1.halo
  48.7 0.0 copy-done
  48.7 0.0 copy-done.1
  48.8 2.2 %shard_map.78.refs_4_ = f32[20,8,512]{2,1,0:T(8,128)} custom-call(s32[161]{0:T(256)S(1)} %pad_add_fusion.1.index, bf16[40,8,512]{2,1,0:T(8,128)(2,1)S(1)} %get-tuple-element.16.own.tilted.refs_3_, bf16[20,8,512]{2,1,0:T(8,128)(2,1)S(1)} %collective-permute-done.1.halo, bf16[4,512,512]{2,1,0:T(8,128)(2,1)S(1)} %copy-done, bf16[12,40,512]{2,1,0:T(8,128)(2,1)S(1)} %bitcast.13), custom_call_target="tpu_custom_call" | custom-call | flops 671088640 | bytes 3408516 | tf_op jit(solution)/shard_map/pallas_call | solution.py:231
  51.0 30.1 %collective-permute-done.refs_2_ = bf16[20,8,512]{2,1,0:T(8,128)(2,1)S(1)} collective-permute-done((bf16[20,8,512]{2,1,0:T(8,128)(2,1)S(1)}, bf16[20,8,512]{2,1,0:T(8,128)(2,1)S(1)}, u32[]{:S(2)}, u32[]{:S(2)}) %collective-permute-start) | collective-permute-done | bytes 163872 | tf_op jit(solution)/shard_map/ppermute | solution.py:340
  81.1 12.3 %all-to-all-done.1.refs_5_ = bf16[256,8,512]{2,1,0:T(8,128)(2,1)} async-done(((bf16[256,8,512]{2,1,0:T(8,128)(2,1)}), bf16[256,8,512]{2,1,0:T(8,128)(2,1)}, u32[]{:S(2)}, u32[]{:S(2)}) %all-to-all-start.1) | async-done | bytes 2097184 | tf_op jit(solution)/shard_map/all_to_all | solution.py:337
  93.4 4.7 %shard_map.80 = (bf16[40,8,512]{2,1,0:T(8,128)(2,1)S(1)}, bf16[256,8,512]{2,1,0:T(8,128)(2,1)}, f32[8,512]{1,0:T(8,128)S(1)}) custom-call(s32[128,1]{1,0:T(8,128)S(1)} %bitcast.18, f32[40,8,512]{2,1,0:T(8,128)} %get-tuple-element.17.factor, s32[161]{0:T(256)S(1)} %pad_add_fusion.refs_0_, s32[160]{0:T(256)S(1)} %convert_add_fusion.refs_1_, ...), custom_call_target="tpu_custom_call" | custom-call | flops 1342177280 | bytes 8603396 | tf_op jit(solution)/shard_map/pallas_call | solution.py:231
  98.1 8.9 %all-to-all-start.2 = ((bf16[256,8,512]{2,1,0:T(8,128)(2,1)}), bf16[256,8,512]{2,1,0:T(8,128)(2,1)}, u32[]{:S(2)}, u32[]{:S(2)}) async-start(bf16[256,8,512]{2,1,0:T(8,128)(2,1)} %get-tuple-element.9), calls=%async_computation.2 | async-start | bytes 4194304 | tf_op jit(solution)/shard_map/all_to_all | solution.py:337
  107.1 2.9 %collective-permute-start.3 = (bf16[20,8,512]{2,1,0:T(8,128)(2,1)S(1)}, bf16[20,8,512]{2,1,0:T(8,128)(2,1)S(1)}, u32[]{:S(2)}, u32[]{:S(2)}) collective-permute-start(bf16[20,8,512]{2,1,0:T(8,128)(2,1)S(1)} %get-tuple-element.12), channel_id=1, source_target_pairs={{0,4},{4,0},{8,12},{12,8},{16,20},{20,16},{24,28},{28,24},{32,36},... | collective-permute-start | bytes 491528 | tf_op jit(solution)/shard_map/ppermute | solution.py:339
  110.0 2.9 %collective-permute-start.2 = (bf16[20,8,512]{2,1,0:T(8,128)(2,1)S(1)}, bf16[20,8,512]{2,1,0:T(8,128)(2,1)S(1)}, u32[]{:S(2)}, u32[]{:S(2)}) collective-permute-start(bf16[20,8,512]{2,1,0:T(8,128)(2,1)S(1)} %get-tuple-element.13), channel_id=1, source_target_pairs={{0,508},{4,8},{8,4},{12,16},{16,12},{20,24},{24,20},{28,32},{32,28... | collective-permute-start | bytes 491528 | tf_op jit(solution)/shard_map/ppermute | solution.py:340
  112.9 0.0 collective-permute-done.3.halo
  112.9 2.2 %shard_map.81.refs_4_ = f32[20,8,512]{2,1,0:T(8,128)} custom-call(s32[161]{0:T(256)S(1)} %pad_add_fusion.1.index, bf16[40,8,512]{2,1,0:T(8,128)(2,1)S(1)} %get-tuple-element.8.own.refs_3_, bf16[20,8,512]{2,1,0:T(8,128)(2,1)S(1)} %collective-permute-done.3.halo, bf16[4,512,512]{2,1,0:T(8,128)(2,1)S(1)} %copy-done, bf16[12,40,512]{2,1,0:T(8,128)(2,1)S(1)} %bitcast.15), custom_call_target="tpu_custom_call" | custom-call | flops 671088640 | bytes 3408516 | tf_op jit(solution)/shard_map/pallas_call | solution.py:231
  115.2 31.6 %collective-permute-done.2.refs_2_ = bf16[20,8,512]{2,1,0:T(8,128)(2,1)S(1)} collective-permute-done((bf16[20,8,512]{2,1,0:T(8,128)(2,1)S(1)}, bf16[20,8,512]{2,1,0:T(8,128)(2,1)S(1)}, u32[]{:S(2)}, u32[]{:S(2)}) %collective-permute-start.2) | collective-permute-done | bytes 163872 | tf_op jit(solution)/shard_map/ppermute | solution.py:340
  146.8 12.3 %all-to-all-done.2.refs_5_ = bf16[256,8,512]{2,1,0:T(8,128)(2,1)} async-done(((bf16[256,8,512]{2,1,0:T(8,128)(2,1)}), bf16[256,8,512]{2,1,0:T(8,128)(2,1)}, u32[]{:S(2)}, u32[]{:S(2)}) %all-to-all-start.2) | async-done | bytes 2097184 | tf_op jit(solution)/shard_map/all_to_all | solution.py:337
  159.1 3.1 %shard_map.82 = (f32[8,20480]{1,0:T(8,128)S(1)}, f32[128,16]{1,0:T(8,128)S(1)}) custom-call(f32[8,512]{1,0:T(8,128)S(1)} %get-tuple-element.7.first_squares, s32[161]{0:T(256)S(1)} %pad_add_fusion.refs_0_, s32[160]{0:T(256)S(1)} %convert_add_fusion.refs_1_, bf16[20,8,512]{2,1,0:T(8,128)(2,1)S(1)} %collective-permute-done.2.refs_2_, ...), custom_call_target="tpu_custom_call" | custom-call | flops 1342177280 | bytes 6186244 | tf_op jit(solution)/shard_map/pallas_call | solution.py:231
  162.2 19.8 %all_to_all.32 = f32[128,1,16]{2,1,0:T(1,128)S(1)} all-to-all(f32[128,1,16]{2,1,0:T(1,128)S(1)} %bitcast.20), channel_id=1, replica_groups=mesh['rows'=128,'tilt'=4] {'rows'}, dimensions={0} | all-to-all | bytes 16384 | tf_op jit(solution)/shard_map/all_to_all | solution.py:384
  182.1 1.6 shard_map.83
  (6 shorter events, 0.1 us)
Async XLA Ops:
  2.2 30.0 %all-to-all-start = ((s32[128,1,1]{2,1,0:T(1,128)}), s32[128,1,1]{2,1,0:T(1,128)S(1)}, u32[]{:S(2)}, u32[]{:S(2)}) async-start(s32[128,1,1]{2,1,0:T(1,128)} %bitcast.22), calls=%async_computation | async-start | bytes 131072 | tf_op jit(solution)/shard_map/all_to_all | solution.py:265
  34.3 13.3 %copy-start.2 = (s32[40,12]{0,1:T(8,128)S(1)}, s32[40,12]{0,1:T(8,128)}, u32[]{:S(2)}) copy-start(s32[40,12]{0,1:T(8,128)} %param.11) | copy-start | bytes 5764
  34.3 14.4 %copy-start = (bf16[4,512,512]{2,1,0:T(8,128)(2,1)S(1)}, bf16[4,512,512]{2,1,0:T(8,128)(2,1)}, u32[]{:S(2)}) copy-start(bf16[4,512,512]{2,1,0:T(8,128)(2,1)} %refs_6_.3) | copy-start | bytes 6291460
  34.3 14.4 %copy-start.1 = (bf16[40,12,512]{2,0,1:T(8,128)(2,1)S(1)}, bf16[40,12,512]{2,0,1:T(8,128)(2,1)}, u32[]{:S(2)}) copy-start(bf16[40,12,512]{2,0,1:T(8,128)(2,1)} %param.10) | copy-start | bytes 1474564
  34.3 59.1 %all-to-all-start.1 = ((bf16[256,8,512]{2,1,0:T(8,128)(2,1)}), bf16[256,8,512]{2,1,0:T(8,128)(2,1)}, u32[]{:S(2)}, u32[]{:S(2)}) async-start(bf16[256,8,512]{2,1,0:T(8,128)(2,1)} %shard_map.79), calls=%async_computation.1 | async-start | bytes 4194304 | tf_op jit(solution)/shard_map/all_to_all | solution.py:337
  42.0 6.7 %collective-permute-start.1 = (bf16[20,8,512]{2,1,0:T(8,128)(2,1)}, bf16[20,8,512]{2,1,0:T(8,128)(2,1)S(1)}, u32[]{:S(2)}, u32[]{:S(2)}) collective-permute-start(bf16[20,8,512]{2,1,0:T(8,128)(2,1)} %get-tuple-element.14), channel_id=1, source_target_pairs={{0,4},{4,0},{8,12},{12,8},{16,20},{20,16},{24,28},{28,24},{32,36},... | collective-permute-start | bytes 491528 | tf_op jit(solution)/shard_map/ppermute | solution.py:339
  45.0 36.1 %collective-permute-start = (bf16[20,8,512]{2,1,0:T(8,128)(2,1)S(1)}, bf16[20,8,512]{2,1,0:T(8,128)(2,1)S(1)}, u32[]{:S(2)}, u32[]{:S(2)}) collective-permute-start(bf16[20,8,512]{2,1,0:T(8,128)(2,1)S(1)} %get-tuple-element.15), channel_id=1, source_target_pairs={{0,508},{4,8},{8,4},{12,16},{16,12},{20,24},{24,20},{28,32},{32,28... | collective-permute-start | bytes 491528 | tf_op jit(solution)/shard_map/ppermute | solution.py:340
  98.1 61.0 %all-to-all-start.2 = ((bf16[256,8,512]{2,1,0:T(8,128)(2,1)}), bf16[256,8,512]{2,1,0:T(8,128)(2,1)}, u32[]{:S(2)}, u32[]{:S(2)}) async-start(bf16[256,8,512]{2,1,0:T(8,128)(2,1)} %get-tuple-element.9), calls=%async_computation.2 | async-start | bytes 4194304 | tf_op jit(solution)/shard_map/all_to_all | solution.py:337
  107.1 5.8 %collective-permute-start.3 = (bf16[20,8,512]{2,1,0:T(8,128)(2,1)S(1)}, bf16[20,8,512]{2,1,0:T(8,128)(2,1)S(1)}, u32[]{:S(2)}, u32[]{:S(2)}) collective-permute-start(bf16[20,8,512]{2,1,0:T(8,128)(2,1)S(1)} %get-tuple-element.12), channel_id=1, source_target_pairs={{0,4},{4,0},{8,12},{12,8},{16,20},{20,16},{24,28},{28,24},{32,36},... | collective-permute-start | bytes 491528 | tf_op jit(solution)/shard_map/ppermute | solution.py:339
  110.0 36.8 %collective-permute-start.2 = (bf16[20,8,512]{2,1,0:T(8,128)(2,1)S(1)}, bf16[20,8,512]{2,1,0:T(8,128)(2,1)S(1)}, u32[]{:S(2)}, u32[]{:S(2)}) collective-permute-start(bf16[20,8,512]{2,1,0:T(8,128)(2,1)S(1)} %get-tuple-element.13), channel_id=1, source_target_pairs={{0,508},{4,8},{8,4},{12,16},{16,12},{20,24},{24,20},{28,32},{32,28... | collective-permute-start | bytes 491528 | tf_op jit(solution)/shard_map/ppermute | solution.py:340
